TPU v7x, 32 devices: a whole 2x2x4 slice. The times are simulated.
32 devices in a mesh: ctx: 8 (over z, x), wshard: 4 (over y, core).
Axes of the slice: x: 2, y: 2, z: 4, core: 2. Of those that a mesh axis runs over, the one named last changes fastest.
Arguments:
- tokens: bfloat16 [4, 4096, 1024], P('wshard', 'ctx'), may hold values from -6 to 6
- cotangent: bfloat16 [4, 4096, 1024], P('wshard', 'ctx'), may hold values from -6 to 6
- doc_lengths: int32 [4, 4], P('wshard'), may hold values from 1 to 4093, as said below
- decay: float32 [4, 24, 4096], P('wshard', None, 'ctx')
- norm_gain: bfloat16 [1024], P('wshard'), may hold values from 0.25 to 1.75
- in_proj: bfloat16 [1024, 3328], P('wshard'), may hold values from -0.1875 to 0.1875
- conv_weight: bfloat16 [4, 1792], P(None, 'wshard'), may hold values from -3 to 3
- conv_bias: bfloat16 [1792], P('wshard'), may hold values from -3 to 3
- skip_gain: bfloat16 [24], P('wshard'), may hold values from 0.5 to 1.5
- mixer_gain: bfloat16 [1536], P('wshard'), may hold values from 0.25 to 1.75
- mixer_out: bfloat16 [1536, 1024], P('wshard'), may hold values from -0.15625 to 0.15625
- query_proj: bfloat16 [1024, 512], P('wshard'), may hold values from -0.1875 to 0.1875
- key_value_projection: bfloat16 [1024, 256], P('wshard'), may hold values from -0.1875 to 0.1875
- attn_out: bfloat16 [512, 1024], P('wshard'), may hold values from -3 to 3
- ffn_gain: bfloat16 [1024], P('wshard'), may hold values from 0.25 to 1.75
- gate_up: bfloat16 [1024, 4096], P('wshard'), may hold values from -0.1875 to 0.1875
- down_proj: bfloat16 [2048, 1024], P('wshard'), may hold values from -0.125 to 0.125
Outputs:
- layer_out: bfloat16 [4, 4096, 1024], P('wshard', 'ctx')
- tokens_grad: float32 [4, 4096, 1024], P('wshard', 'ctx')
- norm_gain_grad: float32 [1024], P('wshard')
- in_proj_grad: float32 [1024, 3328], P('wshard')
- conv_weight_grad: float32 [4, 1792], P(None, 'wshard')
- conv_bias_grad: float32 [1792], P('wshard')
- skip_gain_grad: float32 [24], P('wshard')
- mixer_gain_grad: float32 [1536], P('wshard')
- mixer_out_grad: float32 [1536, 1024], P('wshard')
- query_proj_grad: float32 [1024, 512], P('wshard')
- keyval_proj_grad: float32 [1024, 256], P('wshard')
- attn_out_grad: float32 [512, 1024], P('wshard')
- ffn_gain_grad: float32 [1024], P('wshard')
- gate_up_grad: float32 [1024, 4096], P('wshard')
- down_proj_grad: float32 [2048, 1024], P('wshard')
Inputs may be any that keep to these rules, and one draw needn't show every extreme that they name: `doc_lengths`: each row sums to 4096; in every group one document, never the first or the last, begins on the group's first device and ends on its last; in the first group every other document has length 1.
All inputs are finite; a program needn't handle non-finite values.
Results may differ from a plain program's by a relative error of at most 0.025.
The roundings to bfloat16 on the way count: a program that leaves them out, or rounds other values in their place, can miss the bound.
Values may be sent and summed in bfloat16 or wider, within the bound.
No kernel may reach another device: no remote copies, remote signals or barrier semaphores. Data moves between devices by JAX's collectives and lax.ppermute only.
A program may use at most 256 MiB of HBM per device.

v0:
```python
from functools import partial
import math

import jax
import jax.numpy as jnp
from jax import lax
from jax.sharding import PartitionSpec as P

FF = 2048
QUERY_HEADS = 8
KEY_VALUE_HEADS = 2
HEAD_SIZE = 64
HM = 24
PM = 64
NS = 128
KW = 4
DSSM = 1536


eps_norm = 1e-05
rope_base = 100000000000.0
mask_fill_value = -1e30
highest = lax.Precision.HIGHEST


def from_behind(block, axis, distance):
    devices = range(lax.axis_size(axis))
    route = [(i - distance, i) for i in devices if i - distance in devices]
    return lax.ppermute(block, axis, route)


def prefix(array, axis, combine, identity, reverse):
    count, position = (lax.axis_size(axis), lax.axis_index(axis))
    everything = jax.tree.map(
        lambda part, kind: lax.all_gather(part.astype(kind), axis),
        array,
        (jnp.bfloat16, jnp.bfloat16),
    )
    start = jax.tree.map(
        lambda part, zero: jnp.broadcast_to(jnp.asarray(zero, part.dtype), part.shape),
        array,
        identity,
    )

    def prefix_turn(k, before):
        at = count - 1 - k if reverse else k
        reached = at > position if reverse else at < position
        new = combine(
            before, jax.tree.map(lambda part, own: part[at].astype(own.dtype), everything, array)
        )
        return jax.tree.map(lambda a, b: jnp.where(reached, a, b), new, before)

    return lax.fori_loop(0, count, prefix_turn, start)


def mixed_dot(left, right):
    return jnp.dot(left, right, preferred_element_type=jnp.float32)


def rms_scale(value, gain):
    return value * lax.rsqrt(jnp.mean(value * value, axis=-1, keepdims=True) + eps_norm) * gain


def doc_numbers(lengths, position_index):
    ends = jnp.cumsum(lengths)[:-1]
    tally_count = jnp.sum((position_index[:, None] >= ends[None, :]).astype(jnp.int32), axis=1)
    return jnp.where(position_index >= 0, tally_count, -1)


def rotary_apply(value, position_index):
    half = value.shape[-1] // 2
    freq = rope_base ** (-jnp.arange(half, dtype=jnp.float32) / half)
    angle = position_index.astype(jnp.float32)[:, None] * freq[None, :]
    cosine = jnp.cos(angle)[:, None, :]
    sine = jnp.sin(angle)[:, None, :]
    first = value[..., :half]
    second = value[..., half:]
    return jnp.concatenate(
        [first * cosine - second * sine, second * cosine + first * sine], axis=-1
    )


def conv_local(taps, extended, weight, bias):
    tally_count = extended.shape[0] - (KW - 1)
    total = bias[None, :]
    for tap in range(KW):
        total = (
            total + weight[tap][None, :] * extended[tap : tap + tally_count] * taps[tap][:, None]
        )
    return jax.nn.silu(total)


def gate_norm(mixed, gate_z, gain):
    return rms_scale(mixed * jax.nn.silu(gate_z), gain)


def swiglu(gate_up_v):
    return jax.nn.silu(gate_up_v[:, :FF]) * gate_up_v[:, FF:]


def chain_combine(earlier, later):
    return (earlier[0] * later[0], later[0][:, None, None] * earlier[1] + later[1])


def per_device(
    tokens,
    cotangent,
    doc_lengths,
    decay,
    norm_gain,
    in_proj,
    conv_weight,
    conv_bias,
    skip_gain,
    mixer_gain,
    mixer_out,
    query_proj,
    key_value_projection,
    attn_out,
    ffn_gain,
    gate_up,
    down_proj,
):
    (
        norm_w,
        in_w,
        conv_w,
        conv_b,
        skip_w,
        mixer_g,
        mixer_w,
        query_w,
        keyval_w,
        attn_w,
        ffn_g,
        gate_up_w,
        down_w,
    ) = (
        lax.all_gather(norm_gain, "wshard", axis=0, tiled=True),
        lax.all_gather(in_proj, "wshard", axis=0, tiled=True),
        lax.all_gather(conv_weight, "wshard", axis=1, tiled=True),
        lax.all_gather(conv_bias, "wshard", axis=0, tiled=True),
        lax.all_gather(skip_gain, "wshard", axis=0, tiled=True),
        lax.all_gather(mixer_gain, "wshard", axis=0, tiled=True),
        lax.all_gather(mixer_out, "wshard", axis=0, tiled=True),
        lax.all_gather(query_proj, "wshard", axis=0, tiled=True),
        lax.all_gather(key_value_projection, "wshard", axis=0, tiled=True),
        lax.all_gather(attn_out, "wshard", axis=0, tiled=True),
        lax.all_gather(ffn_gain, "wshard", axis=0, tiled=True),
        lax.all_gather(gate_up, "wshard", axis=0, tiled=True),
        lax.all_gather(down_proj, "wshard", axis=0, tiled=True),
    )
    row_listing = tokens.shape[1]
    sequence_total = row_listing * lax.axis_size("ctx")
    key_tile_block = math.gcd(sequence_total, 1024)
    heads_per_group = QUERY_HEADS // KEY_VALUE_HEADS
    scale = HEAD_SIZE ** (-0.5)
    lengths = doc_lengths[0]
    position_index = lax.axis_index("ctx") * row_listing + jnp.arange(row_listing, dtype=jnp.int32)
    docs = doc_numbers(lengths, position_index)
    doc_prev = doc_numbers(lengths, position_index[:1] - 1)[0]
    log_decay = jnp.log(decay[0])
    source = tokens[0].astype(jnp.float32)
    normed, norm_pull = jax.vjp(rms_scale, source, norm_w.astype(jnp.float32))
    normed_b = normed.astype(jnp.bfloat16)
    projected = mixed_dot(normed_b, in_w)
    gate_z = projected[:, :DSSM]
    pre_b = projected[:, DSSM:].astype(jnp.bfloat16)
    rim = from_behind(pre_b[row_listing - (KW - 1) :], "ctx", 1)
    extended = jnp.concatenate([rim, pre_b], axis=0).astype(jnp.float32)
    taps = jnp.stack(
        [
            (doc_numbers(lengths, position_index - (KW - 1) + tap) == docs).astype(jnp.float32)
            for tap in range(KW)
        ]
    )
    conv_f, conv_pull = jax.vjp(
        partial(conv_local, taps), extended, conv_w.astype(jnp.float32), conv_b.astype(jnp.float32)
    )
    conv_b16 = conv_f.astype(jnp.bfloat16)
    xs_b = conv_b16[:, :DSSM].reshape(row_listing, HM, PM)
    bs_b = conv_b16[:, DSSM : DSSM + NS]
    cs_b = conv_b16[:, DSSM + NS :]
    xs_f = xs_b.astype(jnp.float32)
    bs_f = bs_b.astype(jnp.float32)
    cs_f = cs_b.astype(jnp.float32)
    running = jnp.cumsum(log_decay, axis=1)
    order = jnp.arange(row_listing)
    causal = ((order[:, None] >= order[None, :]) & (docs[:, None] == docs[None, :]))[None]
    decay_map = jnp.where(
        causal, jnp.exp(jnp.where(causal, running[:, :, None] - running[:, None, :], 0.0)), 0.0
    )
    entry = jnp.where((docs == doc_prev)[None, :], jnp.exp(running), 0.0)
    tail = jnp.where((docs == docs[-1])[None, :], jnp.exp(running[:, -1:] - running), 0.0)
    carry_gain = jnp.where(docs[-1] == doc_prev, jnp.exp(running[:, -1]), 0.0)
    weights_b = (
        jnp.einsum("tn,sn->ts", cs_b, bs_b, preferred_element_type=jnp.float32)[None] * decay_map
    ).astype(jnp.bfloat16)
    local = jnp.einsum("hts,shp->thp", weights_b, xs_b, preferred_element_type=jnp.float32)
    tail_x = xs_f * tail.T[:, :, None]
    fresh = jnp.einsum("shp,sn->hpn", tail_x, bs_f, precision=highest)
    identity = (jnp.ones((HM,), jnp.float32), jnp.zeros((HM, PM, NS), jnp.float32))
    _, state_in = prefix((carry_gain, fresh), "ctx", chain_combine, identity, False)
    inner = jnp.einsum("tn,hpn->thp", cs_f, state_in, precision=highest) * entry.T[:, :, None]
    skip_f = skip_w.astype(jnp.float32)
    mixed = (local + inner + skip_f[None, :, None] * xs_f).reshape(row_listing, DSSM)
    gated, gate_pull = jax.vjp(gate_norm, mixed, gate_z, mixer_g.astype(jnp.float32))
    gated_b = gated.astype(jnp.bfloat16)
    mamba = mixed_dot(gated_b, mixer_w)
    query_b = (
        rotary_apply(
            mixed_dot(normed_b, query_w).reshape(row_listing, QUERY_HEADS, HEAD_SIZE),
            position_index,
        )
        .astype(jnp.bfloat16)
        .reshape(row_listing, KEY_VALUE_HEADS, heads_per_group, HEAD_SIZE)
    )
    key_value_pair = mixed_dot(normed_b, keyval_w)
    keys_b = (
        rotary_apply(
            key_value_pair[:, : KEY_VALUE_HEADS * HEAD_SIZE].reshape(
                row_listing, KEY_VALUE_HEADS, HEAD_SIZE
            ),
            position_index,
        )
        .reshape(row_listing, KEY_VALUE_HEADS * HEAD_SIZE)
        .astype(jnp.bfloat16)
    )
    values_backward = key_value_pair[:, KEY_VALUE_HEADS * HEAD_SIZE :].astype(jnp.bfloat16)

    def keep_state(state):
        return state

    def attend_block(carry, key_matrix, value_matrix, begin_offset):
        tally_count = key_matrix.shape[0]
        key_pos = begin_offset + jnp.arange(tally_count, dtype=jnp.int32)
        key_docs = doc_numbers(lengths, key_pos)

        def work(state):
            run_max, run_total, weighted = state
            scores = (
                jnp.einsum(
                    "qgrd,kgd->grqk",
                    query_b,
                    key_matrix.reshape(tally_count, KEY_VALUE_HEADS, HEAD_SIZE),
                    preferred_element_type=jnp.float32,
                )
                * scale
            )
            mask = (key_pos[None, :] <= position_index[:, None]) & (
                key_docs[None, :] == docs[:, None]
            )
            new_max = jnp.maximum(
                run_max, jnp.max(jnp.where(mask, scores, mask_fill_value), axis=-1)
            )
            probs = jnp.where(mask, jnp.exp(jnp.where(mask, scores - new_max[..., None], 0.0)), 0.0)
            shrink = jnp.exp(run_max - new_max)
            added = jnp.einsum(
                "grqk,kgd->grqd",
                probs.astype(jnp.bfloat16),
                value_matrix.reshape(tally_count, KEY_VALUE_HEADS, HEAD_SIZE),
                preferred_element_type=jnp.float32,
            )
            return (
                new_max,
                run_total * shrink + jnp.sum(probs, axis=-1),
                weighted * shrink[..., None] + added,
            )

        return lax.cond(begin_offset <= position_index[-1], work, keep_state, carry)

    start_state = (
        jnp.full((KEY_VALUE_HEADS, heads_per_group, row_listing), mask_fill_value, jnp.float32),
        jnp.zeros((KEY_VALUE_HEADS, heads_per_group, row_listing), jnp.float32),
        jnp.zeros((KEY_VALUE_HEADS, heads_per_group, row_listing, HEAD_SIZE), jnp.float32),
    )
    key_row_set, value_row_set = (
        lax.all_gather(keys_b, "ctx", axis=0, tiled=True),
        lax.all_gather(values_backward, "ctx", axis=0, tiled=True),
    )
    key_matrix = key_row_set
    value_matrix = value_row_set
    tally_count = key_matrix.shape[0]
    span_width = math.gcd(tally_count, 1024)

    def attend_turn(index, state):
        begin = index * span_width
        return attend_block(
            state,
            lax.dynamic_slice_in_dim(key_matrix, begin, span_width, 0),
            lax.dynamic_slice_in_dim(value_matrix, begin, span_width, 0),
            0 + begin,
        )

    run_max, run_total, weighted = lax.fori_loop(
        0, tally_count // span_width, attend_turn, start_state
    )
    heads_f = weighted / run_total[..., None]
    log_total = run_max + jnp.log(run_total)
    heads_b = (
        heads_f.transpose(2, 0, 1, 3)
        .reshape(row_listing, QUERY_HEADS * HEAD_SIZE)
        .astype(jnp.bfloat16)
    )
    attn = mixed_dot(heads_b, attn_w)
    middle = source + attn + mamba
    normed2, ffn_pull = jax.vjp(rms_scale, middle, ffn_g.astype(jnp.float32))
    normed2_b = normed2.astype(jnp.bfloat16)
    gate_up_v = mixed_dot(normed2_b, gate_up_w)
    activated, act_pull = jax.vjp(swiglu, gate_up_v)
    activated_b = activated.astype(jnp.bfloat16)
    layer_out = (middle + mixed_dot(activated_b, down_w)).astype(jnp.bfloat16)
    out_grad = cotangent[0].astype(jnp.float32)
    out_low = cotangent[0]
    down_grad = jnp.einsum("tf,td->fd", activated_b, out_low, preferred_element_type=jnp.float32)
    (gate_up_grad_v,) = act_pull(
        jnp.einsum("td,fd->tf", out_low, down_w, preferred_element_type=jnp.float32)
    )
    gate_up_low = gate_up_grad_v.astype(jnp.bfloat16)
    gate_up_grad = jnp.einsum(
        "td,tf->df", normed2_b, gate_up_low, preferred_element_type=jnp.float32
    )
    normed2_grad = jnp.einsum(
        "tf,df->td", gate_up_low, gate_up_w, preferred_element_type=jnp.float32
    )
    middle_norm_grad, ffn_gain_grad = ffn_pull(normed2_grad)
    middle_grad = out_grad + middle_norm_grad
    middle_low = middle_grad.astype(jnp.bfloat16)
    attn_grad = jnp.einsum("tc,td->cd", heads_b, middle_low, preferred_element_type=jnp.float32)
    heads_reduced = jnp.einsum(
        "td,cd->tc", middle_low, attn_w, preferred_element_type=jnp.float32
    ).astype(jnp.bfloat16)
    mixer_out_grad = jnp.einsum(
        "tc,td->cd", gated_b, middle_low, preferred_element_type=jnp.float32
    )
    gated_grad = jnp.einsum("td,cd->tc", middle_low, mixer_w, preferred_element_type=jnp.float32)
    mixed_grad, gate_z_grad, mixer_gain_grad = gate_pull(gated_grad)
    mixed_grad = mixed_grad.reshape(row_listing, HM, PM)
    sum_low = mixed_grad.astype(jnp.bfloat16)
    sum_low_f = sum_low.astype(jnp.float32)
    skip_grad = jnp.sum(mixed_grad * xs_f, axis=(0, 2))
    xs_grad = skip_f[None, :, None] * mixed_grad
    weights_grad = jnp.einsum("thp,shp->hts", sum_low, xs_b, preferred_element_type=jnp.float32)
    xs_grad = xs_grad + jnp.einsum(
        "hts,thp->shp", weights_b, sum_low, preferred_element_type=jnp.float32
    )
    scores_low = jnp.sum(weights_grad * decay_map, axis=0).astype(jnp.bfloat16)
    cs_grad = jnp.einsum("ts,sn->tn", scores_low, bs_b, preferred_element_type=jnp.float32)
    bs_grad = jnp.einsum("ts,tn->sn", scores_low, cs_b, preferred_element_type=jnp.float32)
    entry_grad = sum_low_f * entry.T[:, :, None]
    cs_grad = cs_grad + jnp.einsum("thp,hpn->tn", entry_grad, state_in, precision=highest)
    upward = jnp.einsum("thp,tn->hpn", entry_grad, cs_f, precision=highest)
    _, state_out_grad = prefix((carry_gain, upward), "ctx", chain_combine, identity, True)
    xs_grad = xs_grad + tail.T[:, :, None] * jnp.einsum(
        "sn,hpn->shp", bs_f, state_out_grad, precision=highest
    )
    bs_grad = bs_grad + jnp.einsum("shp,hpn->sn", tail_x, state_out_grad, precision=highest)
    conv_grad = jnp.concatenate([xs_grad.reshape(row_listing, DSSM), bs_grad, cs_grad], axis=1)
    extended_grad, conv_weight_grad, conv_bias_grad = conv_pull(conv_grad)
    from_above = from_behind(extended_grad[: KW - 1], "ctx", -1)
    pre_grad = extended_grad[KW - 1 :] + jnp.concatenate(
        [jnp.zeros((row_listing - (KW - 1), from_above.shape[1]), jnp.float32), from_above], axis=0
    )
    projected_low = jnp.concatenate([gate_z_grad, pre_grad], axis=1).astype(jnp.bfloat16)
    in_grad = jnp.einsum("td,tc->dc", normed_b, projected_low, preferred_element_type=jnp.float32)
    normed_grad = jnp.einsum("tc,dc->td", projected_low, in_w, preferred_element_type=jnp.float32)
    heads_bundled = heads_reduced.reshape(row_listing, KEY_VALUE_HEADS, heads_per_group, HEAD_SIZE)
    delta = jnp.einsum("qgrd,grqd->grq", heads_bundled.astype(jnp.float32), heads_f)

    def block_terms(begin_offset, span_width):
        key_matrix = lax.dynamic_slice_in_dim(key_row_set, begin_offset, span_width, 0).reshape(
            span_width, KEY_VALUE_HEADS, HEAD_SIZE
        )
        value_matrix = lax.dynamic_slice_in_dim(value_row_set, begin_offset, span_width, 0).reshape(
            span_width, KEY_VALUE_HEADS, HEAD_SIZE
        )
        key_pos = begin_offset + jnp.arange(span_width, dtype=jnp.int32)
        key_docs = doc_numbers(lengths, key_pos)
        scores = (
            jnp.einsum("qgrd,kgd->grqk", query_b, key_matrix, preferred_element_type=jnp.float32)
            * scale
        )
        mask = (key_pos[None, :] <= position_index[:, None]) & (key_docs[None, :] == docs[:, None])
        probs = jnp.where(mask, jnp.exp(jnp.where(mask, scores - log_total[..., None], 0.0)), 0.0)
        probs_grad = jnp.einsum(
            "qgrd,kgd->grqk", heads_bundled, value_matrix, preferred_element_type=jnp.float32
        )
        score_low = (probs * (probs_grad - delta[..., None])).astype(jnp.bfloat16)
        return (key_matrix, probs, score_low)

    def query_part(key_matrix, score_low):
        return (
            jnp.einsum("grqk,kgd->qgrd", score_low, key_matrix, preferred_element_type=jnp.float32)
            * scale
        )

    def keyval_part(probs, score_low, span_width):
        key_gradient = (
            jnp.einsum("grqk,qgrd->kgd", score_low, query_b, preferred_element_type=jnp.float32)
            * scale
        )
        value_gradient = jnp.einsum(
            "grqk,qgrd->kgd",
            probs.astype(jnp.bfloat16),
            heads_bundled,
            preferred_element_type=jnp.float32,
        )
        return (
            key_gradient.reshape(span_width, KEY_VALUE_HEADS * HEAD_SIZE),
            value_gradient.reshape(span_width, KEY_VALUE_HEADS * HEAD_SIZE),
        )

    block_count = sequence_total // key_tile_block
    block_starts = jnp.arange(block_count, dtype=jnp.int32) * key_tile_block
    query_zeroed = jnp.zeros(
        (row_listing, KEY_VALUE_HEADS, heads_per_group, HEAD_SIZE), jnp.float32
    )

    def attend_back(query_acc, begin_offset):

        def work(acc):
            key_matrix, probs, score_low = block_terms(begin_offset, key_tile_block)
            return (
                acc + query_part(key_matrix, score_low),
                keyval_part(probs, score_low, key_tile_block),
            )

        def skip_block(acc):
            blank_fill = jnp.zeros((key_tile_block, KEY_VALUE_HEADS * HEAD_SIZE), jnp.float32)
            return (acc, (blank_fill, blank_fill))

        return lax.cond(begin_offset <= position_index[-1], work, skip_block, query_acc)

    query_turned, (keys_complete, values_complete) = lax.scan(
        attend_back, query_zeroed, block_starts
    )
    keys_owned, values_mine = (
        lax.psum_scatter(
            keys_complete.reshape(sequence_total, KEY_VALUE_HEADS * HEAD_SIZE).astype(jnp.bfloat16),
            "ctx",
            scatter_dimension=0,
            tiled=True,
        ).astype(jnp.float32),
        lax.psum_scatter(
            values_complete.reshape(sequence_total, KEY_VALUE_HEADS * HEAD_SIZE).astype(
                jnp.bfloat16
            ),
            "ctx",
            scatter_dimension=0,
            tiled=True,
        ).astype(jnp.float32),
    )
    query_low = (
        rotary_apply(query_turned.reshape(row_listing, QUERY_HEADS, HEAD_SIZE), -position_index)
        .reshape(row_listing, QUERY_HEADS * HEAD_SIZE)
        .astype(jnp.bfloat16)
    )
    key_reverse = rotary_apply(
        keys_owned.reshape(row_listing, KEY_VALUE_HEADS, HEAD_SIZE), -position_index
    ).reshape(row_listing, KEY_VALUE_HEADS * HEAD_SIZE)
    keyval_low = jnp.concatenate([key_reverse, values_mine], axis=1).astype(jnp.bfloat16)
    query_grad = jnp.einsum("td,tc->dc", normed_b, query_low, preferred_element_type=jnp.float32)
    keyval_grad = jnp.einsum("td,tc->dc", normed_b, keyval_low, preferred_element_type=jnp.float32)
    normed_grad = normed_grad + jnp.einsum(
        "tc,dc->td", query_low, query_w, preferred_element_type=jnp.float32
    )
    normed_grad = normed_grad + jnp.einsum(
        "tc,dc->td", keyval_low, keyval_w, preferred_element_type=jnp.float32
    )
    source_grad, norm_grad = norm_pull(normed_grad)
    tokens_grad = (middle_grad + source_grad)[None]
    shares = (
        lax.psum_scatter(
            norm_grad.astype(jnp.bfloat16), "wshard", scatter_dimension=0, tiled=True
        ).astype(jnp.float32),
        lax.psum_scatter(
            in_grad.astype(jnp.bfloat16), "wshard", scatter_dimension=0, tiled=True
        ).astype(jnp.float32),
        lax.psum_scatter(
            conv_weight_grad.astype(jnp.bfloat16), "wshard", scatter_dimension=1, tiled=True
        ).astype(jnp.float32),
        lax.psum_scatter(
            conv_bias_grad.astype(jnp.bfloat16), "wshard", scatter_dimension=0, tiled=True
        ).astype(jnp.float32),
        lax.psum_scatter(
            skip_grad.astype(jnp.bfloat16), "wshard", scatter_dimension=0, tiled=True
        ).astype(jnp.float32),
        lax.psum_scatter(
            mixer_gain_grad.astype(jnp.bfloat16), "wshard", scatter_dimension=0, tiled=True
        ).astype(jnp.float32),
        lax.psum_scatter(
            mixer_out_grad.astype(jnp.bfloat16), "wshard", scatter_dimension=0, tiled=True
        ).astype(jnp.float32),
        lax.psum_scatter(
            query_grad.astype(jnp.bfloat16), "wshard", scatter_dimension=0, tiled=True
        ).astype(jnp.float32),
        lax.psum_scatter(
            keyval_grad.astype(jnp.bfloat16), "wshard", scatter_dimension=0, tiled=True
        ).astype(jnp.float32),
        lax.psum_scatter(
            attn_grad.astype(jnp.bfloat16), "wshard", scatter_dimension=0, tiled=True
        ).astype(jnp.float32),
        lax.psum_scatter(
            ffn_gain_grad.astype(jnp.bfloat16), "wshard", scatter_dimension=0, tiled=True
        ).astype(jnp.float32),
        lax.psum_scatter(
            gate_up_grad.astype(jnp.bfloat16), "wshard", scatter_dimension=0, tiled=True
        ).astype(jnp.float32),
        lax.psum_scatter(
            down_grad.astype(jnp.bfloat16), "wshard", scatter_dimension=0, tiled=True
        ).astype(jnp.float32),
    )
    shares = tuple(
        (
            lax.psum(shares[0].astype(jnp.bfloat16), "ctx").astype(jnp.float32),
            lax.psum(shares[1].astype(jnp.bfloat16), "ctx").astype(jnp.float32),
            lax.psum(shares[2].astype(jnp.bfloat16), "ctx").astype(jnp.float32),
            lax.psum(shares[3].astype(jnp.bfloat16), "ctx").astype(jnp.float32),
            lax.psum(shares[4].astype(jnp.bfloat16), "ctx").astype(jnp.float32),
            lax.psum(shares[5].astype(jnp.bfloat16), "ctx").astype(jnp.float32),
            lax.psum(shares[6].astype(jnp.bfloat16), "ctx").astype(jnp.float32),
            lax.psum(shares[7].astype(jnp.bfloat16), "ctx").astype(jnp.float32),
            lax.psum(shares[8].astype(jnp.bfloat16), "ctx").astype(jnp.float32),
            lax.psum(shares[9].astype(jnp.bfloat16), "ctx").astype(jnp.float32),
            lax.psum(shares[10].astype(jnp.bfloat16), "ctx").astype(jnp.float32),
            lax.psum(shares[11].astype(jnp.bfloat16), "ctx").astype(jnp.float32),
            lax.psum(shares[12].astype(jnp.bfloat16), "ctx").astype(jnp.float32),
        )
    )
    return (layer_out[None], tokens_grad) + shares


def solution(mesh):
    in_specs = (
        P("wshard", "ctx", None),
        P("wshard", "ctx", None),
        P("wshard", None),
        P("wshard", None, "ctx"),
        P("wshard"),
        P("wshard", None),
        P(None, "wshard"),
        P("wshard"),
        P("wshard"),
        P("wshard"),
        P("wshard", None),
        P("wshard", None),
        P("wshard", None),
        P("wshard", None),
        P("wshard"),
        P("wshard", None),
        P("wshard", None),
    )
    out_specs = (
        P("wshard", "ctx", None),
        P("wshard", "ctx", None),
        P("wshard"),
        P("wshard", None),
        P(None, "wshard"),
        P("wshard"),
        P("wshard"),
        P("wshard"),
        P("wshard", None),
        P("wshard", None),
        P("wshard", None),
        P("wshard", None),
        P("wshard"),
        P("wshard", None),
        P("wshard", None),
    )
    return jax.shard_map(
        per_device, mesh=mesh, in_specs=in_specs, out_specs=out_specs, check_vma=False
    )
```

profile of v0, /device:TPU:0, one launch (start us, length us, event | category | flops | bytes accessed | tf_op | source)
XLA Modules:
  0.0 1318.1 jit_solution(9866732175260557442)
XLA Ops:
  9.4 6.0 all-gather.3
  15.4 8.1 all_gather.64
  31.1 5.8 all-gather.4
  39.6 22.2 %all-gather.26.cloned.1.call-done = bf16[1024,3328]{1,0:T(8,128)(2,1)} async-done(((bf16[256,3328]{1,0:T(8,128)(2,1)}), bf16[1024,3328]{1,0:T(8,128)(2,1)}) %all-gather.26.cloned.1.call-update) | async-done | bytes 6815760 | tf_op jit(solution)/shard_map/all_gather | solution.py:140
  61.8 8.7 fusion.142
  72.3 3.4 collective-permute-start
  78.2 6.2 all-reduce.22
  86.6 4.5 multiply_convert_fusion.4
  95.1 3.9 fusion.73
  104.6 5.1 all-gather.6
  109.7 5.2 all-gather.5
  116.0 20.0 %all-reduce.12 = bf16[192]{0:T(256)(128)(2,1)S(1)} all-reduce(bf16[192]{0:T(256)(128)(2,1)S(1)} %dynamic-update-slice.1), channel_id=2, replica_groups=mesh['ctx'=8,'wshard'=4] {'ctx'}, use_global_device_ids=true, to_apply=%add.12 | all-reduce | flops 192 | bytes 768
  140.9 22.8 %all-gather.22.cloned.1.call-done = bf16[4096,128]{0,1:T(8,128)(2,1)} async-done(((bf16[512,128]{0,1:T(8,128)(2,1)}), bf16[4096,128]{0,1:T(8,128)(2,1)}) %all-gather.22.cloned.1.call-update) | async-done | bytes 1048592 | tf_op jit(solution)/shard_map/all_gather | solution.py:279
  164.8 19.4 %while.66 = (s32[]{:T(128)}, f32[2,4,512]{2,1,0:T(4,128)S(1)}, f32[2,4,512]{2,1,0:T(4,128)S(1)}, f32[2,4,512,64]{2,3,1,0:T(8,128)}, s32[512]{0:T(512)S(1)}, /*in...) while((s32[]{:T(128)}, f32[2,4,512]{2,1,0:T(4,128)S(1)}, ...), condition=%wide.region_9.10_spmd, body=%wide.region_3.9_spmd.sunk | while | flops 1130384384 | bytes 65335728 | solution.py:295
  166.2 14.1 %conditional.4 = ((f32[2,4,512]{2,1,0:T(4,128)S(1)}, f32[2,4,512]{2,1,0:T(4,128)S(1)}, f32[2,4,512,64]{2,3,1,0:T(8,128)})) conditional(s32[]{:T(128)} %convert_element_type.660, (f32[2,4,512]{2,1,0:T(4,128)S(1)}, f32[2,4,512]{2,1,0:T(4,128)S(1)}, f32[2,4,512,64]{2,3,1,0:T(8,128)}) %tuple.203, (s32[1024]{0:T(1024)S(1)}, s32[512]{0:T(512)S(1)}, ...), branch_computations={%region_4.4_spmd, %region_5.8_spmd} | conditional | flops 1130377216 | bytes 65314944 | solution.py:270
  170.9 4.0 fusion.5
  174.9 4.3 fusion.9
  187.7 10.1 fusion.31
  197.8 27.9 %all-gather.34.cloned.1.call-done = bf16[192,64,128]{2,1,0:T(8,128)(2,1)} async-done(((bf16[24,64,128]{2,1,0:T(8,128)(2,1)}), bf16[192,64,128]{2,1,0:T(8,128)(2,1)}) %all-gather.34.cloned.1.call-update) | async-done | bytes 3145744 | tf_op jit(solution)/shard_map/all_gather | solution.py:35
  225.7 9.9 while.68
  235.6 6.0 fusion.40
  241.6 3.9 copy.127
  245.5 5.5 multiply_reduce_fusion.8
  254.3 6.0 fusion.129
  260.4 12.3 all-gather.24.cloned.1.call-done
  275.7 56.8 %all-gather.30.cloned.1.call-done = bf16[1024,4096]{1,0:T(8,128)(2,1)} async-done(((bf16[256,4096]{1,0:T(8,128)(2,1)}), bf16[1024,4096]{1,0:T(8,128)(2,1)}) %all-gather.30.cloned.1.call-update) | async-done | bytes 8388624 | tf_op jit(solution)/shard_map/all_gather | solution.py:150
  332.5 10.2 fusion.128
  342.7 25.9 %all-gather.32.cloned.1.call-done = bf16[2048,1024]{1,0:T(8,128)(2,1)} async-done(((bf16[512,1024]{1,0:T(8,128)(2,1)}), bf16[2048,1024]{1,0:T(8,128)(2,1)}) %all-gather.32.cloned.1.call-update) | async-done | bytes 4194320 | tf_op jit(solution)/shard_map/all_gather | solution.py:151
  368.6 12.6 fusion.85
  381.2 10.6 multiply_reduce_fusion.9
  395.9 50.4 %while.67 = (s32[]{:T(128)}, f32[512,2,4,64]{0,3,2,1:T(8,128)S(1)}, bf16[4,1024,128]{2,1,0:T(8,128)(2,1)}, bf16[4,1024,128]{2,1,0:T(8,128)(2,1)}, s32[4]{0:T(128...) while((s32[]{:T(128)}, f32[512,2,4,64]{0,3,2,1:T(8,128)S(1)}, ...), condition=%wide.region_30.31_spmd, body=%wide.region_25.30_spmd.sunk | while | flops 2737057792 | bytes 87900608 | solution.py:434
  398.4 35.5 %conditional.5 = (f32[512,2,4,64]{0,3,2,1:T(8,128)S(1)}, bf16[1,1024,128]{1,2,0:T(8,128)(2,1)S(1)}, bf16[1,1024,128]{1,2,0:T(8,128)(2,1)S(1)}) conditional(s32[]{:T(128)} %convert_element_type.661, f32[512,2,4,64]{0,3,2,1:T(8,128)S(1)} %get-tuple-element.1282, (s32[]{:T(128)}, bf16[4096,128]{0,1:T(8,128)(2,1)}, s32[512]{0:T(512)S(1)}, ...), branch_computations={%region_26.26_spmd, %region_27.29_spmd} | conditional | flops 2737057792 | bytes 85803176 | solution.py:432
  404.1 8.1 fusion.143
  412.2 8.1 fusion.20
  420.3 9.3 fusion.15
  449.0 6.1 multiply_reduce_fusion.5
  455.1 5.7 multiply_reduce_fusion.6
  460.8 3.5 copy.129
  476.4 139.8 %reduce-scatter.13.cloned.1.call-done = bf16[512,128]{1,0:T(8,128)(2,1)} async-done(((bf16[4096,128]{1,0:T(8,128)(2,1)}), bf16[512,128]{1,0:T(8,128)(2,1)}) %reduce-scatter.13.cloned.1.call-update) | async-done | bytes 131088 | tf_op jit(solution)/shard_map/reduce_scatter | solution.py:438
  617.3 66.2 %reduce-scatter.15.cloned.1.call-done = bf16[512,128]{0,1:T(8,128)(2,1)} async-done(((bf16[4096,128]{0,1:T(8,128)(2,1)}), bf16[512,128]{0,1:T(8,128)(2,1)}) %reduce-scatter.15.cloned.1.call-update) | async-done | bytes 131088 | tf_op jit(solution)/shard_map/reduce_scatter | solution.py:444
  686.3 4.8 convolution_convert_fusion.3
  693.2 4.5 convolution_convert_fusion.2
  699.2 10.4 convolution_convert_fusion
  710.8 6.4 fusion.74
  717.3 10.1 multiply_reduce_fusion
  729.5 9.7 fusion.30
  739.2 5.8 all-gather.36.cloned.1.call-done
  745.0 23.5 %while.69 = (s32[]{:T(128)}, f32[24,64,128]{2,1,0:T(8,128)}, s32[]{:T(128)}, bf16[8,24]{1,0:T(8,128)(2,1)}, bf16[8,24,64,128]{3,2,1,0:T(8,128)(2,1)}, /*index=5*/s32[]{:T(128)}, s32[]{:T(128)}, s32[]{:T(128)}, s32[]{:T(128)}) while((s32[]{:T(128)}, f32[24,64,128]{2,1,0:T(8,128)}, s32[]{:T(128)}, bf16[8,24]{1,0:T(8,128)(2,1)}, ...), condition=%wide.region_23.24_spmd.clone, body=%wide.region_22.23_spmd.clone.sunk | while | flops 983072 | bytes 1966495 | solution.py:53
  768.5 5.5 fusion.44
  774.1 3.9 copy.134
  778.0 5.0 fusion.75
  784.4 6.4 multiply_reduce_fusion.4
  799.6 5.9 convolution_convert_fusion.1
  807.1 15.5 %reduce-scatter.23.cloned.1.call-done = bf16[256,256]{1,0:T(8,128)(2,1)} async-done(((bf16[1024,256]{1,0:T(8,128)(2,1)}), bf16[256,256]{1,0:T(8,128)(2,1)}) %reduce-scatter.23.cloned.1.call-update) | async-done | bytes 131088 | tf_op jit(solution)/shard_map/reduce_scatter | solution.py:497
  822.6 40.5 %reduce-scatter.19.cloned.1.call-done = bf16[384,1024]{1,0:T(8,128)(2,1)} async-done(((bf16[1536,1024]{1,0:T(8,128)(2,1)}), bf16[384,1024]{1,0:T(8,128)(2,1)}) %reduce-scatter.19.cloned.1.call-update) | async-done | bytes 786448 | tf_op jit(solution)/shard_map/reduce_scatter | solution.py:491
  863.1 46.9 %reduce-scatter.29.cloned.1.call-done = bf16[512,1024]{1,0:T(8,128)(2,1)} async-done(((bf16[2048,1024]{1,0:T(8,128)(2,1)}), bf16[512,1024]{1,0:T(8,128)(2,1)}) %reduce-scatter.29.cloned.1.call-update) | async-done | bytes 1048592 | tf_op jit(solution)/shard_map/reduce_scatter | solution.py:509
  910.0 74.4 %reduce-scatter.27.cloned.1.call-done = bf16[256,4096]{1,0:T(8,128)(2,1)} async-done(((bf16[1024,4096]{1,0:T(8,128)(2,1)}), bf16[256,4096]{1,0:T(8,128)(2,1)}) %reduce-scatter.27.cloned.1.call-update) | async-done | bytes 2097168 | tf_op jit(solution)/shard_map/reduce_scatter | solution.py:506
  984.4 64.4 %reduce-scatter.17.cloned.1.call-done = bf16[256,3328]{1,0:T(8,128)(2,1)} async-done(((bf16[1024,3328]{1,0:T(8,128)(2,1)}), bf16[256,3328]{1,0:T(8,128)(2,1)}) %reduce-scatter.17.cloned.1.call-update) | async-done | bytes 1703952 | tf_op jit(solution)/shard_map/reduce_scatter | solution.py:476
  1053.7 6.3 fusion.71
  1060.6 8.4 fusion.57
  1069.0 10.1 all-reduce.21
  1079.5 4.8 fusion.65
  1085.4 23.0 %all-reduce.19 = (bf16[256]{0:T(256)(128)(2,1)S(1)}, bf16[4,448]{1,0:T(4,128)(2,1)S(1)}, bf16[448]{0:T(512)(128)(2,1)S(1)}, bf16[6]{0:T(256)(128)(2,1)S(1)}, bf1...) all-reduce(bf16[256]{0:T(256)(128)(2,1)S(1)} %dynamic-slice.4, ...), channel_id=1, replica_groups=mesh['ctx'=8,'wshard'=4] {'ctx'}, use_global_device_ids=true, to_apply=%region_36.37 | all-reduce | flops 3142 | bytes 12568 | tf_op jit(solution)/shard_map/psum | solution.py:515
  1111.8 185.2 %all-reduce.25.cloned.1.call-done = (bf16[256,3328]{1,0:T(8,128)(2,1)}, bf16[384,1024]{1,0:T(8,128)(2,1)}, bf16[256,512]{1,0:T(8,128)(2,1)}, bf16[256,256]{1,0:T...) async-done(((bf16[256,3328]{1,0:T(8,128)(2,1)}, bf16[384,1024]{1,0:T(8,128)(2,1)}, bf16[256,512]{1,0:T(8,128)(2,1)}, ...) | async-done | bytes 6291472 | tf_op jit(solution)/shard_map/psum | solution.py:516
  (506 shorter events, 162.2 us)
Async XLA Ops:
  7.2 16.3 %copy-start.14 = (bf16[1,512,1024]{2,1,0:T(8,128)(2,1)S(1)}, bf16[1,512,1024]{2,1,0:T(8,128)(2,1)}, u32[]{:S(2)}) copy-start(bf16[1,512,1024]{2,1,0:T(8,128)(2,1)} %param.29) | copy-start | bytes 3145732
  7.2 54.6 %all-gather.26.cloned.1.call-start = ((), (), s32[]{:S(2)}) async-start(), calls=%async_computation.14 | async-start | bytes 8519680 | tf_op jit(solution)/shard_map/all_gather | solution.py:140
  7.9 128.1 %all-gather.20.cloned.1.call-start = ((), (), s32[]{:S(2)}) async-start(), calls=%async_computation.11 | async-start | bytes 1310720 | tf_op jit(solution)/shard_map/all_gather | solution.py:146
  8.7 132.3 %all-gather.18.cloned.1.call-start = ((), (), s32[]{:S(2)}) async-start(), calls=%async_computation.10 | async-start | bytes 1179648 | tf_op jit(solution)/shard_map/all_gather | solution.py:278
  15.4 123.0 %copy-start.90 = (f32[4,1,256]{2,1,0:T(1,128)}, f32[4,1,256]{2,1,0:T(1,128)S(1)}, u32[]{:S(2)}) copy-start(f32[4,1,256]{2,1,0:T(1,128)S(1)} %convert_element_type.499) | copy-start | bytes 12292
  15.4 12.9 copy-start.110
  15.4 15.7 %copy-start.100 = (bf16[4,448]{1,0:T(4,128)(2,1)S(1)}, bf16[4,448]{1,0:T(4,128)(2,1)}, u32[]{:S(2)}) copy-start(bf16[4,448]{1,0:T(4,128)(2,1)} %param.35) | copy-start | bytes 10756
  23.5 13.6 %copy-start.70 = (f32[1,24,512]{2,1,0:T(8,128)S(1)}, f32[1,24,512]{2,1,0:T(8,128)}, u32[]{:S(2)}) copy-start(f32[1,24,512]{2,1,0:T(8,128)} %param.32) | copy-start | bytes 147460
  23.8 114.6 %copy-start.94 = (f32[512]{0:T(512)}, f32[512]{0:T(512)S(1)}, u32[]{:S(2)}) copy-start(f32[512]{0:T(512)S(1)} %fusion.116) | copy-start | bytes 6148
  26.9 136.8 %all-gather.22.cloned.1.call-start = ((), (), s32[]{:S(2)}) async-start(), calls=%async_computation.12 | async-start | bytes 1179648 | tf_op jit(solution)/shard_map/all_gather | solution.py:279
  27.7 198.0 %all-gather.34.cloned.1.call-start = ((), (), s32[]{:S(2)}) async-start(), calls=%async_computation.27 | async-start | bytes 3538944 | tf_op jit(solution)/shard_map/all_gather | solution.py:35
  38.6 148.1 %copy-start.59 = (f32[24,512]{1,0:T(8,128)}, f32[24,512]{1,0:T(8,128)S(1)}, u32[]{:S(2)}) copy-start(f32[24,512]{1,0:T(8,128)S(1)} %copy_bitcast_fusion) | copy-start | bytes 147460
  39.4 47.1 %copy-start.75 = (f32[512]{0:T(512)}, f32[512]{0:T(512)S(1)}, u32[]{:S(2)}) copy-start(f32[512]{0:T(512)S(1)} %get-tuple-element.949) | copy-start | bytes 6148
  39.4 47.1 %copy-start.77 = (f32[512]{0:T(512)}, f32[512]{0:T(512)S(1)}, u32[]{:S(2)}) copy-start(f32[512]{0:T(512)S(1)} %get-tuple-element.950) | copy-start | bytes 6148
  39.4 47.1 %copy-start.79 = (f32[512]{0:T(512)}, f32[512]{0:T(512)S(1)}, u32[]{:S(2)}) copy-start(f32[512]{0:T(512)S(1)} %get-tuple-element.951) | copy-start | bytes 6148
  39.5 55.5 %copy-start.53 = (f32[512,24]{0,1:T(8,128)}, f32[512,24]{0,1:T(8,128)S(1)}, u32[]{:S(2)}) copy-start(f32[512,24]{0,1:T(8,128)S(1)} %get-tuple-element.943) | copy-start | bytes 147460
  39.6 196.1 %copy-start.55 = (f32[512,24]{0,1:T(8,128)}, f32[512,24]{0,1:T(8,128)S(1)}, u32[]{:S(2)}) copy-start(f32[512,24]{0,1:T(8,128)S(1)} %get-tuple-element.942) | copy-start | bytes 147460
  39.6 36.2 %copy-start.103 = (u32[32]{0:T(128)S(1)}, u32[32]{0:T(128)}, u32[]{:S(2)}) copy-start(u32[32]{0:T(128)} %constant.277) | copy-start | bytes 388
  39.6 38.1 %copy-start.108 = (bf16[6]{0:T(256)(128)(2,1)S(1)}, bf16[6]{0:T(256)(128)(2,1)}, u32[]{:S(2)}) copy-start(bf16[6]{0:T(256)(128)(2,1)} %param.37) | copy-start | bytes 40
  39.6 38.4 %copy-start.106 = (bf16[448]{0:T(512)(128)(2,1)S(1)}, bf16[448]{0:T(512)(128)(2,1)}, u32[]{:S(2)}) copy-start(bf16[448]{0:T(512)(128)(2,1)} %param.36) | copy-start | bytes 2692
  72.3 13.8 %collective-permute-start = (bf16[3,1792]{1,0:T(4,128)(2,1)S(1)}, bf16[3,1792]{1,0:T(4,128)(2,1)S(1)}, u32[]{:S(2)}, u32[]{:S(2)}) collective-permute-start(bf16[3,1792]{1,0:T(4,128)(2,1)S(1)} %slice.180), channel_id=1, source_target_pairs={{0,4},{4,8},{8,12},{12,16},{16,20},{20,24},{24,28},{1,5},{5,9},{9,... | collective-permute-start | bytes 32264 | tf_op jit(solution)/shard_map/ppermute | solution.py:29
  75.7 10.8 copy-start.62
  75.7 10.8 copy-start.64
  75.7 10.8 copy-start.66
  75.7 10.8 copy-start.68
  91.0 144.6 %copy-start.10 = (bf16[512,1792]{1,0:T(8,128)(2,1)}, bf16[512,1792]{1,0:T(8,128)(2,1)S(1)}, u32[]{:S(2)}) copy-start(bf16[512,1792]{1,0:T(8,128)(2,1)S(1)} %get-tuple-element.916) | copy-start | bytes 5505028
  95.1 9.5 copy-start.109
  95.1 9.5 copy-start.107
  99.0 155.3 %all-gather.28.cloned.1.call-start = ((), (), s32[]{:S(2)}) async-start(), calls=%async_computation.15 | async-start | bytes 3932160 | tf_op jit(solution)/shard_map/all_gather | solution.py:145
  99.6 173.1 %all-gather.24.cloned.1.call-start = ((), (), s32[]{:S(2)}) async-start(), calls=%async_computation.13 | async-start | bytes 1310720 | tf_op jit(solution)/shard_map/all_gather | solution.py:148
  100.3 232.2 %all-gather.30.cloned.1.call-start = ((), (), s32[]{:S(2)}) async-start(), calls=%async_computation.16 | async-start | bytes 10485760 | tf_op jit(solution)/shard_map/all_gather | solution.py:150
  101.1 267.5 %all-gather.32.cloned.1.call-start = ((), (), s32[]{:S(2)}) async-start(), calls=%async_computation.17 | async-start | bytes 5242880 | tf_op jit(solution)/shard_map/all_gather | solution.py:151
  101.8 514.4 %reduce-scatter.13.cloned.1.call-start = ((), (), s32[]{:S(2)}) async-start(), calls=%async_computation.18 | async-start | bytes 1179648 | tf_op jit(solution)/shard_map/reduce_scatter | solution.py:438
  109.6 282.3 %copy-start.71 = (f32[4,1,256]{2,1,0:T(1,128)}, f32[4,1,256]{2,1,0:T(1,128)S(1)}, u32[]{:S(2)}) copy-start(f32[4,1,256]{2,1,0:T(1,128)S(1)} %convert_element_type.502) | copy-start | bytes 12292
  109.7 126.0 %copy-start.105 = (f32[24]{0:T(128)}, f32[24]{0:T(128)S(1)}, u32[]{:S(2)}) copy-start(f32[24]{0:T(128)S(1)} %convert_element_type.445) | copy-start | bytes 292
  114.9 139.5 %copy-start.73 = (f32[1536]{0:T(1024)}, f32[1536]{0:T(1024)S(1)}, u32[]{:S(2)}) copy-start(f32[1536]{0:T(1024)S(1)} %reshape.652) | copy-start | bytes 18436
  251.0 9.4 copy-start.88
  251.0 9.4 copy-start.97
  254.3 18.3 %copy-start.30 = (bf16[2,4,512,64]{2,3,1,0:T(8,128)(2,1)S(1)}, bf16[2,4,512,64]{2,3,1,0:T(8,128)(2,1)}, u32[]{:S(2)}) copy-start(bf16[2,4,512,64]{2,3,1,0:T(8,128)(2,1)} %fusion.86) | copy-start | bytes 1572868
  275.7 116.2 %copy-start.7 = (f32[512,1024]{1,0:T(8,128)}, f32[512,1024]{1,0:T(8,128)S(1)}, u32[]{:S(2)}) copy-start(f32[512,1024]{1,0:T(8,128)S(1)} %get-tuple-element.961) | copy-start | bytes 6291460
  275.7 116.2 %copy-start.83 = (f32[512]{0:T(512)}, f32[512]{0:T(512)S(1)}, u32[]{:S(2)}) copy-start(f32[512]{0:T(512)S(1)} %fusion.118) | copy-start | bytes 6148
  381.2 10.7 copy-start.26
  446.3 237.2 %reduce-scatter.15.cloned.1.call-start = ((), (), s32[]{:S(2)}) async-start(), calls=%async_computation.19 | async-start | bytes 1179648 | tf_op jit(solution)/shard_map/reduce_scatter | solution.py:444
  448.9 296.1 %all-gather.36.cloned.1.call-start = ((), (), s32[]{:S(2)}) async-start(), calls=%async_computation.28 | async-start | bytes 3538944 | tf_op jit(solution)/shard_map/all_gather | solution.py:35
  470.2 336.8 %reduce-scatter.25.cloned.1.call-start = ((), (), s32[]{:S(2)}) async-start(), calls=%async_computation.24 | async-start | bytes 1310720 | tf_op jit(solution)/shard_map/reduce_scatter | solution.py:500
  473.3 333.8 %reduce-scatter.21.cloned.1.call-start = ((), (), s32[]{:S(2)}) async-start(), calls=%async_computation.22 | async-start | bytes 1310720 | tf_op jit(solution)/shard_map/reduce_scatter | solution.py:494
  476.3 210.0 %copy-start.13 = (f32[512,1536]{1,0:T(8,128)S(1)}, f32[512,1536]{1,0:T(8,128)}, u32[]{:S(2)}) copy-start(f32[512,1536]{1,0:T(8,128)} %get-tuple-element.913) | copy-start | bytes 9437188
  476.3 346.3 %reduce-scatter.23.cloned.1.call-start = ((), (), s32[]{:S(2)}) async-start(), calls=%async_computation.23 | async-start | bytes 655360 | tf_op jit(solution)/shard_map/reduce_scatter | solution.py:497
  617.2 69.0 %copy-start.99 = (f32[512]{0:T(512)S(1)}, f32[512]{0:T(512)}, u32[]{:S(2)}) copy-start(f32[512]{0:T(512)} %copy-done.97) | copy-start | bytes 6148
  686.2 176.9 %reduce-scatter.19.cloned.1.call-start = ((), (), s32[]{:S(2)}) async-start(), calls=%async_computation.21 | async-start | bytes 3932160 | tf_op jit(solution)/shard_map/reduce_scatter | solution.py:491
  691.1 218.9 %reduce-scatter.29.cloned.1.call-start = ((), (), s32[]{:S(2)}) async-start(), calls=%async_computation.26 | async-start | bytes 5242880 | tf_op jit(solution)/shard_map/reduce_scatter | solution.py:509
  697.7 286.7 %reduce-scatter.27.cloned.1.call-start = ((), (), s32[]{:S(2)}) async-start(), calls=%async_computation.25 | async-start | bytes 10485760 | tf_op jit(solution)/shard_map/reduce_scatter | solution.py:506
  709.7 339.1 %reduce-scatter.17.cloned.1.call-start = ((), (), s32[]{:S(2)}) async-start(), calls=%async_computation.20 | async-start | bytes 8519680 | tf_op jit(solution)/shard_map/reduce_scatter | solution.py:476
  717.3 12.1 copy-start.43
  717.3 12.1 copy-start.46
  717.3 12.1 copy-start.52
  717.3 12.1 copy-start.61
  729.5 39.0 %copy-start.5 = (f32[512,1536]{0,1:T(8,128)S(1)}, f32[512,1536]{0,1:T(8,128)}, u32[]{:S(2)}) copy-start(f32[512,1536]{0,1:T(8,128)} %copy.129) | copy-start | bytes 9437188
  792.3 5.8 collective-permute-start.1
  805.6 278.8 %reduce-scatter.31.cloned.1.call-start = ((), (), s32[]{:S(2)}) async-start(), calls=%async_computation.29 | async-start | bytes 573440
  806.7 490.3 %all-reduce.25.cloned.1.call-start = ((), (), s32[]{:S(2)}) async-start(), calls=%async_computation.30 | async-start | bytes 12582912 | tf_op jit(solution)/shard_map/psum | solution.py:516
  1060.6 18.9 %copy-start.87 = (f32[512]{0:T(512)S(1)}, f32[512]{0:T(512)}, u32[]{:S(2)}) copy-start(f32[512]{0:T(512)} %copy-done.86) | copy-start | bytes 6148
  1060.6 18.9 %copy-start.82 = (f32[512]{0:T(512)S(1)}, f32[512]{0:T(512)}, u32[]{:S(2)}) copy-start(f32[512]{0:T(512)} %copy-done.81) | copy-start | bytes 6148
  1060.6 18.9 %copy-start.85 = (f32[512]{0:T(512)S(1)}, f32[512]{0:T(512)}, u32[]{:S(2)}) copy-start(f32[512]{0:T(512)} %copy-done.83) | copy-start | bytes 6148
  (74 other events, 326.1 us)
Sparse Core Ops, SparseCore 0:
  9.6 52.1 all-gather.25
  63.3 17.2 all-gather.19
  83.2 39.5 all-gather.17
  125.3 38.4 all-gather.21
  166.3 59.3 all-gather.33
  227.1 27.1 all-gather.27
  255.9 16.7 all-gather.23
  274.2 58.2 all-gather.29
  334.1 34.4 all-gather.31
  446.4 169.6 reduce-scatter.12
  620.6 62.8 reduce-scatter.14
  685.5 59.4 all-gather.35
  747.6 23.5 reduce-scatter.24
  773.7 24.8 reduce-scatter.20
  800.9 21.6 reduce-scatter.22
  825.2 37.9 reduce-scatter.18
  865.5 44.4 reduce-scatter.28
  912.6 71.7 reduce-scatter.26
  986.9 61.8 reduce-scatter.16
  1051.9 21.2 reduce-scatter.30
  1079.3 217.6 all-reduce.24
where the time goes:
time: 1330 us; the launch traced here: 1320 us
  waiting for transfers between devices  817 us (61%)
  matrix products  211 us (16%)
  other arithmetic  100 us (8%)
  blocking collectives  89.5 us (7%)
  local copies, waits for them, and re-layouts  60.3 us (5%)
  between operations  23.1 us (2%)
    psum x1, waiting for transfers between devices, per_device(): lax.psum(shares[1].astype(jnp.bfloat16), 'ctx').astype(jnp.float32)  185 us
    reduce_scatter x1, waiting for transfers between devices, per_device(): lax.psum_scatter(keys_complete.reshape(sequence_total, KEY_VALUE_HEADS *...  140 us
    reduce_scatter x1, waiting for transfers between devices, per_device(): lax.psum_scatter(gate_up_grad.astype(jnp.bfloat16), 'wshard', scatter_dim...  74.4 us
    reduce_scatter x1, waiting for transfers between devices, per_device(): lax.psum_scatter(values_complete.reshape(sequence_total, KEY_VALUE_HEADS...  66.2 us
    reduce_scatter x1, waiting for transfers between devices, per_device(): lax.psum_scatter(in_grad.astype(jnp.bfloat16), 'wshard', scatter_dimensio...  64.4 us
    all_gather x1, waiting for transfers between devices, per_device(): lax.all_gather(gate_up, 'wshard', axis=0, tiled=True)  56.8 us
    reduce_scatter x1, waiting for transfers between devices, per_device(): lax.psum_scatter(down_grad.astype(jnp.bfloat16), 'wshard', scatter_dimens...  46.9 us
    reduce_scatter x1, waiting for transfers between devices, per_device(): lax.psum_scatter(mixer_out_grad.astype(jnp.bfloat16), 'wshard', scatter_d...  40.5 us
  transfers between devices with their start and end apart: 23, of which 17 were waited for; matrix products, arithmetic and copies ran while one was open for 21% of the time, Pallas kernels for 0%

commit v1 on v0

v1 whole, which is shorter than its diff:
```python
from functools import partial

import jax
import jax.numpy as jnp
from jax import lax
from jax.experimental import pallas as pl
from jax.experimental.pallas import tpu as pltpu
from jax.sharding import PartitionSpec as P

FF = 2048
QUERY_HEADS = 8
KEY_VALUE_HEADS = 2
HEAD_SIZE = 64
HM = 24
PM = 64
NS = 128
KW = 4
DSSM = 1536

eps_norm = 1e-05
rope_base = 100000000000.0
mask_fill_value = -1e30
highest = lax.Precision.HIGHEST
MESH_AXES = ("ctx", "wshard")


def exchange(block, ctx_flip, shard_flip):
    blocks, shards = lax.axis_size("ctx"), lax.axis_size("wshard")
    route = [
        (c * shards + w, (c ^ ctx_flip) * shards + (w ^ shard_flip))
        for c in range(blocks)
        for w in range(shards)
    ]
    return lax.ppermute(block, MESH_AXES, route)


def from_behind(block, axis, distance):
    devices = range(lax.axis_size(axis))
    route = [(i - distance, i) for i in devices if i - distance in devices]
    return lax.ppermute(block, axis, route)


def swap_mirrored(block):
    count = lax.axis_size("ctx")
    return lax.ppermute(block, "ctx", [(i, count - 1 - i) for i in range(count)])


def place(pieces):
    total = sum(piece.shape[0] for _, piece in pieces)
    whole = jnp.zeros((total,) + pieces[0][1].shape[1:], pieces[0][1].dtype)
    for start, piece in pieces:
        whole = lax.dynamic_update_slice_in_dim(whole, piece, start, 0)
    return whole


def gather_shards(shard):
    rows = shard.shape[0]
    half = rows // 2
    w = lax.axis_index("wshard")
    side = lax.axis_index("ctx") % 2
    mine = lax.dynamic_slice_in_dim(shard, side * half, half, 0)
    beside = exchange(shard, 0, 1)
    across = exchange(mine, 0, 2)
    across_rest = exchange(across, 1, 0)
    far = exchange(across, 0, 1)
    far_rest = exchange(across_rest, 0, 1)
    here, there = side * half, (1 - side) * half
    return place(
        [
            (w * rows, shard),
            ((w ^ 1) * rows, beside),
            ((w ^ 2) * rows + here, across),
            ((w ^ 2) * rows + there, across_rest),
            ((w ^ 3) * rows + here, far),
            ((w ^ 3) * rows + there, far_rest),
        ]
    )


def gather_small(shard):
    rows = shard.shape[0]
    w = lax.axis_index("wshard")
    return place(
        [(w * rows, shard)]
        + [((w ^ flip) * rows, exchange(shard, 0, flip)) for flip in (1, 2, 3)]
    )


def add_low(first, *others):
    total = first.astype(jnp.float32)
    for other in others:
        total = total + other.astype(jnp.float32)
    return total.astype(jnp.bfloat16)


def ctx_sum(block):
    position = lax.axis_index("ctx")
    bits = []
    bit = 1
    while bit < lax.axis_size("ctx"):
        bits.append(bit)
        bit *= 2
    for bit in bits:
        half = block.shape[0] // 2
        up = (position // bit) % 2
        got = exchange(lax.dynamic_slice_in_dim(block, (1 - up) * half, half, 0), bit, 0)
        block = add_low(lax.dynamic_slice_in_dim(block, up * half, half, 0), got)
    for bit in reversed(bits):
        up = (position // bit) % 2
        got = exchange(block, bit, 0)
        block = jnp.where(
            up == 0, jnp.concatenate([block, got], axis=0), jnp.concatenate([got, block], axis=0)
        )
    return block.astype(jnp.float32)


def shard_pieces(array, axis):
    w = lax.axis_index("wshard")
    size = array.shape[axis] // 4

    def piece(flip):
        return lax.dynamic_slice_in_dim(array, (w ^ flip) * size, size, axis)

    return jnp.concatenate([piece(1), piece(3)], axis=axis), piece(2), piece(0)


def shard_sum(beside, across, own):
    rows = own.shape[0]
    got = exchange(beside.astype(jnp.bfloat16), 0, 1)
    got_across = exchange(add_low(across, got[rows:]), 0, 2)
    return add_low(own, got[:rows], got_across)


def weight_grad(left, right, axis=1):
    products = [
        lax.dot_general(
            piece, right, (((1 - axis,), (0,)), ((), ())), preferred_element_type=jnp.float32
        )
        for piece in shard_pieces(left, axis)
    ]
    return shard_sum(*products)


def mixed_dot(left, right):
    return jnp.dot(left, right, preferred_element_type=jnp.float32)


def rms_scale(value, gain):
    return value * lax.rsqrt(jnp.mean(value * value, axis=-1, keepdims=True) + eps_norm) * gain


def doc_numbers(lengths, position_index):
    ends = jnp.cumsum(lengths)[:-1]
    tally_count = jnp.sum((position_index[:, None] >= ends[None, :]).astype(jnp.int32), axis=1)
    return jnp.where(position_index >= 0, tally_count, -1)


def turn(value, position_index):
    half = value.shape[-2] // 2
    freq = rope_base ** (-jnp.arange(half, dtype=jnp.float32) / half)
    angle = freq[:, None] * position_index.astype(jnp.float32)[None, :]
    cosine = jnp.cos(angle)
    sine = jnp.sin(angle)
    first = value[..., :half, :]
    second = value[..., half:, :]
    return jnp.concatenate(
        [first * cosine - second * sine, second * cosine + first * sine], axis=-2
    )


def conv_local(taps, extended, weight, bias):
    tally_count = extended.shape[0] - (KW - 1)
    total = bias[None, :]
    for tap in range(KW):
        total = (
            total + weight[tap][None, :] * extended[tap : tap + tally_count] * taps[tap][:, None]
        )
    return jax.nn.silu(total)


def gate_norm(mixed, gate_z, gain):
    return rms_scale(mixed * jax.nn.silu(gate_z), gain)


def swiglu(gate_up_v):
    return jax.nn.silu(gate_up_v[:, :FF]) * gate_up_v[:, FF:]


def split_three(value):
    high = value.astype(jnp.bfloat16)
    rest = value - high.astype(jnp.float32)
    middle = rest.astype(jnp.bfloat16)
    low = (rest - middle.astype(jnp.float32)).astype(jnp.bfloat16)
    return [high, middle, low]


def nt_dot(left, right):
    return lax.dot_general(left, right, (((1,), (1,)), ((), ())), preferred_element_type=jnp.float32)


def causal_tile(scores, group, width):
    rows = lax.broadcasted_iota(jnp.int32, scores.shape, 0)
    columns = lax.broadcasted_iota(jnp.int32, scores.shape, 1)
    return jnp.where(rows <= lax.rem(columns, width) + group * width, scores, mask_fill_value)


def load_extended(extended, lower, value_ref, side_ref):
    for group in range(2):
        extended[group] = jnp.zeros(extended.shape[1:], extended.dtype)
        extended[group, lower : lower + HEAD_SIZE, :] = value_ref[group, 0]
        extended[group, 128:144, :] = side_ref[group, 0]


def attend_forward_body(
    width, blocks, pair_ref, side_ref, query_ref, query_side_ref, heads_ref, log_ref, query_x, peak, total
):
    step = pl.program_id(1)

    @pl.when(step == 0)
    def start():
        load_extended(query_x, 0, query_ref, query_side_ref)
        peak[...] = jnp.full(peak.shape, mask_fill_value, jnp.float32)
        total[...] = jnp.zeros(total.shape, jnp.float32)

    @pl.when(step <= jnp.maximum(blocks[0], blocks[1]))
    def work():
        keys = jnp.concatenate([pair_ref[0, 0], side_ref[...]], axis=1)
        values = keys.T[HEAD_SIZE:144]

        def tile(group, masked):
            scores = mixed_dot(keys, query_x[group])
            if masked:
                scores = causal_tile(scores, group, width)
            old = peak[group]
            new = jnp.maximum(old, jnp.max(scores, axis=0, keepdims=True))
            probs = jnp.exp(scores - new)
            total[group] = total[group] * jnp.exp(old - new) + mixed_dot(
                values, probs.astype(jnp.bfloat16)
            )
            peak[group] = new

        for group in range(2):
            pl.when(step < blocks[group])(partial(tile, group, False))
            pl.when(step == blocks[group])(partial(tile, group, True))

    @pl.when(step == pl.num_programs(1) - 1)
    def finish():
        for group in range(2):
            weight = total[group, HEAD_SIZE + 8 : HEAD_SIZE + 9, :]
            heads_ref[group, 0] = total[group, :HEAD_SIZE, :] / weight
            log_ref[group, 0] = peak[group] + jnp.log(weight)


def attend_backward_body(
    width,
    blocks,
    pair_ref,
    side_ref,
    query_ref,
    query_side_ref,
    grad_ref,
    grad_side_ref,
    query_grad_ref,
    pair_grad_ref,
    query_x,
    grad_x,
    pair_acc,
):
    step = pl.program_id(1)

    @pl.when(step == 0)
    def start():
        load_extended(query_x, 0, query_ref, query_side_ref)
        load_extended(grad_x, HEAD_SIZE, grad_ref, grad_side_ref)
        query_grad_ref[...] = jnp.zeros(query_grad_ref.shape, jnp.float32)

    pair_acc[...] = jnp.zeros(pair_acc.shape, jnp.float32)

    @pl.when(step <= jnp.maximum(blocks[0], blocks[1]))
    def work():
        pair = pair_ref[0, 0]
        keys = jnp.concatenate([pair, side_ref[...]], axis=1)
        turned = pair.T[:HEAD_SIZE]

        def tile(group, masked):
            scores = mixed_dot(keys, query_x[group])
            if masked:
                scores = causal_tile(scores, group, width)
            probs = jnp.exp(scores)
            low = (probs * mixed_dot(keys, grad_x[group])).astype(jnp.bfloat16)
            pair_acc[...] += nt_dot(low, query_x[group, :128, :]) + nt_dot(
                probs.astype(jnp.bfloat16), grad_x[group, :128, :]
            )
            query_grad_ref[group, 0] += mixed_dot(turned, low)

        for group in range(2):
            pl.when(step < blocks[group])(partial(tile, group, False))
            pl.when(step == blocks[group])(partial(tile, group, True))

    pair_grad_ref[0, 0] = pair_acc[...].astype(jnp.bfloat16)


def attention_calls(rows, count):
    width = rows // 2
    span = width * (QUERY_HEADS // KEY_VALUE_HEADS)

    def last(blocks):
        return jnp.maximum(blocks[0], blocks[1])

    pair_spec = pl.BlockSpec(
        (1, 1, rows, 128), lambda g, k, blocks: (jnp.minimum(k, last(blocks)), g, 0, 0)
    )
    side_spec = pl.BlockSpec((rows, 128), lambda g, k, blocks: (jnp.minimum(k, last(blocks)), 0))

    def per_group(height):
        return pl.BlockSpec((2, 1, height, span), lambda g, k, blocks: (0, g, 0, 0))

    elements = KEY_VALUE_HEADS * (count + 1) * rows * span
    params = pltpu.CompilerParams(
        dimension_semantics=("arbitrary", "arbitrary"), vmem_limit_bytes=48 * 1024 * 1024
    )
    forward = pl.pallas_call(
        partial(attend_forward_body, width),
        grid_spec=pltpu.PrefetchScalarGridSpec(
            num_scalar_prefetch=1,
            grid=(KEY_VALUE_HEADS, count),
            in_specs=[pair_spec, side_spec, per_group(HEAD_SIZE), per_group(16)],
            out_specs=[per_group(HEAD_SIZE), per_group(1)],
            scratch_shapes=[
                pltpu.VMEM((2, 256, span), jnp.bfloat16),
                pltpu.VMEM((2, 1, span), jnp.float32),
                pltpu.VMEM((2, 144 - HEAD_SIZE, span), jnp.float32),
            ],
        ),
        out_shape=[
            jax.ShapeDtypeStruct((2, KEY_VALUE_HEADS, HEAD_SIZE, span), jnp.float32),
            jax.ShapeDtypeStruct((2, KEY_VALUE_HEADS, 1, span), jnp.float32),
        ],
        compiler_params=params,
        cost_estimate=pl.CostEstimate(
            flops=elements * 512, bytes_accessed=8 * rows * 1024 * count, transcendentals=elements
        ),
        name="attend_forward",
    )
    backward = pl.pallas_call(
        partial(attend_backward_body, width),
        grid_spec=pltpu.PrefetchScalarGridSpec(
            num_scalar_prefetch=1,
            grid=(KEY_VALUE_HEADS, count),
            in_specs=[
                pair_spec,
                side_spec,
                per_group(HEAD_SIZE),
                per_group(16),
                per_group(HEAD_SIZE),
                per_group(16),
            ],
            out_specs=[
                per_group(HEAD_SIZE),
                pl.BlockSpec((1, 1, rows, 128), lambda g, k, blocks: (k, g, 0, 0)),
            ],
            scratch_shapes=[
                pltpu.VMEM((2, 256, span), jnp.bfloat16),
                pltpu.VMEM((2, 256, span), jnp.bfloat16),
                pltpu.VMEM((rows, 128), jnp.float32),
            ],
        ),
        out_shape=[
            jax.ShapeDtypeStruct((2, KEY_VALUE_HEADS, HEAD_SIZE, span), jnp.float32),
            jax.ShapeDtypeStruct((count, KEY_VALUE_HEADS, rows, 128), jnp.bfloat16),
        ],
        compiler_params=params,
        cost_estimate=pl.CostEstimate(
            flops=elements * 1280, bytes_accessed=8 * rows * 1024 * count, transcendentals=elements
        ),
        name="attend_backward",
    )
    return forward, backward


def pick(pair):
    lane = lax.broadcasted_iota(jnp.int32, (pair.shape[0], 2 * PM), 1)
    return jnp.where(lane < PM, pair[:, 0:1], pair[:, 1:2])


def outer_body(rows_ref, left_ref, right_ref, out_ref):
    for at in range(rows_ref.shape[0]):
        scale = pick(rows_ref[at])
        left = left_ref[:, at * 128 : (at + 1) * 128].astype(jnp.float32) * scale
        out_ref[at * 128 : (at + 1) * 128, :] = lax.dot_general(
            left.astype(jnp.bfloat16),
            right_ref[...],
            (((0,), (0,)), ((), ())),
            preferred_element_type=jnp.float32,
        ).astype(out_ref.dtype)


def mixed_body(
    skip_ref, x_ref, b_ref, c_ref, column_ref, row_ref, entry_ref, docs_column, docs_row, state_ref, out_ref, fill, products
):
    rows = x_ref.shape[0]
    half = rows // 2

    @pl.when(pl.program_id(0) == 0)
    def start():
        at = lax.broadcasted_iota(jnp.int32, (rows, rows), 0)
        source = lax.broadcasted_iota(jnp.int32, (rows, rows), 1)
        same = (at >= source) & (docs_column[...] == docs_row[...])
        fill[...] = jnp.where(same, 0.0, mask_fill_value)
        products[...] = nt_dot(c_ref[...], b_ref[...])

    x = x_ref[...]
    lane = lax.broadcasted_iota(jnp.int32, (half, 2 * PM), 1)
    for block in range(2):
        here = slice(block * half, (block + 1) * half)
        width = (block + 1) * half
        parts = []
        for head in range(2):
            decay = jnp.exp(
                (column_ref[0, here, head : head + 1] - row_ref[0, head : head + 1, :width])
                + fill[here, :width]
            )
            weights = (products[here, :width] * decay).astype(jnp.bfloat16)
            parts.append(mixed_dot(weights, x[:width]))
        local = jnp.where(lane < PM, parts[0], parts[1])
        inner = nt_dot(c_ref[here, :], state_ref[...].astype(jnp.bfloat16))
        out_ref[here, :] = (
            local + inner * pick(entry_ref[0, here, :]) + x[here].astype(jnp.float32) * skip_ref[0]
        )


def mixed_grad_body(
    skip_ref,
    x_ref,
    b_ref,
    c_ref,
    column_ref,
    row_ref,
    entry_ref,
    tail_ref,
    docs_column,
    docs_row,
    state_ref,
    state_grad_ref,
    grad_ref,
    out_ref,
    skip_grad_ref,
    fill,
    products,
    scores,
    b_grad,
    c_grad,
):
    rows = x_ref.shape[0]
    half = rows // 2
    step = pl.program_id(0)
    pairs = HM // 2

    @pl.when(step == 0)
    def start():
        source = lax.broadcasted_iota(jnp.int32, (rows, rows), 0)
        at = lax.broadcasted_iota(jnp.int32, (rows, rows), 1)
        same = (at >= source) & (docs_column[...] == docs_row[...])
        fill[...] = jnp.where(same, 0.0, mask_fill_value)
        products[...] = nt_dot(b_ref[...], c_ref[...])
        scores[...] = jnp.zeros(scores.shape, jnp.float32)
        b_grad[...] = jnp.zeros(b_grad.shape, jnp.float32)
        c_grad[...] = jnp.zeros(c_grad.shape, jnp.float32)

    @pl.when(step < pairs)
    def work():
        x = x_ref[...]
        x_f = x.astype(jnp.float32)
        grad = grad_ref[...]
        low = grad.astype(jnp.bfloat16)
        lane = lax.broadcasted_iota(jnp.int32, (half, 2 * PM), 1)
        lane_all = lax.broadcasted_iota(jnp.int32, (rows, 2 * PM), 1)
        skip_grad_ref[0] = jnp.sum(grad * x_f, axis=0, keepdims=True)
        state_grad = state_grad_ref[...].astype(jnp.bfloat16)
        tail = pick(tail_ref[0])
        b_grad[...] += mixed_dot((x_f * tail).astype(jnp.bfloat16), state_grad)
        entered = (low.astype(jnp.float32) * pick(entry_ref[0])).astype(jnp.bfloat16)
        c_grad[...] += mixed_dot(entered, state_ref[...].astype(jnp.bfloat16))
        passed = nt_dot(b_ref[...], state_grad) * tail + grad * skip_ref[0]
        chosen = [
            jnp.where((lane_all < PM) == (head == 0), x_f, 0.0).astype(jnp.bfloat16)
            for head in range(2)
        ]
        for block in range(2):
            here = slice(block * half, (block + 1) * half)
            start_at = block * half
            parts = []
            for head in range(2):
                decay = jnp.exp(
                    (row_ref[0, head : head + 1, start_at:] - column_ref[0, here, head : head + 1])
                    + fill[here, start_at:]
                )
                weights = (products[here, start_at:] * decay).astype(jnp.bfloat16)
                parts.append(mixed_dot(weights, low[start_at:]))
                scores[here, start_at:] += nt_dot(chosen[head][here], low[start_at:]) * decay
            out_ref[here, :] = jnp.where(lane < PM, parts[0], parts[1]) + passed[here]

    @pl.when(step == pairs)
    def give_b():
        out_ref[...] = b_grad[...] + mixed_dot(scores[...].astype(jnp.bfloat16), c_ref[...])

    @pl.when(step == pairs + 1)
    def give_c():
        out_ref[...] = c_grad[...] + lax.dot_general(
            scores[...].astype(jnp.bfloat16),
            b_ref[...],
            (((0,), (0,)), ((), ())),
            preferred_element_type=jnp.float32,
        )


def mixer_calls(rows):
    pairs = HM // 2
    wide = 2 * PM
    params = pltpu.CompilerParams(
        dimension_semantics=("arbitrary",), vmem_limit_bytes=48 * 1024 * 1024
    )

    def capped(p):
        return jnp.minimum(p, pairs - 1)

    def outer(right_at):
        each = 2
        return pl.pallas_call(
            outer_body,
            grid=(pairs // each,),
            in_specs=[
                pl.BlockSpec((each, rows, 2), lambda p: (p, 0, 0)),
                pl.BlockSpec((rows, each * wide), lambda p: (0, p)),
                pl.BlockSpec((rows, NS), lambda p: (0, right_at)),
            ],
            out_specs=pl.BlockSpec((each * wide, NS), lambda p: (p, 0)),
            out_shape=jax.ShapeDtypeStruct((DSSM, NS), jnp.bfloat16),
            compiler_params=params,
            cost_estimate=pl.CostEstimate(
                flops=2 * rows * DSSM * NS, bytes_accessed=6 * rows * DSSM, transcendentals=0
            ),
            name="state_outer",
        )

    x_spec = pl.BlockSpec((rows, wide), lambda p: (0, capped(p)))
    b_spec = pl.BlockSpec((rows, NS), lambda p: (0, DSSM // NS))
    c_spec = pl.BlockSpec((rows, NS), lambda p: (0, DSSM // NS + 1))
    column_spec = pl.BlockSpec((1, rows, 2), lambda p: (capped(p), 0, 0))
    row_spec = pl.BlockSpec((1, 2, rows), lambda p: (capped(p), 0, 0))
    skip_spec = pl.BlockSpec((1, 1, wide), lambda p: (capped(p), 0, 0))
    state_spec = pl.BlockSpec((wide, NS), lambda p: (capped(p), 0))
    docs_specs = [pl.BlockSpec((rows, 1), lambda p: (0, 0)), pl.BlockSpec((1, rows), lambda p: (0, 0))]
    square = pltpu.VMEM((rows, rows), jnp.float32)
    narrow = pltpu.VMEM((rows, NS), jnp.float32)
    forward = pl.pallas_call(
        mixed_body,
        grid=(pairs,),
        in_specs=[skip_spec, x_spec, b_spec, c_spec, column_spec, row_spec, column_spec]
        + docs_specs
        + [state_spec],
        out_specs=pl.BlockSpec((rows, wide), lambda p: (0, p)),
        out_shape=jax.ShapeDtypeStruct((rows, DSSM), jnp.float32),
        scratch_shapes=[square, square],
        compiler_params=params,
        cost_estimate=pl.CostEstimate(
            flops=4 * rows * rows * DSSM, bytes_accessed=8 * rows * DSSM, transcendentals=HM * rows * rows
        ),
        name="mixer_forward",
    )
    backward = pl.pallas_call(
        mixed_grad_body,
        grid=(pairs + 2,),
        in_specs=[skip_spec, x_spec, b_spec, c_spec, column_spec, row_spec, column_spec, column_spec]
        + docs_specs
        + [state_spec, state_spec, x_spec],
        out_specs=[
            pl.BlockSpec((rows, wide), lambda p: (0, p)),
            pl.BlockSpec((1, 1, wide), lambda p: (capped(p), 0, 0)),
        ],
        out_shape=[
            jax.ShapeDtypeStruct((rows, DSSM + 2 * NS), jnp.float32),
            jax.ShapeDtypeStruct((pairs, 1, wide), jnp.float32),
        ],
        scratch_shapes=[square, square, square, narrow, narrow],
        compiler_params=params,
        cost_estimate=pl.CostEstimate(
            flops=8 * rows * rows * DSSM, bytes_accessed=12 * rows * DSSM, transcendentals=HM * rows * rows
        ),
        name="mixer_backward",
    )
    return outer, forward, backward


def chain(parts, gains, reverse):
    count, position = lax.axis_size("ctx"), lax.axis_index("ctx")
    factor = jnp.ones((HM,), jnp.float32)
    total = jnp.zeros((HM, PM, NS), jnp.float32)
    for at in range(count) if reverse else reversed(range(count)):
        reached = at > position if reverse else at < position
        part = parts[at].reshape(HM, PM, NS).astype(jnp.float32)
        total = total + jnp.where(reached, factor, 0.0)[:, None, None] * part
        factor = factor * jnp.where(reached, gains[at], 1.0)
    return total.reshape(DSSM, NS)


def pack_small(norm, conv_weight, conv_bias, skip, mixer, ffn, shards):
    pieces = [
        norm.reshape(shards, -1),
        conv_weight.reshape(KW, shards, -1).transpose(1, 0, 2).reshape(shards, -1),
        conv_bias.reshape(shards, -1),
        mixer.reshape(shards, -1),
        ffn.reshape(shards, -1),
        skip.reshape(shards, -1),
    ]
    packed = jnp.concatenate(pieces, axis=1)
    packed = jnp.pad(packed, ((0, 0), (0, 4096 - packed.shape[1])))
    return packed.reshape(shards * 32, 128)


def unpack_small(packed, model, channels, heads, shards):
    packed = packed.reshape(shards, 4096)
    sizes = [model, KW * channels, channels, DSSM, model, heads]
    parts, start = [], 0
    for size in sizes:
        width = size // 4
        parts.append(packed[:, start : start + width])
        start += width
    norm, conv_weight, conv_bias, mixer, ffn, skip = parts
    conv_weight = conv_weight.reshape(shards, KW, -1).transpose(1, 0, 2).reshape(KW, -1)
    return (
        norm.reshape(-1),
        conv_weight,
        conv_bias.reshape(-1),
        skip.reshape(-1),
        mixer.reshape(-1),
        ffn.reshape(-1),
    )


def per_device(
    tokens,
    cotangent,
    doc_lengths,
    decay,
    norm_gain,
    in_proj,
    conv_weight,
    conv_bias,
    skip_gain,
    mixer_gain,
    mixer_out,
    query_proj,
    key_value_projection,
    attn_out,
    ffn_gain,
    gate_up,
    down_proj,
):
    rows, model = tokens.shape[1:]
    width = rows // 2
    shards = lax.axis_size("wshard")
    channels = conv_bias.shape[0] * shards
    count, block_at = lax.axis_size("ctx"), lax.axis_index("ctx")
    sequence_total = rows * count
    heads_per_group = QUERY_HEADS // KEY_VALUE_HEADS
    scale = HEAD_SIZE ** (-0.5)
    attend_forward, attend_backward = attention_calls(rows, count)
    state_outer, mixer_forward, mixer_backward = mixer_calls(rows)

    small = gather_small(
        pack_small(norm_gain, conv_weight, conv_bias, skip_gain, mixer_gain, ffn_gain, 1)
    )
    norm_w, conv_w, conv_b, skip_w, mixer_g, ffn_g = (
        part.astype(jnp.float32) for part in unpack_small(small, model, channels, HM, shards)
    )
    attn_pair_w = gather_shards(jnp.concatenate([query_proj, key_value_projection], axis=1))
    in_w = gather_shards(in_proj)
    mixer_w = gather_shards(mixer_out)
    attn_w = gather_shards(attn_out)
    gate_up_w = gather_shards(gate_up)
    down_w = gather_shards(down_proj)
    query_w = attn_pair_w[:, : QUERY_HEADS * HEAD_SIZE]
    keyval_w = attn_pair_w[:, QUERY_HEADS * HEAD_SIZE :]

    lengths = doc_lengths[0]
    doc_count = lengths.shape[0]
    position_index = block_at * rows + jnp.arange(rows, dtype=jnp.int32)
    docs = doc_numbers(lengths, position_index)
    doc_prev = doc_numbers(lengths, position_index[:1] - 1)[0]
    log_decay = jnp.log(decay[0])
    source = tokens[0].astype(jnp.float32)
    normed, norm_pull = jax.vjp(rms_scale, source, norm_w)
    normed_b = normed.astype(jnp.bfloat16)

    turned_q = turn(
        lax.dot_general(
            query_w, normed_b, (((0,), (1,)), ((), ())), preferred_element_type=jnp.float32
        ).reshape(QUERY_HEADS, HEAD_SIZE, rows),
        position_index,
    ).astype(jnp.bfloat16)
    key_value_pair = lax.dot_general(
        keyval_w, normed_b, (((0,), (1,)), ((), ())), preferred_element_type=jnp.float32
    ).reshape(2, KEY_VALUE_HEADS, HEAD_SIZE, rows)
    keys_b = turn(key_value_pair[0], position_index).astype(jnp.bfloat16)
    values_b = key_value_pair[1].astype(jnp.bfloat16)
    pairs = lax.all_gather(
        jnp.concatenate([keys_b, values_b], axis=1).transpose(0, 2, 1), "ctx"
    )

    def to_groups(array):
        return (
            array.reshape(KEY_VALUE_HEADS, heads_per_group, HEAD_SIZE, 2, width)
            .transpose(3, 0, 2, 1, 4)
            .reshape(2, KEY_VALUE_HEADS, HEAD_SIZE, heads_per_group * width)
        )

    def from_groups(array):
        return (
            array.reshape(2, KEY_VALUE_HEADS, HEAD_SIZE, heads_per_group, width)
            .transpose(1, 3, 2, 0, 4)
            .reshape(QUERY_HEADS * HEAD_SIZE, rows)
        )

    def balance(array):
        return jnp.stack([array[0], swap_mirrored(array[1])])

    query_x = balance(to_groups(turned_q) * jnp.asarray(scale, jnp.bfloat16))
    mirrored = count - 1 - block_at
    group_blocks = jnp.stack([block_at, mirrored]).astype(jnp.int32)
    group_positions = jnp.stack(
        [
            block_at * rows + jnp.arange(width, dtype=jnp.int32),
            mirrored * rows + width + jnp.arange(width, dtype=jnp.int32),
        ]
    )
    group_docs = jnp.stack([doc_numbers(lengths, group_positions[at]) for at in range(2)])
    key_docs = doc_numbers(lengths, jnp.arange(sequence_total, dtype=jnp.int32))
    lane = jnp.arange(128)[None, :]
    key_side = ((key_docs[:, None] == lane) | ((lane >= 8) & (lane < 11))).astype(jnp.bfloat16)
    doc_rows = jnp.where(
        jnp.arange(doc_count)[None, :, None] == group_docs[:, None, :], 0.0, mask_fill_value
    ).astype(jnp.bfloat16)
    doc_rows = jnp.tile(doc_rows, (1, 1, heads_per_group))[:, None]
    doc_rows = jnp.broadcast_to(doc_rows, (2, KEY_VALUE_HEADS) + doc_rows.shape[2:])

    def side_rows(first, extra):
        first = jnp.pad(first, ((0, 0), (0, 0), (0, 8 - first.shape[2]), (0, 0)))
        if extra is None:
            return jnp.pad(first, ((0, 0), (0, 0), (0, 8), (0, 0)))
        extra = jnp.concatenate(split_three(-extra), axis=2)
        return jnp.concatenate(
            [first, jnp.pad(extra, ((0, 0), (0, 0), (0, 5), (0, 0)))], axis=2
        )

    projected = mixed_dot(normed_b, in_w)
    gate_z = projected[:, :DSSM]
    pre_b = projected[:, DSSM:].astype(jnp.bfloat16)
    rim = from_behind(pre_b[rows - (KW - 1) :], "ctx", 1)
    extended = jnp.concatenate([rim, pre_b], axis=0).astype(jnp.float32)
    taps = jnp.stack(
        [
            (doc_numbers(lengths, position_index - (KW - 1) + tap) == docs).astype(jnp.float32)
            for tap in range(KW)
        ]
    )
    conv_f, conv_pull = jax.vjp(partial(conv_local, taps), extended, conv_w, conv_b)
    conv_b16 = conv_f.astype(jnp.bfloat16)
    order = jnp.arange(rows)
    running = jnp.dot(
        log_decay, (order[:, None] <= order[None, :]).astype(jnp.float32), precision=highest
    )
    entry = jnp.where((docs == doc_prev)[None, :], jnp.exp(running), 0.0)
    tail = jnp.where((docs == docs[-1])[None, :], jnp.exp(running[:, -1:] - running), 0.0)
    carry_gain = jnp.where(docs[-1] == doc_prev, jnp.exp(running[:, -1]), 0.0)

    def columns(array):
        return array.reshape(HM // 2, 2, rows).transpose(0, 2, 1)

    running_rows = running.reshape(HM // 2, 2, rows)
    running_columns, entry_columns, tail_columns = columns(running), columns(entry), columns(tail)
    skip_wide = jnp.repeat(skip_w, PM).reshape(HM // 2, 1, 2 * PM)
    docs_column, docs_row = docs[:, None], docs[None, :]
    fresh = state_outer(DSSM // NS)(tail_columns, conv_b16, conv_b16)
    gain_rows = jnp.pad(jnp.stack(split_three(carry_gain)), ((0, 13), (0, NS - HM)))
    collected = lax.all_gather(jnp.concatenate([fresh, gain_rows], axis=0), "ctx")
    gains = jnp.sum(collected[:, DSSM : DSSM + 3, :HM].astype(jnp.float32), axis=1)
    state_in = chain(collected[:, :DSSM], gains, False)

    doc_side = side_rows(doc_rows, None)
    heads_x, log_x = attend_forward(group_blocks, pairs, key_side, query_x, doc_side)
    heads_t = from_groups(balance(heads_x.astype(jnp.bfloat16)))

    mixed = mixer_forward(
        skip_wide,
        conv_b16,
        conv_b16,
        conv_b16,
        running_columns,
        running_rows,
        entry_columns,
        docs_column,
        docs_row,
        state_in,
    )
    gated, gate_pull = jax.vjp(gate_norm, mixed, gate_z, mixer_g)
    gated_b = gated.astype(jnp.bfloat16)
    mamba = mixed_dot(gated_b, mixer_w)
    attn = lax.dot_general(
        heads_t, attn_w, (((0,), (0,)), ((), ())), preferred_element_type=jnp.float32
    )
    middle = source + attn + mamba
    normed2, ffn_pull = jax.vjp(rms_scale, middle, ffn_g)
    normed2_b = normed2.astype(jnp.bfloat16)
    gate_up_v = mixed_dot(normed2_b, gate_up_w)
    activated, act_pull = jax.vjp(swiglu, gate_up_v)
    activated_b = activated.astype(jnp.bfloat16)
    layer_out = (middle + mixed_dot(activated_b, down_w)).astype(jnp.bfloat16)

    out_low = cotangent[0]
    down_share = ctx_sum(weight_grad(activated_b, out_low))
    (gate_up_grad_v,) = act_pull(nt_dot(out_low, down_w))
    gate_up_low = gate_up_grad_v.astype(jnp.bfloat16)
    gate_up_share = ctx_sum(weight_grad(normed2_b, gate_up_low))
    middle_norm_grad, ffn_gain_grad = ffn_pull(nt_dot(gate_up_low, gate_up_w))
    middle_grad = out_low.astype(jnp.float32) + middle_norm_grad
    middle_low = middle_grad.astype(jnp.bfloat16)
    heads_low = nt_dot(attn_w, middle_low).astype(jnp.bfloat16)
    grad_x = balance(to_groups(heads_low))
    gated_grad = nt_dot(middle_low, mixer_w)
    mixed_grad, gate_z_grad, mixer_gain_grad = gate_pull(gated_grad)
    upward = state_outer(DSSM // NS + 1)(entry_columns, mixed_grad.astype(jnp.bfloat16), conv_b16)
    state_out_grad = chain(lax.all_gather(upward, "ctx"), gains, True)
    attn_share = ctx_sum(weight_grad(heads_t, middle_low, 0))
    mixer_share = ctx_sum(weight_grad(gated_b, middle_low))
    gate_z_low = gate_z_grad.astype(jnp.bfloat16)
    in_share_z = ctx_sum(weight_grad(normed_b, gate_z_low))

    delta = jnp.sum(grad_x.astype(jnp.float32) * heads_x, axis=2, keepdims=True)
    query_grad_x, pairs_grad = attend_backward(
        group_blocks,
        pairs,
        key_side,
        query_x,
        side_rows(doc_rows, log_x),
        grad_x,
        side_rows(jnp.zeros_like(doc_rows), delta),
    )
    pair_grad = (
        lax.psum_scatter(pairs_grad, "ctx", scatter_dimension=0)
        .astype(jnp.float32)
        .transpose(0, 2, 1)
    )
    query_back = jnp.stack(
        [
            turn(
                query_grad_x[at].reshape(KEY_VALUE_HEADS, HEAD_SIZE, heads_per_group * width),
                -jnp.tile(group_positions[at], heads_per_group),
            )
            for at in range(2)
        ]
    )
    query_low = from_groups(balance((query_back * scale).astype(jnp.bfloat16)))

    conv_grad, skip_parts = mixer_backward(
        skip_wide,
        conv_b16,
        conv_b16,
        conv_b16,
        running_columns,
        running_rows,
        entry_columns,
        tail_columns,
        docs_column,
        docs_row,
        state_in,
        state_out_grad,
        mixed_grad,
    )
    skip_grad = jnp.sum(skip_parts.reshape(HM, PM), axis=1)
    extended_grad, conv_weight_grad, conv_bias_grad = conv_pull(conv_grad)
    from_above = from_behind(extended_grad[: KW - 1], "ctx", -1)
    pre_grad = extended_grad[KW - 1 :] + jnp.pad(from_above, ((rows - (KW - 1), 0), (0, 0)))
    pre_low = pre_grad.astype(jnp.bfloat16)
    in_share_pre = ctx_sum(weight_grad(normed_b, pre_low))
    projected_low = jnp.concatenate([gate_z_low, pre_low], axis=1)
    normed_grad = nt_dot(projected_low, in_w)

    keys_low = turn(pair_grad[:, :HEAD_SIZE], -position_index)
    keyval_low = jnp.concatenate(
        [
            keys_low.reshape(KEY_VALUE_HEADS * HEAD_SIZE, rows),
            pair_grad[:, HEAD_SIZE:].reshape(KEY_VALUE_HEADS * HEAD_SIZE, rows),
        ],
        axis=0,
    ).astype(jnp.bfloat16)
    attn_pair_low = jnp.concatenate([query_low, keyval_low], axis=0).T
    attn_pair_share = ctx_sum(weight_grad(normed_b, attn_pair_low))
    normed_grad = normed_grad + nt_dot(attn_pair_low, attn_pair_w)
    source_grad, norm_grad = norm_pull(normed_grad)
    tokens_grad = (middle_grad + source_grad)[None]

    small_grad = pack_small(
        norm_grad, conv_weight_grad, conv_bias_grad, skip_grad, mixer_gain_grad, ffn_gain_grad, shards
    )
    small_share = ctx_sum(shard_sum(*shard_pieces(small_grad, 0)))
    norm_share, conv_w_share, conv_b_share, skip_share, mixer_g_share, ffn_share = unpack_small(
        small_share, model, channels, HM, 1
    )
    return (
        layer_out[None],
        tokens_grad,
        norm_share,
        jnp.concatenate([in_share_z, in_share_pre], axis=1),
        conv_w_share,
        conv_b_share,
        skip_share,
        mixer_g_share,
        mixer_share,
        attn_pair_share[:, : QUERY_HEADS * HEAD_SIZE],
        attn_pair_share[:, QUERY_HEADS * HEAD_SIZE :],
        attn_share,
        ffn_share,
        gate_up_share,
        down_share,
    )


def solution(mesh):
    in_specs = (
        P("wshard", "ctx", None),
        P("wshard", "ctx", None),
        P("wshard", None),
        P("wshard", None, "ctx"),
        P("wshard"),
        P("wshard", None),
        P(None, "wshard"),
        P("wshard"),
        P("wshard"),
        P("wshard"),
        P("wshard", None),
        P("wshard", None),
        P("wshard", None),
        P("wshard", None),
        P("wshard"),
        P("wshard", None),
        P("wshard", None),
    )
    out_specs = (
        P("wshard", "ctx", None),
        P("wshard", "ctx", None),
        P("wshard"),
        P("wshard", None),
        P(None, "wshard"),
        P("wshard"),
        P("wshard"),
        P("wshard"),
        P("wshard", None),
        P("wshard", None),
        P("wshard", None),
        P("wshard", None),
        P("wshard"),
        P("wshard", None),
        P("wshard", None),
    )
    return jax.shard_map(
        per_device, mesh=mesh, in_specs=in_specs, out_specs=out_specs, check_vma=False
    )
```

time: 1330 us -> 893 us (0.67)
  waiting for transfers between devices: 817 us -> 290 us
  local copies, waits for them, and re-layouts: 60.3 us -> 163 us
  starting transfers between devices: 6.16 us -> 103 us
  matrix products: 211 us -> 116 us
  Pallas kernels: 0 us -> 91.9 us
  blocking collectives: 89.5 us -> 0 us
    reduce_scatter x9 -> x1, waiting for transfers between devices: 448 us -> 0.01 us  [per_device(): lax.psum_scatter(pairs_grad, 'ctx', scatter_dimension=0).astype(jnp.float32)]
    ppermute x0 -> x101, waiting for transfers between devices: none -> 286 us  [the longest x97 274 us: exchange(): return lax.ppermute(block, MESH_AXES, route)]
    psum x1 -> x0, waiting for transfers between devices: 185 us -> none  [per_device(): lax.psum(shares[1].astype(jnp.bfloat16), 'ctx').astype(jnp.float32)]
    all_gather x10 -> x3, waiting for transfers between devices: 177 us -> 0.01 us  [the longest x1 0.01 us: per_device(): lax.all_gather(jnp.concatenate([keys_b, values_b], axis=1).transpose(0, 2...]
    ppermute x0 -> x101, starting transfers between devices: none -> 98.8 us  [the longest x97 83.5 us: exchange(): return lax.ppermute(block, MESH_AXES, route)]
    pallas_call x0 -> x6, Pallas kernels: none -> 91.9 us  [the longest x1 30.6 us: per_device(): attend_backward(group_blocks, pairs, key_side, query_x, side_rows(doc_row...]
    dot_general x33 -> x31, matrix products: 174 us -> 91.6 us  [the longest x21 42.2 us: weight_grad(): lax.dot_general(piece, right, (((1 - axis,), (0,)), ((), ())), preferred_...]
    dynamic_update_slice x12 -> x40, local copies, waits for them, and re-layouts: 4.69 us -> 50.2 us  [place(): whole = lax.dynamic_update_slice_in_dim(whole, piece, start, 0)]
  transfers between devices with their start and end apart: 23 -> 107, of which waited for: 17 -> 47; matrix products, arithmetic and copies ran while one was open for 21% -> 33% of each run, Pallas kernels for 0% -> 9%
where the time goes in v1:
time: 893 us; the launch traced here: 886 us
  waiting for transfers between devices  290 us (32%)
  local copies, waits for them, and re-layouts  163 us (18%)
  matrix products  116 us (13%)
  starting transfers between devices  103 us (12%)
  other arithmetic  102 us (11%)
  Pallas kernels  91.9 us (10%)
  between operations  19 us (2%)
    ppermute x97, waiting for transfers between devices, exchange(): return lax.ppermute(block, MESH_AXES, route)  274 us
    ppermute x97, starting transfers between devices, exchange(): return lax.ppermute(block, MESH_AXES, route)  83.5 us
    dynamic_update_slice x40, local copies, waits for them, and re-layouts, place(): whole = lax.dynamic_update_slice_in_dim(whole, piece, start, 0)  50.2 us
    dot_general x21, matrix products, weight_grad(): lax.dot_general(piece, right, (((1 - axis,), (0,)), ((), ())), preferred_...  42.2 us
    dot_general x6, matrix products, nt_dot(): lax.dot_general(left, right, (((1,), (1,)), ((), ())), preferred_element_...  41.1 us
    pallas_call x1, Pallas kernels, per_device(): attend_backward(group_blocks, pairs, key_side, query_x, side_rows(doc_row...  30.6 us
    dot_general x4, matrix products, mixed_dot(): return jnp.dot(left, right, preferred_element_type=jnp.float32)  24.7 us
    pallas_call x1, Pallas kernels, per_device(): attend_forward(group_blocks, pairs, key_side, query_x, doc_side)  21.3 us
  transfers between devices with their start and end apart: 107, of which 47 were waited for; matrix products, arithmetic and copies ran while one was open for 33% of the time, Pallas kernels for 9%

profile of v1, /device:TPU:0, one launch (start us, length us, event | category | flops | bytes accessed | tf_op | source)
XLA Modules:
  0.0 885.8 jit_solution(6804549217568631731)
XLA Ops:
  42.2 3.3 broadcast_in_dim.227
  92.0 4.8 collective-permute-done.11
  114.2 4.1 collective-permute-done.2
  140.5 18.1 %collective-permute-done.17 = bf16[128,3328]{1,0:T(8,128)(2,1)} collective-permute-done((bf16[128,3328]{1,0:T(8,128)(2,1)}, bf16[128,3328]{1,0:T(8,128)(2,1)}, u32[]{:S(2)}, u32[]{:S(2)}) %collective-permute-start.17) | collective-permute-done | bytes 852000 | tf_op jit(solution)/shard_map/ppermute | solution.py:34
  169.4 8.5 fusion.238
  183.5 4.4 multiply_convert_fusion.1
  187.9 4.2 state_outer.2
  192.2 10.7 %collective-permute-done.32 = bf16[256,1024]{1,0:T(8,128)(2,1)S(1)} collective-permute-done((bf16[256,1024]{1,0:T(8,128)(2,1)S(1)}, bf16[256,1024]{1,0:T(8,128)(2,1)S(1)}, u32[]{:S(2)}, u32[]{:S(2)}) %collective-permute-start.32) | collective-permute-done | bytes 524320 | tf_op jit(solution)/shard_map/ppermute | solution.py:34
  210.6 4.1 collective-permute-done.23
  215.1 4.6 collective-permute-start.8
  226.0 5.2 collective-permute-done.8
  234.4 4.3 collective-permute-done.33
  245.5 26.1 %collective-permute-done.28 = bf16[128,4096]{1,0:T(8,128)(2,1)S(1)} collective-permute-done((bf16[128,4096]{1,0:T(8,128)(2,1)}, bf16[128,4096]{1,0:T(8,128)(2,1)S(1)}, u32[]{:S(2)}, u32[]{:S(2)}) %collective-permute-start.28) | collective-permute-done | bytes 1048608 | tf_op jit(solution)/shard_map/ppermute | solution.py:34
  282.9 21.3 %attend_forward.1 = (f32[2,2,64,1024]{3,2,1,0:T(8,128)S(1)}, f32[2,2,1,1024]{3,2,1,0:T(1,128)S(1)}) custom-call(s32[2]{0:T(128)S(1)} %pad_add_fusion.4.blocks, bf16[8,2,512,128]{3,2,1,0:T(8,128)(2,1)S(1)} %bitcast.272, bf16[4096,128]{1,0:T(8,128)(2,1)S(1)} %fusion.36.side_ref, bf16[2,2,64,1024]{3,2,1,0:T(8,128)(2,1)S(1)} %copy-done.10, ...), custom_call_target="tpu_custom_call" | custom-call | flops 4831838208 | bytes 33554432 | tf_op jit(solution)/shard_map/attend_forward/pallas_call | solution.py:791
  305.9 3.9 collective-permute-start.9
  310.6 7.1 collective-permute-done.9
  320.4 3.3 fusion.239
  327.5 3.9 fusion.65.state_ref
  331.4 11.8 %mixer_forward.1 = f32[512,1536]{1,0:T(8,128)S(1)} custom-call(f32[12,1,128]{2,1,0:T(1,128)S(1)} %broadcast_in_dim.226.skip_ref, bf16[512,1792]{1,0:T(8,128)(2,1)S(1)} %get-tuple-element.71.left_ref.right_ref.x_ref.b_ref.c_ref, bf16[512,1792]{1,0:T(8,128)(2,1)S(1)} %get-tuple-element.71.left_ref.right_ref.x_ref.b_ref.c_ref, ...), custom_call_target="tpu_custom_call" | custom-call | flops 1610612736 | bytes 6291456 | tf_op jit(solution)/shard_map/mixer_forward/pallas_call | solution.py:794
  343.2 4.1 multiply_reduce_fusion.6
  350.3 4.7 multiply_reduce_fusion.9
  355.4 4.5 fusion.240
  359.9 8.5 bitcast_multiply_fusion.1
  368.4 4.1 add_convert_fusion
  372.5 9.6 %multiply_reduce_fusion.7 = (f32[1024]{0:T(1024)}, f32[512]{0:T(512)S(1)}, f32[512,1024]{1,0:T(8,128)S(1)}) fusion(f32[512,1024]{1,0:T(8,128)S(1)} %get-tuple-element.60, f32[512]{0:T(512)S(1)} %fusion.179, f32[1024]{0:T(1024)S(1)} %bitcast.307, bf16[512,4096]{1,0:T(8,128)(2,1)S(1)} %add_convert_fusion, ...), kind=kOutput, calls=%fused_computation.76 | convolution fusion | flops 4298111488 | bytes 16789504 | tf_op jit(solution)/shard_map/dot_general | solution.py:198
  386.7 6.4 multiply_reduce_fusion.4
  394.0 3.3 fusion.102
  402.4 3.9 collective-permute-start.37
  407.5 7.4 fusion.224
  427.6 4.3 convolution_convert_fusion
  436.4 30.6 %attend_backward.1 = (f32[2,2,64,1024]{3,2,1,0:T(8,128)S(1)}, bf16[8,2,512,128]{3,2,1,0:T(8,128)(2,1)S(1)}) custom-call(s32[2]{0:T(128)S(1)} %pad_add_fusion.4.blocks, bf16[8,2,512,128]{3,2,1,0:T(8,128)(2,1)} %bitcast.271, bf16[4096,128]{1,0:T(8,128)(2,1)S(1)} %copy-done.7, bf16[2,2,64,1024]{3,2,1,0:T(8,128)(2,1)S(1)} %copy-done.11, ...), custom_call_target="tpu_custom_call" | custom-call | flops 12079595520 | bytes 33554432 | tf_op jit(solution)/shard_map/attend_backward/pallas_call | solution.py:840
  469.5 6.9 fusion.41
  479.6 6.8 collective-permute-done.80
  489.3 5.5 collective-permute-done.81
  497.4 3.7 collective-permute-done.82
  514.5 6.7 state_outer.3
  542.5 9.7 %collective-permute-done.48 = bf16[256,1536]{1,0:T(8,128)(2,1)S(1)} collective-permute-done((bf16[256,1536]{1,0:T(8,128)(2,1)S(1)}, bf16[256,1536]{1,0:T(8,128)(2,1)S(1)}, u32[]{:S(2)}, u32[]{:S(2)}) %collective-permute-start.48) | collective-permute-done | bytes 786464 | tf_op jit(solution)/shard_map/ppermute | solution.py:34
  553.8 15.2 %collective-permute-done.64 = bf16[384,1024]{1,0:T(8,128)(2,1)S(1)} collective-permute-done((bf16[384,1024]{1,0:T(8,128)(2,1)S(1)}, bf16[384,1024]{1,0:T(8,128)(2,1)S(1)}, u32[]{:S(2)}, u32[]{:S(2)}) %collective-permute-start.64) | collective-permute-done | bytes 786464 | tf_op jit(solution)/shard_map/ppermute | solution.py:34
  572.6 9.6 %collective-permute-done.65 = bf16[192,1024]{1,0:T(8,128)(2,1)S(1)} collective-permute-done((bf16[192,1024]{1,0:T(8,128)(2,1)S(1)}, bf16[192,1024]{1,0:T(8,128)(2,1)S(1)}, u32[]{:S(2)}, u32[]{:S(2)}) %collective-permute-start.65) | collective-permute-done | bytes 393248 | tf_op jit(solution)/shard_map/ppermute | solution.py:34
  584.1 17.0 %collective-permute-done.66 = bf16[96,1024]{1,0:T(8,128)(2,1)S(1)} collective-permute-done((bf16[96,1024]{1,0:T(8,128)(2,1)S(1)}, bf16[96,1024]{1,0:T(8,128)(2,1)S(1)}, u32[]{:S(2)}, u32[]{:S(2)}) %collective-permute-start.66) | collective-permute-done | bytes 196640 | tf_op jit(solution)/shard_map/ppermute | solution.py:34
  604.3 12.7 %collective-permute-done.67 = bf16[48,1024]{1,0:T(8,128)(2,1)S(1)} collective-permute-done((bf16[48,1024]{1,0:T(8,128)(2,1)S(1)}, bf16[48,1024]{1,0:T(8,128)(2,1)S(1)}, u32[]{:S(2)}, u32[]{:S(2)}) %collective-permute-start.67) | collective-permute-done | bytes 98336 | tf_op jit(solution)/shard_map/ppermute | solution.py:34
  624.5 4.9 collective-permute-done.53
  631.6 3.8 collective-permute-start.98
  635.6 6.0 collective-permute-done.54
  642.8 3.6 collective-permute-start.99
  653.8 4.4 add_convert_fusion.2
  667.6 4.0 fusion.218
  671.6 3.8 fusion.77.state_grad_ref
  675.5 17.3 %mixer_backward.1 = (f32[512,1792]{1,0:T(8,128)}, f32[12,1,128]{2,1,0:T(1,128)S(1)}) custom-call(f32[12,1,128]{2,1,0:T(1,128)S(1)} %broadcast_in_dim.226.skip_ref, bf16[512,1792]{1,0:T(8,128)(2,1)S(1)} %get-tuple-element.71.left_ref.right_ref.x_ref.b_ref.c_ref, bf16[512,1792]{1,0:T(8,128)(2,1)S(1)} %get-tuple-element.71.left_ref.right_ref.x_ref.b_ref.c_ref, ...), custom_call_target="tpu_custom_call" | custom-call | flops 3221225472 | bytes 9437184 | tf_op jit(solution)/shard_map/mixer_backward/pallas_call | solution.py:865
  692.8 5.6 multiply_reduce_fusion.3
  705.0 3.8 collective-permute-done.36
  711.2 9.4 %fusion.25 = (f32[1024]{0:T(1024)S(1)}, f32[512]{0:T(512)S(1)}, f32[512,1024]{1,0:T(8,128)}) fusion(bf16[1,512,1024]{2,1,0:T(8,128)(2,1)S(1)} %copy-done.30, f32[512]{0:T(512)S(1)} %copy-done.110, f32[1024]{0:T(1024)S(1)} %bitcast.317, f32[512,1024]{1,0:T(8,128)S(1)} %copy-done.141, bf16[1024,3328]{1,0:T(8,128)(2,1)} %constant_dynamic-update-slice_fusion.18, ...), kind=kOutput, calls=%fused_computation.62 | convolution fusion | flops 3500669440 | bytes 15478784 | tf_op jit(solution)/shard_map/dot_general | solution.py:198
  728.2 8.4 collective-permute-done.102
  747.9 3.2 collective-permute-done.44
  765.1 3.2 add_convert_fusion.1
  778.1 9.7 %collective-permute-done.89 = bf16[128,4096]{1,0:T(8,128)(2,1)S(1)} collective-permute-done((bf16[128,4096]{1,0:T(8,128)(2,1)S(1)}, bf16[128,4096]{1,0:T(8,128)(2,1)S(1)}, u32[]{:S(2)}, u32[]{:S(2)}) %collective-permute-start.89) | collective-permute-done | bytes 1048608 | tf_op jit(solution)/shard_map/ppermute | solution.py:34
  789.1 3.7 collective-permute-done.56
  797.5 4.6 collective-permute-done.57
  805.0 6.8 collective-permute-done.58
  812.0 8.7 collective-permute-done.91
  823.9 7.9 collective-permute-done.92
  836.4 10.0 %collective-permute-done.61 = bf16[64,1792]{1,0:T(8,128)(2,1)S(1)} collective-permute-done((bf16[64,1792]{1,0:T(8,128)(2,1)S(1)}, bf16[64,1792]{1,0:T(8,128)(2,1)S(1)}, u32[]{:S(2)}, u32[]{:S(2)}) %collective-permute-start.61) | collective-permute-done | bytes 229408 | tf_op jit(solution)/shard_map/ppermute | solution.py:34
  851.2 8.8 collective-permute-done.62
  862.2 14.1 %collective-permute-done.94 = bf16[128,4096]{1,0:T(8,128)(2,1)S(1)} collective-permute-done((bf16[128,4096]{1,0:T(8,128)(2,1)S(1)}, bf16[128,4096]{1,0:T(8,128)(2,1)S(1)}, u32[]{:S(2)}, u32[]{:S(2)}) %collective-permute-start.94) | collective-permute-done | bytes 1048608 | tf_op jit(solution)/shard_map/ppermute | solution.py:34
  (862 shorter events, 372.0 us)
Async XLA Ops:
  7.2 273.0 %all-gather.7.cloned.1.call-start = ((), (), s32[]{:S(2)}) async-start(), calls=%async_computation.2 | async-start | bytes 2359296 | tf_op jit(solution)/shard_map/all_gather | solution.py:707
  11.6 74.3 %collective-permute-start.5 = (bf16[32,128]{1,0:T(8,128)(2,1)S(1)}, bf16[32,128]{1,0:T(8,128)(2,1)}, u32[]{:S(2)}, u32[]{:S(2)}) collective-permute-start(bf16[32,128]{1,0:T(8,128)(2,1)S(1)} %bitcast.321), channel_id=1, source_target_pairs={{0,1},{1,0},{2,3},{3,2},{4,5},{5,4},{6,7},{7,6},{8,9},{9,8},{10,11... | collective-permute-start | bytes 24584 | tf_op jit(solution)/shard_map/ppermute | solution.py:34
  12.1 74.7 %collective-permute-start.6 = (bf16[32,128]{1,0:T(8,128)(2,1)S(1)}, bf16[32,128]{1,0:T(8,128)(2,1)}, u32[]{:S(2)}, u32[]{:S(2)}) collective-permute-start(bf16[32,128]{1,0:T(8,128)(2,1)S(1)} %bitcast.322), channel_id=1, source_target_pairs={{0,2},{1,3},{2,0},{3,1},{4,6},{5,7},{6,4},{7,5},{8,10},{9,11},{10,... | collective-permute-start | bytes 24584 | tf_op jit(solution)/shard_map/ppermute | solution.py:34
  14.7 74.8 %collective-permute-start.7 = (bf16[32,128]{1,0:T(8,128)(2,1)S(1)}, bf16[32,128]{1,0:T(8,128)(2,1)}, u32[]{:S(2)}, u32[]{:S(2)}) collective-permute-start(bf16[32,128]{1,0:T(8,128)(2,1)S(1)} %bitcast.323), channel_id=1, source_target_pairs={{0,3},{1,2},{2,1},{3,0},{4,7},{5,6},{6,5},{7,4},{8,11},{9,10},{10,... | collective-permute-start | bytes 24584 | tf_op jit(solution)/shard_map/ppermute | solution.py:34
  18.2 94.0 %collective-permute-start = (bf16[256,768]{1,0:T(8,128)(2,1)}, bf16[256,768]{1,0:T(8,128)(2,1)}, u32[]{:S(2)}, u32[]{:S(2)}) collective-permute-start(bf16[256,768]{1,0:T(8,128)(2,1)} %constant_dynamic-update-slice_fusion.40), channel_id=1, source_target_pairs={{0,1},{1,0},{2,3},{3,2},{4,5},{5,4},{6,7},{7,6},{8,9},{9,8},{10,11... | collective-permute-start | bytes 1179656 | tf_op jit(solution)/shard_map/ppermute | solution.py:34
  18.3 86.8 %collective-permute-start.10 = (bf16[128,1024]{1,0:T(8,128)(2,1)}, bf16[128,1024]{1,0:T(8,128)(2,1)}, u32[]{:S(2)}, u32[]{:S(2)}) collective-permute-start(bf16[128,1024]{1,0:T(8,128)(2,1)} %param.30), channel_id=1, source_target_pairs={{0,1},{1,0},{2,3},{3,2},{4,5},{5,4},{6,7},{7,6},{8,9},{9,8},{10,11... | collective-permute-start | bytes 786440 | tf_op jit(solution)/shard_map/ppermute | solution.py:34
  85.9 54.5 %collective-permute-start.15 = (bf16[256,3328]{1,0:T(8,128)(2,1)}, bf16[256,3328]{1,0:T(8,128)(2,1)}, u32[]{:S(2)}, u32[]{:S(2)}) collective-permute-start(bf16[256,3328]{1,0:T(8,128)(2,1)} %param.22), channel_id=1, source_target_pairs={{0,1},{1,0},{2,3},{3,2},{4,5},{5,4},{6,7},{7,6},{8,9},{9,8},{10,11... | collective-permute-start | bytes 5111816 | tf_op jit(solution)/shard_map/ppermute | solution.py:34
  86.9 17.2 %collective-permute-start.1 = (bf16[128,768]{1,0:T(8,128)(2,1)S(1)}, bf16[128,768]{1,0:T(8,128)(2,1)}, u32[]{:S(2)}, u32[]{:S(2)}) collective-permute-start(bf16[128,768]{1,0:T(8,128)(2,1)S(1)} %copy-done.80), channel_id=1, source_target_pairs={{0,2},{1,3},{2,0},{3,1},{4,6},{5,7},{6,4},{7,5},{8,10},{9,11},{10,... | collective-permute-start | bytes 589832 | tf_op jit(solution)/shard_map/ppermute | solution.py:34
  104.1 100.0 %collective-permute-start.21 = (bf16[384,1024]{1,0:T(8,128)(2,1)}, bf16[384,1024]{1,0:T(8,128)(2,1)}, u32[]{:S(2)}, u32[]{:S(2)}) collective-permute-start(bf16[384,1024]{1,0:T(8,128)(2,1)} %param.27), channel_id=1, source_target_pairs={{0,1},{1,0},{2,3},{3,2},{4,5},{5,4},{6,7},{7,6},{8,9},{9,8},{10,11... | collective-permute-start | bytes 2359304 | tf_op jit(solution)/shard_map/ppermute | solution.py:34
  108.8 26.2 %collective-permute-start.16 = (bf16[128,3328]{1,0:T(8,128)(2,1)}, bf16[128,3328]{1,0:T(8,128)(2,1)}, u32[]{:S(2)}, u32[]{:S(2)}) collective-permute-start(bf16[128,3328]{1,0:T(8,128)(2,1)} %constant_dynamic-slice_fusion.44), channel_id=1, source_target_pairs={{0,2},{1,3},{2,0},{3,1},{4,6},{5,7},{6,4},{7,5},{8,10},{9,11},{10,... | collective-permute-start | bytes 2555912 | tf_op jit(solution)/shard_map/ppermute | solution.py:34
  120.9 150.8 %collective-permute-start.26 = (bf16[256,4096]{1,0:T(8,128)(2,1)}, bf16[256,4096]{1,0:T(8,128)(2,1)}, u32[]{:S(2)}, u32[]{:S(2)}) collective-permute-start(bf16[256,4096]{1,0:T(8,128)(2,1)} %param.32), channel_id=1, source_target_pairs={{0,1},{1,0},{2,3},{3,2},{4,5},{5,4},{6,7},{7,6},{8,9},{9,8},{10,11... | collective-permute-start | bytes 6291464 | tf_op jit(solution)/shard_map/ppermute | solution.py:34
  123.2 68.9 %collective-permute-start.22 = (bf16[192,1024]{1,0:T(8,128)(2,1)}, bf16[192,1024]{1,0:T(8,128)(2,1)}, u32[]{:S(2)}, u32[]{:S(2)}) collective-permute-start(bf16[192,1024]{1,0:T(8,128)(2,1)} %constant_dynamic-slice_fusion.43), channel_id=1, source_target_pairs={{0,2},{1,3},{2,0},{3,1},{4,6},{5,7},{6,4},{7,5},{8,10},{9,11},{10,... | collective-permute-start | bytes 1179656 | tf_op jit(solution)/shard_map/ppermute | solution.py:34
  135.0 23.7 %collective-permute-start.17 = (bf16[128,3328]{1,0:T(8,128)(2,1)}, bf16[128,3328]{1,0:T(8,128)(2,1)}, u32[]{:S(2)}, u32[]{:S(2)}) collective-permute-start(bf16[128,3328]{1,0:T(8,128)(2,1)} %collective-permute-done.16), channel_id=1, source_target_pairs={{0,4},{1,5},{2,6},{3,7},{4,0},{5,1},{6,2},{7,3},{8,12},{9,13},{10,... | collective-permute-start | bytes 2555912 | tf_op jit(solution)/shard_map/ppermute | solution.py:34
  137.6 186.0 %all-gather.9.cloned.1.call-start = ((), (), s32[]{:S(2)}) async-start(), calls=%async_computation.3 | async-start | bytes 3575808 | tf_op jit(solution)/shard_map/all_gather | solution.py:786
  140.5 25.4 %collective-permute-start.18 = (bf16[128,3328]{1,0:T(8,128)(2,1)}, bf16[128,3328]{1,0:T(8,128)(2,1)S(1)}, u32[]{:S(2)}, u32[]{:S(2)}) collective-permute-start(bf16[128,3328]{1,0:T(8,128)(2,1)} %collective-permute-done.16), channel_id=1, source_target_pairs={{0,1},{1,0},{2,3},{3,2},{4,5},{5,4},{6,7},{7,6},{8,9},{9,8},{10,11... | collective-permute-start | bytes 2555912 | tf_op jit(solution)/shard_map/ppermute | solution.py:34
  165.8 57.8 %collective-permute-start.27 = (bf16[128,4096]{1,0:T(8,128)(2,1)}, bf16[128,4096]{1,0:T(8,128)(2,1)}, u32[]{:S(2)}, u32[]{:S(2)}) collective-permute-start(bf16[128,4096]{1,0:T(8,128)(2,1)} %constant_dynamic-slice_fusion.42), channel_id=1, source_target_pairs={{0,2},{1,3},{2,0},{3,1},{4,6},{5,7},{6,4},{7,5},{8,10},{9,11},{10,... | collective-permute-start | bytes 3145736 | tf_op jit(solution)/shard_map/ppermute | solution.py:34
  182.3 20.5 %collective-permute-start.32 = (bf16[256,1024]{1,0:T(8,128)(2,1)S(1)}, bf16[256,1024]{1,0:T(8,128)(2,1)S(1)}, u32[]{:S(2)}, u32[]{:S(2)}) collective-permute-start(bf16[256,1024]{1,0:T(8,128)(2,1)S(1)} %copy-done.71), channel_id=1, source_target_pairs={{0,2},{1,3},{2,0},{3,1},{4,6},{5,7},{6,4},{7,5},{8,10},{9,11},{10,... | collective-permute-start | bytes 1572872 | tf_op jit(solution)/shard_map/ppermute | solution.py:34
  192.1 41.8 %collective-permute-start.31 = (bf16[512,1024]{1,0:T(8,128)(2,1)}, bf16[512,1024]{1,0:T(8,128)(2,1)}, u32[]{:S(2)}, u32[]{:S(2)}) collective-permute-start(bf16[512,1024]{1,0:T(8,128)(2,1)} %param.33), channel_id=1, source_target_pairs={{0,1},{1,0},{2,3},{3,2},{4,5},{5,4},{6,7},{7,6},{8,9},{9,8},{10,11... | collective-permute-start | bytes 3145736 | tf_op jit(solution)/shard_map/ppermute | solution.py:34
  204.9 454.7 %reduce-scatter.2.cloned.1.call-start = ((), (), s32[]{:S(2)}) async-start(), calls=%async_computation.1 | async-start | bytes 2359296 | tf_op jit(solution)/shard_map/reduce_scatter | solution.py:850
  214.7 24.0 %collective-permute-start.33 = (bf16[256,1024]{1,0:T(8,128)(2,1)}, bf16[256,1024]{1,0:T(8,128)(2,1)S(1)}, u32[]{:S(2)}, u32[]{:S(2)}) collective-permute-start(bf16[256,1024]{1,0:T(8,128)(2,1)} %copy-done.72), channel_id=1, source_target_pairs={{0,4},{1,5},{2,6},{3,7},{4,0},{5,1},{6,2},{7,3},{8,12},{9,13},{10,... | collective-permute-start | bytes 1572872 | tf_op jit(solution)/shard_map/ppermute | solution.py:34
  215.1 16.1 %collective-permute-start.8 = (bf16[2,64,1024]{2,1,0:T(8,128)(2,1)}, bf16[2,64,1024]{2,1,0:T(8,128)(2,1)S(1)}, u32[]{:S(2)}, u32[]{:S(2)}) collective-permute-start(bf16[2,64,1024]{2,1,0:T(8,128)(2,1)} %squeeze.21), channel_id=1, source_target_pairs={{0,28},{4,24},{8,20},{12,16},{16,12},{20,8},{24,4},{28,0},{1,29},{... | collective-permute-start | bytes 786440 | tf_op jit(solution)/shard_map/ppermute | solution.py:45
  223.6 48.0 %collective-permute-start.28 = (bf16[128,4096]{1,0:T(8,128)(2,1)}, bf16[128,4096]{1,0:T(8,128)(2,1)S(1)}, u32[]{:S(2)}, u32[]{:S(2)}) collective-permute-start(bf16[128,4096]{1,0:T(8,128)(2,1)} %collective-permute-done.27), channel_id=1, source_target_pairs={{0,4},{1,5},{2,6},{3,7},{4,0},{5,1},{6,2},{7,3},{8,12},{9,13},{10,... | collective-permute-start | bytes 3145736 | tf_op jit(solution)/shard_map/ppermute | solution.py:34
  242.6 35.5 %collective-permute-start.29 = (bf16[128,4096]{1,0:T(8,128)(2,1)}, bf16[128,4096]{1,0:T(8,128)(2,1)S(1)}, u32[]{:S(2)}, u32[]{:S(2)}) collective-permute-start(bf16[128,4096]{1,0:T(8,128)(2,1)} %collective-permute-done.27), channel_id=1, source_target_pairs={{0,1},{1,0},{2,3},{3,2},{4,5},{5,4},{6,7},{7,6},{8,9},{9,8},{10,11... | collective-permute-start | bytes 3145736 | tf_op jit(solution)/shard_map/ppermute | solution.py:34
  305.9 11.8 %collective-permute-start.9 = (bf16[2,64,1024]{2,1,0:T(8,128)(2,1)}, bf16[2,64,1024]{2,1,0:T(8,128)(2,1)S(1)}, u32[]{:S(2)}, u32[]{:S(2)}) collective-permute-start(bf16[2,64,1024]{2,1,0:T(8,128)(2,1)} %get-tuple-element.108), channel_id=1, source_target_pairs={{0,28},{4,24},{8,20},{12,16},{16,12},{20,8},{24,4},{28,0},{1,29},{... | collective-permute-start | bytes 786440 | tf_op jit(solution)/shard_map/ppermute | solution.py:45
  402.4 31.6 %collective-permute-start.37 = (bf16[2,64,1024]{2,1,0:T(8,128)(2,1)}, bf16[2,64,1024]{2,1,0:T(8,128)(2,1)}, u32[]{:S(2)}, u32[]{:S(2)}) collective-permute-start(bf16[2,64,1024]{2,1,0:T(8,128)(2,1)} %squeeze.26), channel_id=1, source_target_pairs={{0,28},{4,24},{8,20},{12,16},{16,12},{20,8},{24,4},{28,0},{1,29},{... | collective-permute-start | bytes 786440 | tf_op jit(solution)/shard_map/ppermute | solution.py:45
  420.2 109.3 %collective-permute-start.47 = (bf16[512,1536]{1,0:T(8,128)(2,1)}, bf16[512,1536]{1,0:T(8,128)(2,1)}, u32[]{:S(2)}, u32[]{:S(2)}) collective-permute-start(bf16[512,1536]{1,0:T(8,128)(2,1)} %convolution_convert_fusion.1), channel_id=1, source_target_pairs={{0,1},{1,0},{2,3},{3,2},{4,5},{5,4},{6,7},{7,6},{8,9},{9,8},{10,11... | collective-permute-start | bytes 4718600 | tf_op jit(solution)/shard_map/ppermute | solution.py:34
  422.5 113.8 %collective-permute-start.63 = (bf16[768,1024]{1,0:T(8,128)(2,1)}, bf16[768,1024]{1,0:T(8,128)(2,1)}, u32[]{:S(2)}, u32[]{:S(2)}) collective-permute-start(bf16[768,1024]{1,0:T(8,128)(2,1)} %convolution_convert_fusion.4), channel_id=1, source_target_pairs={{0,1},{1,0},{2,3},{3,2},{4,5},{5,4},{6,7},{7,6},{8,9},{9,8},{10,11... | collective-permute-start | bytes 4718600 | tf_op jit(solution)/shard_map/ppermute | solution.py:34
  424.2 52.6 %collective-permute-start.79 = (bf16[256,1024]{1,0:T(8,128)(2,1)}, bf16[256,1024]{1,0:T(8,128)(2,1)}, u32[]{:S(2)}, u32[]{:S(2)}) collective-permute-start(bf16[256,1024]{1,0:T(8,128)(2,1)} %convolution_convert_fusion.6), channel_id=1, source_target_pairs={{0,1},{1,0},{2,3},{3,2},{4,5},{5,4},{6,7},{7,6},{8,9},{9,8},{10,11... | collective-permute-start | bytes 1572872 | tf_op jit(solution)/shard_map/ppermute | solution.py:34
  427.1 112.6 %collective-permute-start.95 = (bf16[1024,1024]{1,0:T(8,128)(2,1)}, bf16[1024,1024]{1,0:T(8,128)(2,1)}, u32[]{:S(2)}, u32[]{:S(2)}) collective-permute-start(bf16[1024,1024]{1,0:T(8,128)(2,1)} %convolution_convert_fusion.3), channel_id=1, source_target_pairs={{0,1},{1,0},{2,3},{3,2},{4,5},{5,4},{6,7},{7,6},{8,9},{9,8},{10,11... | collective-permute-start | bytes 6291464 | tf_op jit(solution)/shard_map/ppermute | solution.py:34
  469.4 202.2 %all-gather.11.cloned.1.call-start = ((), (), s32[]{:S(2)}) async-start(), calls=%async_computation.4 | async-start | bytes 3538944 | tf_op jit(solution)/shard_map/all_gather | solution.py:833
  502.6 20.9 %collective-permute-start.38 = (bf16[2,64,1024]{2,1,0:T(8,128)(2,1)}, bf16[2,64,1024]{2,1,0:T(8,128)(2,1)}, u32[]{:S(2)}, u32[]{:S(2)}) collective-permute-start(bf16[2,64,1024]{2,1,0:T(8,128)(2,1)} %get-tuple-element.104), channel_id=1, source_target_pairs={{0,28},{4,24},{8,20},{12,16},{16,12},{20,8},{24,4},{28,0},{1,29},{... | collective-permute-start | bytes 786440 | tf_op jit(solution)/shard_map/ppermute | solution.py:45
  506.8 20.0 %collective-permute-start.84 = (bf16[16,1024]{1,0:T(8,128)(2,1)S(1)}, bf16[16,1024]{1,0:T(8,128)(2,1)}, u32[]{:S(2)}, u32[]{:S(2)}) collective-permute-start(bf16[16,1024]{1,0:T(8,128)(2,1)S(1)} %add_convert_fusion.37), channel_id=1, source_target_pairs={{0,16},{1,17},{2,18},{3,19},{4,20},{5,21},{6,22},{7,23},{8,24},{9,... | collective-permute-start | bytes 98312 | tf_op jit(solution)/shard_map/ppermute | solution.py:34
  523.5 130.3 %collective-permute-start.87 = (bf16[512,4096]{1,0:T(8,128)(2,1)}, bf16[512,4096]{1,0:T(8,128)(2,1)}, u32[]{:S(2)}, u32[]{:S(2)}) collective-permute-start(bf16[512,4096]{1,0:T(8,128)(2,1)} %convolution_convert_fusion), channel_id=1, source_target_pairs={{0,1},{1,0},{2,3},{3,2},{4,5},{5,4},{6,7},{7,6},{8,9},{9,8},{10,11... | collective-permute-start | bytes 12582920 | tf_op jit(solution)/shard_map/ppermute | solution.py:34
  531.8 20.4 %collective-permute-start.48 = (bf16[256,1536]{1,0:T(8,128)(2,1)S(1)}, bf16[256,1536]{1,0:T(8,128)(2,1)S(1)}, u32[]{:S(2)}, u32[]{:S(2)}) collective-permute-start(bf16[256,1536]{1,0:T(8,128)(2,1)S(1)} %add_convert_fusion.10), channel_id=1, source_target_pairs={{0,2},{1,3},{2,0},{3,1},{4,6},{5,7},{6,4},{7,5},{8,10},{9,11},{10,... | collective-permute-start | bytes 2359304 | tf_op jit(solution)/shard_map/ppermute | solution.py:34
  535.2 86.5 %collective-permute-start.86 = (bf16[64,1024]{1,0:T(8,128)(2,1)S(1)}, bf16[64,1024]{1,0:T(8,128)(2,1)S(1)}, u32[]{:S(2)}, u32[]{:S(2)}) collective-permute-start(bf16[64,1024]{1,0:T(8,128)(2,1)S(1)} %maximum_select_fusion.18), channel_id=1, source_target_pairs={{0,4},{1,5},{2,6},{3,7},{4,0},{5,1},{6,2},{7,3},{8,12},{9,13},{10,... | collective-permute-start | bytes 393224 | tf_op jit(solution)/shard_map/ppermute | solution.py:34
  538.2 30.9 %collective-permute-start.64 = (bf16[384,1024]{1,0:T(8,128)(2,1)S(1)}, bf16[384,1024]{1,0:T(8,128)(2,1)S(1)}, u32[]{:S(2)}, u32[]{:S(2)}) collective-permute-start(bf16[384,1024]{1,0:T(8,128)(2,1)S(1)} %add_convert_fusion.8), channel_id=1, source_target_pairs={{0,2},{1,3},{2,0},{3,1},{4,6},{5,7},{6,4},{7,5},{8,10},{9,11},{10,... | collective-permute-start | bytes 2359304 | tf_op jit(solution)/shard_map/ppermute | solution.py:34
  541.8 75.3 %collective-permute-start.96 = (bf16[512,1024]{1,0:T(8,128)(2,1)S(1)}, bf16[512,1024]{1,0:T(8,128)(2,1)S(1)}, u32[]{:S(2)}, u32[]{:S(2)}) collective-permute-start(bf16[512,1024]{1,0:T(8,128)(2,1)S(1)} %add_convert_fusion.4), channel_id=1, source_target_pairs={{0,2},{1,3},{2,0},{3,1},{4,6},{5,7},{6,4},{7,5},{8,10},{9,11},{10,... | collective-permute-start | bytes 3145736 | tf_op jit(solution)/shard_map/ppermute | solution.py:34
  553.7 17.0 %collective-permute-start.49 = (bf16[128,1536]{1,0:T(8,128)(2,1)S(1)}, bf16[128,1536]{1,0:T(8,128)(2,1)S(1)}, u32[]{:S(2)}, u32[]{:S(2)}) collective-permute-start(bf16[128,1536]{1,0:T(8,128)(2,1)S(1)} %constant_dynamic-slice_fusion.28), channel_id=1, source_target_pairs={{0,4},{1,5},{2,6},{3,7},{4,0},{5,1},{6,2},{7,3},{8,12},{9,13},{10,... | collective-permute-start | bytes 1179656 | tf_op jit(solution)/shard_map/ppermute | solution.py:34
  570.6 11.6 %collective-permute-start.65 = (bf16[192,1024]{1,0:T(8,128)(2,1)S(1)}, bf16[192,1024]{1,0:T(8,128)(2,1)S(1)}, u32[]{:S(2)}, u32[]{:S(2)}) collective-permute-start(bf16[192,1024]{1,0:T(8,128)(2,1)S(1)} %constant_dynamic-slice_fusion.20), channel_id=1, source_target_pairs={{0,4},{1,5},{2,6},{3,7},{4,0},{5,1},{6,2},{7,3},{8,12},{9,13},{10,... | collective-permute-start | bytes 1179656 | tf_op jit(solution)/shard_map/ppermute | solution.py:34
  570.9 11.6 %collective-permute-start.50 = (bf16[64,1536]{1,0:T(8,128)(2,1)S(1)}, bf16[64,1536]{1,0:T(8,128)(2,1)S(1)}, u32[]{:S(2)}, u32[]{:S(2)}) collective-permute-start(bf16[64,1536]{1,0:T(8,128)(2,1)S(1)} %constant_dynamic-slice_fusion.27), channel_id=1, source_target_pairs={{0,8},{1,9},{2,10},{3,11},{4,12},{5,13},{6,14},{7,15},{8,0},{9,1},... | collective-permute-start | bytes 589832 | tf_op jit(solution)/shard_map/ppermute | solution.py:34
  582.4 18.7 %collective-permute-start.66 = (bf16[96,1024]{1,0:T(8,128)(2,1)S(1)}, bf16[96,1024]{1,0:T(8,128)(2,1)S(1)}, u32[]{:S(2)}, u32[]{:S(2)}) collective-permute-start(bf16[96,1024]{1,0:T(8,128)(2,1)S(1)} %constant_dynamic-slice_fusion.19), channel_id=1, source_target_pairs={{0,8},{1,9},{2,10},{3,11},{4,12},{5,13},{6,14},{7,15},{8,0},{9,1},... | collective-permute-start | bytes 589832 | tf_op jit(solution)/shard_map/ppermute | solution.py:34
  582.6 18.8 %collective-permute-start.51 = (bf16[32,1536]{1,0:T(8,128)(2,1)S(1)}, bf16[32,1536]{1,0:T(8,128)(2,1)S(1)}, u32[]{:S(2)}, u32[]{:S(2)}) collective-permute-start(bf16[32,1536]{1,0:T(8,128)(2,1)S(1)} %constant_dynamic-slice_fusion.26), channel_id=1, source_target_pairs={{0,16},{1,17},{2,18},{3,19},{4,20},{5,21},{6,22},{7,23},{8,24},{9,... | collective-permute-start | bytes 294920 | tf_op jit(solution)/shard_map/ppermute | solution.py:34
  601.2 15.8 %collective-permute-start.67 = (bf16[48,1024]{1,0:T(8,128)(2,1)S(1)}, bf16[48,1024]{1,0:T(8,128)(2,1)S(1)}, u32[]{:S(2)}, u32[]{:S(2)}) collective-permute-start(bf16[48,1024]{1,0:T(8,128)(2,1)S(1)} %constant_dynamic-slice_fusion.18), channel_id=1, source_target_pairs={{0,16},{1,17},{2,18},{3,19},{4,20},{5,21},{6,22},{7,23},{8,24},{9,... | collective-permute-start | bytes 294920 | tf_op jit(solution)/shard_map/ppermute | solution.py:34
  601.4 20.1 %collective-permute-start.52 = (bf16[32,1536]{1,0:T(8,128)(2,1)S(1)}, bf16[32,1536]{1,0:T(8,128)(2,1)S(1)}, u32[]{:S(2)}, u32[]{:S(2)}) collective-permute-start(bf16[32,1536]{1,0:T(8,128)(2,1)S(1)} %add_convert_fusion.34), channel_id=1, source_target_pairs={{0,16},{1,17},{2,18},{3,19},{4,20},{5,21},{6,22},{7,23},{8,24},{9,... | collective-permute-start | bytes 294920 | tf_op jit(solution)/shard_map/ppermute | solution.py:34
  618.9 12.4 %collective-permute-start.97 = (bf16[256,1024]{1,0:T(8,128)(2,1)S(1)}, bf16[256,1024]{1,0:T(8,128)(2,1)S(1)}, u32[]{:S(2)}, u32[]{:S(2)}) collective-permute-start(bf16[256,1024]{1,0:T(8,128)(2,1)S(1)} %constant_dynamic-slice_fusion.2), channel_id=1, source_target_pairs={{0,4},{1,5},{2,6},{3,7},{4,0},{5,1},{6,2},{7,3},{8,12},{9,13},{10,... | collective-permute-start | bytes 1572872 | tf_op jit(solution)/shard_map/ppermute | solution.py:34
  623.2 12.2 %collective-permute-start.69 = (bf16[96,1024]{1,0:T(8,128)(2,1)S(1)}, bf16[96,1024]{1,0:T(8,128)(2,1)S(1)}, u32[]{:S(2)}, u32[]{:S(2)}) collective-permute-start(bf16[96,1024]{1,0:T(8,128)(2,1)S(1)} %maximum_select_fusion.16), channel_id=1, source_target_pairs={{0,8},{1,9},{2,10},{3,11},{4,12},{5,13},{6,14},{7,15},{8,0},{9,1},... | collective-permute-start | bytes 589832 | tf_op jit(solution)/shard_map/ppermute | solution.py:34
  629.5 12.1 %collective-permute-start.54 = (bf16[128,1536]{1,0:T(8,128)(2,1)S(1)}, bf16[128,1536]{1,0:T(8,128)(2,1)S(1)}, u32[]{:S(2)}, u32[]{:S(2)}) collective-permute-start(bf16[128,1536]{1,0:T(8,128)(2,1)S(1)} %maximum_select_fusion.9), channel_id=1, source_target_pairs={{0,4},{1,5},{2,6},{3,7},{4,0},{5,1},{6,2},{7,3},{8,12},{9,13},{10,... | collective-permute-start | bytes 1179656 | tf_op jit(solution)/shard_map/ppermute | solution.py:34
  635.5 11.5 %collective-permute-start.70 = (bf16[192,1024]{1,0:T(8,128)(2,1)S(1)}, bf16[192,1024]{1,0:T(8,128)(2,1)S(1)}, u32[]{:S(2)}, u32[]{:S(2)}) collective-permute-start(bf16[192,1024]{1,0:T(8,128)(2,1)S(1)} %maximum_select_fusion.10), channel_id=1, source_target_pairs={{0,4},{1,5},{2,6},{3,7},{4,0},{5,1},{6,2},{7,3},{8,12},{9,13},{10,... | collective-permute-start | bytes 1179656 | tf_op jit(solution)/shard_map/ppermute | solution.py:34
  658.1 107.0 %collective-permute-start.88 = (bf16[256,4096]{1,0:T(8,128)(2,1)}, bf16[256,4096]{1,0:T(8,128)(2,1)}, u32[]{:S(2)}, u32[]{:S(2)}) collective-permute-start(bf16[256,4096]{1,0:T(8,128)(2,1)} %add_convert_fusion.2), channel_id=1, source_target_pairs={{0,2},{1,3},{2,0},{3,1},{4,6},{5,7},{6,4},{7,5},{8,10},{9,11},{10,... | collective-permute-start | bytes 6291464 | tf_op jit(solution)/shard_map/ppermute | solution.py:34
  658.2 62.8 %collective-permute-start.101 = (bf16[128,1024]{1,0:T(8,128)(2,1)S(1)}, bf16[128,1024]{1,0:T(8,128)(2,1)}, u32[]{:S(2)}, u32[]{:S(2)}) collective-permute-start(bf16[128,1024]{1,0:T(8,128)(2,1)S(1)} %maximum_select_fusion.13), channel_id=1, source_target_pairs={{0,8},{1,9},{2,10},{3,11},{4,12},{5,13},{6,14},{7,15},{8,0},{9,1},... | collective-permute-start | bytes 786440 | tf_op jit(solution)/shard_map/ppermute | solution.py:34
  722.2 14.4 %collective-permute-start.102 = (bf16[256,1024]{1,0:T(8,128)(2,1)S(1)}, bf16[256,1024]{1,0:T(8,128)(2,1)S(1)}, u32[]{:S(2)}, u32[]{:S(2)}) collective-permute-start(bf16[256,1024]{1,0:T(8,128)(2,1)S(1)} %maximum_select_fusion.7), channel_id=1, source_target_pairs={{0,4},{1,5},{2,6},{3,7},{4,0},{5,1},{6,2},{7,3},{8,12},{9,13},{10,... | collective-permute-start | bytes 1572872 | tf_op jit(solution)/shard_map/ppermute | solution.py:34
  724.9 14.2 %collective-permute-start.71 = (bf16[512,768]{1,0:T(8,128)(2,1)S(1)}, bf16[512,768]{1,0:T(8,128)(2,1)S(1)}, u32[]{:S(2)}, u32[]{:S(2)}) collective-permute-start(bf16[512,768]{1,0:T(8,128)(2,1)S(1)} %copy-done.140), channel_id=1, source_target_pairs={{0,1},{1,0},{2,3},{3,2},{4,5},{5,4},{6,7},{7,6},{8,9},{9,8},{10,11... | collective-permute-start | bytes 2359304 | tf_op jit(solution)/shard_map/ppermute | solution.py:34
  726.3 12.0 %collective-permute-start.41 = (bf16[16,128]{1,0:T(8,128)(2,1)S(1)}, bf16[16,128]{1,0:T(8,128)(2,1)S(1)}, u32[]{:S(2)}, u32[]{:S(2)}) collective-permute-start(bf16[16,128]{1,0:T(8,128)(2,1)S(1)} %constant_dynamic-slice_fusion.35), channel_id=1, source_target_pairs={{0,4},{1,5},{2,6},{3,7},{4,0},{5,1},{6,2},{7,3},{8,12},{9,13},{10,... | collective-permute-start | bytes 12296 | tf_op jit(solution)/shard_map/ppermute | solution.py:34
  739.6 12.3 %collective-permute-start.72 = (bf16[256,768]{1,0:T(8,128)(2,1)S(1)}, bf16[256,768]{1,0:T(8,128)(2,1)S(1)}, u32[]{:S(2)}, u32[]{:S(2)}) collective-permute-start(bf16[256,768]{1,0:T(8,128)(2,1)S(1)} %add_convert_fusion.15), channel_id=1, source_target_pairs={{0,2},{1,3},{2,0},{3,1},{4,6},{5,7},{6,4},{7,5},{8,10},{9,11},{10,... | collective-permute-start | bytes 1179656 | tf_op jit(solution)/shard_map/ppermute | solution.py:34
  747.8 28.2 %collective-permute-start.55 = (bf16[512,1792]{1,0:T(8,128)(2,1)S(1)}, bf16[512,1792]{1,0:T(8,128)(2,1)S(1)}, u32[]{:S(2)}, u32[]{:S(2)}) collective-permute-start(bf16[512,1792]{1,0:T(8,128)(2,1)S(1)} %convolution_convert_fusion.2), channel_id=1, source_target_pairs={{0,1},{1,0},{2,3},{3,2},{4,5},{5,4},{6,7},{7,6},{8,9},{9,8},{10,11... | collective-permute-start | bytes 5505032 | tf_op jit(solution)/shard_map/ppermute | solution.py:34
  768.5 19.3 %collective-permute-start.89 = (bf16[128,4096]{1,0:T(8,128)(2,1)S(1)}, bf16[128,4096]{1,0:T(8,128)(2,1)S(1)}, u32[]{:S(2)}, u32[]{:S(2)}) collective-permute-start(bf16[128,4096]{1,0:T(8,128)(2,1)S(1)} %constant_dynamic-slice_fusion.7), channel_id=1, source_target_pairs={{0,4},{1,5},{2,6},{3,7},{4,0},{5,1},{6,2},{7,3},{8,12},{9,13},{10,... | collective-permute-start | bytes 3145736 | tf_op jit(solution)/shard_map/ppermute | solution.py:34
  774.7 60.0 %collective-permute-start.77 = (bf16[64,768]{1,0:T(8,128)(2,1)S(1)}, bf16[64,768]{1,0:T(8,128)(2,1)S(1)}, u32[]{:S(2)}, u32[]{:S(2)}) collective-permute-start(bf16[64,768]{1,0:T(8,128)(2,1)S(1)} %maximum_select_fusion.19), channel_id=1, source_target_pairs={{0,8},{1,9},{2,10},{3,11},{4,12},{5,13},{6,14},{7,15},{8,0},{9,1},... | collective-permute-start | bytes 294920 | tf_op jit(solution)/shard_map/ppermute | solution.py:34
  776.7 16.0 %collective-permute-start.56 = (bf16[256,1792]{1,0:T(8,128)(2,1)S(1)}, bf16[256,1792]{1,0:T(8,128)(2,1)S(1)}, u32[]{:S(2)}, u32[]{:S(2)}) collective-permute-start(bf16[256,1792]{1,0:T(8,128)(2,1)S(1)} %fusion.21), channel_id=1, source_target_pairs={{0,2},{1,3},{2,0},{3,1},{4,6},{5,7},{6,4},{7,5},{8,10},{9,11},{10,... | collective-permute-start | bytes 2752520 | tf_op jit(solution)/shard_map/ppermute | solution.py:34
  804.1 16.6 %collective-permute-start.91 = (bf16[32,4096]{1,0:T(8,128)(2,1)S(1)}, bf16[32,4096]{1,0:T(8,128)(2,1)S(1)}, u32[]{:S(2)}, u32[]{:S(2)}) collective-permute-start(bf16[32,4096]{1,0:T(8,128)(2,1)S(1)} %constant_dynamic-slice_fusion.5), channel_id=1, source_target_pairs={{0,16},{1,17},{2,18},{3,19},{4,20},{5,21},{6,22},{7,23},{8,24},{9,... | collective-permute-start | bytes 786440 | tf_op jit(solution)/shard_map/ppermute | solution.py:34
  831.8 14.8 %collective-permute-start.93 = (bf16[64,4096]{1,0:T(8,128)(2,1)S(1)}, bf16[64,4096]{1,0:T(8,128)(2,1)S(1)}, u32[]{:S(2)}, u32[]{:S(2)}) collective-permute-start(bf16[64,4096]{1,0:T(8,128)(2,1)S(1)} %maximum_select_fusion.6), channel_id=1, source_target_pairs={{0,8},{1,9},{2,10},{3,11},{4,12},{5,13},{6,14},{7,15},{8,0},{9,1},... | collective-permute-start | bytes 1572872 | tf_op jit(solution)/shard_map/ppermute | solution.py:34
  833.0 13.4 %collective-permute-start.61 = (bf16[64,1792]{1,0:T(8,128)(2,1)S(1)}, bf16[64,1792]{1,0:T(8,128)(2,1)S(1)}, u32[]{:S(2)}, u32[]{:S(2)}) collective-permute-start(bf16[64,1792]{1,0:T(8,128)(2,1)S(1)} %maximum_select_fusion.14), channel_id=1, source_target_pairs={{0,8},{1,9},{2,10},{3,11},{4,12},{5,13},{6,14},{7,15},{8,0},{9,1},... | collective-permute-start | bytes 688136 | tf_op jit(solution)/shard_map/ppermute | solution.py:34
  834.8 14.8 %collective-permute-start.78 = (bf16[128,768]{1,0:T(8,128)(2,1)S(1)}, bf16[128,768]{1,0:T(8,128)(2,1)S(1)}, u32[]{:S(2)}, u32[]{:S(2)}) collective-permute-start(bf16[128,768]{1,0:T(8,128)(2,1)S(1)} %maximum_select_fusion.17), channel_id=1, source_target_pairs={{0,4},{1,5},{2,6},{3,7},{4,0},{5,1},{6,2},{7,3},{8,12},{9,13},{10,... | collective-permute-start | bytes 589832 | tf_op jit(solution)/shard_map/ppermute | solution.py:34
  846.5 13.5 %collective-permute-start.62 = (bf16[128,1792]{1,0:T(8,128)(2,1)S(1)}, bf16[128,1792]{1,0:T(8,128)(2,1)S(1)}, u32[]{:S(2)}, u32[]{:S(2)}) collective-permute-start(bf16[128,1792]{1,0:T(8,128)(2,1)S(1)} %maximum_select_fusion.8), channel_id=1, source_target_pairs={{0,4},{1,5},{2,6},{3,7},{4,0},{5,1},{6,2},{7,3},{8,12},{9,13},{10,... | collective-permute-start | bytes 1376264 | tf_op jit(solution)/shard_map/ppermute | solution.py:34
  846.8 29.5 %collective-permute-start.94 = (bf16[128,4096]{1,0:T(8,128)(2,1)S(1)}, bf16[128,4096]{1,0:T(8,128)(2,1)S(1)}, u32[]{:S(2)}, u32[]{:S(2)}) collective-permute-start(bf16[128,4096]{1,0:T(8,128)(2,1)S(1)} %maximum_select_fusion.1), channel_id=1, source_target_pairs={{0,4},{1,5},{2,6},{3,7},{4,0},{5,1},{6,2},{7,3},{8,12},{9,13},{10,... | collective-permute-start | bytes 3145736 | tf_op jit(solution)/shard_map/ppermute | solution.py:34
  (187 other events, 1916.9 us)
Sparse Core Ops, SparseCore 0:
  137.7 53.2 all-gather.6
  205.0 84.5 all-gather.8
  469.5 73.7 reduce-scatter.1
  545.3 72.6 all-gather.10

commit v2 on v1

--- a/solution.py
+++ b/solution.py
@@ -45,44 +45,79 @@
     return lax.ppermute(block, "ctx", [(i, count - 1 - i) for i in range(count)])
 
 
-def place(pieces):
-    total = sum(piece.shape[0] for _, piece in pieces)
-    whole = jnp.zeros((total,) + pieces[0][1].shape[1:], pieces[0][1].dtype)
-    for start, piece in pieces:
-        whole = lax.dynamic_update_slice_in_dim(whole, piece, start, 0)
-    return whole
-
-
-def gather_shards(shard):
+def assemble_body(routes, at_ref, *refs):
+    pieces, wholes, semaphores = refs[: len(routes)], refs[len(routes) : -1], refs[-1]
+    copies = []
+    for piece, route in zip(pieces, routes):
+        for target, source, size in route:
+            start = pl.multiple_of(at_ref[len(copies)], 16)
+            copy = pltpu.make_async_copy(
+                piece.at[pl.ds(source, size), :],
+                wholes[target].at[pl.ds(start, size), :],
+                semaphores.at[len(copies)],
+            )
+            copy.start()
+            copies.append(copy)
+    for copy in copies:
+        copy.wait()
+
+
+def assemble(pieces, sizes):
+    routes, starts = [], []
+    for piece, places in pieces:
+        route, source = [], 0
+        for target, start, size in places:
+            route.append((target, source, size))
+            starts.append(start)
+            source += size
+        routes.append(route)
+    columns, kind = pieces[0][0].shape[1], pieces[0][0].dtype
+    anywhere = pl.BlockSpec(memory_space=pl.ANY)
+    return pl.pallas_call(
+        partial(assemble_body, routes),
+        in_specs=[pl.BlockSpec(memory_space=pltpu.SMEM)] + [anywhere] * len(pieces),
+        out_specs=[anywhere] * len(sizes),
+        out_shape=[jax.ShapeDtypeStruct((size, columns), kind) for size in sizes],
+        scratch_shapes=[pltpu.SemaphoreType.DMA((len(starts),))],
+        cost_estimate=pl.CostEstimate(
+            flops=0, bytes_accessed=4 * columns * sum(sizes), transcendentals=0
+        ),
+        name="assemble",
+    )(jnp.stack([jnp.asarray(start, jnp.int32) for start in starts]), *[p for p, _ in pieces])
+
+
+def gather_first(shard):
     rows = shard.shape[0]
-    half = rows // 2
+    relayed = rows * 5 // 256 * 16
     w = lax.axis_index("wshard")
     side = lax.axis_index("ctx") % 2
-    mine = lax.dynamic_slice_in_dim(shard, side * half, half, 0)
+    across = exchange(lax.dynamic_slice_in_dim(shard, side * relayed, relayed, 0), 0, 2)
+    across_direct = exchange(shard[2 * relayed :], 0, 2)
     beside = exchange(shard, 0, 1)
-    across = exchange(mine, 0, 2)
-    across_rest = exchange(across, 1, 0)
-    far = exchange(across, 0, 1)
-    far_rest = exchange(across_rest, 0, 1)
-    here, there = side * half, (1 - side) * half
-    return place(
+    across_relayed = exchange(across, 1, 0)
+    parts = [
+        (across, side * relayed, relayed),
+        (across_direct, 2 * relayed, rows - 2 * relayed),
+        (across_relayed, (1 - side) * relayed, relayed),
+    ]
+    pieces = [(shard, [(0, w * rows, rows)]), (beside, [(0, (w ^ 1) * rows, rows)])]
+    for part, start, size in parts:
+        pieces.append((part, [(0, (w ^ 2) * rows + start, size)]))
+        pieces.append((exchange(part, 0, 1), [(0, (w ^ 3) * rows + start, size)]))
+    return assemble(pieces, [4 * rows])[0], across_direct
+
+
+def gather_shards(stacked, sizes, after):
+    stacked, _ = lax.optimization_barrier((stacked, after))
+    w = lax.axis_index("wshard")
+    across = exchange(stacked, 0, 2)
+    parts = [(stacked, 0), (exchange(stacked, 0, 1), 1), (across, 2), (exchange(across, 0, 1), 3)]
+    return assemble(
         [
-            (w * rows, shard),
-            ((w ^ 1) * rows, beside),
-            ((w ^ 2) * rows + here, across),
-            ((w ^ 2) * rows + there, across_rest),
-            ((w ^ 3) * rows + here, far),
-            ((w ^ 3) * rows + there, far_rest),
-        ]
-    )
-
-
-def gather_small(shard):
-    rows = shard.shape[0]
-    w = lax.axis_index("wshard")
-    return place(
-        [(w * rows, shard)]
-        + [((w ^ flip) * rows, exchange(shard, 0, flip)) for flip in (1, 2, 3)]
+            (part, [(at, (w ^ flip) * size, size) for at, size in enumerate(sizes)])
+            for part, flip in parts
+        ],
+        [4 * size for size in sizes],
     )
 
 
@@ -93,25 +128,41 @@
     return total.astype(jnp.bfloat16)
 
 
-def ctx_sum(block):
-    position = lax.axis_index("ctx")
-    bits = []
-    bit = 1
-    while bit < lax.axis_size("ctx"):
-        bits.append(bit)
-        bit *= 2
-    for bit in bits:
-        half = block.shape[0] // 2
-        up = (position // bit) % 2
-        got = exchange(lax.dynamic_slice_in_dim(block, (1 - up) * half, half, 0), bit, 0)
-        block = add_low(lax.dynamic_slice_in_dim(block, up * half, half, 0), got)
-    for bit in reversed(bits):
-        up = (position // bit) % 2
-        got = exchange(block, bit, 0)
-        block = jnp.where(
-            up == 0, jnp.concatenate([block, got], axis=0), jnp.concatenate([got, block], axis=0)
-        )
-    return block.astype(jnp.float32)
+def lay_side_by_side(blocks, rows):
+    parts = []
+    for block in blocks:
+        for start in range(0, block.shape[0], rows):
+            part = block[start : start + rows]
+            parts.append(jnp.pad(part, ((0, rows - part.shape[0]), (0, 0))))
+    return jnp.concatenate(parts, axis=1)
+
+
+def take_apart(array, shapes):
+    rows, start, blocks = array.shape[0], 0, []
+    for height, columns in shapes:
+        parts = []
+        for _ in range(0, height, rows):
+            parts.append(array[: min(height, rows), start : start + columns])
+            start += columns
+        blocks.append(parts[0] if len(parts) == 1 else jnp.concatenate(parts, axis=0))
+    return blocks
+
+
+def ctx_sum(blocks, rows, turn_at):
+    side = lax.axis_index("ctx") % 2
+    count = lax.axis_size("ctx")
+    whole = lay_side_by_side(blocks, rows)
+    half = rows // 2
+    got = exchange(lax.dynamic_slice_in_dim(whole, (1 - side) * half, half, 0), 1, 0)
+    mine = add_low(lax.dynamic_slice_in_dim(whole, side * half, half, 0), got)
+    lines = [list(range(start, count, 2)) for start in range(2)]
+    lines = [lines, lines[::-1], [line[::-1] for line in lines]][turn_at]
+    mine = lax.psum(mine, "ctx", axis_index_groups=lines)
+    got = exchange(mine, 1, 0)
+    whole = jnp.where(
+        side == 0, jnp.concatenate([mine, got], axis=0), jnp.concatenate([got, mine], axis=0)
+    ).astype(jnp.float32)
+    return take_apart(whole, [block.shape for block in blocks])
 
 
 def shard_pieces(array, axis):
@@ -131,14 +182,17 @@
     return add_low(own, got[:rows], got_across)
 
 
-def weight_grad(left, right, axis=1):
-    products = [
+def split_products(left, right, axis=1):
+    return [
         lax.dot_general(
             piece, right, (((1 - axis,), (0,)), ((), ())), preferred_element_type=jnp.float32
         )
         for piece in shard_pieces(left, axis)
     ]
-    return shard_sum(*products)
+
+
+def weight_grad(left, right):
+    return shard_sum(*split_products(left, right))
 
 
 def mixed_dot(left, right):
@@ -668,18 +722,25 @@
     attend_forward, attend_backward = attention_calls(rows, count)
     state_outer, mixer_forward, mixer_backward = mixer_calls(rows)
 
-    small = gather_small(
-        pack_small(norm_gain, conv_weight, conv_bias, skip_gain, mixer_gain, ffn_gain, 1)
+    small = lax.all_gather(
+        pack_small(norm_gain, conv_weight, conv_bias, skip_gain, mixer_gain, ffn_gain, 1),
+        "wshard",
+        tiled=True,
     )
     norm_w, conv_w, conv_b, skip_w, mixer_g, ffn_g = (
         part.astype(jnp.float32) for part in unpack_small(small, model, channels, HM, shards)
     )
-    attn_pair_w = gather_shards(jnp.concatenate([query_proj, key_value_projection], axis=1))
-    in_w = gather_shards(in_proj)
-    mixer_w = gather_shards(mixer_out)
-    attn_w = gather_shards(attn_out)
-    gate_up_w = gather_shards(gate_up)
-    down_w = gather_shards(down_proj)
+    first_w, arrived = gather_first(
+        jnp.concatenate([in_proj, query_proj, key_value_projection], axis=1)
+    )
+    projected_width = in_proj.shape[1]
+    in_w, attn_pair_w = first_w[:, :projected_width], first_w[:, projected_width:]
+    mixer_w, attn_w, down_w = gather_shards(
+        jnp.concatenate([mixer_out, attn_out, down_proj], axis=0),
+        [mixer_out.shape[0], attn_out.shape[0], down_proj.shape[0]],
+        arrived,
+    )
+    (gate_up_w,) = gather_shards(gate_up, [gate_up.shape[0]], arrived)
     query_w = attn_pair_w[:, : QUERY_HEADS * HEAD_SIZE]
     keyval_w = attn_pair_w[:, QUERY_HEADS * HEAD_SIZE :]
 
@@ -818,10 +879,12 @@
     layer_out = (middle + mixed_dot(activated_b, down_w)).astype(jnp.bfloat16)
 
     out_low = cotangent[0]
-    down_share = ctx_sum(weight_grad(activated_b, out_low))
+    down_sum = weight_grad(activated_b, out_low)
     (gate_up_grad_v,) = act_pull(nt_dot(out_low, down_w))
     gate_up_low = gate_up_grad_v.astype(jnp.bfloat16)
-    gate_up_share = ctx_sum(weight_grad(normed2_b, gate_up_low))
+    gate_up_share, down_share = ctx_sum(
+        [weight_grad(normed2_b, gate_up_low), down_sum], model // shards, 0
+    )
     middle_norm_grad, ffn_gain_grad = ffn_pull(nt_dot(gate_up_low, gate_up_w))
     middle_grad = out_low.astype(jnp.float32) + middle_norm_grad
     middle_low = middle_grad.astype(jnp.bfloat16)
@@ -831,10 +894,29 @@
     mixed_grad, gate_z_grad, mixer_gain_grad = gate_pull(gated_grad)
     upward = state_outer(DSSM // NS + 1)(entry_columns, mixed_grad.astype(jnp.bfloat16), conv_b16)
     state_out_grad = chain(lax.all_gather(upward, "ctx"), gains, True)
-    attn_share = ctx_sum(weight_grad(heads_t, middle_low, 0))
-    mixer_share = ctx_sum(weight_grad(gated_b, middle_low))
     gate_z_low = gate_z_grad.astype(jnp.bfloat16)
-    in_share_z = ctx_sum(weight_grad(normed_b, gate_z_low))
+    mixer_products = split_products(gated_b, middle_low)
+    attn_products = split_products(heads_t, middle_low, 0)
+    shard_sizes = [mixer_out.shape[0], attn_out.shape[0]]
+
+    def interleaved(parts):
+        return jnp.concatenate(
+            [
+                part[start * size : (start + 1) * size]
+                for start in range(parts[0].shape[0] // shard_sizes[0])
+                for part, size in zip(parts, shard_sizes)
+            ],
+            axis=0,
+        ).astype(jnp.bfloat16)
+
+    mixer_attn_sum = shard_sum(
+        *[interleaved(parts) for parts in zip(mixer_products, attn_products)]
+    )
+    mixer_attn_share, in_share_z = ctx_sum(
+        [mixer_attn_sum, weight_grad(normed_b, gate_z_low)], model // shards, 1
+    )
+    mixer_share = mixer_attn_share[: mixer_out.shape[0]]
+    attn_share = mixer_attn_share[mixer_out.shape[0] :]
 
     delta = jnp.sum(grad_x.astype(jnp.float32) * heads_x, axis=2, keepdims=True)
     query_grad_x, pairs_grad = attend_backward(
@@ -882,7 +964,7 @@
     from_above = from_behind(extended_grad[: KW - 1], "ctx", -1)
     pre_grad = extended_grad[KW - 1 :] + jnp.pad(from_above, ((rows - (KW - 1), 0), (0, 0)))
     pre_low = pre_grad.astype(jnp.bfloat16)
-    in_share_pre = ctx_sum(weight_grad(normed_b, pre_low))
+    in_sum_pre = weight_grad(normed_b, pre_low)
     projected_low = jnp.concatenate([gate_z_low, pre_low], axis=1)
     normed_grad = nt_dot(projected_low, in_w)
 
@@ -895,7 +977,7 @@
         axis=0,
     ).astype(jnp.bfloat16)
     attn_pair_low = jnp.concatenate([query_low, keyval_low], axis=0).T
-    attn_pair_share = ctx_sum(weight_grad(normed_b, attn_pair_low))
+    attn_pair_sum = weight_grad(normed_b, attn_pair_low)
     normed_grad = normed_grad + nt_dot(attn_pair_low, attn_pair_w)
     source_grad, norm_grad = norm_pull(normed_grad)
     tokens_grad = (middle_grad + source_grad)[None]
@@ -903,7 +985,9 @@
     small_grad = pack_small(
         norm_grad, conv_weight_grad, conv_bias_grad, skip_grad, mixer_gain_grad, ffn_gain_grad, shards
     )
-    small_share = ctx_sum(shard_sum(*shard_pieces(small_grad, 0)))
+    in_share_pre, attn_pair_share, small_share = ctx_sum(
+        [in_sum_pre, attn_pair_sum, shard_sum(*shard_pieces(small_grad, 0))], model // shards, 2
+    )
     norm_share, conv_w_share, conv_b_share, skip_share, mixer_g_share, ffn_share = unpack_small(
         small_share, model, channels, HM, 1
     )

time: 893 us -> 1600 us (1.79)
  Pallas kernels: 91.9 us -> 860 us
  local copies, waits for them, and re-layouts: 163 us -> 106 us
  starting transfers between devices: 103 us -> 58.9 us
  blocking collectives: 0 us -> 25.7 us
    pallas_call x0 -> x3, Pallas kernels: none -> 768 us  [assemble(): pl.pallas_call(partial(assemble_body, routes), in_specs=[pl.BlockSpec(mem...]
    psum x0 -> x3, waiting for transfers between devices: none -> 97.1 us  [ctx_sum(): mine = lax.psum(mine, 'ctx', axis_index_groups=lines)]
    ppermute x97 -> x33, waiting for transfers between devices: 274 us -> 187 us  [exchange(): return lax.ppermute(block, MESH_AXES, route)]
    dynamic_update_slice x40 -> x0, local copies, waits for them, and re-layouts: 50.2 us -> none  [place(): whole = lax.dynamic_update_slice_in_dim(whole, piece, start, 0)]
    ppermute x97 -> x33, starting transfers between devices: 83.5 us -> 43.1 us  [exchange(): return lax.ppermute(block, MESH_AXES, route)]
    all_gather x0 -> x1, blocking collectives: none -> 25.7 us  [per_device(): lax.all_gather(pack_small(norm_gain, conv_weight, conv_bias, skip_gain, m...]
  transfers between devices with their start and end apart: 107 -> 46, of which waited for: 47 -> 17; matrix products, arithmetic and copies ran while one was open for 33% -> 16% of each run, Pallas kernels for 9% -> 37%
where the time goes in v2:
time: 1600 us; the launch traced here: 1590 us
  Pallas kernels  860 us (54%)
  waiting for transfers between devices  298 us (19%)
  other arithmetic  117 us (7%)
  matrix products  108 us (7%)
  local copies, waits for them, and re-layouts  106 us (7%)
  starting transfers between devices  58.9 us (4%)
  blocking collectives  25.7 us (2%)
  between operations  19.3 us (1%)
    pallas_call x3, Pallas kernels, assemble(): pl.pallas_call(partial(assemble_body, routes), in_specs=[pl.BlockSpec(mem...  768 us
    ppermute x33, waiting for transfers between devices, exchange(): return lax.ppermute(block, MESH_AXES, route)  187 us
    psum x3, waiting for transfers between devices, ctx_sum(): mine = lax.psum(mine, 'ctx', axis_index_groups=lines)  97.1 us
    dot_general x21, matrix products, split_products(): lax.dot_general(piece, right, (((1 - axis,), (0,)), ((), ())), preferred_...  51.4 us
    ppermute x33, starting transfers between devices, exchange(): return lax.ppermute(block, MESH_AXES, route)  43.1 us
    dot_general x6, matrix products, nt_dot(): lax.dot_general(left, right, (((1,), (1,)), ((), ())), preferred_element_...  32.3 us
  transfers between devices with their start and end apart: 46, of which 17 were waited for; matrix products, arithmetic and copies ran while one was open for 16% of the time, Pallas kernels for 37%

profile of v2, /device:TPU:0, one launch (start us, length us, event | category | flops | bytes accessed | tf_op | source)
XLA Modules:
  0.0 1592.3 jit_solution(2460521899043957945)
XLA Ops:
  10.5 2.6 collective-permute-start.1
  20.9 25.7 %all_gather.21 = bf16[128,128]{1,0:T(8,128)(2,1)S(1)} all-gather(bf16[32,128]{1,0:T(8,128)(2,1)S(1)} %bitcast.338), channel_id=1, replica_groups=mesh['ctx'=8,'wshard'=4] {'wshard'}, dimensions={0}, use_global_device_ids=true | all-gather | bytes 40960 | tf_op jit(solution)/shard_map/all_gather | solution.py:725
  58.4 9.6 collective-permute-done.5.refs_6_
  68.1 3.0 pad_maximum_fusion.2.refs_0_
  73.1 256.1 %assemble.3 = bf16[1024,4096]{1,0:T(8,128)(2,1)} custom-call(s32[8]{0:T(128)} %stack.147.at_ref, bf16[256,4096]{1,0:T(8,128)(2,1)} %copy-done.28, bf16[256,4096]{1,0:T(8,128)(2,1)} %collective-permute-done.refs_1_, bf16[80,4096]{1,0:T(8,128)(2,1)} %collective-permute-done.1.refs_2_, bf16[80,4096]{1,0:T(8,128)(2,1)} %collective-permute-done.2.refs_3_, ...), custom_call_target="tpu_custom_call" | custom-call | bytes 16777216 | tf_op jit(solution)/shard_map/assemble/pallas_call | solution.py:76
  336.7 8.6 fusion.234
  347.1 3.6 collective-permute-start.12
  357.5 4.4 multiply_convert_fusion.1
  361.9 4.2 state_outer.2
  373.1 29.1 %collective-permute-done.10.refs_2_ = bf16[1024,1024]{1,0:T(8,128)(2,1)} collective-permute-done((bf16[1024,1024]{1,0:T(8,128)(2,1)}, bf16[1024,1024]{1,0:T(8,128)(2,1)}, u32[]{:S(2)}, u32[]{:S(2)}) %collective-permute-start.10) | collective-permute-done | bytes 2097184 | tf_op jit(solution)/shard_map/ppermute | solution.py:34
  402.2 44.2 %collective-permute-done.14.refs_2_ = bf16[256,4096]{1,0:T(8,128)(2,1)} collective-permute-done((bf16[256,4096]{1,0:T(8,128)(2,1)}, bf16[256,4096]{1,0:T(8,128)(2,1)}, u32[]{:S(2)}, u32[]{:S(2)}) %collective-permute-start.14) | collective-permute-done | bytes 2097184 | tf_op jit(solution)/shard_map/ppermute | solution.py:34
  462.8 2.7 collective-permute-start.7
  476.2 2.5 multiply_cosine_fusion.1
  482.4 256.0 %assemble.4 = (bf16[1536,1024]{1,0:T(8,128)(2,1)}, bf16[512,1024]{1,0:T(8,128)(2,1)}, bf16[2048,1024]{1,0:T(8,128)(2,1)}) custom-call(s32[12]{0:T(128)} %stack.166.at_ref, bf16[1024,1024]{1,0:T(8,128)(2,1)} %pad_maximum_fusion.2.refs_0_, bf16[1024,1024]{1,0:T(8,128)(2,1)} %collective-permute-done.9.refs_1_, ...), custom_call_target="tpu_custom_call" | custom-call | bytes 16777216 | tf_op jit(solution)/shard_map/assemble/pallas_call | solution.py:76
  738.4 255.9 %assemble.5 = bf16[1024,4096]{1,0:T(8,128)(2,1)} custom-call(s32[4]{0:T(128)} %pad_add_fusion.5.at_ref, bf16[256,4096]{1,0:T(8,128)(2,1)} %refs_0_, bf16[256,4096]{1,0:T(8,128)(2,1)} %collective-permute-done.13.refs_1_, bf16[256,4096]{1,0:T(8,128)(2,1)} %collective-permute-done.14.refs_2_, bf16[256,4096]{1,0:T(8,128)(2,1)} %collective-permute-done.15.refs_3_), custom_call_target="tpu_custom_call" | custom-call | bytes 16777216 | tf_op jit(solution)/shard_map/assemble/pallas_call | solution.py:76
  997.0 21.5 %attend_forward.1 = (f32[2,2,64,1024]{3,2,1,0:T(8,128)S(1)}, f32[2,2,1,1024]{3,2,1,0:T(1,128)S(1)}) custom-call(s32[2]{0:T(128)S(1)} %pad_add_fusion.4.blocks, bf16[8,2,512,128]{3,2,1,0:T(8,128)(2,1)S(1)} %bitcast.290, bf16[4096,128]{1,0:T(8,128)(2,1)S(1)} %fusion.40.side_ref, bf16[2,2,64,1024]{3,2,1,0:T(8,128)(2,1)S(1)} %copy-done.10, ...), custom_call_target="tpu_custom_call" | custom-call | flops 4831838208 | bytes 33554432 | tf_op jit(solution)/shard_map/attend_forward/pallas_call | solution.py:852
  1023.2 8.6 collective-permute-done.8
  1039.9 3.9 fusion.74.state_ref
  1043.7 11.6 mixer_forward.1
  1055.4 4.1 multiply_reduce_fusion.6
  1065.7 4.5 fusion.236
  1070.3 6.5 bitcast_multiply_fusion.1
  1076.8 4.1 add_convert_fusion
  1080.9 8.8 multiply_reduce_fusion.7
  1089.7 4.4 convolution_convert_fusion
  1094.2 2.6 convolution_convert_fusion.3
  1107.8 2.5 convolution_convert_fusion.8
  1120.7 30.5 %attend_backward.1 = (f32[2,2,64,1024]{3,2,1,0:T(8,128)S(1)}, bf16[8,2,512,128]{3,2,1,0:T(8,128)(2,1)S(1)}) custom-call(s32[2]{0:T(128)S(1)} %pad_add_fusion.4.blocks, bf16[8,2,512,128]{3,2,1,0:T(8,128)(2,1)} %bitcast.289, bf16[4096,128]{1,0:T(8,128)(2,1)S(1)} %copy-done.7, bf16[2,2,64,1024]{3,2,1,0:T(8,128)(2,1)S(1)} %copy-done.11, ...), custom_call_target="tpu_custom_call" | custom-call | flops 12079595520 | bytes 33554432 | tf_op jit(solution)/shard_map/attend_backward/pallas_call | solution.py:922
  1153.7 2.5 convolution_convert_fusion.4
  1161.2 5.3 fusion.214
  1176.9 6.6 state_outer.3
  1183.5 3.0 convolution_convert_fusion.6
  1186.6 3.3 fusion.117
  1189.8 4.3 fusion.105
  1208.9 3.0 add_convert_fusion.5
  1213.2 9.1 collective-permute-done.30
  1223.7 21.0 %collective-permute-done.28 = bf16[512,1024]{1,0:T(8,128)(2,1)S(1)} collective-permute-done((bf16[512,1024]{1,0:T(8,128)(2,1)S(1)}, bf16[512,1024]{1,0:T(8,128)(2,1)S(1)}, u32[]{:S(2)}, u32[]{:S(2)}) %collective-permute-start.28) | collective-permute-done | bytes 1048608 | tf_op jit(solution)/shard_map/ppermute | solution.py:34
  1247.8 2.6 collective-permute-start.31
  1260.1 6.5 collective-permute-done.36
  1269.8 8.8 collective-permute-done.31
  1286.8 5.7 add_convert_fusion.2
  1293.9 3.8 fusion.42
  1297.8 2.4 add_convert_fusion.14
  1302.9 3.9 fusion.86.state_grad_ref
  1306.8 17.5 %mixer_backward.1 = (f32[512,1792]{1,0:T(8,128)}, f32[12,1,128]{2,1,0:T(1,128)S(1)}) custom-call(f32[12,1,128]{2,1,0:T(1,128)S(1)} %broadcast_in_dim.108.skip_ref, bf16[512,1792]{1,0:T(8,128)(2,1)S(1)} %get-tuple-element.81.left_ref.right_ref.x_ref.b_ref.c_ref, bf16[512,1792]{1,0:T(8,128)(2,1)S(1)} %get-tuple-element.81.left_ref.right_ref.x_ref.b_ref.c_ref, ...), custom_call_target="tpu_custom_call" | custom-call | flops 3221225472 | bytes 9437184 | tf_op jit(solution)/shard_map/mixer_backward/pallas_call | solution.py:947
  1324.3 5.6 multiply_reduce_fusion.3
  1331.4 3.0 pad_add_fusion
  1340.1 2.4 fusion.9
  1342.6 9.5 fusion.30
  1353.9 2.8 convolution_convert_fusion.2
  1361.1 3.4 add_convert_fusion.1
  1368.5 8.9 collective-permute-start.37
  1377.4 9.3 collective-permute-done.20
  1389.6 9.0 collective-permute-start.25
  1398.6 3.3 fusion.52
  1403.4 24.4 %collective-permute-done.25 = bf16[128,2688]{1,0:T(8,128)(2,1)} collective-permute-done((bf16[128,2688]{1,0:T(8,128)(2,1)}, bf16[128,2688]{1,0:T(8,128)(2,1)}, u32[]{:S(2)}, u32[]{:S(2)}) %collective-permute-start.25) | collective-permute-done | bytes 688160 | tf_op jit(solution)/shard_map/ppermute | solution.py:34
  1430.3 3.4 add_convert_fusion.3
  1433.8 5.0 fusion.38
  1438.8 33.2 %all-reduce.24.cloned.1.call-done = bf16[128,2688]{1,0:T(8,128)(2,1)} async-done(((bf16[128,2688]{1,0:T(8,128)(2,1)}), bf16[128,2688]{1,0:T(8,128)(2,1)}) %all-reduce.24.cloned.1.call-update) | async-done | bytes 688144 | tf_op jit(solution)/shard_map/psum | solution.py:160
  1473.5 2.7 fusion.41
  1479.6 63.9 %all-reduce.28.cloned.1.call-done = bf16[128,6144]{1,0:T(8,128)(2,1)} async-done(((bf16[128,6144]{1,0:T(8,128)(2,1)}), bf16[128,6144]{1,0:T(8,128)(2,1)}) %all-reduce.28.cloned.1.call-update) | async-done | bytes 1572880 | tf_op jit(solution)/shard_map/psum | solution.py:160
  1551.2 3.6 pad_maximum_fusion
  1554.8 24.0 %collective-permute-done.38 = bf16[128,6144]{1,0:T(8,128)(2,1)} collective-permute-done((bf16[128,6144]{1,0:T(8,128)(2,1)}, bf16[128,6144]{1,0:T(8,128)(2,1)}, u32[]{:S(2)}, u32[]{:S(2)}) %collective-permute-start.38) | collective-permute-done | bytes 1572896 | tf_op jit(solution)/shard_map/ppermute | solution.py:34
  1578.8 2.5 fusion.16
  (687 shorter events, 222.1 us)
Async XLA Ops:
  7.2 987.2 %all-gather.7.cloned.1.call-start = ((), (), s32[]{:S(2)}) async-start(), calls=%async_computation.5 | async-start | bytes 2359296 | tf_op jit(solution)/shard_map/all_gather | solution.py:768
  9.0 37.6 %copy-start.30 = (bf16[1,512,1024]{2,1,0:T(8,128)(2,1)S(1)}, bf16[1,512,1024]{2,1,0:T(8,128)(2,1)}, u32[]{:S(2)}) copy-start(bf16[1,512,1024]{2,1,0:T(8,128)(2,1)} %param.17) | copy-start | bytes 3145732
  9.1 46.6 %copy-start.28 = (bf16[256,4096]{1,0:T(8,128)(2,1)}, bf16[256,4096]{1,0:T(8,128)(2,1)S(1)}, u32[]{:S(2)}) copy-start(bf16[256,4096]{1,0:T(8,128)(2,1)S(1)} %constant_dynamic-update-slice_fusion.refs_0_) | copy-start | bytes 6291460
  9.1 63.9 %collective-permute-start = (bf16[256,4096]{1,0:T(8,128)(2,1)S(1)}, bf16[256,4096]{1,0:T(8,128)(2,1)}, u32[]{:S(2)}, u32[]{:S(2)}) collective-permute-start(bf16[256,4096]{1,0:T(8,128)(2,1)S(1)} %constant_dynamic-update-slice_fusion.refs_0_), channel_id=1, source_target_pairs={{0,1},{1,0},{2,3},{3,2},{4,5},{5,4},{6,7},{7,6},{8,9},{9,8},{10,11... | collective-permute-start | bytes 6291464 | tf_op jit(solution)/shard_map/ppermute | solution.py:34
  10.5 40.2 %collective-permute-start.1 = (bf16[80,4096]{1,0:T(8,128)(2,1)}, bf16[80,4096]{1,0:T(8,128)(2,1)}, u32[]{:S(2)}, u32[]{:S(2)}) collective-permute-start(bf16[80,4096]{1,0:T(8,128)(2,1)} %constant_dynamic-slice_fusion.13), channel_id=1, source_target_pairs={{0,2},{1,3},{2,0},{3,1},{4,6},{5,7},{6,4},{7,5},{8,10},{9,11},{10,... | collective-permute-start | bytes 1966088 | tf_op jit(solution)/shard_map/ppermute | solution.py:34
  14.0 39.0 %collective-permute-start.3 = (bf16[96,4096]{1,0:T(8,128)(2,1)}, bf16[96,4096]{1,0:T(8,128)(2,1)}, u32[]{:S(2)}, u32[]{:S(2)}) collective-permute-start(bf16[96,4096]{1,0:T(8,128)(2,1)} %slice.539), channel_id=1, source_target_pairs={{0,2},{1,3},{2,0},{3,1},{4,6},{5,7},{6,4},{7,5},{8,10},{9,11},{10,... | collective-permute-start | bytes 2359304 | tf_op jit(solution)/shard_map/ppermute | solution.py:34
  17.4 53.7 %copy-start.111 = (s32[512]{0:T(512)}, s32[512]{0:T(512)S(1)}, u32[]{:S(2)}) copy-start(s32[512]{0:T(512)S(1)} %get-tuple-element.57) | copy-start | bytes 6148
  19.6 315.7 %copy-start.83 = (f32[24,512]{1,0:T(8,128)}, f32[24,512]{1,0:T(8,128)S(1)}, u32[]{:S(2)}) copy-start(f32[24,512]{1,0:T(8,128)S(1)} %convolution_bitcast_fusion) | copy-start | bytes 147460
  46.9 26.1 %copy-start.126 = (f32[512]{0:T(512)}, f32[512]{0:T(512)S(1)}, u32[]{:S(2)}) copy-start(f32[512]{0:T(512)S(1)} %fusion.168) | copy-start | bytes 6148
  48.3 24.7 %copy-start.138 = (f32[32]{0:T(128)}, f32[32]{0:T(128)S(1)}, u32[]{:S(2)}) copy-start(f32[32]{0:T(128)S(1)} %multiply_power_fusion) | copy-start | bytes 388
  50.8 17.3 %collective-permute-start.5 = (bf16[80,4096]{1,0:T(8,128)(2,1)}, bf16[80,4096]{1,0:T(8,128)(2,1)}, u32[]{:S(2)}, u32[]{:S(2)}) collective-permute-start(bf16[80,4096]{1,0:T(8,128)(2,1)} %collective-permute-done.1.refs_2_), channel_id=1, source_target_pairs={{0,4},{1,5},{2,6},{3,7},{4,0},{5,1},{6,2},{7,3},{8,12},{9,13},{10,... | collective-permute-start | bytes 1966088 | tf_op jit(solution)/shard_map/ppermute | solution.py:34
  53.1 19.9 %collective-permute-start.4 = (bf16[96,4096]{1,0:T(8,128)(2,1)}, bf16[96,4096]{1,0:T(8,128)(2,1)}, u32[]{:S(2)}, u32[]{:S(2)}) collective-permute-start(bf16[96,4096]{1,0:T(8,128)(2,1)} %collective-permute-done.3.refs_4_), channel_id=1, source_target_pairs={{0,1},{1,0},{2,3},{3,2},{4,5},{5,4},{6,7},{7,6},{8,9},{9,8},{10,11... | collective-permute-start | bytes 2359304 | tf_op jit(solution)/shard_map/ppermute | solution.py:34
  57.9 15.1 collective-permute-start.2
  68.1 5.0 collective-permute-start.6
  73.0 256.1 %copy-start.36 = (bf16[512,1024]{1,0:T(8,128)(2,1)S(1)}, bf16[512,1024]{1,0:T(8,128)(2,1)}, u32[]{:S(2)}) copy-start(bf16[512,1024]{1,0:T(8,128)(2,1)} %fusion.29) | copy-start | bytes 3145732
  332.6 703.9 %all-gather.9.cloned.1.call-start = ((), (), s32[]{:S(2)}) async-start(), calls=%async_computation.6 | async-start | bytes 3575808 | tf_op jit(solution)/shard_map/all_gather | solution.py:847
  335.3 22.1 %copy-start.117 = (f32[512]{0:T(512)}, f32[512]{0:T(512)S(1)}, u32[]{:S(2)}) copy-start(f32[512]{0:T(512)S(1)} %get-tuple-element.174) | copy-start | bytes 6148
  335.3 22.1 %copy-start.119 = (f32[512]{0:T(512)}, f32[512]{0:T(512)S(1)}, u32[]{:S(2)}) copy-start(f32[512]{0:T(512)S(1)} %get-tuple-element.175) | copy-start | bytes 6148
  335.3 22.1 %copy-start.121 = (f32[512]{0:T(512)}, f32[512]{0:T(512)S(1)}, u32[]{:S(2)}) copy-start(f32[512]{0:T(512)S(1)} %get-tuple-element.176) | copy-start | bytes 6148
  347.1 10.0 collective-permute-start.12
  353.4 48.8 %collective-permute-start.10 = (bf16[1024,1024]{1,0:T(8,128)(2,1)}, bf16[1024,1024]{1,0:T(8,128)(2,1)}, u32[]{:S(2)}, u32[]{:S(2)}) collective-permute-start(bf16[1024,1024]{1,0:T(8,128)(2,1)} %pad_maximum_fusion.2.refs_0_), channel_id=1, source_target_pairs={{0,2},{1,3},{2,0},{3,1},{4,6},{5,7},{6,4},{7,5},{8,10},{9,11},{10,... | collective-permute-start | bytes 6291464 | tf_op jit(solution)/shard_map/ppermute | solution.py:34
  354.9 91.5 %collective-permute-start.14 = (bf16[256,4096]{1,0:T(8,128)(2,1)}, bf16[256,4096]{1,0:T(8,128)(2,1)}, u32[]{:S(2)}, u32[]{:S(2)}) collective-permute-start(bf16[256,4096]{1,0:T(8,128)(2,1)} %refs_0_), channel_id=1, source_target_pairs={{0,2},{1,3},{2,0},{3,1},{4,6},{5,7},{6,4},{7,5},{8,10},{9,11},{10,... | collective-permute-start | bytes 6291464 | tf_op jit(solution)/shard_map/ppermute | solution.py:34
  361.9 84.5 %copy-start.112 = (s32[512]{0:T(512)S(1)}, s32[512]{0:T(512)}, u32[]{:S(2)}) copy-start(s32[512]{0:T(512)} %copy-done.111) | copy-start | bytes 6148
  367.0 914.3 %reduce-scatter.2.cloned.1.call-start = ((), (), s32[]{:S(2)}) async-start(), calls=%async_computation.1 | async-start | bytes 2359296 | tf_op jit(solution)/shard_map/reduce_scatter | solution.py:932
  372.5 621.9 %copy-start.6 = (bf16[4096,128]{1,0:T(8,128)(2,1)}, bf16[4096,128]{1,0:T(8,128)(2,1)S(1)}, u32[]{:S(2)}) copy-start(bf16[4096,128]{1,0:T(8,128)(2,1)S(1)} %fusion.40.side_ref) | copy-start | bytes 3145732
  372.5 109.9 %collective-permute-start.9 = (bf16[1024,1024]{1,0:T(8,128)(2,1)}, bf16[1024,1024]{1,0:T(8,128)(2,1)}, u32[]{:S(2)}, u32[]{:S(2)}) collective-permute-start(bf16[1024,1024]{1,0:T(8,128)(2,1)} %pad_maximum_fusion.2.refs_0_), channel_id=1, source_target_pairs={{0,1},{1,0},{2,3},{3,2},{4,5},{5,4},{6,7},{7,6},{8,9},{9,8},{10,11... | collective-permute-start | bytes 6291464 | tf_op jit(solution)/shard_map/ppermute | solution.py:34
  372.6 365.8 %collective-permute-start.13 = (bf16[256,4096]{1,0:T(8,128)(2,1)}, bf16[256,4096]{1,0:T(8,128)(2,1)}, u32[]{:S(2)}, u32[]{:S(2)}) collective-permute-start(bf16[256,4096]{1,0:T(8,128)(2,1)} %refs_0_), channel_id=1, source_target_pairs={{0,1},{1,0},{2,3},{3,2},{4,5},{5,4},{6,7},{7,6},{8,9},{9,8},{10,11... | collective-permute-start | bytes 6291464 | tf_op jit(solution)/shard_map/ppermute | solution.py:34
  402.2 80.2 %collective-permute-start.11 = (bf16[1024,1024]{1,0:T(8,128)(2,1)}, bf16[1024,1024]{1,0:T(8,128)(2,1)}, u32[]{:S(2)}, u32[]{:S(2)}) collective-permute-start(bf16[1024,1024]{1,0:T(8,128)(2,1)} %collective-permute-done.10.refs_2_), channel_id=1, source_target_pairs={{0,1},{1,0},{2,3},{3,2},{4,5},{5,4},{6,7},{7,6},{8,9},{9,8},{10,11... | collective-permute-start | bytes 6291464 | tf_op jit(solution)/shard_map/ppermute | solution.py:34
  446.4 292.0 %collective-permute-start.15 = (bf16[256,4096]{1,0:T(8,128)(2,1)}, bf16[256,4096]{1,0:T(8,128)(2,1)}, u32[]{:S(2)}, u32[]{:S(2)}) collective-permute-start(bf16[256,4096]{1,0:T(8,128)(2,1)} %collective-permute-done.14.refs_2_), channel_id=1, source_target_pairs={{0,1},{1,0},{2,3},{3,2},{4,5},{5,4},{6,7},{7,6},{8,9},{9,8},{10,11... | collective-permute-start | bytes 6291464 | tf_op jit(solution)/shard_map/ppermute | solution.py:34
  462.8 17.7 %collective-permute-start.7 = (bf16[2,64,1024]{2,1,0:T(8,128)(2,1)}, bf16[2,64,1024]{2,1,0:T(8,128)(2,1)}, u32[]{:S(2)}, u32[]{:S(2)}) collective-permute-start(bf16[2,64,1024]{2,1,0:T(8,128)(2,1)} %squeeze.21), channel_id=1, source_target_pairs={{0,28},{4,24},{8,20},{12,16},{16,12},{20,8},{24,4},{28,0},{1,29},{... | collective-permute-start | bytes 786440 | tf_op jit(solution)/shard_map/ppermute | solution.py:45
  1020.3 11.4 collective-permute-start.8
  1065.1 32.2 %copy-start.19 = (f32[512,1024]{1,0:T(8,128)}, f32[512,1024]{1,0:T(8,128)S(1)}, u32[]{:S(2)}) copy-start(f32[512,1024]{1,0:T(8,128)S(1)} %get-tuple-element.70) | copy-start | bytes 6291460
  1094.1 192.7 %collective-permute-start.33 = (bf16[512,4096]{1,0:T(8,128)(2,1)}, bf16[512,4096]{1,0:T(8,128)(2,1)}, u32[]{:S(2)}, u32[]{:S(2)}) collective-permute-start(bf16[512,4096]{1,0:T(8,128)(2,1)} %convolution_convert_fusion), channel_id=1, source_target_pairs={{0,1},{1,0},{2,3},{3,2},{4,5},{5,4},{6,7},{7,6},{8,9},{9,8},{10,11... | collective-permute-start | bytes 12582920 | tf_op jit(solution)/shard_map/ppermute | solution.py:34
  1096.8 112.2 %collective-permute-start.35 = (bf16[1024,1024]{1,0:T(8,128)(2,1)}, bf16[1024,1024]{1,0:T(8,128)(2,1)}, u32[]{:S(2)}, u32[]{:S(2)}) collective-permute-start(bf16[1024,1024]{1,0:T(8,128)(2,1)} %convolution_convert_fusion.3), channel_id=1, source_target_pairs={{0,1},{1,0},{2,3},{3,2},{4,5},{5,4},{6,7},{7,6},{8,9},{9,8},{10,11... | collective-permute-start | bytes 6291464 | tf_op jit(solution)/shard_map/ppermute | solution.py:34
  1105.7 11.3 collective-permute-start.17
  1120.7 33.0 %copy-start.75 = (bf16[512,384]{1,0:T(8,128)(2,1)S(1)}, bf16[512,384]{1,0:T(8,128)(2,1)}, u32[]{:S(2)}) copy-start(bf16[512,384]{1,0:T(8,128)(2,1)} %get-tuple-element.99) | copy-start | bytes 1179652
  1153.6 149.2 %all-gather.11.cloned.1.call-start = ((), (), s32[]{:S(2)}) async-start(), calls=%async_computation.7 | async-start | bytes 3538944 | tf_op jit(solution)/shard_map/all_gather | solution.py:896
  1158.8 44.7 %collective-permute-start.27 = (bf16[1024,1024]{1,0:T(8,128)(2,1)}, bf16[1024,1024]{1,0:T(8,128)(2,1)}, u32[]{:S(2)}, u32[]{:S(2)}) collective-permute-start(bf16[1024,1024]{1,0:T(8,128)(2,1)} %pad_maximum_fusion.3), channel_id=1, source_target_pairs={{0,1},{1,0},{2,3},{3,2},{4,5},{5,4},{6,7},{7,6},{8,9},{9,8},{10,11... | collective-permute-start | bytes 6291464 | tf_op jit(solution)/shard_map/ppermute | solution.py:34
  1168.8 30.4 %collective-permute-start.29 = (bf16[512,1536]{1,0:T(8,128)(2,1)}, bf16[512,1536]{1,0:T(8,128)(2,1)}, u32[]{:S(2)}, u32[]{:S(2)}) collective-permute-start(bf16[512,1536]{1,0:T(8,128)(2,1)} %convolution_convert_fusion.1), channel_id=1, source_target_pairs={{0,1},{1,0},{2,3},{3,2},{4,5},{5,4},{6,7},{7,6},{8,9},{9,8},{10,11... | collective-permute-start | bytes 4718600 | tf_op jit(solution)/shard_map/ppermute | solution.py:34
  1194.2 207.7 %all-reduce.26.cloned.1.call-start = ((), (), s32[]{:S(2)}) async-start(), calls=%async_computation.3 | async-start | bytes 1835008 | tf_op jit(solution)/shard_map/psum | solution.py:160
  1201.9 20.4 %collective-permute-start.30 = (bf16[256,1536]{1,0:T(8,128)(2,1)S(1)}, bf16[256,1536]{1,0:T(8,128)(2,1)S(1)}, u32[]{:S(2)}, u32[]{:S(2)}) collective-permute-start(bf16[256,1536]{1,0:T(8,128)(2,1)S(1)} %add_convert_fusion.11), channel_id=1, source_target_pairs={{0,2},{1,3},{2,0},{3,1},{4,6},{5,7},{6,4},{7,5},{8,10},{9,11},{10,... | collective-permute-start | bytes 2359304 | tf_op jit(solution)/shard_map/ppermute | solution.py:34
  1205.0 39.8 %collective-permute-start.28 = (bf16[512,1024]{1,0:T(8,128)(2,1)S(1)}, bf16[512,1024]{1,0:T(8,128)(2,1)S(1)}, u32[]{:S(2)}, u32[]{:S(2)}) collective-permute-start(bf16[512,1024]{1,0:T(8,128)(2,1)S(1)} %add_convert_fusion.7), channel_id=1, source_target_pairs={{0,2},{1,3},{2,0},{3,1},{4,6},{5,7},{6,4},{7,5},{8,10},{9,11},{10,... | collective-permute-start | bytes 3145736 | tf_op jit(solution)/shard_map/ppermute | solution.py:34
  1206.6 48.1 %collective-permute-start.18 = (bf16[2,64,1024]{2,1,0:T(8,128)(2,1)}, bf16[2,64,1024]{2,1,0:T(8,128)(2,1)}, u32[]{:S(2)}, u32[]{:S(2)}) collective-permute-start(bf16[2,64,1024]{2,1,0:T(8,128)(2,1)} %get-tuple-element.126), channel_id=1, source_target_pairs={{0,28},{4,24},{8,20},{12,16},{16,12},{20,8},{24,4},{28,0},{1,29},{... | collective-permute-start | bytes 786440 | tf_op jit(solution)/shard_map/ppermute | solution.py:45
  1211.9 32.8 %copy-start.66 = (bf16[384,1024]{1,0:T(8,128)(2,1)S(1)}, bf16[384,1024]{1,0:T(8,128)(2,1)}, u32[]{:S(2)}) copy-start(bf16[384,1024]{1,0:T(8,128)(2,1)} %convolution_convert_fusion.6) | copy-start | bytes 2359300
  1211.9 54.8 %collective-permute-start.36 = (bf16[512,1024]{1,0:T(8,128)(2,1)}, bf16[512,1024]{1,0:T(8,128)(2,1)}, u32[]{:S(2)}, u32[]{:S(2)}) collective-permute-start(bf16[512,1024]{1,0:T(8,128)(2,1)} %add_convert_fusion.5), channel_id=1, source_target_pairs={{0,2},{1,3},{2,0},{3,1},{4,6},{5,7},{6,4},{7,5},{8,10},{9,11},{10,... | collective-permute-start | bytes 3145736 | tf_op jit(solution)/shard_map/ppermute | solution.py:34
  1247.8 30.8 %collective-permute-start.31 = (bf16[128,3584]{1,0:T(8,128)(2,1)}, bf16[128,3584]{1,0:T(8,128)(2,1)}, u32[]{:S(2)}, u32[]{:S(2)}) collective-permute-start(bf16[128,3584]{1,0:T(8,128)(2,1)} %constant_dynamic-slice_fusion.5), channel_id=1, source_target_pairs={{0,4},{1,5},{2,6},{3,7},{4,0},{5,1},{6,2},{7,3},{8,12},{9,13},{10,... | collective-permute-start | bytes 2752520 | tf_op jit(solution)/shard_map/ppermute | solution.py:34
  1281.0 191.0 %all-reduce.24.cloned.1.call-start = ((), (), s32[]{:S(2)}) async-start(), calls=%async_computation.2 | async-start | bytes 1376256 | tf_op jit(solution)/shard_map/psum | solution.py:160
  1286.7 11.0 collective-permute-start.21
  1292.5 68.5 %collective-permute-start.34 = (bf16[256,4096]{1,0:T(8,128)(2,1)}, bf16[256,4096]{1,0:T(8,128)(2,1)}, u32[]{:S(2)}, u32[]{:S(2)}) collective-permute-start(bf16[256,4096]{1,0:T(8,128)(2,1)} %add_convert_fusion.2), channel_id=1, source_target_pairs={{0,2},{1,3},{2,0},{3,1},{4,6},{5,7},{6,4},{7,5},{8,10},{9,11},{10,... | collective-permute-start | bytes 6291464 | tf_op jit(solution)/shard_map/ppermute | solution.py:34
  1300.2 60.7 %collective-permute-start.22 = (bf16[256,768]{1,0:T(8,128)(2,1)}, bf16[256,768]{1,0:T(8,128)(2,1)S(1)}, u32[]{:S(2)}, u32[]{:S(2)}) collective-permute-start(bf16[256,768]{1,0:T(8,128)(2,1)} %add_convert_fusion.14), channel_id=1, source_target_pairs={{0,2},{1,3},{2,0},{3,1},{4,6},{5,7},{6,4},{7,5},{8,10},{9,11},{10,... | collective-permute-start | bytes 1179656 | tf_op jit(solution)/shard_map/ppermute | solution.py:34
  1334.4 5.8 collective-permute-start.16
  1353.8 3.3 collective-permute-start.23
  1356.7 7.8 collective-permute-start.19
  1357.1 3.7 collective-permute-start.24
  1365.2 21.4 %collective-permute-start.20 = (bf16[256,1792]{1,0:T(8,128)(2,1)S(1)}, bf16[256,1792]{1,0:T(8,128)(2,1)S(1)}, u32[]{:S(2)}, u32[]{:S(2)}) collective-permute-start(bf16[256,1792]{1,0:T(8,128)(2,1)S(1)} %fusion.26), channel_id=1, source_target_pairs={{0,2},{1,3},{2,0},{3,1},{4,6},{5,7},{6,4},{7,5},{8,10},{9,11},{10,... | collective-permute-start | bytes 2752520 | tf_op jit(solution)/shard_map/ppermute | solution.py:34
  1367.1 20.4 %copy-start.29 = (bf16[256,6144]{1,0:T(8,128)(2,1)}, bf16[256,6144]{1,0:T(8,128)(2,1)S(1)}, u32[]{:S(2)}) copy-start(bf16[256,6144]{1,0:T(8,128)(2,1)S(1)} %pad_maximum_fusion.1) | copy-start | bytes 9437188
  1368.5 61.8 %collective-permute-start.37 = (bf16[128,6144]{1,0:T(8,128)(2,1)}, bf16[128,6144]{1,0:T(8,128)(2,1)}, u32[]{:S(2)}, u32[]{:S(2)}) collective-permute-start(bf16[128,6144]{1,0:T(8,128)(2,1)} %constant_dynamic-slice_fusion), channel_id=1, source_target_pairs={{0,4},{1,5},{2,6},{3,7},{4,0},{5,1},{6,2},{7,3},{8,12},{9,13},{10,... | collective-permute-start | bytes 4718600 | tf_op jit(solution)/shard_map/ppermute | solution.py:34
  1389.6 38.2 %collective-permute-start.25 = (bf16[128,2688]{1,0:T(8,128)(2,1)}, bf16[128,2688]{1,0:T(8,128)(2,1)}, u32[]{:S(2)}, u32[]{:S(2)}) collective-permute-start(bf16[128,2688]{1,0:T(8,128)(2,1)} %constant_dynamic-slice_fusion.10), channel_id=1, source_target_pairs={{0,4},{1,5},{2,6},{3,7},{4,0},{5,1},{6,2},{7,3},{8,12},{9,13},{10,... | collective-permute-start | bytes 2064392 | tf_op jit(solution)/shard_map/ppermute | solution.py:34
  1401.9 71.6 %collective-permute-start.32 = (bf16[128,3584]{1,0:T(8,128)(2,1)}, bf16[128,3584]{1,0:T(8,128)(2,1)}, u32[]{:S(2)}, u32[]{:S(2)}) collective-permute-start(bf16[128,3584]{1,0:T(8,128)(2,1)} %all-reduce.26.cloned.1.call-done), channel_id=1, source_target_pairs={{0,4},{1,5},{2,6},{3,7},{4,0},{5,1},{6,2},{7,3},{8,12},{9,13},{10,... | collective-permute-start | bytes 2752520 | tf_op jit(solution)/shard_map/ppermute | solution.py:34
  1430.1 113.3 %all-reduce.28.cloned.1.call-start = ((), (), s32[]{:S(2)}) async-start(), calls=%async_computation.4 | async-start | bytes 3145728 | tf_op jit(solution)/shard_map/psum | solution.py:160
  1472.0 72.9 %collective-permute-start.26 = (bf16[128,2688]{1,0:T(8,128)(2,1)}, bf16[128,2688]{1,0:T(8,128)(2,1)S(1)}, u32[]{:S(2)}, u32[]{:S(2)}) collective-permute-start(bf16[128,2688]{1,0:T(8,128)(2,1)} %all-reduce.24.cloned.1.call-done), channel_id=1, source_target_pairs={{0,4},{1,5},{2,6},{3,7},{4,0},{5,1},{6,2},{7,3},{8,12},{9,13},{10,... | collective-permute-start | bytes 2064392 | tf_op jit(solution)/shard_map/ppermute | solution.py:34
  1478.2 66.7 %copy-start.67 = (bf16[128,2688]{1,0:T(8,128)(2,1)S(1)}, bf16[128,2688]{1,0:T(8,128)(2,1)}, u32[]{:S(2)}) copy-start(bf16[128,2688]{1,0:T(8,128)(2,1)} %all-reduce.24.cloned.1.call-done) | copy-start | bytes 2064388
  1543.4 35.3 %collective-permute-start.38 = (bf16[128,6144]{1,0:T(8,128)(2,1)}, bf16[128,6144]{1,0:T(8,128)(2,1)}, u32[]{:S(2)}, u32[]{:S(2)}) collective-permute-start(bf16[128,6144]{1,0:T(8,128)(2,1)} %all-reduce.28.cloned.1.call-done), channel_id=1, source_target_pairs={{0,4},{1,5},{2,6},{3,7},{4,0},{5,1},{6,2},{7,3},{8,12},{9,13},{10,... | collective-permute-start | bytes 4718600 | tf_op jit(solution)/shard_map/ppermute | solution.py:34
  1551.2 27.6 %copy-start.54 = (bf16[128,6144]{1,0:T(8,128)(2,1)S(1)}, bf16[128,6144]{1,0:T(8,128)(2,1)}, u32[]{:S(2)}) copy-start(bf16[128,6144]{1,0:T(8,128)(2,1)} %all-reduce.28.cloned.1.call-done) | copy-start | bytes 4718596
  (145 other events, 883.0 us)
Sparse Core Ops, SparseCore 0:
  332.7 50.8 all-gather.6
  386.4 59.1 all-gather.8
  1153.7 78.2 reduce-scatter.1
  1234.1 68.7 all-gather.10
  1305.1 47.2 all-reduce.25
  1430.2 41.7 all-reduce.23
  1475.1 68.3 all-reduce.27

commit v3 on v2

--- a/solution.py
+++ b/solution.py
@@ -22,6 +22,7 @@
 mask_fill_value = -1e30
 highest = lax.Precision.HIGHEST
 MESH_AXES = ("ctx", "wshard")
+small_cost = pl.CostEstimate(flops=1024, bytes_accessed=1024, transcendentals=0)
 
 
 def exchange(block, ctx_flip, shard_flip):
@@ -45,80 +46,115 @@
     return lax.ppermute(block, "ctx", [(i, count - 1 - i) for i in range(count)])
 
 
-def assemble_body(routes, at_ref, *refs):
-    pieces, wholes, semaphores = refs[: len(routes)], refs[len(routes) : -1], refs[-1]
-    copies = []
-    for piece, route in zip(pieces, routes):
-        for target, source, size in route:
-            start = pl.multiple_of(at_ref[len(copies)], 16)
-            copy = pltpu.make_async_copy(
-                piece.at[pl.ds(source, size), :],
-                wholes[target].at[pl.ds(start, size), :],
-                semaphores.at[len(copies)],
-            )
-            copy.start()
-            copies.append(copy)
-    for copy in copies:
-        copy.wait()
-
-
-def assemble(pieces, sizes):
-    routes, starts = [], []
-    for piece, places in pieces:
-        route, source = [], 0
-        for target, start, size in places:
-            route.append((target, source, size))
-            starts.append(start)
-            source += size
-        routes.append(route)
-    columns, kind = pieces[0][0].shape[1], pieces[0][0].dtype
+def tie_body(*refs):
+    pass
+
+
+def tie(value, *after):
     anywhere = pl.BlockSpec(memory_space=pl.ANY)
     return pl.pallas_call(
-        partial(assemble_body, routes),
-        in_specs=[pl.BlockSpec(memory_space=pltpu.SMEM)] + [anywhere] * len(pieces),
-        out_specs=[anywhere] * len(sizes),
-        out_shape=[jax.ShapeDtypeStruct((size, columns), kind) for size in sizes],
-        scratch_shapes=[pltpu.SemaphoreType.DMA((len(starts),))],
-        cost_estimate=pl.CostEstimate(
-            flops=0, bytes_accessed=4 * columns * sum(sizes), transcendentals=0
+        tie_body,
+        in_specs=[anywhere] * (1 + len(after)),
+        out_specs=anywhere,
+        out_shape=jax.ShapeDtypeStruct(value.shape, value.dtype),
+        input_output_aliases={0: 0},
+        cost_estimate=pl.CostEstimate(flops=0, bytes_accessed=0, transcendentals=0),
+        name="tie",
+    )(value, *after)
+
+
+def assemble_body(spans, target_ref, *refs):
+    out_ref = refs[len(spans)]
+    step = pl.program_id(0)
+    for piece, (first, size) in zip(refs, spans):
+
+        def put(piece=piece):
+            out_ref[...] = piece[...]
+
+        pl.when((step >= first) & (step < first + size))(put)
+
+
+def assemble(pieces, rows):
+    spans, offsets, targets = [], [], []
+    for _, source, start, size in pieces:
+        spans.append((len(targets), size // rows))
+        offsets.append(source // rows)
+        targets += [start // rows + at for at in range(size // rows)]
+    columns, kind = pieces[0][0].shape[1], pieces[0][0].dtype
+
+    def source_map(offset, first, size):
+        return lambda i, target: (offset + jnp.clip(i - first, 0, size - 1), 0)
+
+    return pl.pallas_call(
+        partial(assemble_body, spans),
+        grid_spec=pltpu.PrefetchScalarGridSpec(
+            num_scalar_prefetch=1,
+            grid=(len(targets),),
+            in_specs=[
+                pl.BlockSpec((rows, columns), source_map(offset, first, size))
+                for offset, (first, size) in zip(offsets, spans)
+            ],
+            out_specs=pl.BlockSpec((rows, columns), lambda i, target: (target[i], 0)),
         ),
+        out_shape=jax.ShapeDtypeStruct((rows * len(targets), columns), kind),
+        compiler_params=pltpu.CompilerParams(
+            dimension_semantics=("arbitrary",), vmem_limit_bytes=32 * 1024 * 1024
+        ),
+        cost_estimate=small_cost,
         name="assemble",
-    )(jnp.stack([jnp.asarray(start, jnp.int32) for start in starts]), *[p for p, _ in pieces])
-
-
-def gather_first(shard):
-    rows = shard.shape[0]
-    relayed = rows * 5 // 256 * 16
+    )(jnp.stack([jnp.asarray(target, jnp.int32) for target in targets]), *[p[0] for p in pieces])
+
+
+def gather_first(shard, rows):
+    part = rows // 4
     w = lax.axis_index("wshard")
     side = lax.axis_index("ctx") % 2
-    across = exchange(lax.dynamic_slice_in_dim(shard, side * relayed, relayed, 0), 0, 2)
-    across_direct = exchange(shard[2 * relayed :], 0, 2)
+    direct = shard[2 * part :]
+    across = exchange(lax.dynamic_slice_in_dim(shard, side * part, part, 0), 0, 2)
+    across_direct = exchange(direct, 0, 2)
     beside = exchange(shard, 0, 1)
     across_relayed = exchange(across, 1, 0)
-    parts = [
-        (across, side * relayed, relayed),
-        (across_direct, 2 * relayed, rows - 2 * relayed),
-        (across_relayed, (1 - side) * relayed, relayed),
-    ]
-    pieces = [(shard, [(0, w * rows, rows)]), (beside, [(0, (w ^ 1) * rows, rows)])]
-    for part, start, size in parts:
-        pieces.append((part, [(0, (w ^ 2) * rows + start, size)]))
-        pieces.append((exchange(part, 0, 1), [(0, (w ^ 3) * rows + start, size)]))
-    return assemble(pieces, [4 * rows])[0], across_direct
-
-
-def gather_shards(stacked, sizes, after):
+    far, far_direct, far_relayed = (
+        exchange(piece, 0, 1) for piece in (across, across_direct, across_relayed)
+    )
+    pieces = [(shard, 0, w * rows, rows), (beside, 0, (w ^ 1) * rows, rows)]
+    for flip, early, late, rest in (
+        (2, across, across_relayed, across_direct),
+        (3, far, far_relayed, far_direct),
+    ):
+        start = (w ^ flip) * rows
+        pieces.append((early, 0, start + side * part, part))
+        pieces.append((late, 0, start + (1 - side) * part, part))
+        pieces.append((rest, 0, start + 2 * part, 2 * part))
+    tails = [shard[rows], beside[rows], across_direct[2 * part], far_direct[2 * part]]
+    small = jnp.zeros((4, shard.shape[1]), shard.dtype)
+    for flip, tail in enumerate(tails):
+        small = lax.dynamic_update_slice_in_dim(small, tail[None], w ^ flip, 0)
+    return assemble(pieces, part), small, across_direct
+
+
+def start_shards(stacked, after):
     stacked, _ = lax.optimization_barrier((stacked, after))
+    return stacked, exchange(stacked, 0, 1), exchange(stacked, 0, 2)
+
+
+def finish_shards(pieces, sizes, after, rows):
+    own, beside, across = pieces
+    far = exchange(tie(across, after), 0, 1)
     w = lax.axis_index("wshard")
-    across = exchange(stacked, 0, 2)
-    parts = [(stacked, 0), (exchange(stacked, 0, 1), 1), (across, 2), (exchange(across, 0, 1), 3)]
-    return assemble(
-        [
-            (part, [(at, (w ^ flip) * size, size) for at, size in enumerate(sizes)])
-            for part, flip in parts
-        ],
-        [4 * size for size in sizes],
-    )
+    wholes, source = [], 0
+    for size in sizes:
+        wholes.append(
+            assemble(
+                [
+                    (part, source, (w ^ flip) * size, size)
+                    for flip, part in enumerate((own, beside, across, far))
+                ],
+                rows,
+            )
+        )
+        source += size
+    return wholes
 
 
 def add_low(first, *others):
@@ -148,21 +184,32 @@
     return blocks
 
 
-def ctx_sum(blocks, rows, turn_at):
+def ctx_half(blocks, rows):
     side = lax.axis_index("ctx") % 2
-    count = lax.axis_size("ctx")
     whole = lay_side_by_side(blocks, rows)
     half = rows // 2
     got = exchange(lax.dynamic_slice_in_dim(whole, (1 - side) * half, half, 0), 1, 0)
-    mine = add_low(lax.dynamic_slice_in_dim(whole, side * half, half, 0), got)
-    lines = [list(range(start, count, 2)) for start in range(2)]
-    lines = [lines, lines[::-1], [line[::-1] for line in lines]][turn_at]
+    return add_low(lax.dynamic_slice_in_dim(whole, side * half, half, 0), got), got
+
+
+def ctx_lines():
+    count = lax.axis_size("ctx")
+    return [list(range(start, count, 2)) for start in range(2)]
+
+
+def ctx_finish(mine, shapes, turn_at):
+    side = lax.axis_index("ctx") % 2
+    lines = ctx_lines()
+    if turn_at % 2:
+        lines = lines[::-1]
+    if turn_at // 2:
+        lines = [line[::-1] for line in lines]
     mine = lax.psum(mine, "ctx", axis_index_groups=lines)
     got = exchange(mine, 1, 0)
     whole = jnp.where(
         side == 0, jnp.concatenate([mine, got], axis=0), jnp.concatenate([got, mine], axis=0)
     ).astype(jnp.float32)
-    return take_apart(whole, [block.shape for block in blocks])
+    return take_apart(whole, shapes)
 
 
 def shard_pieces(array, axis):
@@ -179,7 +226,7 @@
     rows = own.shape[0]
     got = exchange(beside.astype(jnp.bfloat16), 0, 1)
     got_across = exchange(add_low(across, got[rows:]), 0, 2)
-    return add_low(own, got[:rows], got_across)
+    return add_low(own, got[:rows], got_across), got, got_across
 
 
 def split_products(left, right, axis=1):
@@ -266,8 +313,9 @@
 
 
 def attend_forward_body(
-    width, blocks, pair_ref, side_ref, query_ref, query_side_ref, heads_ref, log_ref, query_x, peak, total
+    width, blocks, pair_ref, side_ref, query_ref, query_side_ref, *refs
 ):
+    heads_ref, log_ref, query_x, peak, total = refs[-5:]
     step = pl.program_id(1)
 
     @pl.when(step == 0)
@@ -314,12 +362,9 @@
     query_side_ref,
     grad_ref,
     grad_side_ref,
-    query_grad_ref,
-    pair_grad_ref,
-    query_x,
-    grad_x,
-    pair_acc,
+    *refs,
 ):
+    query_grad_ref, pair_grad_ref, query_x, grad_x, pair_acc = refs[-5:]
     step = pl.program_id(1)
 
     @pl.when(step == 0)
@@ -354,7 +399,7 @@
     pair_grad_ref[0, 0] = pair_acc[...].astype(jnp.bfloat16)
 
 
-def attention_calls(rows, count):
+def attention_calls(rows, count, anchors):
     width = rows // 2
     span = width * (QUERY_HEADS // KEY_VALUE_HEADS)
 
@@ -369,7 +414,7 @@
     def per_group(height):
         return pl.BlockSpec((2, 1, height, span), lambda g, k, blocks: (0, g, 0, 0))
 
-    elements = KEY_VALUE_HEADS * (count + 1) * rows * span
+    anywhere = pl.BlockSpec(memory_space=pl.ANY)
     params = pltpu.CompilerParams(
         dimension_semantics=("arbitrary", "arbitrary"), vmem_limit_bytes=48 * 1024 * 1024
     )
@@ -378,7 +423,8 @@
         grid_spec=pltpu.PrefetchScalarGridSpec(
             num_scalar_prefetch=1,
             grid=(KEY_VALUE_HEADS, count),
-            in_specs=[pair_spec, side_spec, per_group(HEAD_SIZE), per_group(16)],
+            in_specs=[pair_spec, side_spec, per_group(HEAD_SIZE), per_group(16)]
+            + [anywhere] * anchors[0],
             out_specs=[per_group(HEAD_SIZE), per_group(1)],
             scratch_shapes=[
                 pltpu.VMEM((2, 256, span), jnp.bfloat16),
@@ -391,9 +437,7 @@
             jax.ShapeDtypeStruct((2, KEY_VALUE_HEADS, 1, span), jnp.float32),
         ],
         compiler_params=params,
-        cost_estimate=pl.CostEstimate(
-            flops=elements * 512, bytes_accessed=8 * rows * 1024 * count, transcendentals=elements
-        ),
+        cost_estimate=small_cost,
         name="attend_forward",
     )
     backward = pl.pallas_call(
@@ -408,7 +452,8 @@
                 per_group(16),
                 per_group(HEAD_SIZE),
                 per_group(16),
-            ],
+            ]
+            + [anywhere] * anchors[1],
             out_specs=[
                 per_group(HEAD_SIZE),
                 pl.BlockSpec((1, 1, rows, 128), lambda g, k, blocks: (k, g, 0, 0)),
@@ -424,9 +469,7 @@
             jax.ShapeDtypeStruct((count, KEY_VALUE_HEADS, rows, 128), jnp.bfloat16),
         ],
         compiler_params=params,
-        cost_estimate=pl.CostEstimate(
-            flops=elements * 1280, bytes_accessed=8 * rows * 1024 * count, transcendentals=elements
-        ),
+        cost_estimate=small_cost,
         name="attend_backward",
     )
     return forward, backward
@@ -437,7 +480,8 @@
     return jnp.where(lane < PM, pair[:, 0:1], pair[:, 1:2])
 
 
-def outer_body(rows_ref, left_ref, right_ref, out_ref):
+def outer_body(rows_ref, left_ref, right_ref, *refs):
+    out_ref = refs[-1]
     for at in range(rows_ref.shape[0]):
         scale = pick(rows_ref[at])
         left = left_ref[:, at * 128 : (at + 1) * 128].astype(jnp.float32) * scale
@@ -449,8 +493,16 @@
         ).astype(out_ref.dtype)
 
 
+def join_body(c_ref, entry_ref, state_ref, local_ref, *refs):
+    out_ref = refs[-1]
+    for at in range(entry_ref.shape[0]):
+        here = slice(at * 2 * PM, (at + 1) * 2 * PM)
+        inner = nt_dot(c_ref[...], state_ref[here, :])
+        out_ref[:, here] = local_ref[:, here] + inner * pick(entry_ref[at])
+
+
 def mixed_body(
-    skip_ref, x_ref, b_ref, c_ref, column_ref, row_ref, entry_ref, docs_column, docs_row, state_ref, out_ref, fill, products
+    skip_ref, x_ref, b_ref, c_ref, column_ref, row_ref, docs_column, docs_row, out_ref, fill, products
 ):
     rows = x_ref.shape[0]
     half = rows // 2
@@ -477,10 +529,7 @@
             weights = (products[here, :width] * decay).astype(jnp.bfloat16)
             parts.append(mixed_dot(weights, x[:width]))
         local = jnp.where(lane < PM, parts[0], parts[1])
-        inner = nt_dot(c_ref[here, :], state_ref[...].astype(jnp.bfloat16))
-        out_ref[here, :] = (
-            local + inner * pick(entry_ref[0, here, :]) + x[here].astype(jnp.float32) * skip_ref[0]
-        )
+        out_ref[here, :] = local + x[here].astype(jnp.float32) * skip_ref[0]
 
 
 def mixed_grad_body(
@@ -497,14 +546,9 @@
     state_ref,
     state_grad_ref,
     grad_ref,
-    out_ref,
-    skip_grad_ref,
-    fill,
-    products,
-    scores,
-    b_grad,
-    c_grad,
+    *refs,
 ):
+    out_ref, skip_grad_ref, fill, products, scores, b_grad, c_grad = refs[-7:]
     rows = x_ref.shape[0]
     half = rows // 2
     step = pl.program_id(0)
@@ -530,11 +574,11 @@
         lane = lax.broadcasted_iota(jnp.int32, (half, 2 * PM), 1)
         lane_all = lax.broadcasted_iota(jnp.int32, (rows, 2 * PM), 1)
         skip_grad_ref[0] = jnp.sum(grad * x_f, axis=0, keepdims=True)
-        state_grad = state_grad_ref[...].astype(jnp.bfloat16)
+        state_grad = state_grad_ref[...]
         tail = pick(tail_ref[0])
         b_grad[...] += mixed_dot((x_f * tail).astype(jnp.bfloat16), state_grad)
         entered = (low.astype(jnp.float32) * pick(entry_ref[0])).astype(jnp.bfloat16)
-        c_grad[...] += mixed_dot(entered, state_ref[...].astype(jnp.bfloat16))
+        c_grad[...] += mixed_dot(entered, state_ref[...])
         passed = nt_dot(b_ref[...], state_grad) * tail + grad * skip_ref[0]
         chosen = [
             jnp.where((lane_all < PM) == (head == 0), x_f, 0.0).astype(jnp.bfloat16)
@@ -568,7 +612,7 @@
         )
 
 
-def mixer_calls(rows):
+def mixer_calls(rows, anchors):
     pairs = HM // 2
     wide = 2 * PM
     params = pltpu.CompilerParams(
@@ -578,7 +622,29 @@
     def capped(p):
         return jnp.minimum(p, pairs - 1)
 
-    def outer(right_at):
+    anywhere = pl.BlockSpec(memory_space=pl.ANY)
+
+    def join(after):
+        each = 4
+        wide_spec = pl.BlockSpec((rows, each * wide), lambda p: (0, p))
+        return pl.pallas_call(
+            join_body,
+            grid=(pairs // each,),
+            in_specs=[
+                pl.BlockSpec((rows, NS), lambda p: (0, DSSM // NS + 1)),
+                pl.BlockSpec((each, rows, 2), lambda p: (p, 0, 0)),
+                pl.BlockSpec((each * wide, NS), lambda p: (p, 0)),
+                wide_spec,
+            ]
+            + [anywhere] * after,
+            out_specs=wide_spec,
+            out_shape=jax.ShapeDtypeStruct((rows, DSSM), jnp.float32),
+            compiler_params=params,
+            cost_estimate=small_cost,
+            name="mixer_join",
+        )
+
+    def outer(right_at, after):
         each = 2
         return pl.pallas_call(
             outer_body,
@@ -587,13 +653,12 @@
                 pl.BlockSpec((each, rows, 2), lambda p: (p, 0, 0)),
                 pl.BlockSpec((rows, each * wide), lambda p: (0, p)),
                 pl.BlockSpec((rows, NS), lambda p: (0, right_at)),
-            ],
+            ]
+            + [anywhere] * after,
             out_specs=pl.BlockSpec((each * wide, NS), lambda p: (p, 0)),
             out_shape=jax.ShapeDtypeStruct((DSSM, NS), jnp.bfloat16),
             compiler_params=params,
-            cost_estimate=pl.CostEstimate(
-                flops=2 * rows * DSSM * NS, bytes_accessed=6 * rows * DSSM, transcendentals=0
-            ),
+            cost_estimate=small_cost,
             name="state_outer",
         )
 
@@ -610,16 +675,12 @@
     forward = pl.pallas_call(
         mixed_body,
         grid=(pairs,),
-        in_specs=[skip_spec, x_spec, b_spec, c_spec, column_spec, row_spec, column_spec]
-        + docs_specs
-        + [state_spec],
+        in_specs=[skip_spec, x_spec, b_spec, c_spec, column_spec, row_spec] + docs_specs,
         out_specs=pl.BlockSpec((rows, wide), lambda p: (0, p)),
         out_shape=jax.ShapeDtypeStruct((rows, DSSM), jnp.float32),
         scratch_shapes=[square, square],
         compiler_params=params,
-        cost_estimate=pl.CostEstimate(
-            flops=4 * rows * rows * DSSM, bytes_accessed=8 * rows * DSSM, transcendentals=HM * rows * rows
-        ),
+        cost_estimate=small_cost,
         name="mixer_forward",
     )
     backward = pl.pallas_call(
@@ -627,7 +688,8 @@
         grid=(pairs + 2,),
         in_specs=[skip_spec, x_spec, b_spec, c_spec, column_spec, row_spec, column_spec, column_spec]
         + docs_specs
-        + [state_spec, state_spec, x_spec],
+        + [state_spec, state_spec, x_spec]
+        + [anywhere] * anchors,
         out_specs=[
             pl.BlockSpec((rows, wide), lambda p: (0, p)),
             pl.BlockSpec((1, 1, wide), lambda p: (capped(p), 0, 0)),
@@ -638,24 +700,64 @@
         ],
         scratch_shapes=[square, square, square, narrow, narrow],
         compiler_params=params,
-        cost_estimate=pl.CostEstimate(
-            flops=8 * rows * rows * DSSM, bytes_accessed=12 * rows * DSSM, transcendentals=HM * rows * rows
-        ),
+        cost_estimate=small_cost,
         name="mixer_backward",
     )
-    return outer, forward, backward
-
-
-def chain(parts, gains, reverse):
+    return outer, join, forward, backward
+
+
+def pass_state(part, gains, reverse, after=()):
     count, position = lax.axis_size("ctx"), lax.axis_index("ctx")
+    side, line_at = position % 2, position // 2
+    half = DSSM // 2
+    heads = HM // 2
+    mine = lax.dynamic_slice_in_dim(part, side * half, half, 0)
+    sent = lax.dynamic_slice_in_dim(part, (1 - side) * half, half, 0)
+    if gains is None:
+        rows = jnp.pad(jnp.stack(split_three(reverse[1])), ((0, 13), (0, NS - HM)))
+        got = exchange(jnp.concatenate([sent, rows], axis=0), 1, 0)
+        other = jnp.sum(got[half : half + 3, :HM].astype(jnp.float32), axis=0)
+        own = reverse[1]
+        got, reverse = got[:half], False
+        pair_gain = own * other
+    else:
+        own, other, line_gains = gains
+        got = exchange(sent, 1, 0)
+    is_first = (side == 1) if reverse else (side == 0)
+
+    def mine_of(gain):
+        chosen = lax.dynamic_slice_in_dim(gain, side * heads, heads, gain.ndim - 1)
+        return jnp.repeat(chosen, PM, axis=-1)[..., None]
+
+    own_f, got_f = mine.astype(jnp.float32), got.astype(jnp.float32)
+    first = jnp.where(is_first, own_f, got_f)
+    second = jnp.where(is_first, got_f, own_f)
+    first_gain = jnp.where(is_first, own, other)
+    second_gain = jnp.where(is_first, other, own)
+    total = (mine_of(second_gain) * first + second).astype(jnp.bfloat16)
+    if gains is None:
+        rows = jnp.pad(jnp.stack(split_three(pair_gain)), ((0, 13), (0, NS - HM)))
+        total = jnp.concatenate([total, rows], axis=0)
+    totals = lax.all_gather(total, "ctx", axis_index_groups=ctx_lines())
+    if gains is None:
+        line_gains = jnp.sum(totals[:, half : half + 3, :HM].astype(jnp.float32), axis=1)
+        totals = totals[:, :half]
     factor = jnp.ones((HM,), jnp.float32)
-    total = jnp.zeros((HM, PM, NS), jnp.float32)
-    for at in range(count) if reverse else reversed(range(count)):
-        reached = at > position if reverse else at < position
-        part = parts[at].reshape(HM, PM, NS).astype(jnp.float32)
-        total = total + jnp.where(reached, factor, 0.0)[:, None, None] * part
-        factor = factor * jnp.where(reached, gains[at], 1.0)
-    return total.reshape(DSSM, NS)
+    entering = jnp.zeros((half, NS), jnp.float32)
+    lines = range(count // 2)
+    for at in lines if reverse else reversed(lines):
+        reached = at > line_at if reverse else at < line_at
+        weight = mine_of(jnp.where(reached, factor, 0.0))
+        entering = entering + weight * totals[at].astype(jnp.float32)
+        factor = factor * jnp.where(reached, line_gains[at], 1.0)
+    later = mine_of(first_gain) * entering + first
+    kept = jnp.where(is_first, entering, later).astype(jnp.bfloat16)
+    passed = jnp.where(is_first, later, entering).astype(jnp.bfloat16)
+    back = exchange(passed, 1, 0)
+    state = jnp.where(
+        side == 0, jnp.concatenate([kept, back], axis=0), jnp.concatenate([back, kept], axis=0)
+    )
+    return state, (own, other, line_gains)
 
 
 def pack_small(norm, conv_weight, conv_bias, skip, mixer, ffn, shards):
@@ -719,28 +821,25 @@
     sequence_total = rows * count
     heads_per_group = QUERY_HEADS // KEY_VALUE_HEADS
     scale = HEAD_SIZE ** (-0.5)
-    attend_forward, attend_backward = attention_calls(rows, count)
-    state_outer, mixer_forward, mixer_backward = mixer_calls(rows)
-
-    small = lax.all_gather(
-        pack_small(norm_gain, conv_weight, conv_bias, skip_gain, mixer_gain, ffn_gain, 1),
-        "wshard",
-        tiled=True,
+    attend_forward, attend_backward = attention_calls(rows, count, (2, 2))
+    state_outer, mixer_join, mixer_forward, mixer_backward = mixer_calls(rows, 4)
+
+    packed = pack_small(norm_gain, conv_weight, conv_bias, skip_gain, mixer_gain, ffn_gain, 1)
+    first_shard = jnp.concatenate([in_proj, query_proj, key_value_projection], axis=1)
+    packed = jnp.pad(packed.reshape(1, -1), ((0, 15), (0, first_shard.shape[1] - 4096)))
+    first_w, small, arrived = gather_first(
+        jnp.concatenate([first_shard, packed], axis=0), in_proj.shape[0]
     )
     norm_w, conv_w, conv_b, skip_w, mixer_g, ffn_g = (
-        part.astype(jnp.float32) for part in unpack_small(small, model, channels, HM, shards)
-    )
-    first_w, arrived = gather_first(
-        jnp.concatenate([in_proj, query_proj, key_value_projection], axis=1)
+        part.astype(jnp.float32)
+        for part in unpack_small(small[:, :4096], model, channels, HM, shards)
     )
     projected_width = in_proj.shape[1]
     in_w, attn_pair_w = first_w[:, :projected_width], first_w[:, projected_width:]
-    mixer_w, attn_w, down_w = gather_shards(
-        jnp.concatenate([mixer_out, attn_out, down_proj], axis=0),
-        [mixer_out.shape[0], attn_out.shape[0], down_proj.shape[0]],
-        arrived,
-    )
-    (gate_up_w,) = gather_shards(gate_up, [gate_up.shape[0]], arrived)
+    out_pieces = start_shards(
+        jnp.concatenate([mixer_out, attn_out, down_proj], axis=0), arrived
+    )
+    gate_up_pieces = start_shards(gate_up, arrived)
     query_w = attn_pair_w[:, : QUERY_HEADS * HEAD_SIZE]
     keyval_w = attn_pair_w[:, QUERY_HEADS * HEAD_SIZE :]
 
@@ -842,28 +941,33 @@
     running_columns, entry_columns, tail_columns = columns(running), columns(entry), columns(tail)
     skip_wide = jnp.repeat(skip_w, PM).reshape(HM // 2, 1, 2 * PM)
     docs_column, docs_row = docs[:, None], docs[None, :]
-    fresh = state_outer(DSSM // NS)(tail_columns, conv_b16, conv_b16)
-    gain_rows = jnp.pad(jnp.stack(split_three(carry_gain)), ((0, 13), (0, NS - HM)))
-    collected = lax.all_gather(jnp.concatenate([fresh, gain_rows], axis=0), "ctx")
-    gains = jnp.sum(collected[:, DSSM : DSSM + 3, :HM].astype(jnp.float32), axis=1)
-    state_in = chain(collected[:, :DSSM], gains, False)
+    fresh = state_outer(DSSM // NS, 0)(tail_columns, conv_b16, conv_b16)
+    state_in, gains = pass_state(fresh, None, (False, carry_gain))
 
     doc_side = side_rows(doc_rows, None)
-    heads_x, log_x = attend_forward(group_blocks, pairs, key_side, query_x, doc_side)
+    heads_x, log_x = attend_forward(
+        group_blocks, pairs, key_side, query_x, doc_side, out_pieces[1], gate_up_pieces[1]
+    )
+    mixer_w, attn_w, down_w = finish_shards(
+        out_pieces,
+        [mixer_out.shape[0], attn_out.shape[0], down_proj.shape[0]],
+        log_x,
+        attn_out.shape[0],
+    )
+    (gate_up_w,) = finish_shards(gate_up_pieces, [gate_up.shape[0]], log_x, gate_up.shape[0] // 2)
     heads_t = from_groups(balance(heads_x.astype(jnp.bfloat16)))
 
-    mixed = mixer_forward(
+    local = mixer_forward(
         skip_wide,
         conv_b16,
         conv_b16,
         conv_b16,
         running_columns,
         running_rows,
-        entry_columns,
         docs_column,
         docs_row,
-        state_in,
-    )
+    )
+    mixed = mixer_join(0)(conv_b16, entry_columns, state_in, local)
     gated, gate_pull = jax.vjp(gate_norm, mixed, gate_z, mixer_g)
     gated_b = gated.astype(jnp.bfloat16)
     mamba = mixed_dot(gated_b, mixer_w)
@@ -879,12 +983,12 @@
     layer_out = (middle + mixed_dot(activated_b, down_w)).astype(jnp.bfloat16)
 
     out_low = cotangent[0]
-    down_sum = weight_grad(activated_b, out_low)
+    down_sum, down_beside, down_across = weight_grad(activated_b, out_low)
+    down_half, down_got = ctx_half([down_sum], model // shards)
     (gate_up_grad_v,) = act_pull(nt_dot(out_low, down_w))
     gate_up_low = gate_up_grad_v.astype(jnp.bfloat16)
-    gate_up_share, down_share = ctx_sum(
-        [weight_grad(normed2_b, gate_up_low), down_sum], model // shards, 0
-    )
+    gate_up_sum, gate_up_beside, gate_up_across = weight_grad(normed2_b, gate_up_low)
+    gate_up_half, gate_up_got = ctx_half([gate_up_sum], model // shards)
     middle_norm_grad, ffn_gain_grad = ffn_pull(nt_dot(gate_up_low, gate_up_w))
     middle_grad = out_low.astype(jnp.float32) + middle_norm_grad
     middle_low = middle_grad.astype(jnp.bfloat16)
@@ -892,8 +996,10 @@
     grad_x = balance(to_groups(heads_low))
     gated_grad = nt_dot(middle_low, mixer_w)
     mixed_grad, gate_z_grad, mixer_gain_grad = gate_pull(gated_grad)
-    upward = state_outer(DSSM // NS + 1)(entry_columns, mixed_grad.astype(jnp.bfloat16), conv_b16)
-    state_out_grad = chain(lax.all_gather(upward, "ctx"), gains, True)
+    upward = state_outer(DSSM // NS + 1, 2)(
+        entry_columns, mixed_grad.astype(jnp.bfloat16), conv_b16, down_beside, gate_up_beside
+    )
+    state_out_grad, _ = pass_state(upward, gains, True)
     gate_z_low = gate_z_grad.astype(jnp.bfloat16)
     mixer_products = split_products(gated_b, middle_low)
     attn_products = split_products(heads_t, middle_low, 0)
@@ -909,14 +1015,11 @@
             axis=0,
         ).astype(jnp.bfloat16)
 
-    mixer_attn_sum = shard_sum(
+    mixer_attn_sum, mixer_beside, mixer_across = shard_sum(
         *[interleaved(parts) for parts in zip(mixer_products, attn_products)]
     )
-    mixer_attn_share, in_share_z = ctx_sum(
-        [mixer_attn_sum, weight_grad(normed_b, gate_z_low)], model // shards, 1
-    )
-    mixer_share = mixer_attn_share[: mixer_out.shape[0]]
-    attn_share = mixer_attn_share[mixer_out.shape[0] :]
+    in_sum_z, in_z_beside, in_z_across = weight_grad(normed_b, gate_z_low)
+    mixer_half, mixer_got = ctx_half([mixer_attn_sum, in_sum_z], model // shards)
 
     delta = jnp.sum(grad_x.astype(jnp.float32) * heads_x, axis=2, keepdims=True)
     query_grad_x, pairs_grad = attend_backward(
@@ -927,6 +1030,8 @@
         side_rows(doc_rows, log_x),
         grad_x,
         side_rows(jnp.zeros_like(doc_rows), delta),
+        down_across,
+        mixer_beside,
     )
     pair_grad = (
         lax.psum_scatter(pairs_grad, "ctx", scatter_dimension=0)
@@ -958,13 +1063,17 @@
         state_in,
         state_out_grad,
         mixed_grad,
+        gate_up_across,
+        in_z_beside,
+        down_got,
+        mixer_across,
     )
     skip_grad = jnp.sum(skip_parts.reshape(HM, PM), axis=1)
     extended_grad, conv_weight_grad, conv_bias_grad = conv_pull(conv_grad)
     from_above = from_behind(extended_grad[: KW - 1], "ctx", -1)
     pre_grad = extended_grad[KW - 1 :] + jnp.pad(from_above, ((rows - (KW - 1), 0), (0, 0)))
-    pre_low = pre_grad.astype(jnp.bfloat16)
-    in_sum_pre = weight_grad(normed_b, pre_low)
+    pre_low = tie(pre_grad.astype(jnp.bfloat16), gate_up_got, in_z_across)
+    in_sum_pre, _, _ = weight_grad(normed_b, pre_low)
     projected_low = jnp.concatenate([gate_z_low, pre_low], axis=1)
     normed_grad = nt_dot(projected_low, in_w)
 
@@ -977,7 +1086,7 @@
         axis=0,
     ).astype(jnp.bfloat16)
     attn_pair_low = jnp.concatenate([query_low, keyval_low], axis=0).T
-    attn_pair_sum = weight_grad(normed_b, attn_pair_low)
+    attn_pair_sum, _, _ = weight_grad(normed_b, attn_pair_low)
     normed_grad = normed_grad + nt_dot(attn_pair_low, attn_pair_w)
     source_grad, norm_grad = norm_pull(normed_grad)
     tokens_grad = (middle_grad + source_grad)[None]
@@ -985,8 +1094,19 @@
     small_grad = pack_small(
         norm_grad, conv_weight_grad, conv_bias_grad, skip_grad, mixer_gain_grad, ffn_gain_grad, shards
     )
-    in_share_pre, attn_pair_share, small_share = ctx_sum(
-        [in_sum_pre, attn_pair_sum, shard_sum(*shard_pieces(small_grad, 0))], model // shards, 2
+    small_sum, _, _ = shard_sum(*shard_pieces(small_grad, 0))
+    last_half, _ = ctx_half([in_sum_pre, attn_pair_sum, small_sum], model // shards)
+    (down_share,) = ctx_finish(down_half, [down_sum.shape], 0)
+    (gate_up_share,) = ctx_finish(gate_up_half, [gate_up_sum.shape], 1)
+    mixer_attn_share, in_share_z = ctx_finish(
+        tie(mixer_half, gate_up_half), [mixer_attn_sum.shape, in_sum_z.shape], 2
+    )
+    mixer_share = mixer_attn_share[: mixer_out.shape[0]]
+    attn_share = mixer_attn_share[mixer_out.shape[0] :]
+    in_share_pre, attn_pair_share, small_share = ctx_finish(
+        tie(last_half, mixer_half),
+        [in_sum_pre.shape, attn_pair_sum.shape, small_sum.shape],
+        3,
     )
     norm_share, conv_w_share, conv_b_share, skip_share, mixer_g_share, ffn_share = unpack_small(
         small_share, model, channels, HM, 1

time: 1600 us -> 907 us (0.57)
  Pallas kernels: 860 us -> 128 us
  local copies, waits for them, and re-layouts: 106 us -> 173 us
  waiting for transfers between devices: 298 us -> 241 us
  other arithmetic: 117 us -> 134 us
  blocking collectives: 25.7 us -> 41.7 us
    pallas_call x6 -> x14, Pallas kernels: 800 us -> 68.6 us  [the longest x5 32.2 us: assemble(): pl.pallas_call(partial(assemble_body, spans), grid_spec=pltpu.PrefetchSca...]
    ppermute x33 -> x39, waiting for transfers between devices: 187 us -> 110 us  [exchange(): return lax.ppermute(block, MESH_AXES, route)]
    psum x3 -> x4, waiting for transfers between devices: 97.1 us -> 123 us  [ctx_finish(): mine = lax.psum(mine, 'ctx', axis_index_groups=lines)]
    unnamed x336 -> x370, local copies, waits for them, and re-layouts: 25.8 us -> 48.5 us
    all_gather x1 -> x2, blocking collectives: 25.7 us -> 41.7 us  [pass_state(): totals = lax.all_gather(total, 'ctx', axis_index_groups=ctx_lines())]
    ppermute x33 -> x39, starting transfers between devices: 43.1 us -> 32.5 us  [exchange(): return lax.ppermute(block, MESH_AXES, route)]
  transfers between devices with their start and end apart: 46 -> 51, of which waited for: 17 -> 16; matrix products, arithmetic and copies ran while one was open for 16% -> 36% of each run, Pallas kernels for 37% -> 13%
where the time goes in v3:
time: 907 us; the launch traced here: 894 us
  waiting for transfers between devices  241 us (27%)
  local copies, waits for them, and re-layouts  173 us (19%)
  other arithmetic  134 us (15%)
  Pallas kernels  128 us (14%)
  matrix products  109 us (12%)
  starting transfers between devices  48.2 us (5%)
  blocking collectives  41.7 us (5%)
  between operations  19 us (2%)
    psum x4, waiting for transfers between devices, ctx_finish(): mine = lax.psum(mine, 'ctx', axis_index_groups=lines)  123 us
    ppermute x39, waiting for transfers between devices, exchange(): return lax.ppermute(block, MESH_AXES, route)  110 us
    dot_general x21, matrix products, split_products(): lax.dot_general(piece, right, (((1 - axis,), (0,)), ((), ())), preferred_...  48.6 us
    unnamed x370, local copies, waits for them, and re-layouts  48.5 us
    all_gather x2, blocking collectives, pass_state(): totals = lax.all_gather(total, 'ctx', axis_index_groups=ctx_lines())  41.7 us
    dot_general x6, matrix products, nt_dot(): lax.dot_general(left, right, (((1,), (1,)), ((), ())), preferred_element_...  34.1 us
    ppermute x39, starting transfers between devices, exchange(): return lax.ppermute(block, MESH_AXES, route)  32.5 us
    pallas_call x5, Pallas kernels, assemble(): pl.pallas_call(partial(assemble_body, spans), grid_spec=pltpu.PrefetchSca...  32.2 us
  transfers between devices with their start and end apart: 51, of which 16 were waited for; matrix products, arithmetic and copies ran while one was open for 36% of the time, Pallas kernels for 13%

profile of v3, /device:TPU:0, one launch (start us, length us, event | category | flops | bytes accessed | tf_op | source)
XLA Modules:
  0.0 893.6 jit_solution(3219049546850013640)
XLA Ops:
  15.6 2.5 collective-permute-start.3
  37.0 2.9 pad_maximum_fusion.1.refs_0_
  49.3 7.0 collective-permute-done.1.refs_2_
  63.7 6.7 collective-permute-done.2.refs_3_
  80.6 2.9 copy.146
  84.9 2.9 copy.147
  87.8 2.9 copy.149.column_ref
  111.9 8.4 assemble.5
  121.1 6.2 fusion.231
  139.3 3.4 collective-permute-start.13
  145.7 4.4 multiply_convert_fusion.1
  150.1 4.2 state_outer.2
  169.1 10.5 %mixer_forward.1.local_ref = f32[512,1536]{1,0:T(8,128)S(1)} custom-call(f32[12,1,128]{2,1,0:T(1,128)S(1)} %broadcast_in_dim.218.skip_ref, bf16[512,1792]{1,0:T(8,128)(2,1)S(1)} %get-tuple-element.69.left_ref.right_ref.x_ref.b_ref.c_ref, bf16[512,1792]{1,0:T(8,128)(2,1)S(1)} %get-tuple-element.69.left_ref.right_ref.x_ref.b_ref.c_ref, ...), custom_call_target="tpu_custom_call" | custom-call | flops 1024 | bytes 1024 | tf_op jit(solution)/shard_map/mixer_forward/pallas_call | solution.py:960
  181.3 4.2 collective-permute-start.7
  191.3 21.4 %all-gather.1 = bf16[3136,128]{1,0:T(8,128)(2,1)S(1)} all-gather(bf16[784,128]{1,0:T(8,128)(2,1)S(1)} %pad_maximum_fusion.14), channel_id=3, replica_groups={{0,8,16,24},{4,12,20,28},{1,9,17,25},{5,13,21,29},{2,10,18,26},{6,14,22..., dimensions={0}, use_global_device_ids=true | all-gather | bytes 1003520 | tf_op jit(solution)/shard_map/all_gather | solution.py:741
  249.3 4.9 mixer_join.1
  255.9 3.1 copy.175.refs_0_
  261.7 21.2 %attend_forward.1 = (f32[2,2,64,1024]{3,2,1,0:T(8,128)S(1)}, f32[2,2,1,1024]{3,2,1,0:T(1,128)S(1)}) custom-call(s32[2]{0:T(128)S(1)} %copy-done.33, bf16[8,2,512,128]{3,2,1,0:T(8,128)(2,1)S(1)} %bitcast.319, bf16[4096,128]{1,0:T(8,128)(2,1)S(1)} %fusion.42.side_ref, bf16[2,2,64,1024]{3,2,1,0:T(8,128)(2,1)S(1)} %copy-done.7, ...), custom_call_target="tpu_custom_call" | custom-call | flops 1024 | bytes 1024 | tf_op jit(solution)/shard_map/attend_forward/pallas_call | solution.py:948
  284.4 3.9 multiply_reduce_fusion.6
  291.0 3.2 copy.176.refs_0_
  299.4 7.6 collective-permute-done.10
  313.6 6.2 assemble.7
  327.1 6.6 assemble.8
  333.8 6.9 fusion.233
  340.7 9.0 %assemble.9 = bf16[2048,1024]{1,0:T(8,128)(2,1)S(1)} custom-call(s32[16]{0:T(128)S(1)} %copy-done.35, bf16[1024,1024]{1,0:T(8,128)(2,1)} %pad_maximum_fusion.1.refs_0_, bf16[1024,1024]{1,0:T(8,128)(2,1)} %collective-permute-done.8.refs_0_.refs_1_, bf16[1024,1024]{1,0:T(8,128)(2,1)} %collective-permute-done.11.refs_2_, ...), custom_call_target="tpu_custom_call" | custom-call | flops 1024 | bytes 1024 | tf_op jit(solution)/shard_map/assemble/pallas_call | solution.py:88
  349.8 10.0 %bitcast_multiply_fusion.1 = (f32[512,2048]{1,0:T(8,128)}, f32[512,2048]{1,0:T(8,128)}, bf16[512,2048]{1,0:T(8,128)(2,1)}) fusion(f32[512,4096]{1,0:T(8,128)} %fusion.233, bf16[2048,1024]{1,0:T(8,128)(2,1)S(1)} %assemble.9, bf16[1,512,1024]{2,1,0:T(8,128)(2,1)S(1)} %copy-done.73), kind=kOutput, calls=%fused_computation.15 | convolution fusion | flops 2162163712 | bytes 24117248 | tf_op jit(solution)/shard_map/dot_general | solution.py:299
  359.8 6.2 add_convert_fusion
  365.9 7.8 multiply_reduce_fusion.7
  378.0 3.7 multiply_reduce_fusion.4
  391.1 3.9 convolution_convert_fusion.3
  400.9 5.6 fusion.213
  410.0 4.4 convolution_convert_fusion
  431.9 2.6 add_convert_fusion.5
  435.7 12.1 %collective-permute-done.30.refs_2_ = bf16[256,1536]{1,0:T(8,128)(2,1)S(1)} collective-permute-done((bf16[256,1536]{1,0:T(8,128)(2,1)S(1)}, bf16[256,1536]{1,0:T(8,128)(2,1)S(1)}, u32[]{:S(2)}, u32[]{:S(2)}) %collective-permute-start.30) | collective-permute-done | bytes 786464 | tf_op jit(solution)/shard_map/ppermute | solution.py:35
  447.8 3.0 add_convert_fusion.10
  450.7 19.5 %collective-permute-done.24.refs_0_ = bf16[512,1024]{1,0:T(8,128)(2,1)S(1)} collective-permute-done((bf16[512,1024]{1,0:T(8,128)(2,1)S(1)}, bf16[512,1024]{1,0:T(8,128)(2,1)S(1)}, u32[]{:S(2)}, u32[]{:S(2)}) %collective-permute-start.24) | collective-permute-done | bytes 1048608 | tf_op jit(solution)/shard_map/ppermute | solution.py:35
  470.2 31.4 %attend_backward.1 = (f32[2,2,64,1024]{3,2,1,0:T(8,128)S(1)}, bf16[8,2,512,128]{3,2,1,0:T(8,128)(2,1)}) custom-call(s32[2]{0:T(128)S(1)} %copy-done.33, bf16[8,2,512,128]{3,2,1,0:T(8,128)(2,1)} %bitcast.318, bf16[4096,128]{1,0:T(8,128)(2,1)S(1)} %fusion.42.side_ref, bf16[2,2,64,1024]{3,2,1,0:T(8,128)(2,1)S(1)} %copy-done.8, ...), custom_call_target="tpu_custom_call" | custom-call | flops 1024 | bytes 1024 | tf_op jit(solution)/shard_map/attend_backward/pallas_call | solution.py:1025
  506.1 4.0 collective-permute-start.32
  512.5 2.5 add_convert_fusion.6
  520.1 2.6 copy-done.40
  522.8 4.3 add_convert_fusion.2
  528.6 6.1 state_outer.3
  544.6 20.2 %all-gather.2 = bf16[3072,128]{1,0:T(8,128)(2,1)S(1)} all-gather(bf16[768,128]{1,0:T(8,128)(2,1)S(1)} %fusion.92), channel_id=4, replica_groups={{0,8,16,24},{4,12,20,28},{1,9,17,25},{5,13,21,29},{2,10,18,26},{6,14,22..., dimensions={0}, use_global_device_ids=true | all-gather | bytes 983040 | tf_op jit(solution)/shard_map/all_gather | solution.py:741
  570.5 5.3 collective-permute-done.21
  577.8 17.4 %mixer_backward.1 = (f32[512,1792]{1,0:T(8,128)}, f32[12,1,128]{2,1,0:T(1,128)S(1)}) custom-call(f32[12,1,128]{2,1,0:T(1,128)S(1)} %broadcast_in_dim.218.skip_ref, bf16[512,1792]{1,0:T(8,128)(2,1)S(1)} %get-tuple-element.69.left_ref.right_ref.x_ref.b_ref.c_ref, bf16[512,1792]{1,0:T(8,128)(2,1)S(1)} %get-tuple-element.69.left_ref.right_ref.x_ref.b_ref.c_ref, ...), custom_call_target="tpu_custom_call" | custom-call | flops 1024 | bytes 1024 | tf_op jit(solution)/shard_map/mixer_backward/pallas_call | solution.py:1052
  595.3 5.5 multiply_reduce_fusion.3
  604.5 3.9 add_convert_fusion.1
  611.9 2.9 pad_add_fusion
  616.6 3.6 fusion.10.refs_0_
  621.5 9.3 %collective-permute-done.29.refs_1_ = bf16[128,4096]{1,0:T(8,128)(2,1)S(1)} collective-permute-done((bf16[128,4096]{1,0:T(8,128)(2,1)}, bf16[128,4096]{1,0:T(8,128)(2,1)S(1)}, u32[]{:S(2)}, u32[]{:S(2)}) %collective-permute-start.29) | collective-permute-done | bytes 1048608 | tf_op jit(solution)/shard_map/ppermute | solution.py:35
  631.8 3.9 convolution_convert_fusion.2
  639.2 2.8 fusion.44
  642.0 8.3 fusion.31
  658.5 25.6 %collective-permute-done.38 = bf16[32,128]{1,0:T(8,128)(2,1)S(1)} collective-permute-done((bf16[32,128]{1,0:T(8,128)(2,1)S(1)}, bf16[32,128]{1,0:T(8,128)(2,1)S(1)}, u32[]{:S(2)}, u32[]{:S(2)}) %collective-permute-start.38) | collective-permute-done | bytes 8224 | tf_op jit(solution)/shard_map/ppermute | solution.py:35
  693.7 13.4 %collective-permute-done.39 = bf16[128,2688]{1,0:T(8,128)(2,1)} collective-permute-done((bf16[128,2688]{1,0:T(8,128)(2,1)}, bf16[128,2688]{1,0:T(8,128)(2,1)}, u32[]{:S(2)}, u32[]{:S(2)}) %collective-permute-start.39) | collective-permute-done | bytes 688160 | tf_op jit(solution)/shard_map/ppermute | solution.py:35
  713.6 6.2 fusion.54
  719.8 2.8 fusion.62
  725.8 27.1 %all-reduce.27.cloned.1.call-done = bf16[128,2688]{1,0:T(8,128)(2,1)} async-done(((bf16[128,2688]{1,0:T(8,128)(2,1)}), bf16[128,2688]{1,0:T(8,128)(2,1)}) %all-reduce.27.cloned.1.call-update) | async-done | bytes 688144 | tf_op jit(solution)/shard_map/psum | solution.py:207
  754.4 4.8 fusion.39
  759.2 43.6 %all-reduce.29.cloned.1.call-done = bf16[128,3584]{1,0:T(8,128)(2,1)} async-done(((bf16[128,3584]{1,0:T(8,128)(2,1)}), bf16[128,3584]{1,0:T(8,128)(2,1)}) %all-reduce.29.cloned.1.call-update) | async-done | bytes 917520 | tf_op jit(solution)/shard_map/psum | solution.py:207
  804.3 52.5 %all-reduce.31.cloned.1.call-done = bf16[128,4096]{1,0:T(8,128)(2,1)} async-done(((bf16[128,4096]{1,0:T(8,128)(2,1)}), bf16[128,4096]{1,0:T(8,128)(2,1)}) %all-reduce.31.cloned.1.call-update) | async-done | bytes 1048592 | tf_op jit(solution)/shard_map/psum | solution.py:207
  865.9 2.6 fusion.43
  875.0 7.2 collective-permute-done.43
  882.2 4.1 fusion.40
  (758 shorter events, 308.2 us)
Async XLA Ops:
  7.2 251.8 %all-gather.5.cloned.1.call-start = ((), (), s32[]{:S(2)}) async-start(), calls=%async_computation.6 | async-start | bytes 2359296 | tf_op jit(solution)/shard_map/all_gather | solution.py:867
  14.0 85.7 %collective-permute-start = (bf16[272,4096]{1,0:T(8,128)(2,1)S(1)}, bf16[272,4096]{1,0:T(8,128)(2,1)}, u32[]{:S(2)}, u32[]{:S(2)}) collective-permute-start(bf16[272,4096]{1,0:T(8,128)(2,1)S(1)} %fusion.29.refs_0_), channel_id=1, source_target_pairs={{0,1},{1,0},{2,3},{3,2},{4,5},{5,4},{6,7},{7,6},{8,9},{9,8},{10,11... | collective-permute-start | bytes 6684680 | tf_op jit(solution)/shard_map/ppermute | solution.py:35
  15.6 29.7 %collective-permute-start.3 = (bf16[144,4096]{1,0:T(8,128)(2,1)}, bf16[144,4096]{1,0:T(8,128)(2,1)}, u32[]{:S(2)}, u32[]{:S(2)}) collective-permute-start(bf16[144,4096]{1,0:T(8,128)(2,1)} %slice.496), channel_id=1, source_target_pairs={{0,2},{1,3},{2,0},{3,1},{4,6},{5,7},{6,4},{7,5},{8,10},{9,11},{10,... | collective-permute-start | bytes 3538952 | tf_op jit(solution)/shard_map/ppermute | solution.py:35
  19.0 37.3 %collective-permute-start.1 = (bf16[64,4096]{1,0:T(8,128)(2,1)}, bf16[64,4096]{1,0:T(8,128)(2,1)}, u32[]{:S(2)}, u32[]{:S(2)}) collective-permute-start(bf16[64,4096]{1,0:T(8,128)(2,1)} %constant_dynamic-slice_fusion.21), channel_id=1, source_target_pairs={{0,2},{1,3},{2,0},{3,1},{4,6},{5,7},{6,4},{7,5},{8,10},{9,11},{10,... | collective-permute-start | bytes 1572872 | tf_op jit(solution)/shard_map/ppermute | solution.py:35
  45.3 60.3 %collective-permute-start.6 = (bf16[144,4096]{1,0:T(8,128)(2,1)}, bf16[144,4096]{1,0:T(8,128)(2,1)}, u32[]{:S(2)}, u32[]{:S(2)}) collective-permute-start(bf16[144,4096]{1,0:T(8,128)(2,1)} %collective-permute-done.3.refs_4_), channel_id=1, source_target_pairs={{0,1},{1,0},{2,3},{3,2},{4,5},{5,4},{6,7},{7,6},{8,9},{9,8},{10,11... | collective-permute-start | bytes 3538952 | tf_op jit(solution)/shard_map/ppermute | solution.py:35
  56.3 14.1 %collective-permute-start.2 = (bf16[64,4096]{1,0:T(8,128)(2,1)}, bf16[64,4096]{1,0:T(8,128)(2,1)}, u32[]{:S(2)}, u32[]{:S(2)}) collective-permute-start(bf16[64,4096]{1,0:T(8,128)(2,1)} %collective-permute-done.1.refs_2_), channel_id=1, source_target_pairs={{0,4},{1,5},{2,6},{3,7},{4,0},{5,1},{6,2},{7,3},{8,12},{9,13},{10,... | collective-permute-start | bytes 1572872 | tf_op jit(solution)/shard_map/ppermute | solution.py:35
  63.7 47.7 %collective-permute-start.4 = (bf16[64,4096]{1,0:T(8,128)(2,1)}, bf16[64,4096]{1,0:T(8,128)(2,1)}, u32[]{:S(2)}, u32[]{:S(2)}) collective-permute-start(bf16[64,4096]{1,0:T(8,128)(2,1)} %collective-permute-done.1.refs_2_), channel_id=1, source_target_pairs={{0,1},{1,0},{2,3},{3,2},{4,5},{5,4},{6,7},{7,6},{8,9},{9,8},{10,11... | collective-permute-start | bytes 1572872 | tf_op jit(solution)/shard_map/ppermute | solution.py:35
  70.4 41.6 %collective-permute-start.5 = (bf16[64,4096]{1,0:T(8,128)(2,1)}, bf16[64,4096]{1,0:T(8,128)(2,1)}, u32[]{:S(2)}, u32[]{:S(2)}) collective-permute-start(bf16[64,4096]{1,0:T(8,128)(2,1)} %collective-permute-done.2.refs_3_), channel_id=1, source_target_pairs={{0,1},{1,0},{2,3},{3,2},{4,5},{5,4},{6,7},{7,6},{8,9},{9,8},{10,11... | collective-permute-start | bytes 1572872 | tf_op jit(solution)/shard_map/ppermute | solution.py:35
  97.7 161.3 %collective-permute-start.8 = (bf16[1024,1024]{1,0:T(8,128)(2,1)}, bf16[1024,1024]{1,0:T(8,128)(2,1)}, u32[]{:S(2)}, u32[]{:S(2)}) collective-permute-start(bf16[1024,1024]{1,0:T(8,128)(2,1)} %pad_maximum_fusion.1.refs_0_), channel_id=1, source_target_pairs={{0,1},{1,0},{2,3},{3,2},{4,5},{5,4},{6,7},{7,6},{8,9},{9,8},{10,11... | collective-permute-start | bytes 6291464 | tf_op jit(solution)/shard_map/ppermute | solution.py:35
  99.7 156.2 %collective-permute-start.11 = (bf16[1024,1024]{1,0:T(8,128)(2,1)}, bf16[1024,1024]{1,0:T(8,128)(2,1)}, u32[]{:S(2)}, u32[]{:S(2)}) collective-permute-start(bf16[1024,1024]{1,0:T(8,128)(2,1)} %pad_maximum_fusion.1.refs_0_), channel_id=1, source_target_pairs={{0,2},{1,3},{2,0},{3,1},{4,6},{5,7},{6,4},{7,5},{8,10},{9,11},{10,... | collective-permute-start | bytes 6291464 | tf_op jit(solution)/shard_map/ppermute | solution.py:35
  105.6 153.4 %collective-permute-start.9 = (bf16[256,4096]{1,0:T(8,128)(2,1)}, bf16[256,4096]{1,0:T(8,128)(2,1)}, u32[]{:S(2)}, u32[]{:S(2)}) collective-permute-start(bf16[256,4096]{1,0:T(8,128)(2,1)} %refs_0_), channel_id=1, source_target_pairs={{0,1},{1,0},{2,3},{3,2},{4,5},{5,4},{6,7},{7,6},{8,9},{9,8},{10,11... | collective-permute-start | bytes 6291464 | tf_op jit(solution)/shard_map/ppermute | solution.py:35
  111.4 179.6 %collective-permute-start.16 = (bf16[256,4096]{1,0:T(8,128)(2,1)}, bf16[256,4096]{1,0:T(8,128)(2,1)}, u32[]{:S(2)}, u32[]{:S(2)}) collective-permute-start(bf16[256,4096]{1,0:T(8,128)(2,1)} %refs_0_), channel_id=1, source_target_pairs={{0,2},{1,3},{2,0},{3,1},{4,6},{5,7},{6,4},{7,5},{8,10},{9,11},{10,... | collective-permute-start | bytes 6291464 | tf_op jit(solution)/shard_map/ppermute | solution.py:35
  132.7 487.5 %reduce-scatter.2.cloned.1.call-start = ((), (), s32[]{:S(2)}) async-start(), calls=%async_computation.1 | async-start | bytes 2359296 | tf_op jit(solution)/shard_map/reduce_scatter | solution.py:1037
  139.3 5.7 collective-permute-start.13
  155.1 26.2 %collective-permute-start.14 = (bf16[784,128]{1,0:T(8,128)(2,1)}, bf16[784,128]{1,0:T(8,128)(2,1)}, u32[]{:S(2)}, u32[]{:S(2)}) collective-permute-start(bf16[784,128]{1,0:T(8,128)(2,1)} %pad_maximum_fusion.13), channel_id=1, source_target_pairs={{0,4},{1,5},{2,6},{3,7},{4,0},{5,1},{6,2},{7,3},{8,12},{9,13},{10,... | collective-permute-start | bytes 602120 | tf_op jit(solution)/shard_map/ppermute | solution.py:35
  181.3 57.6 %copy-start.17 = (bf16[1536,128]{1,0:T(8,128)(2,1)S(1)}, bf16[1536,128]{1,0:T(8,128)(2,1)}, u32[]{:S(2)}) copy-start(bf16[1536,128]{1,0:T(8,128)(2,1)} %copy-done.16) | copy-start | bytes 1179652
  181.3 60.1 %collective-permute-start.7 = (bf16[2,64,1024]{2,1,0:T(8,128)(2,1)}, bf16[2,64,1024]{2,1,0:T(8,128)(2,1)}, u32[]{:S(2)}, u32[]{:S(2)}) collective-permute-start(bf16[2,64,1024]{2,1,0:T(8,128)(2,1)} %squeeze.21), channel_id=1, source_target_pairs={{0,28},{4,24},{8,20},{12,16},{16,12},{20,8},{24,4},{28,0},{1,29},{... | collective-permute-start | bytes 786440 | tf_op jit(solution)/shard_map/ppermute | solution.py:46
  241.4 5.9 collective-permute-start.15
  284.4 27.2 %collective-permute-start.12 = (bf16[1024,1024]{1,0:T(8,128)(2,1)}, bf16[1024,1024]{1,0:T(8,128)(2,1)}, u32[]{:S(2)}, u32[]{:S(2)}) collective-permute-start(bf16[1024,1024]{1,0:T(8,128)(2,1)} %tie.5), channel_id=1, source_target_pairs={{0,1},{1,0},{2,3},{3,2},{4,5},{5,4},{6,7},{7,6},{8,9},{9,8},{10,11... | collective-permute-start | bytes 6291464 | tf_op jit(solution)/shard_map/ppermute | solution.py:35
  295.1 11.8 %collective-permute-start.10 = (bf16[2,64,1024]{2,1,0:T(8,128)(2,1)}, bf16[2,64,1024]{2,1,0:T(8,128)(2,1)}, u32[]{:S(2)}, u32[]{:S(2)}) collective-permute-start(bf16[2,64,1024]{2,1,0:T(8,128)(2,1)} %get-tuple-element.122), channel_id=1, source_target_pairs={{0,28},{4,24},{8,20},{12,16},{16,12},{20,8},{24,4},{28,0},{1,29},{... | collective-permute-start | bytes 786440 | tf_op jit(solution)/shard_map/ppermute | solution.py:46
  296.0 29.9 %collective-permute-start.17 = (bf16[256,4096]{1,0:T(8,128)(2,1)}, bf16[256,4096]{1,0:T(8,128)(2,1)}, u32[]{:S(2)}, u32[]{:S(2)}) collective-permute-start(bf16[256,4096]{1,0:T(8,128)(2,1)} %tie.6), channel_id=1, source_target_pairs={{0,1},{1,0},{2,3},{3,2},{4,5},{5,4},{6,7},{7,6},{8,9},{9,8},{10,11... | collective-permute-start | bytes 6291464 | tf_op jit(solution)/shard_map/ppermute | solution.py:35
  324.7 49.1 %copy-start.142 = (f32[512]{0:T(512)}, f32[512]{0:T(512)S(1)}, u32[]{:S(2)}) copy-start(f32[512]{0:T(512)S(1)} %fusion.185) | copy-start | bytes 6148
  326.0 55.7 %copy-start.72 = (bf16[512,1024]{1,0:T(8,128)(2,1)}, bf16[512,1024]{1,0:T(8,128)(2,1)S(1)}, u32[]{:S(2)}) copy-start(bf16[512,1024]{1,0:T(8,128)(2,1)S(1)} %multiply_convert_fusion.3) | copy-start | bytes 3145732
  387.7 35.3 %collective-permute-start.31 = (bf16[2,64,1024]{2,1,0:T(8,128)(2,1)}, bf16[2,64,1024]{2,1,0:T(8,128)(2,1)}, u32[]{:S(2)}, u32[]{:S(2)}) collective-permute-start(bf16[2,64,1024]{2,1,0:T(8,128)(2,1)} %squeeze.26), channel_id=1, source_target_pairs={{0,28},{4,24},{8,20},{12,16},{16,12},{20,8},{24,4},{28,0},{1,29},{... | collective-permute-start | bytes 786440 | tf_op jit(solution)/shard_map/ppermute | solution.py:46
  395.0 33.6 %collective-permute-start.18 = (bf16[1024,1024]{1,0:T(8,128)(2,1)}, bf16[1024,1024]{1,0:T(8,128)(2,1)}, u32[]{:S(2)}, u32[]{:S(2)}) collective-permute-start(bf16[1024,1024]{1,0:T(8,128)(2,1)} %convolution_convert_fusion.3), channel_id=1, source_target_pairs={{0,1},{1,0},{2,3},{3,2},{4,5},{5,4},{6,7},{7,6},{8,9},{9,8},{10,11... | collective-permute-start | bytes 6291464 | tf_op jit(solution)/shard_map/ppermute | solution.py:35
  398.8 33.0 %collective-permute-start.26 = (bf16[1024,1024]{1,0:T(8,128)(2,1)}, bf16[1024,1024]{1,0:T(8,128)(2,1)}, u32[]{:S(2)}, u32[]{:S(2)}) collective-permute-start(bf16[1024,1024]{1,0:T(8,128)(2,1)} %pad_maximum_fusion.2), channel_id=1, source_target_pairs={{0,1},{1,0},{2,3},{3,2},{4,5},{5,4},{6,7},{7,6},{8,9},{9,8},{10,11... | collective-permute-start | bytes 6291464 | tf_op jit(solution)/shard_map/ppermute | solution.py:35
  408.7 16.9 %collective-permute-start.23 = (bf16[512,1536]{1,0:T(8,128)(2,1)}, bf16[512,1536]{1,0:T(8,128)(2,1)}, u32[]{:S(2)}, u32[]{:S(2)}) collective-permute-start(bf16[512,1536]{1,0:T(8,128)(2,1)} %convolution_convert_fusion.1), channel_id=1, source_target_pairs={{0,1},{1,0},{2,3},{3,2},{4,5},{5,4},{6,7},{7,6},{8,9},{9,8},{10,11... | collective-permute-start | bytes 4718600 | tf_op jit(solution)/shard_map/ppermute | solution.py:35
  414.4 105.7 %collective-permute-start.19 = (bf16[512,4096]{1,0:T(8,128)(2,1)}, bf16[512,4096]{1,0:T(8,128)(2,1)}, u32[]{:S(2)}, u32[]{:S(2)}) collective-permute-start(bf16[512,4096]{1,0:T(8,128)(2,1)} %convolution_convert_fusion), channel_id=1, source_target_pairs={{0,1},{1,0},{2,3},{3,2},{4,5},{5,4},{6,7},{7,6},{8,9},{9,8},{10,11... | collective-permute-start | bytes 12582920 | tf_op jit(solution)/shard_map/ppermute | solution.py:35
  427.4 20.4 %collective-permute-start.30 = (bf16[256,1536]{1,0:T(8,128)(2,1)S(1)}, bf16[256,1536]{1,0:T(8,128)(2,1)S(1)}, u32[]{:S(2)}, u32[]{:S(2)}) collective-permute-start(bf16[256,1536]{1,0:T(8,128)(2,1)S(1)} %add_convert_fusion.11), channel_id=1, source_target_pairs={{0,2},{1,3},{2,0},{3,1},{4,6},{5,7},{6,4},{7,5},{8,10},{9,11},{10,... | collective-permute-start | bytes 2359304 | tf_op jit(solution)/shard_map/ppermute | solution.py:35
  430.7 39.5 %collective-permute-start.24 = (bf16[512,1024]{1,0:T(8,128)(2,1)S(1)}, bf16[512,1024]{1,0:T(8,128)(2,1)S(1)}, u32[]{:S(2)}, u32[]{:S(2)}) collective-permute-start(bf16[512,1024]{1,0:T(8,128)(2,1)S(1)} %add_convert_fusion.7), channel_id=1, source_target_pairs={{0,2},{1,3},{2,0},{3,1},{4,6},{5,7},{6,4},{7,5},{8,10},{9,11},{10,... | collective-permute-start | bytes 3145736 | tf_op jit(solution)/shard_map/ppermute | solution.py:35
  434.5 35.7 %copy-start.8 = (bf16[2,2,64,1024]{3,2,1,0:T(8,128)(2,1)S(1)}, bf16[2,2,64,1024]{3,2,1,0:T(8,128)(2,1)}, u32[]{:S(2)}) copy-start(bf16[2,2,64,1024]{3,2,1,0:T(8,128)(2,1)} %pad_maximum_fusion.7.query_ref) | copy-start | bytes 1572868
  434.5 35.7 %copy-start.28 = (bf16[2,2,16,1024]{3,2,1,0:T(8,128)(2,1)S(1)}, bf16[2,2,16,1024]{3,2,1,0:T(8,128)(2,1)}, u32[]{:S(2)}) copy-start(bf16[2,2,16,1024]{3,2,1,0:T(8,128)(2,1)} %pad_maximum_fusion.18.query_side_ref) | copy-start | bytes 393220
  434.5 83.2 %collective-permute-start.27 = (bf16[512,1024]{1,0:T(8,128)(2,1)}, bf16[512,1024]{1,0:T(8,128)(2,1)}, u32[]{:S(2)}, u32[]{:S(2)}) collective-permute-start(bf16[512,1024]{1,0:T(8,128)(2,1)} %add_convert_fusion.5), channel_id=1, source_target_pairs={{0,2},{1,3},{2,0},{3,1},{4,6},{5,7},{6,4},{7,5},{8,10},{9,11},{10,... | collective-permute-start | bytes 3145736 | tf_op jit(solution)/shard_map/ppermute | solution.py:35
  447.8 53.8 %copy-start.98 = (bf16[256,1536]{1,0:T(8,128)(2,1)}, bf16[256,1536]{1,0:T(8,128)(2,1)S(1)}, u32[]{:S(2)}) copy-start(bf16[256,1536]{1,0:T(8,128)(2,1)S(1)} %collective-permute-done.30.refs_2_) | copy-start | bytes 2359300
  470.2 31.4 %copy-start.23 = (bf16[512,1024]{1,0:T(8,128)(2,1)}, bf16[512,1024]{1,0:T(8,128)(2,1)S(1)}, u32[]{:S(2)}) copy-start(bf16[512,1024]{1,0:T(8,128)(2,1)S(1)} %collective-permute-done.24.refs_0_) | copy-start | bytes 3145732
  502.6 190.0 %all-reduce.33.cloned.1.call-start = ((), (), s32[]{:S(2)}) async-start(), calls=%async_computation.5 | async-start | bytes 1048576 | tf_op jit(solution)/shard_map/psum | solution.py:207
  506.1 32.3 %collective-permute-start.32 = (bf16[2,64,1024]{2,1,0:T(8,128)(2,1)}, bf16[2,64,1024]{2,1,0:T(8,128)(2,1)}, u32[]{:S(2)}, u32[]{:S(2)}) collective-permute-start(bf16[2,64,1024]{2,1,0:T(8,128)(2,1)} %get-tuple-element.114), channel_id=1, source_target_pairs={{0,28},{4,24},{8,20},{12,16},{16,12},{20,8},{24,4},{28,0},{1,29},{... | collective-permute-start | bytes 786440 | tf_op jit(solution)/shard_map/ppermute | solution.py:46
  517.0 51.7 %collective-permute-start.25 = (bf16[128,2048]{1,0:T(8,128)(2,1)}, bf16[128,2048]{1,0:T(8,128)(2,1)S(1)}, u32[]{:S(2)}, u32[]{:S(2)}) collective-permute-start(bf16[128,2048]{1,0:T(8,128)(2,1)} %fusion.80), channel_id=1, source_target_pairs={{0,4},{1,5},{2,6},{3,7},{4,0},{5,1},{6,2},{7,3},{8,12},{9,13},{10,... | collective-permute-start | bytes 1572872 | tf_op jit(solution)/shard_map/ppermute | solution.py:35
  527.1 48.8 %collective-permute-start.22 = (bf16[256,4096]{1,0:T(8,128)(2,1)}, bf16[256,4096]{1,0:T(8,128)(2,1)}, u32[]{:S(2)}, u32[]{:S(2)}) collective-permute-start(bf16[256,4096]{1,0:T(8,128)(2,1)} %add_convert_fusion.2), channel_id=1, source_target_pairs={{0,2},{1,3},{2,0},{3,1},{4,6},{5,7},{6,4},{7,5},{8,10},{9,11},{10,... | collective-permute-start | bytes 6291464 | tf_op jit(solution)/shard_map/ppermute | solution.py:35
  535.4 8.1 collective-permute-start.20
  537.7 152.6 %collective-permute-start.40 = (bf16[128,3584]{1,0:T(8,128)(2,1)}, bf16[128,3584]{1,0:T(8,128)(2,1)}, u32[]{:S(2)}, u32[]{:S(2)}) collective-permute-start(bf16[128,3584]{1,0:T(8,128)(2,1)} %constant_dynamic-slice_fusion), channel_id=1, source_target_pairs={{0,4},{1,5},{2,6},{3,7},{4,0},{5,1},{6,2},{7,3},{8,12},{9,13},{10,... | collective-permute-start | bytes 2752520 | tf_op jit(solution)/shard_map/ppermute | solution.py:35
  540.0 24.9 %copy-start.157 = (f32[768]{0:T(1024)S(1)}, f32[768]{0:T(1024)}, u32[]{:S(2)}) copy-start(f32[768]{0:T(1024)} %mul.1065) | copy-start | bytes 9220
  542.2 26.4 %copy-start.69 = (bf16[256,1024]{1,0:T(8,128)(2,1)S(1)}, bf16[256,1024]{1,0:T(8,128)(2,1)}, u32[]{:S(2)}) copy-start(bf16[256,1024]{1,0:T(8,128)(2,1)} %copy-done.68) | copy-start | bytes 1572868
  542.3 26.4 %copy-start.71 = (bf16[256,1024]{1,0:T(8,128)(2,1)S(1)}, bf16[256,1024]{1,0:T(8,128)(2,1)}, u32[]{:S(2)}) copy-start(bf16[256,1024]{1,0:T(8,128)(2,1)} %copy-done.70) | copy-start | bytes 1572868
  567.1 8.7 collective-permute-start.21
  570.4 182.4 %all-reduce.27.cloned.1.call-start = ((), (), s32[]{:S(2)}) async-start(), calls=%async_computation.2 | async-start | bytes 1376256 | tf_op jit(solution)/shard_map/psum | solution.py:207
  602.3 14.4 %collective-permute-start.28 = (f32[3,1792]{1,0:T(4,128)S(1)}, f32[3,1792]{1,0:T(4,128)S(1)}, u32[]{:S(2)}, u32[]{:S(2)}) collective-permute-start(f32[3,1792]{1,0:T(4,128)S(1)} %pad_add_fusion.1), channel_id=1, source_target_pairs={{4,0},{8,4},{12,8},{16,12},{20,16},{24,20},{28,24},{5,1},{9,5},{13... | collective-permute-start | bytes 64520 | tf_op jit(solution)/shard_map/ppermute | solution.py:41
  609.6 21.3 %collective-permute-start.29 = (bf16[128,4096]{1,0:T(8,128)(2,1)}, bf16[128,4096]{1,0:T(8,128)(2,1)S(1)}, u32[]{:S(2)}, u32[]{:S(2)}) collective-permute-start(bf16[128,4096]{1,0:T(8,128)(2,1)} %constant_dynamic-slice_fusion.2), channel_id=1, source_target_pairs={{0,4},{1,5},{2,6},{3,7},{4,0},{5,1},{6,2},{7,3},{8,12},{9,13},{10,... | collective-permute-start | bytes 3145736 | tf_op jit(solution)/shard_map/ppermute | solution.py:35
  635.8 14.9 %collective-permute-start.33 = (bf16[512,1792]{1,0:T(8,128)(2,1)}, bf16[512,1792]{1,0:T(8,128)(2,1)}, u32[]{:S(2)}, u32[]{:S(2)}) collective-permute-start(bf16[512,1792]{1,0:T(8,128)(2,1)} %convolution_convert_fusion.2), channel_id=1, source_target_pairs={{0,1},{1,0},{2,3},{3,2},{4,5},{5,4},{6,7},{7,6},{8,9},{9,8},{10,11... | collective-permute-start | bytes 5505032 | tf_op jit(solution)/shard_map/ppermute | solution.py:35
  638.6 15.7 %collective-permute-start.35 = (bf16[512,768]{1,0:T(8,128)(2,1)}, bf16[512,768]{1,0:T(8,128)(2,1)}, u32[]{:S(2)}, u32[]{:S(2)}) collective-permute-start(bf16[512,768]{1,0:T(8,128)(2,1)} %convolution_convert_fusion.6), channel_id=1, source_target_pairs={{0,1},{1,0},{2,3},{3,2},{4,5},{5,4},{6,7},{7,6},{8,9},{9,8},{10,11... | collective-permute-start | bytes 2359304 | tf_op jit(solution)/shard_map/ppermute | solution.py:35
  650.6 5.9 collective-permute-start.37
  652.7 32.5 %collective-permute-start.34 = (bf16[256,1792]{1,0:T(8,128)(2,1)S(1)}, bf16[256,1792]{1,0:T(8,128)(2,1)S(1)}, u32[]{:S(2)}, u32[]{:S(2)}) collective-permute-start(bf16[256,1792]{1,0:T(8,128)(2,1)S(1)} %fusion.26), channel_id=1, source_target_pairs={{0,2},{1,3},{2,0},{3,1},{4,6},{5,7},{6,4},{7,5},{8,10},{9,11},{10,... | collective-permute-start | bytes 2752520 | tf_op jit(solution)/shard_map/ppermute | solution.py:35
  655.9 28.2 %collective-permute-start.36 = (bf16[256,768]{1,0:T(8,128)(2,1)S(1)}, bf16[256,768]{1,0:T(8,128)(2,1)S(1)}, u32[]{:S(2)}, u32[]{:S(2)}) collective-permute-start(bf16[256,768]{1,0:T(8,128)(2,1)S(1)} %add_convert_fusion.15), channel_id=1, source_target_pairs={{0,2},{1,3},{2,0},{3,1},{4,6},{5,7},{6,4},{7,5},{8,10},{9,11},{10,... | collective-permute-start | bytes 1179656 | tf_op jit(solution)/shard_map/ppermute | solution.py:35
  656.5 27.6 %collective-permute-start.38 = (bf16[32,128]{1,0:T(8,128)(2,1)S(1)}, bf16[32,128]{1,0:T(8,128)(2,1)S(1)}, u32[]{:S(2)}, u32[]{:S(2)}) collective-permute-start(bf16[32,128]{1,0:T(8,128)(2,1)S(1)} %add_convert_fusion.20), channel_id=1, source_target_pairs={{0,2},{1,3},{2,0},{3,1},{4,6},{5,7},{6,4},{7,5},{8,10},{9,11},{10,... | collective-permute-start | bytes 24584 | tf_op jit(solution)/shard_map/ppermute | solution.py:35
  688.5 18.7 %collective-permute-start.39 = (bf16[128,2688]{1,0:T(8,128)(2,1)}, bf16[128,2688]{1,0:T(8,128)(2,1)}, u32[]{:S(2)}, u32[]{:S(2)}) collective-permute-start(bf16[128,2688]{1,0:T(8,128)(2,1)} %constant_dynamic-slice_fusion.1), channel_id=1, source_target_pairs={{0,4},{1,5},{2,6},{3,7},{4,0},{5,1},{6,2},{7,3},{8,12},{9,13},{10,... | collective-permute-start | bytes 2064392 | tf_op jit(solution)/shard_map/ppermute | solution.py:35
  692.6 27.2 %collective-permute-start.44 = (bf16[128,2048]{1,0:T(8,128)(2,1)}, bf16[128,2048]{1,0:T(8,128)(2,1)}, u32[]{:S(2)}, u32[]{:S(2)}) collective-permute-start(bf16[128,2048]{1,0:T(8,128)(2,1)} %all-reduce.33.cloned.1.call-done), channel_id=1, source_target_pairs={{0,4},{1,5},{2,6},{3,7},{4,0},{5,1},{6,2},{7,3},{8,12},{9,13},{10,... | collective-permute-start | bytes 1572872 | tf_op jit(solution)/shard_map/ppermute | solution.py:35
  709.5 93.3 %all-reduce.29.cloned.1.call-start = ((), (), s32[]{:S(2)}) async-start(), calls=%async_computation.3 | async-start | bytes 1835008 | tf_op jit(solution)/shard_map/psum | solution.py:207
  712.0 144.8 %all-reduce.31.cloned.1.call-start = ((), (), s32[]{:S(2)}) async-start(), calls=%async_computation.4 | async-start | bytes 2097152 | tf_op jit(solution)/shard_map/psum | solution.py:207
  724.3 30.0 %copy-start.154 = (f32[512]{0:T(512)S(1)}, f32[512]{0:T(512)}, u32[]{:S(2)}) copy-start(f32[512]{0:T(512)} %copy-done.153) | copy-start | bytes 6148
  724.3 30.0 %copy-start.138 = (f32[1,2,4,128]{3,1,2,0:T(2,128)S(1)}, f32[1,2,4,128]{3,1,2,0:T(2,128)}, u32[]{:S(2)}) copy-start(f32[1,2,4,128]{3,1,2,0:T(2,128)} %copy.165) | copy-start | bytes 12292
  724.3 30.0 %copy-start.143 = (f32[512]{0:T(512)S(1)}, f32[512]{0:T(512)}, u32[]{:S(2)}) copy-start(f32[512]{0:T(512)} %copy-done.142) | copy-start | bytes 6148
  752.9 105.4 %collective-permute-start.41 = (bf16[128,2688]{1,0:T(8,128)(2,1)}, bf16[128,2688]{1,0:T(8,128)(2,1)}, u32[]{:S(2)}, u32[]{:S(2)}) collective-permute-start(bf16[128,2688]{1,0:T(8,128)(2,1)} %all-reduce.27.cloned.1.call-done), channel_id=1, source_target_pairs={{0,4},{1,5},{2,6},{3,7},{4,0},{5,1},{6,2},{7,3},{8,12},{9,13},{10,... | collective-permute-start | bytes 2064392 | tf_op jit(solution)/shard_map/ppermute | solution.py:35
  802.8 63.1 %collective-permute-start.42 = (bf16[128,3584]{1,0:T(8,128)(2,1)}, bf16[128,3584]{1,0:T(8,128)(2,1)}, u32[]{:S(2)}, u32[]{:S(2)}) collective-permute-start(bf16[128,3584]{1,0:T(8,128)(2,1)} %all-reduce.29.cloned.1.call-done), channel_id=1, source_target_pairs={{0,4},{1,5},{2,6},{3,7},{4,0},{5,1},{6,2},{7,3},{8,12},{9,13},{10,... | collective-permute-start | bytes 2752520 | tf_op jit(solution)/shard_map/ppermute | solution.py:35
  856.8 25.4 %collective-permute-start.43 = (bf16[128,4096]{1,0:T(8,128)(2,1)}, bf16[128,4096]{1,0:T(8,128)(2,1)}, u32[]{:S(2)}, u32[]{:S(2)}) collective-permute-start(bf16[128,4096]{1,0:T(8,128)(2,1)} %all-reduce.31.cloned.1.call-done), channel_id=1, source_target_pairs={{0,4},{1,5},{2,6},{3,7},{4,0},{5,1},{6,2},{7,3},{8,12},{9,13},{10,... | collective-permute-start | bytes 3145736 | tf_op jit(solution)/shard_map/ppermute | solution.py:35
  (168 other events, 885.4 us)
Sparse Core Ops, SparseCore 0:
  132.9 50.9 all-gather.4
  502.7 81.1 reduce-scatter.1
  586.3 37.0 all-reduce.32
  709.6 43.2 all-reduce.26
  755.8 46.9 all-reduce.28
  805.7 51.0 all-reduce.30

commit v4 on v3

--- a/solution.py
+++ b/solution.py
@@ -126,10 +126,11 @@
         pieces.append((early, 0, start + side * part, part))
         pieces.append((late, 0, start + (1 - side) * part, part))
         pieces.append((rest, 0, start + 2 * part, 2 * part))
-    tails = [shard[rows], beside[rows], across_direct[2 * part], far_direct[2 * part]]
-    small = jnp.zeros((4, shard.shape[1]), shard.dtype)
-    for flip, tail in enumerate(tails):
-        small = lax.dynamic_update_slice_in_dim(small, tail[None], w ^ flip, 0)
+    tails = [shard[rows:], beside[rows:], across_direct[2 * part :], far_direct[2 * part :]]
+    tails = jnp.concatenate([tail[:1] for tail in tails], axis=0)
+    small = jnp.concatenate(
+        [lax.dynamic_slice_in_dim(tails, w ^ at, 1, 0) for at in range(4)], axis=0
+    )
     return assemble(pieces, part), small, across_direct
 
 
@@ -138,9 +139,9 @@
     return stacked, exchange(stacked, 0, 1), exchange(stacked, 0, 2)
 
 
-def finish_shards(pieces, sizes, after, rows):
+def finish_shards(pieces, sizes, after):
     own, beside, across = pieces
-    far = exchange(tie(across, after), 0, 1)
+    far = exchange(lax.optimization_barrier((across, after))[0], 0, 1)
     w = lax.axis_index("wshard")
     wholes, source = [], 0
     for size in sizes:
@@ -150,7 +151,7 @@
                     (part, source, (w ^ flip) * size, size)
                     for flip, part in enumerate((own, beside, across, far))
                 ],
-                rows,
+                size,
             )
         )
         source += size
@@ -205,11 +206,12 @@
     if turn_at // 2:
         lines = [line[::-1] for line in lines]
     mine = lax.psum(mine, "ctx", axis_index_groups=lines)
+    summed = mine
     got = exchange(mine, 1, 0)
     whole = jnp.where(
         side == 0, jnp.concatenate([mine, got], axis=0), jnp.concatenate([got, mine], axis=0)
     ).astype(jnp.float32)
-    return take_apart(whole, shapes)
+    return take_apart(whole, shapes), summed
 
 
 def shard_pieces(array, axis):
@@ -305,22 +307,28 @@
     return jnp.where(rows <= lax.rem(columns, width) + group * width, scores, mask_fill_value)
 
 
-def load_extended(extended, lower, value_ref, side_ref):
-    for group in range(2):
-        extended[group] = jnp.zeros(extended.shape[1:], extended.dtype)
-        extended[group, lower : lower + HEAD_SIZE, :] = value_ref[group, 0]
-        extended[group, 128:144, :] = side_ref[group, 0]
-
-
-def attend_forward_body(
-    width, blocks, pair_ref, side_ref, query_ref, query_side_ref, *refs
-):
-    heads_ref, log_ref, query_x, peak, total = refs[-5:]
+def load_extended(extended, group, lower, value_ref, side, extra):
+    width = value_ref.shape[2]
+    extended[group] = jnp.zeros(extended.shape[1:], extended.dtype)
+    for head in range(value_ref.shape[0]):
+        here = slice(head * width, (head + 1) * width)
+        extended[group, lower : lower + HEAD_SIZE, here] = value_ref[head]
+    side = jnp.concatenate([side.astype(jnp.float32)] * value_ref.shape[0], axis=1)
+    if extra is not None:
+        row = lax.broadcasted_iota(jnp.int32, side.shape, 0)
+        for at, part in enumerate(split_three(-extra)):
+            side = jnp.where(row == 8 + at, part.astype(jnp.float32), side)
+    extended[group, 128:144, :] = side.astype(extended.dtype)
+
+
+def attend_forward_body(width, blocks, pair_ref, side_ref, query_a, query_b, query_side_ref, *refs):
+    heads_refs, (log_ref, query_x, peak, total) = refs[-6:-4], refs[-4:]
     step = pl.program_id(1)
 
     @pl.when(step == 0)
     def start():
-        load_extended(query_x, 0, query_ref, query_side_ref)
+        for group, query_ref in enumerate((query_a, query_b)):
+            load_extended(query_x, group, 0, query_ref, query_side_ref[group], None)
         peak[...] = jnp.full(peak.shape, mask_fill_value, jnp.float32)
         total[...] = jnp.zeros(total.shape, jnp.float32)
 
@@ -349,7 +357,9 @@
     def finish():
         for group in range(2):
             weight = total[group, HEAD_SIZE + 8 : HEAD_SIZE + 9, :]
-            heads_ref[group, 0] = total[group, :HEAD_SIZE, :] / weight
+            heads = total[group, :HEAD_SIZE, :] / weight
+            for head in range(heads.shape[1] // width):
+                heads_refs[group][head] = heads[:, head * width : (head + 1) * width]
             log_ref[group, 0] = peak[group] + jnp.log(weight)
 
 
@@ -358,20 +368,33 @@
     blocks,
     pair_ref,
     side_ref,
-    query_ref,
+    query_a,
+    query_b,
     query_side_ref,
-    grad_ref,
-    grad_side_ref,
+    log_ref,
+    heads_a,
+    heads_b,
+    grad_a,
+    grad_b,
     *refs,
 ):
-    query_grad_ref, pair_grad_ref, query_x, grad_x, pair_acc = refs[-5:]
+    query_grad_refs, (pair_grad_ref, query_x, grad_x, pair_acc, query_acc) = refs[-7:-5], refs[-5:]
     step = pl.program_id(1)
 
     @pl.when(step == 0)
     def start():
-        load_extended(query_x, 0, query_ref, query_side_ref)
-        load_extended(grad_x, HEAD_SIZE, grad_ref, grad_side_ref)
-        query_grad_ref[...] = jnp.zeros(query_grad_ref.shape, jnp.float32)
+        groups = ((query_a, heads_a, grad_a), (query_b, heads_b, grad_b))
+        for group, (query_ref, heads_ref, grad_ref) in enumerate(groups):
+            load_extended(query_x, group, 0, query_ref, query_side_ref[group], log_ref[group, 0])
+            delta = [
+                jnp.sum(heads_ref[head] * grad_ref[head].astype(jnp.float32), axis=0, keepdims=True)
+                for head in range(heads_ref.shape[0])
+            ]
+            blank = jnp.zeros(query_side_ref.shape[1:], jnp.float32)
+            load_extended(
+                grad_x, group, HEAD_SIZE, grad_ref, blank, jnp.concatenate(delta, axis=1)
+            )
+        query_acc[...] = jnp.zeros(query_acc.shape, jnp.float32)
 
     pair_acc[...] = jnp.zeros(pair_acc.shape, jnp.float32)
 
@@ -390,7 +413,7 @@
             pair_acc[...] += nt_dot(low, query_x[group, :128, :]) + nt_dot(
                 probs.astype(jnp.bfloat16), grad_x[group, :128, :]
             )
-            query_grad_ref[group, 0] += mixed_dot(turned, low)
+            query_acc[group] += mixed_dot(turned, low)
 
         for group in range(2):
             pl.when(step < blocks[group])(partial(tile, group, False))
@@ -398,6 +421,12 @@
 
     pair_grad_ref[0, 0] = pair_acc[...].astype(jnp.bfloat16)
 
+    @pl.when(step == pl.num_programs(1) - 1)
+    def finish():
+        for group in range(2):
+            for head in range(query_acc.shape[2] // width):
+                query_grad_refs[group][head] = query_acc[group, :, head * width : (head + 1) * width]
+
 
 def attention_calls(rows, count, anchors):
     width = rows // 2
@@ -411,8 +440,12 @@
     )
     side_spec = pl.BlockSpec((rows, 128), lambda g, k, blocks: (jnp.minimum(k, last(blocks)), 0))
 
-    def per_group(height):
-        return pl.BlockSpec((2, 1, height, span), lambda g, k, blocks: (0, g, 0, 0))
+    heads_per_group = QUERY_HEADS // KEY_VALUE_HEADS
+    own = pl.BlockSpec((heads_per_group, HEAD_SIZE, width), lambda g, k, blocks: (g, 0, 0))
+    half_spec = own
+    log_spec = pl.BlockSpec((2, 1, 1, span), lambda g, k, blocks: (0, g, 0, 0))
+    query_side_spec = pl.BlockSpec((2, 16, width), lambda g, k, blocks: (0, 0, 0))
+    half_shape = jax.ShapeDtypeStruct((QUERY_HEADS, HEAD_SIZE, width), jnp.float32)
 
     anywhere = pl.BlockSpec(memory_space=pl.ANY)
     params = pltpu.CompilerParams(
@@ -423,9 +456,9 @@
         grid_spec=pltpu.PrefetchScalarGridSpec(
             num_scalar_prefetch=1,
             grid=(KEY_VALUE_HEADS, count),
-            in_specs=[pair_spec, side_spec, per_group(HEAD_SIZE), per_group(16)]
+            in_specs=[pair_spec, side_spec, own, half_spec, query_side_spec]
             + [anywhere] * anchors[0],
-            out_specs=[per_group(HEAD_SIZE), per_group(1)],
+            out_specs=[half_spec, half_spec, log_spec],
             scratch_shapes=[
                 pltpu.VMEM((2, 256, span), jnp.bfloat16),
                 pltpu.VMEM((2, 1, span), jnp.float32),
@@ -433,7 +466,8 @@
             ],
         ),
         out_shape=[
-            jax.ShapeDtypeStruct((2, KEY_VALUE_HEADS, HEAD_SIZE, span), jnp.float32),
+            half_shape,
+            half_shape,
             jax.ShapeDtypeStruct((2, KEY_VALUE_HEADS, 1, span), jnp.float32),
         ],
         compiler_params=params,
@@ -448,24 +482,31 @@
             in_specs=[
                 pair_spec,
                 side_spec,
-                per_group(HEAD_SIZE),
-                per_group(16),
-                per_group(HEAD_SIZE),
-                per_group(16),
+                own,
+                half_spec,
+                query_side_spec,
+                log_spec,
+                half_spec,
+                half_spec,
+                own,
+                half_spec,
             ]
             + [anywhere] * anchors[1],
             out_specs=[
-                per_group(HEAD_SIZE),
+                half_spec,
+                half_spec,
                 pl.BlockSpec((1, 1, rows, 128), lambda g, k, blocks: (k, g, 0, 0)),
             ],
             scratch_shapes=[
                 pltpu.VMEM((2, 256, span), jnp.bfloat16),
                 pltpu.VMEM((2, 256, span), jnp.bfloat16),
                 pltpu.VMEM((rows, 128), jnp.float32),
+                pltpu.VMEM((2, HEAD_SIZE, span), jnp.float32),
             ],
         ),
         out_shape=[
-            jax.ShapeDtypeStruct((2, KEY_VALUE_HEADS, HEAD_SIZE, span), jnp.float32),
+            half_shape,
+            half_shape,
             jax.ShapeDtypeStruct((count, KEY_VALUE_HEADS, rows, 128), jnp.bfloat16),
         ],
         compiler_params=params,
@@ -480,10 +521,10 @@
     return jnp.where(lane < PM, pair[:, 0:1], pair[:, 1:2])
 
 
-def outer_body(rows_ref, left_ref, right_ref, *refs):
+def outer_body(kind, rows_ref, left_ref, right_ref, *refs):
     out_ref = refs[-1]
     for at in range(rows_ref.shape[0]):
-        scale = pick(rows_ref[at])
+        scale = pick(rows_ref[at].T[:, kind : kind + 2])
         left = left_ref[:, at * 128 : (at + 1) * 128].astype(jnp.float32) * scale
         out_ref[at * 128 : (at + 1) * 128, :] = lax.dot_general(
             left.astype(jnp.bfloat16),
@@ -493,16 +534,16 @@
         ).astype(out_ref.dtype)
 
 
-def join_body(c_ref, entry_ref, state_ref, local_ref, *refs):
+def join_body(c_ref, rows_ref, state_ref, local_ref, *refs):
     out_ref = refs[-1]
-    for at in range(entry_ref.shape[0]):
+    for at in range(rows_ref.shape[0]):
         here = slice(at * 2 * PM, (at + 1) * 2 * PM)
         inner = nt_dot(c_ref[...], state_ref[here, :])
-        out_ref[:, here] = local_ref[:, here] + inner * pick(entry_ref[at])
+        out_ref[:, here] = local_ref[:, here] + inner * pick(rows_ref[at].T[:, 2:4])
 
 
 def mixed_body(
-    skip_ref, x_ref, b_ref, c_ref, column_ref, row_ref, docs_column, docs_row, out_ref, fill, products
+    skip_ref, x_ref, b_ref, c_ref, row_ref, docs_column, docs_row, out_ref, fill, products
 ):
     rows = x_ref.shape[0]
     half = rows // 2
@@ -516,6 +557,7 @@
         products[...] = nt_dot(c_ref[...], b_ref[...])
 
     x = x_ref[...]
+    columns = row_ref[0].T
     lane = lax.broadcasted_iota(jnp.int32, (half, 2 * PM), 1)
     for block in range(2):
         here = slice(block * half, (block + 1) * half)
@@ -523,7 +565,7 @@
         parts = []
         for head in range(2):
             decay = jnp.exp(
-                (column_ref[0, here, head : head + 1] - row_ref[0, head : head + 1, :width])
+                (columns[here, head : head + 1] - row_ref[0, head : head + 1, :width])
                 + fill[here, :width]
             )
             weights = (products[here, :width] * decay).astype(jnp.bfloat16)
@@ -537,10 +579,7 @@
     x_ref,
     b_ref,
     c_ref,
-    column_ref,
     row_ref,
-    entry_ref,
-    tail_ref,
     docs_column,
     docs_row,
     state_ref,
@@ -575,9 +614,10 @@
         lane_all = lax.broadcasted_iota(jnp.int32, (rows, 2 * PM), 1)
         skip_grad_ref[0] = jnp.sum(grad * x_f, axis=0, keepdims=True)
         state_grad = state_grad_ref[...]
-        tail = pick(tail_ref[0])
+        columns = row_ref[0].T
+        tail = pick(columns[:, 4:6])
         b_grad[...] += mixed_dot((x_f * tail).astype(jnp.bfloat16), state_grad)
-        entered = (low.astype(jnp.float32) * pick(entry_ref[0])).astype(jnp.bfloat16)
+        entered = (low.astype(jnp.float32) * pick(columns[:, 2:4])).astype(jnp.bfloat16)
         c_grad[...] += mixed_dot(entered, state_ref[...])
         passed = nt_dot(b_ref[...], state_grad) * tail + grad * skip_ref[0]
         chosen = [
@@ -590,7 +630,7 @@
             parts = []
             for head in range(2):
                 decay = jnp.exp(
-                    (row_ref[0, head : head + 1, start_at:] - column_ref[0, here, head : head + 1])
+                    (row_ref[0, head : head + 1, start_at:] - columns[here, head : head + 1])
                     + fill[here, start_at:]
                 )
                 weights = (products[here, start_at:] * decay).astype(jnp.bfloat16)
@@ -632,7 +672,7 @@
             grid=(pairs // each,),
             in_specs=[
                 pl.BlockSpec((rows, NS), lambda p: (0, DSSM // NS + 1)),
-                pl.BlockSpec((each, rows, 2), lambda p: (p, 0, 0)),
+                pl.BlockSpec((each, 8, rows), lambda p: (p, 0, 0)),
                 pl.BlockSpec((each * wide, NS), lambda p: (p, 0)),
                 wide_spec,
             ]
@@ -644,13 +684,13 @@
             name="mixer_join",
         )
 
-    def outer(right_at, after):
+    def outer(right_at, kind, after):
         each = 2
         return pl.pallas_call(
-            outer_body,
+            partial(outer_body, kind),
             grid=(pairs // each,),
             in_specs=[
-                pl.BlockSpec((each, rows, 2), lambda p: (p, 0, 0)),
+                pl.BlockSpec((each, 8, rows), lambda p: (p, 0, 0)),
                 pl.BlockSpec((rows, each * wide), lambda p: (0, p)),
                 pl.BlockSpec((rows, NS), lambda p: (0, right_at)),
             ]
@@ -665,8 +705,7 @@
     x_spec = pl.BlockSpec((rows, wide), lambda p: (0, capped(p)))
     b_spec = pl.BlockSpec((rows, NS), lambda p: (0, DSSM // NS))
     c_spec = pl.BlockSpec((rows, NS), lambda p: (0, DSSM // NS + 1))
-    column_spec = pl.BlockSpec((1, rows, 2), lambda p: (capped(p), 0, 0))
-    row_spec = pl.BlockSpec((1, 2, rows), lambda p: (capped(p), 0, 0))
+    row_spec = pl.BlockSpec((1, 8, rows), lambda p: (capped(p), 0, 0))
     skip_spec = pl.BlockSpec((1, 1, wide), lambda p: (capped(p), 0, 0))
     state_spec = pl.BlockSpec((wide, NS), lambda p: (capped(p), 0))
     docs_specs = [pl.BlockSpec((rows, 1), lambda p: (0, 0)), pl.BlockSpec((1, rows), lambda p: (0, 0))]
@@ -675,7 +714,7 @@
     forward = pl.pallas_call(
         mixed_body,
         grid=(pairs,),
-        in_specs=[skip_spec, x_spec, b_spec, c_spec, column_spec, row_spec] + docs_specs,
+        in_specs=[skip_spec, x_spec, b_spec, c_spec, row_spec] + docs_specs,
         out_specs=pl.BlockSpec((rows, wide), lambda p: (0, p)),
         out_shape=jax.ShapeDtypeStruct((rows, DSSM), jnp.float32),
         scratch_shapes=[square, square],
@@ -686,7 +725,7 @@
     backward = pl.pallas_call(
         mixed_grad_body,
         grid=(pairs + 2,),
-        in_specs=[skip_spec, x_spec, b_spec, c_spec, column_spec, row_spec, column_spec, column_spec]
+        in_specs=[skip_spec, x_spec, b_spec, c_spec, row_spec]
         + docs_specs
         + [state_spec, state_spec, x_spec]
         + [anywhere] * anchors,
@@ -706,58 +745,48 @@
     return outer, join, forward, backward
 
 
-def pass_state(part, gains, reverse, after=()):
+def gain_rows(gain):
+    return jnp.pad(jnp.stack(split_three(gain)), ((0, 13), (0, NS - HM)))
+
+
+def read_gain(rows):
+    return jnp.sum(rows[..., :3, :HM].astype(jnp.float32), axis=-2)
+
+
+def pass_state(part, gain, gains, reverse):
     count, position = lax.axis_size("ctx"), lax.axis_index("ctx")
     side, line_at = position % 2, position // 2
-    half = DSSM // 2
-    heads = HM // 2
-    mine = lax.dynamic_slice_in_dim(part, side * half, half, 0)
-    sent = lax.dynamic_slice_in_dim(part, (1 - side) * half, half, 0)
-    if gains is None:
-        rows = jnp.pad(jnp.stack(split_three(reverse[1])), ((0, 13), (0, NS - HM)))
-        got = exchange(jnp.concatenate([sent, rows], axis=0), 1, 0)
-        other = jnp.sum(got[half : half + 3, :HM].astype(jnp.float32), axis=0)
-        own = reverse[1]
-        got, reverse = got[:half], False
-        pair_gain = own * other
+    is_first = (side == 1) if reverse else (side == 0)
+
+    def by_head(array):
+        return array.reshape(array.shape[:-2] + (HM, PM, NS)).astype(jnp.float32)
+
+    got = exchange(part if gains else jnp.concatenate([part, gain_rows(gain)], axis=0), 1, 0)
+    if gains:
+        gain, other, line_gains = gains
     else:
-        own, other, line_gains = gains
-        got = exchange(sent, 1, 0)
-    is_first = (side == 1) if reverse else (side == 0)
-
-    def mine_of(gain):
-        chosen = lax.dynamic_slice_in_dim(gain, side * heads, heads, gain.ndim - 1)
-        return jnp.repeat(chosen, PM, axis=-1)[..., None]
-
-    own_f, got_f = mine.astype(jnp.float32), got.astype(jnp.float32)
+        other = read_gain(got[DSSM:])
+    own_f, got_f = by_head(part), by_head(got[:DSSM])
     first = jnp.where(is_first, own_f, got_f)
     second = jnp.where(is_first, got_f, own_f)
-    first_gain = jnp.where(is_first, own, other)
-    second_gain = jnp.where(is_first, other, own)
-    total = (mine_of(second_gain) * first + second).astype(jnp.bfloat16)
-    if gains is None:
-        rows = jnp.pad(jnp.stack(split_three(pair_gain)), ((0, 13), (0, NS - HM)))
-        total = jnp.concatenate([total, rows], axis=0)
+    first_gain = jnp.where(is_first, gain, other)[:, None, None]
+    second_gain = jnp.where(is_first, other, gain)[:, None, None]
+    total = (second_gain * first + second).astype(jnp.bfloat16).reshape(DSSM, NS)
+    if not gains:
+        total = jnp.concatenate([total, gain_rows(gain * other)], axis=0)
     totals = lax.all_gather(total, "ctx", axis_index_groups=ctx_lines())
-    if gains is None:
-        line_gains = jnp.sum(totals[:, half : half + 3, :HM].astype(jnp.float32), axis=1)
-        totals = totals[:, :half]
+    if not gains:
+        line_gains = read_gain(totals[:, DSSM:])
+    totals = by_head(totals[:, :DSSM])
     factor = jnp.ones((HM,), jnp.float32)
-    entering = jnp.zeros((half, NS), jnp.float32)
+    entering = jnp.zeros((HM, PM, NS), jnp.float32)
     lines = range(count // 2)
     for at in lines if reverse else reversed(lines):
         reached = at > line_at if reverse else at < line_at
-        weight = mine_of(jnp.where(reached, factor, 0.0))
-        entering = entering + weight * totals[at].astype(jnp.float32)
+        entering = entering + jnp.where(reached, factor, 0.0)[:, None, None] * totals[at]
         factor = factor * jnp.where(reached, line_gains[at], 1.0)
-    later = mine_of(first_gain) * entering + first
-    kept = jnp.where(is_first, entering, later).astype(jnp.bfloat16)
-    passed = jnp.where(is_first, later, entering).astype(jnp.bfloat16)
-    back = exchange(passed, 1, 0)
-    state = jnp.where(
-        side == 0, jnp.concatenate([kept, back], axis=0), jnp.concatenate([back, kept], axis=0)
-    )
-    return state, (own, other, line_gains)
+    state = jnp.where(is_first, entering, first_gain * entering + first)
+    return state.astype(jnp.bfloat16).reshape(DSSM, NS), (gain, other, line_gains)
 
 
 def pack_small(norm, conv_weight, conv_bias, skip, mixer, ffn, shards):
@@ -868,24 +897,8 @@
         jnp.concatenate([keys_b, values_b], axis=1).transpose(0, 2, 1), "ctx"
     )
 
-    def to_groups(array):
-        return (
-            array.reshape(KEY_VALUE_HEADS, heads_per_group, HEAD_SIZE, 2, width)
-            .transpose(3, 0, 2, 1, 4)
-            .reshape(2, KEY_VALUE_HEADS, HEAD_SIZE, heads_per_group * width)
-        )
-
-    def from_groups(array):
-        return (
-            array.reshape(2, KEY_VALUE_HEADS, HEAD_SIZE, heads_per_group, width)
-            .transpose(1, 3, 2, 0, 4)
-            .reshape(QUERY_HEADS * HEAD_SIZE, rows)
-        )
-
-    def balance(array):
-        return jnp.stack([array[0], swap_mirrored(array[1])])
-
-    query_x = balance(to_groups(turned_q) * jnp.asarray(scale, jnp.bfloat16))
+    turned_q = turned_q * jnp.asarray(scale, jnp.bfloat16)
+    mirrored_q = swap_mirrored(turned_q[:, :, width:])
     mirrored = count - 1 - block_at
     group_blocks = jnp.stack([block_at, mirrored]).astype(jnp.int32)
     group_positions = jnp.stack(
@@ -898,20 +911,10 @@
     key_docs = doc_numbers(lengths, jnp.arange(sequence_total, dtype=jnp.int32))
     lane = jnp.arange(128)[None, :]
     key_side = ((key_docs[:, None] == lane) | ((lane >= 8) & (lane < 11))).astype(jnp.bfloat16)
-    doc_rows = jnp.where(
-        jnp.arange(doc_count)[None, :, None] == group_docs[:, None, :], 0.0, mask_fill_value
+    side_row = jnp.arange(16)[None, :, None]
+    query_side = jnp.where(
+        (side_row == group_docs[:, None, :]) | (side_row >= doc_count), 0.0, mask_fill_value
     ).astype(jnp.bfloat16)
-    doc_rows = jnp.tile(doc_rows, (1, 1, heads_per_group))[:, None]
-    doc_rows = jnp.broadcast_to(doc_rows, (2, KEY_VALUE_HEADS) + doc_rows.shape[2:])
-
-    def side_rows(first, extra):
-        first = jnp.pad(first, ((0, 0), (0, 0), (0, 8 - first.shape[2]), (0, 0)))
-        if extra is None:
-            return jnp.pad(first, ((0, 0), (0, 0), (0, 8), (0, 0)))
-        extra = jnp.concatenate(split_three(-extra), axis=2)
-        return jnp.concatenate(
-            [first, jnp.pad(extra, ((0, 0), (0, 0), (0, 5), (0, 0)))], axis=2
-        )
 
     projected = mixed_dot(normed_b, in_w)
     gate_z = projected[:, :DSSM]
@@ -934,40 +937,41 @@
     tail = jnp.where((docs == docs[-1])[None, :], jnp.exp(running[:, -1:] - running), 0.0)
     carry_gain = jnp.where(docs[-1] == doc_prev, jnp.exp(running[:, -1]), 0.0)
 
-    def columns(array):
-        return array.reshape(HM // 2, 2, rows).transpose(0, 2, 1)
-
-    running_rows = running.reshape(HM // 2, 2, rows)
-    running_columns, entry_columns, tail_columns = columns(running), columns(entry), columns(tail)
+    mixer_rows = (
+        jnp.stack([running, entry, tail, jnp.zeros_like(tail)])
+        .reshape(4, HM // 2, 2, rows)
+        .transpose(1, 0, 2, 3)
+        .reshape(HM // 2, 8, rows)
+    )
     skip_wide = jnp.repeat(skip_w, PM).reshape(HM // 2, 1, 2 * PM)
     docs_column, docs_row = docs[:, None], docs[None, :]
-    fresh = state_outer(DSSM // NS, 0)(tail_columns, conv_b16, conv_b16)
-    state_in, gains = pass_state(fresh, None, (False, carry_gain))
-
-    doc_side = side_rows(doc_rows, None)
-    heads_x, log_x = attend_forward(
-        group_blocks, pairs, key_side, query_x, doc_side, out_pieces[1], gate_up_pieces[1]
+    fresh = state_outer(DSSM // NS, 4, 0)(mixer_rows, conv_b16, conv_b16)
+    state_in, gains = pass_state(fresh, carry_gain, None, False)
+    local = mixer_forward(
+        skip_wide, conv_b16, conv_b16, conv_b16, mixer_rows, docs_column, docs_row
+    )
+
+    heads_own, heads_mirrored, log_x = attend_forward(
+        group_blocks,
+        pairs,
+        key_side,
+        turned_q,
+        mirrored_q,
+        query_side,
+        out_pieces[1],
+        gate_up_pieces[1],
     )
     mixer_w, attn_w, down_w = finish_shards(
         out_pieces,
         [mixer_out.shape[0], attn_out.shape[0], down_proj.shape[0]],
         log_x,
-        attn_out.shape[0],
-    )
-    (gate_up_w,) = finish_shards(gate_up_pieces, [gate_up.shape[0]], log_x, gate_up.shape[0] // 2)
-    heads_t = from_groups(balance(heads_x.astype(jnp.bfloat16)))
-
-    local = mixer_forward(
-        skip_wide,
-        conv_b16,
-        conv_b16,
-        conv_b16,
-        running_columns,
-        running_rows,
-        docs_column,
-        docs_row,
-    )
-    mixed = mixer_join(0)(conv_b16, entry_columns, state_in, local)
+    )
+    (gate_up_w,) = finish_shards(gate_up_pieces, [gate_up.shape[0]], log_x)
+    heads_back = swap_mirrored(heads_mirrored.astype(jnp.bfloat16))
+    heads_t = jnp.concatenate([heads_own.astype(jnp.bfloat16), heads_back], axis=2).reshape(
+        QUERY_HEADS * HEAD_SIZE, rows
+    )
+    mixed = mixer_join(0)(conv_b16, mixer_rows, state_in, local)
     gated, gate_pull = jax.vjp(gate_norm, mixed, gate_z, mixer_g)
     gated_b = gated.astype(jnp.bfloat16)
     mamba = mixed_dot(gated_b, mixer_w)
@@ -993,13 +997,14 @@
     middle_grad = out_low.astype(jnp.float32) + middle_norm_grad
     middle_low = middle_grad.astype(jnp.bfloat16)
     heads_low = nt_dot(attn_w, middle_low).astype(jnp.bfloat16)
-    grad_x = balance(to_groups(heads_low))
+    heads_low = heads_low.reshape(QUERY_HEADS, HEAD_SIZE, rows)
+    mirrored_low = swap_mirrored(heads_low[:, :, width:])
     gated_grad = nt_dot(middle_low, mixer_w)
     mixed_grad, gate_z_grad, mixer_gain_grad = gate_pull(gated_grad)
-    upward = state_outer(DSSM // NS + 1, 2)(
-        entry_columns, mixed_grad.astype(jnp.bfloat16), conv_b16, down_beside, gate_up_beside
-    )
-    state_out_grad, _ = pass_state(upward, gains, True)
+    upward = state_outer(DSSM // NS + 1, 2, 1)(
+        mixer_rows, mixed_grad.astype(jnp.bfloat16), conv_b16, down_beside
+    )
+    state_out_grad, _ = pass_state(upward, None, gains, True)
     gate_z_low = gate_z_grad.astype(jnp.bfloat16)
     mixer_products = split_products(gated_b, middle_low)
     attn_products = split_products(heads_t, middle_low, 0)
@@ -1021,43 +1026,40 @@
     in_sum_z, in_z_beside, in_z_across = weight_grad(normed_b, gate_z_low)
     mixer_half, mixer_got = ctx_half([mixer_attn_sum, in_sum_z], model // shards)
 
-    delta = jnp.sum(grad_x.astype(jnp.float32) * heads_x, axis=2, keepdims=True)
-    query_grad_x, pairs_grad = attend_backward(
+    query_grad_own, query_grad_mirrored, pairs_grad = attend_backward(
         group_blocks,
         pairs,
         key_side,
-        query_x,
-        side_rows(doc_rows, log_x),
-        grad_x,
-        side_rows(jnp.zeros_like(doc_rows), delta),
+        turned_q,
+        mirrored_q,
+        query_side,
+        log_x,
+        heads_own,
+        heads_mirrored,
+        heads_low,
+        mirrored_low,
+        gate_up_beside,
         down_across,
-        mixer_beside,
     )
     pair_grad = (
         lax.psum_scatter(pairs_grad, "ctx", scatter_dimension=0)
         .astype(jnp.float32)
         .transpose(0, 2, 1)
     )
-    query_back = jnp.stack(
-        [
-            turn(
-                query_grad_x[at].reshape(KEY_VALUE_HEADS, HEAD_SIZE, heads_per_group * width),
-                -jnp.tile(group_positions[at], heads_per_group),
-            )
-            for at in range(2)
-        ]
-    )
-    query_low = from_groups(balance((query_back * scale).astype(jnp.bfloat16)))
+    query_low_own, query_low_mirrored = (
+        (turn(grad, -group_positions[at]) * scale).astype(jnp.bfloat16)
+        for at, grad in enumerate((query_grad_own, query_grad_mirrored))
+    )
+    query_low = jnp.concatenate(
+        [query_low_own, swap_mirrored(query_low_mirrored)], axis=2
+    ).reshape(QUERY_HEADS * HEAD_SIZE, rows)
 
     conv_grad, skip_parts = mixer_backward(
         skip_wide,
         conv_b16,
         conv_b16,
         conv_b16,
-        running_columns,
-        running_rows,
-        entry_columns,
-        tail_columns,
+        mixer_rows,
         docs_column,
         docs_row,
         state_in,
@@ -1066,13 +1068,13 @@
         gate_up_across,
         in_z_beside,
         down_got,
-        mixer_across,
+        mixer_beside,
     )
     skip_grad = jnp.sum(skip_parts.reshape(HM, PM), axis=1)
     extended_grad, conv_weight_grad, conv_bias_grad = conv_pull(conv_grad)
     from_above = from_behind(extended_grad[: KW - 1], "ctx", -1)
     pre_grad = extended_grad[KW - 1 :] + jnp.pad(from_above, ((rows - (KW - 1), 0), (0, 0)))
-    pre_low = tie(pre_grad.astype(jnp.bfloat16), gate_up_got, in_z_across)
+    pre_low = tie(pre_grad.astype(jnp.bfloat16), gate_up_got, in_z_across, mixer_across)
     in_sum_pre, _, _ = weight_grad(normed_b, pre_low)
     projected_low = jnp.concatenate([gate_z_low, pre_low], axis=1)
     normed_grad = nt_dot(projected_low, in_w)
@@ -1096,15 +1098,15 @@
     )
     small_sum, _, _ = shard_sum(*shard_pieces(small_grad, 0))
     last_half, _ = ctx_half([in_sum_pre, attn_pair_sum, small_sum], model // shards)
-    (down_share,) = ctx_finish(down_half, [down_sum.shape], 0)
-    (gate_up_share,) = ctx_finish(gate_up_half, [gate_up_sum.shape], 1)
-    mixer_attn_share, in_share_z = ctx_finish(
-        tie(mixer_half, gate_up_half), [mixer_attn_sum.shape, in_sum_z.shape], 2
+    (down_share,), summed = ctx_finish(down_half, [down_sum.shape], 0)
+    (gate_up_share,), summed = ctx_finish(tie(gate_up_half, summed), [gate_up_sum.shape], 1)
+    (mixer_attn_share, in_share_z), summed = ctx_finish(
+        tie(mixer_half, summed), [mixer_attn_sum.shape, in_sum_z.shape], 2
     )
     mixer_share = mixer_attn_share[: mixer_out.shape[0]]
     attn_share = mixer_attn_share[mixer_out.shape[0] :]
-    in_share_pre, attn_pair_share, small_share = ctx_finish(
-        tie(last_half, mixer_half),
+    (in_share_pre, attn_pair_share, small_share), _ = ctx_finish(
+        tie(last_half, summed),
         [in_sum_pre.shape, attn_pair_sum.shape, small_sum.shape],
         3,
     )

time: 907 us -> 743 us (0.82)
  local copies, waits for them, and re-layouts: 173 us -> 77.3 us
  blocking collectives: 41.7 us -> 0 us
  Pallas kernels: 128 us -> 117 us
  other arithmetic: 134 us -> 124 us
    all_gather x2 -> x0, blocking collectives: 41.7 us -> none  [pass_state(): totals = lax.all_gather(total, 'ctx', axis_index_groups=ctx_lines())]
    all_gather x1, waiting for transfers between devices: 0.01 us -> 25.4 us  [per_device(): lax.all_gather(jnp.concatenate([keys_b, values_b], axis=1).transpose(0, 2...]
    unnamed x370 -> x332, local copies, waits for them, and re-layouts: 48.5 us -> 24.8 us
    psum x4, waiting for transfers between devices: 123 us -> 101 us  [ctx_finish(): mine = lax.psum(mine, 'ctx', axis_index_groups=lines)]
    reshape x7 -> x1, local copies, waits for them, and re-layouts: 13.6 us -> 0.14 us  [per_device(): mixer_rows = jnp.stack([running, entry, tail, jnp.zeros_like(tail)]).resh...]
    pallas_call x5, Pallas kernels: 32.2 us -> 19.4 us  [assemble(): pl.pallas_call(partial(assemble_body, spans), grid_spec=pltpu.PrefetchSca...]
    broadcast_in_dim x13 -> x0, local copies, waits for them, and re-layouts: 10.7 us -> none  [the longest x10 9.37 us: mine_of(): return jnp.repeat(chosen, PM, axis=-1)[..., None]]
    another operation x11 -> x5, local copies, waits for them, and re-layouts: 9.73 us -> 0.18 us  [the longest x4 0.17 us: per_device(): jnp.stack([running, entry, tail, jnp.zeros_like(tail)])]
  transfers between devices with their start and end apart: 51 -> 51, of which waited for: 16 -> 16; matrix products, arithmetic and copies ran while one was open for 36% -> 30% of each run, Pallas kernels for 13% -> 13%
where the time goes in v4:
time: 743 us; the launch traced here: 732 us
  waiting for transfers between devices  243 us (33%)
  other arithmetic  124 us (17%)
  Pallas kernels  117 us (16%)
  matrix products  101 us (14%)
  local copies, waits for them, and re-layouts  77.3 us (10%)
  starting transfers between devices  50 us (7%)
  between operations  19.6 us (3%)
    ppermute x37, waiting for transfers between devices, exchange(): return lax.ppermute(block, MESH_AXES, route)  108 us
    psum x4, waiting for transfers between devices, ctx_finish(): mine = lax.psum(mine, 'ctx', axis_index_groups=lines)  101 us
    dot_general x21, matrix products, split_products(): lax.dot_general(piece, right, (((1 - axis,), (0,)), ((), ())), preferred_...  44.3 us
    ppermute x37, starting transfers between devices, exchange(): return lax.ppermute(block, MESH_AXES, route)  34.1 us
    dot_general x6, matrix products, nt_dot(): lax.dot_general(left, right, (((1,), (1,)), ((), ())), preferred_element_...  33.8 us
    pallas_call x1, Pallas kernels, per_device(): attend_backward(group_blocks, pairs, key_side, turned_q, mirrored_q, quer...  31.5 us
    all_gather x1, waiting for transfers between devices, per_device(): lax.all_gather(jnp.concatenate([keys_b, values_b], axis=1).transpose(0, 2...  25.4 us
    unnamed x332, local copies, waits for them, and re-layouts  24.8 us
  transfers between devices with their start and end apart: 51, of which 16 were waited for; matrix products, arithmetic and copies ran while one was open for 30% of the time, Pallas kernels for 13%

profile of v4, /device:TPU:0, one launch (start us, length us, event | category | flops | bytes accessed | tf_op | source)
XLA Modules:
  0.0 732.1 jit_solution(3531234648773767566)
XLA Ops:
  15.0 2.5 collective-permute-start.3
  25.3 19.3 %collective-permute-done.3.refs_4_ = bf16[144,4096]{1,0:T(8,128)(2,1)} collective-permute-done((bf16[144,4096]{1,0:T(8,128)(2,1)}, bf16[144,4096]{1,0:T(8,128)(2,1)}, u32[]{:S(2)}, u32[]{:S(2)}) %collective-permute-start.3) | collective-permute-done | bytes 1179680 | tf_op jit(solution)/shard_map/ppermute | solution.py:35
  47.0 8.6 %collective-permute-done.1.refs_2_ = bf16[64,4096]{1,0:T(8,128)(2,1)S(1)} collective-permute-done((bf16[64,4096]{1,0:T(8,128)(2,1)}, bf16[64,4096]{1,0:T(8,128)(2,1)S(1)}, u32[]{:S(2)}, u32[]{:S(2)}) %collective-permute-start.1) | collective-permute-done | bytes 524320 | tf_op jit(solution)/shard_map/ppermute | solution.py:35
  61.2 8.2 %collective-permute-done.2.refs_3_ = bf16[64,4096]{1,0:T(8,128)(2,1)} collective-permute-done((bf16[64,4096]{1,0:T(8,128)(2,1)S(1)}, bf16[64,4096]{1,0:T(8,128)(2,1)}, u32[]{:S(2)}, u32[]{:S(2)}) %collective-permute-start.2) | collective-permute-done | bytes 524320 | tf_op jit(solution)/shard_map/ppermute | solution.py:35
  74.6 7.9 %assemble.5 = bf16[1024,4096]{1,0:T(8,128)(2,1)S(1)} custom-call(s32[16]{0:T(128)S(1)} %stack.168.target_ref, bf16[272,4096]{1,0:T(8,128)(2,1)S(1)} %fusion.29.refs_0_, bf16[272,4096]{1,0:T(8,128)(2,1)} %collective-permute-done.refs_1_, bf16[64,4096]{1,0:T(8,128)(2,1)S(1)} %collective-permute-done.1.refs_2_, ...), custom_call_target="tpu_custom_call" | custom-call | flops 1024 | bytes 1024 | tf_op jit(solution)/shard_map/assemble/pallas_call | solution.py:88
  82.6 5.8 fusion.221
  90.2 3.4 collective-permute-start.13
  96.4 4.4 multiply_convert_fusion.1
  100.8 5.6 state_outer.2
  109.3 8.5 %collective-permute-done.14 = bf16[1552,128]{1,0:T(8,128)(2,1)S(1)} collective-permute-done((bf16[1552,128]{1,0:T(8,128)(2,1)S(1)}, bf16[1552,128]{1,0:T(8,128)(2,1)S(1)}, u32[]{:S(2)}, u32[]{:S(2)}) %collective-permute-start.14) | collective-permute-done | bytes 397344 | tf_op jit(solution)/shard_map/ppermute | solution.py:35
  122.7 3.0 pad_maximum_fusion.1.refs_0_
  139.0 2.5 fusion.42.side_ref
  148.4 2.4 fusion.56
  152.7 3.5 collective-permute-start.7
  164.6 9.8 %mixer_forward.1.local_ref = f32[512,1536]{1,0:T(8,128)S(1)} custom-call(f32[12,1,128]{2,1,0:T(1,128)S(1)} %broadcast_in_dim.94.skip_ref, bf16[512,1792]{1,0:T(8,128)(2,1)S(1)} %get-tuple-element.77.left_ref.right_ref.x_ref.b_ref.c_ref, bf16[512,1792]{1,0:T(8,128)(2,1)S(1)} %get-tuple-element.77.left_ref.right_ref.x_ref.b_ref.c_ref, ...), custom_call_target="tpu_custom_call" | custom-call | flops 1024 | bytes 1024 | tf_op jit(solution)/shard_map/mixer_forward/pallas_call | solution.py:950
  177.6 3.3 slice_convert_fusion
  185.0 25.4 %all-gather.7.cloned.1.call-done = bf16[16,512,128]{2,1,0:T(8,128)(2,1)} async-done(((bf16[2,512,128]{2,1,0:T(8,128)(2,1)}), bf16[16,512,128]{2,1,0:T(8,128)(2,1)}) %all-gather.7.cloned.1.call-update) | async-done | bytes 2097168 | tf_op jit(solution)/shard_map/all_gather | solution.py:896
  213.1 22.3 %attend_forward.1 = (f32[8,64,256]{2,1,0:T(8,128)S(1)}, f32[8,64,256]{2,1,0:T(8,128)S(1)}, f32[2,2,1,1024]{3,2,1,0:T(1,128)S(1)}) custom-call(s32[2]{0:T(128)S(1)} %pad_add_fusion.4.blocks, bf16[8,2,512,128]{3,2,1,0:T(8,128)(2,1)S(1)} %bitcast.263, bf16[4096,128]{1,0:T(8,128)(2,1)S(1)} %fusion.42.side_ref, bf16[8,64,512]{2,1,0:T(8,128)(2,1)S(1)} %copy-done.7, ...), custom_call_target="tpu_custom_call" | custom-call | flops 1024 | bytes 1024 | tf_op jit(solution)/shard_map/attend_forward/pallas_call | solution.py:954
  239.2 4.5 mixer_join.1
  243.7 4.0 multiply_reduce_fusion.6
  257.8 2.7 collective-permute-done.10
  264.1 2.7 assemble.7
  274.5 4.1 assemble.8
  278.6 6.8 fusion.223
  285.4 2.8 assemble.9
  288.2 10.1 %bitcast_multiply_fusion.1 = (f32[512,2048]{1,0:T(8,128)}, f32[512,2048]{1,0:T(8,128)}, bf16[512,2048]{1,0:T(8,128)(2,1)}) fusion(f32[512,4096]{1,0:T(8,128)} %fusion.223, bf16[2048,1024]{1,0:T(8,128)(2,1)S(1)} %assemble.9, bf16[1,512,1024]{2,1,0:T(8,128)(2,1)S(1)} %copy-done.65), kind=kOutput, calls=%fused_computation.15 | convolution fusion | flops 2162163712 | bytes 24117248 | tf_op jit(solution)/shard_map/dot_general | solution.py:301
  298.4 6.2 add_convert_fusion
  304.6 8.6 %multiply_reduce_fusion.7 = (f32[1024]{0:T(1024)}, f32[512]{0:T(512)S(1)}, f32[512,1024]{1,0:T(8,128)S(1)}) fusion(f32[512,1024]{1,0:T(8,128)} %copy-done.42, f32[512]{0:T(512)S(1)} %fusion.181, f32[1024]{0:T(1024)S(1)} %bitcast.294, bf16[512,4096]{1,0:T(8,128)(2,1)} %add_convert_fusion, bf16[1024,4096]{1,0:T(8,128)(2,1)S(1)} %assemble.8), kind=kOutput, calls=%fused_computation.87 | convolution fusion | flops 4298111488 | bytes 16789504 | tf_op jit(solution)/shard_map/dot_general | solution.py:301
  317.0 2.7 multiply_reduce_fusion.4
  322.4 4.4 convolution_convert_fusion
  328.8 5.8 fusion.207
  346.2 2.6 add_convert_fusion.11
  349.4 17.4 %collective-permute-done.22.refs_1_ = bf16[512,1024]{1,0:T(8,128)(2,1)S(1)} collective-permute-done((bf16[512,1024]{1,0:T(8,128)(2,1)S(1)}, bf16[512,1024]{1,0:T(8,128)(2,1)S(1)}, u32[]{:S(2)}, u32[]{:S(2)}) %collective-permute-start.22) | collective-permute-done | bytes 1048608 | tf_op jit(solution)/shard_map/ppermute | solution.py:35
  375.4 5.6 state_outer.3
  381.1 2.7 add_convert_fusion.5
  387.4 3.5 add_convert_fusion.10
  393.2 14.1 %collective-permute-done.28.refs_3_ = bf16[512,1024]{1,0:T(8,128)(2,1)} collective-permute-done((bf16[512,1024]{1,0:T(8,128)(2,1)}, bf16[512,1024]{1,0:T(8,128)(2,1)}, u32[]{:S(2)}, u32[]{:S(2)}) %collective-permute-start.28) | collective-permute-done | bytes 1048608 | tf_op jit(solution)/shard_map/ppermute | solution.py:35
  407.2 2.6 add_convert_fusion.4
  412.7 3.4 fusion.54
  416.1 4.4 add_convert_fusion.2
  422.0 7.6 %collective-permute-done.38 = bf16[128,3584]{1,0:T(8,128)(2,1)S(1)} collective-permute-done((bf16[128,3584]{1,0:T(8,128)(2,1)S(1)}, bf16[128,3584]{1,0:T(8,128)(2,1)S(1)}, u32[]{:S(2)}, u32[]{:S(2)}) %collective-permute-start.38) | collective-permute-done | bytes 917536 | tf_op jit(solution)/shard_map/ppermute | solution.py:35
  430.9 31.5 %attend_backward.1 = (f32[8,64,256]{2,1,0:T(8,128)S(1)}, f32[8,64,256]{2,1,0:T(8,128)S(1)}, bf16[8,2,512,128]{3,2,1,0:T(8,128)(2,1)}) custom-call(s32[2]{0:T(128)S(1)} %pad_add_fusion.4.blocks, bf16[8,2,512,128]{3,2,1,0:T(8,128)(2,1)} %bitcast.262, bf16[4096,128]{1,0:T(8,128)(2,1)S(1)} %fusion.42.side_ref, bf16[8,64,512]{2,1,0:T(8,128)(2,1)S(1)} %copy-done.8, ...), custom_call_target="tpu_custom_call" | custom-call | flops 1024 | bytes 1024 | tf_op jit(solution)/shard_map/attend_backward/pallas_call | solution.py:1029
  471.2 6.3 collective-permute-done.30
  480.7 2.9 fusion.61
  487.8 18.2 %mixer_backward.1 = (f32[512,1792]{1,0:T(8,128)}, f32[12,1,128]{2,1,0:T(1,128)S(1)}) custom-call(f32[12,1,128]{2,1,0:T(1,128)S(1)} %broadcast_in_dim.94.skip_ref, bf16[512,1792]{1,0:T(8,128)(2,1)S(1)} %get-tuple-element.77.left_ref.right_ref.x_ref.b_ref.c_ref, bf16[512,1792]{1,0:T(8,128)(2,1)S(1)} %get-tuple-element.77.left_ref.right_ref.x_ref.b_ref.c_ref, ...), custom_call_target="tpu_custom_call" | custom-call | flops 1024 | bytes 1024 | tf_op jit(solution)/shard_map/mixer_backward/pallas_call | solution.py:1057
  506.0 5.5 multiply_reduce_fusion.3
  515.1 3.9 add_convert_fusion.1
  520.1 2.6 collective-permute-start.26
  522.7 2.9 pad_add_fusion
  526.3 3.6 fusion.10.refs_0_
  529.9 12.0 %collective-permute-done.26.refs_1_ = bf16[128,4096]{1,0:T(8,128)(2,1)} collective-permute-done((bf16[128,4096]{1,0:T(8,128)(2,1)}, bf16[128,4096]{1,0:T(8,128)(2,1)}, u32[]{:S(2)}, u32[]{:S(2)}) %collective-permute-start.26) | collective-permute-done | bytes 1048608 | tf_op jit(solution)/shard_map/ppermute | solution.py:35
  541.8 3.9 convolution_convert_fusion.2
  545.7 2.4 add_convert_fusion.3.refs_0_
  553.5 2.7 fusion.44
  556.3 8.8 %fusion.31 = (f32[1024]{0:T(1024)S(1)}, f32[512]{0:T(512)}, f32[512,1024]{1,0:T(8,128)}) fusion(bf16[1,512,1024]{2,1,0:T(8,128)(2,1)S(1)} %copy-done.50, f32[512]{0:T(512)S(1)} %copy-done.138, f32[1024]{0:T(1024)S(1)} %bitcast.304, f32[512,1024]{1,0:T(8,128)S(1)} %fusion.44, bf16[1024,4096]{1,0:T(8,128)(2,1)} %copy-done.4, ...), kind=kOutput, calls=%fused_computation.71 | convolution fusion | flops 3500669440 | bytes 15478784 | tf_op jit(solution)/shard_map/dot_general | solution.py:301
  565.5 2.9 fusion.26
  569.9 2.3 add_convert_fusion.15
  576.6 30.5 %all-reduce.24.cloned.1.call-done.refs_1_ = bf16[128,4096]{1,0:T(8,128)(2,1)} async-done(((bf16[128,4096]{1,0:T(8,128)(2,1)}), bf16[128,4096]{1,0:T(8,128)(2,1)}) %all-reduce.24.cloned.1.call-update) | async-done | bytes 1048592 | tf_op jit(solution)/shard_map/psum | solution.py:208
  616.4 40.3 %all-reduce.26.cloned.1.call-done.refs_1_ = bf16[128,3584]{1,0:T(8,128)(2,1)} async-done(((bf16[128,3584]{1,0:T(8,128)(2,1)}), bf16[128,3584]{1,0:T(8,128)(2,1)}) %all-reduce.26.cloned.1.call-update) | async-done | bytes 917520 | tf_op jit(solution)/shard_map/psum | solution.py:208
  658.2 2.3 add_convert_fusion.12.refs_0_
  660.6 4.8 fusion.39
  665.4 5.0 fusion.40
  670.4 30.0 %all-reduce.28.cloned.1.call-done = bf16[128,2688]{1,0:T(8,128)(2,1)} async-done(((bf16[128,2688]{1,0:T(8,128)(2,1)}), bf16[128,2688]{1,0:T(8,128)(2,1)}) %all-reduce.28.cloned.1.call-update) | async-done | bytes 688144 | tf_op jit(solution)/shard_map/psum | solution.py:208
  707.1 10.7 %collective-permute-done.39 = bf16[128,2688]{1,0:T(8,128)(2,1)S(1)} collective-permute-done((bf16[128,2688]{1,0:T(8,128)(2,1)}, bf16[128,2688]{1,0:T(8,128)(2,1)S(1)}, u32[]{:S(2)}, u32[]{:S(2)}) %collective-permute-start.39) | collective-permute-done | bytes 688160 | tf_op jit(solution)/shard_map/ppermute | solution.py:35
  (665 shorter events, 200.8 us)
Async XLA Ops:
  7.2 170.4 %all-gather.9.cloned.1.call-start = ((), (), s32[]{:S(2)}) async-start(), calls=%async_computation.7 | async-start | bytes 1986560 | tf_op jit(solution)/shard_map/all_gather | solution.py:777
  13.4 56.9 %collective-permute-start = (bf16[272,4096]{1,0:T(8,128)(2,1)S(1)}, bf16[272,4096]{1,0:T(8,128)(2,1)}, u32[]{:S(2)}, u32[]{:S(2)}) collective-permute-start(bf16[272,4096]{1,0:T(8,128)(2,1)S(1)} %fusion.29.refs_0_), channel_id=1, source_target_pairs={{0,1},{1,0},{2,3},{3,2},{4,5},{5,4},{6,7},{7,6},{8,9},{9,8},{10,11... | collective-permute-start | bytes 6684680 | tf_op jit(solution)/shard_map/ppermute | solution.py:35
  15.0 29.7 %collective-permute-start.3 = (bf16[144,4096]{1,0:T(8,128)(2,1)}, bf16[144,4096]{1,0:T(8,128)(2,1)}, u32[]{:S(2)}, u32[]{:S(2)}) collective-permute-start(bf16[144,4096]{1,0:T(8,128)(2,1)} %slice.471), channel_id=1, source_target_pairs={{0,2},{1,3},{2,0},{3,1},{4,6},{5,7},{6,4},{7,5},{8,10},{9,11},{10,... | collective-permute-start | bytes 3538952 | tf_op jit(solution)/shard_map/ppermute | solution.py:35
  18.3 37.2 %collective-permute-start.1 = (bf16[64,4096]{1,0:T(8,128)(2,1)}, bf16[64,4096]{1,0:T(8,128)(2,1)S(1)}, u32[]{:S(2)}, u32[]{:S(2)}) collective-permute-start(bf16[64,4096]{1,0:T(8,128)(2,1)} %constant_dynamic-slice_fusion.17), channel_id=1, source_target_pairs={{0,2},{1,3},{2,0},{3,1},{4,6},{5,7},{6,4},{7,5},{8,10},{9,11},{10,... | collective-permute-start | bytes 1572872 | tf_op jit(solution)/shard_map/ppermute | solution.py:35
  20.4 51.7 %copy-start.147 = (s32[3]{0:T(128)}, s32[3]{0:T(128)S(1)}, u32[]{:S(2)}) copy-start(s32[3]{0:T(128)S(1)} %get-tuple-element.163) | copy-start | bytes 40
  21.1 104.6 %copy-start.125 = (s32[512]{0:T(512)}, s32[512]{0:T(512)S(1)}, u32[]{:S(2)}) copy-start(s32[512]{0:T(512)S(1)} %get-tuple-element.59) | copy-start | bytes 6148
  23.3 73.0 %copy-start.127 = (f32[512]{0:T(512)}, f32[512]{0:T(512)S(1)}, u32[]{:S(2)}) copy-start(f32[512]{0:T(512)S(1)} %get-tuple-element.144) | copy-start | bytes 6148
  23.3 73.0 %copy-start.129 = (f32[512]{0:T(512)}, f32[512]{0:T(512)S(1)}, u32[]{:S(2)}) copy-start(f32[512]{0:T(512)S(1)} %get-tuple-element.145) | copy-start | bytes 6148
  23.4 73.0 %copy-start.131 = (f32[512]{0:T(512)}, f32[512]{0:T(512)S(1)}, u32[]{:S(2)}) copy-start(f32[512]{0:T(512)S(1)} %get-tuple-element.146) | copy-start | bytes 6148
  23.6 48.7 %copy-start.151 = (f32[24]{0:T(128)}, f32[24]{0:T(128)S(1)}, u32[]{:S(2)}) copy-start(f32[24]{0:T(128)S(1)} %get-tuple-element.50) | copy-start | bytes 292
  24.2 50.3 %copy-start.149 = (f32[32]{0:T(128)}, f32[32]{0:T(128)S(1)}, u32[]{:S(2)}) copy-start(f32[32]{0:T(128)S(1)} %multiply_power_fusion) | copy-start | bytes 388
  44.6 26.5 %collective-permute-start.6 = (bf16[144,4096]{1,0:T(8,128)(2,1)}, bf16[144,4096]{1,0:T(8,128)(2,1)}, u32[]{:S(2)}, u32[]{:S(2)}) collective-permute-start(bf16[144,4096]{1,0:T(8,128)(2,1)} %collective-permute-done.3.refs_4_), channel_id=1, source_target_pairs={{0,1},{1,0},{2,3},{3,2},{4,5},{5,4},{6,7},{7,6},{8,9},{9,8},{10,11... | collective-permute-start | bytes 3538952 | tf_op jit(solution)/shard_map/ppermute | solution.py:35
  47.0 27.5 %copy-start.90 = (f32[32,512]{1,0:T(8,128)}, f32[32,512]{1,0:T(8,128)S(1)}, u32[]{:S(2)}) copy-start(f32[32,512]{1,0:T(8,128)S(1)} %get-tuple-element.160) | copy-start | bytes 196612
  55.6 13.9 %collective-permute-start.2 = (bf16[64,4096]{1,0:T(8,128)(2,1)S(1)}, bf16[64,4096]{1,0:T(8,128)(2,1)}, u32[]{:S(2)}, u32[]{:S(2)}) collective-permute-start(bf16[64,4096]{1,0:T(8,128)(2,1)S(1)} %collective-permute-done.1.refs_2_), channel_id=1, source_target_pairs={{0,4},{1,5},{2,6},{3,7},{4,0},{5,1},{6,2},{7,3},{8,12},{9,13},{10,... | collective-permute-start | bytes 1572872 | tf_op jit(solution)/shard_map/ppermute | solution.py:35
  61.1 13.5 %collective-permute-start.4 = (bf16[64,4096]{1,0:T(8,128)(2,1)S(1)}, bf16[64,4096]{1,0:T(8,128)(2,1)S(1)}, u32[]{:S(2)}, u32[]{:S(2)}) collective-permute-start(bf16[64,4096]{1,0:T(8,128)(2,1)S(1)} %collective-permute-done.1.refs_2_), channel_id=1, source_target_pairs={{0,1},{1,0},{2,3},{3,2},{4,5},{5,4},{6,7},{7,6},{8,9},{9,8},{10,11... | collective-permute-start | bytes 1572872 | tf_op jit(solution)/shard_map/ppermute | solution.py:35
  69.4 5.2 collective-permute-start.5
  72.9 75.5 %copy-start.114 = (f32[1,2,4,128]{3,1,2,0:T(2,128)}, f32[1,2,4,128]{3,1,2,0:T(2,128)S(1)}, u32[]{:S(2)}) copy-start(f32[1,2,4,128]{3,1,2,0:T(2,128)S(1)} %copy.114) | copy-start | bytes 12292
  90.2 5.7 collective-permute-start.13
  106.5 11.4 %collective-permute-start.14 = (bf16[1552,128]{1,0:T(8,128)(2,1)S(1)}, bf16[1552,128]{1,0:T(8,128)(2,1)S(1)}, u32[]{:S(2)}, u32[]{:S(2)}) collective-permute-start(bf16[1552,128]{1,0:T(8,128)(2,1)S(1)} %pad_maximum_fusion.10), channel_id=1, source_target_pairs={{0,4},{1,5},{2,6},{3,7},{4,0},{5,1},{6,2},{7,3},{8,12},{9,13},{10,... | collective-permute-start | bytes 1191944 | tf_op jit(solution)/shard_map/ppermute | solution.py:35
  120.4 90.0 %all-gather.7.cloned.1.call-start = ((), (), s32[]{:S(2)}) async-start(), calls=%async_computation.6 | async-start | bytes 2359296 | tf_op jit(solution)/shard_map/all_gather | solution.py:896
  134.1 329.9 %all-reduce.22.cloned.1.call-start = ((), (), s32[]{:S(2)}) async-start(), calls=%async_computation.2 | async-start | bytes 1048576 | tf_op jit(solution)/shard_map/psum | solution.py:208
  141.5 43.5 %collective-permute-start.8 = (bf16[1024,1024]{1,0:T(8,128)(2,1)}, bf16[1024,1024]{1,0:T(8,128)(2,1)}, u32[]{:S(2)}, u32[]{:S(2)}) collective-permute-start(bf16[1024,1024]{1,0:T(8,128)(2,1)} %pad_maximum_fusion.1.refs_0_), channel_id=1, source_target_pairs={{0,1},{1,0},{2,3},{3,2},{4,5},{5,4},{6,7},{7,6},{8,9},{9,8},{10,11... | collective-permute-start | bytes 6291464 | tf_op jit(solution)/shard_map/ppermute | solution.py:35
  141.6 93.8 %collective-permute-start.11 = (bf16[1024,1024]{1,0:T(8,128)(2,1)}, bf16[1024,1024]{1,0:T(8,128)(2,1)}, u32[]{:S(2)}, u32[]{:S(2)}) collective-permute-start(bf16[1024,1024]{1,0:T(8,128)(2,1)} %pad_maximum_fusion.1.refs_0_), channel_id=1, source_target_pairs={{0,2},{1,3},{2,0},{3,1},{4,6},{5,7},{6,4},{7,5},{8,10},{9,11},{10,... | collective-permute-start | bytes 6291464 | tf_op jit(solution)/shard_map/ppermute | solution.py:35
  143.2 41.8 %collective-permute-start.9 = (bf16[256,4096]{1,0:T(8,128)(2,1)}, bf16[256,4096]{1,0:T(8,128)(2,1)}, u32[]{:S(2)}, u32[]{:S(2)}) collective-permute-start(bf16[256,4096]{1,0:T(8,128)(2,1)} %refs_0_), channel_id=1, source_target_pairs={{0,1},{1,0},{2,3},{3,2},{4,5},{5,4},{6,7},{7,6},{8,9},{9,8},{10,11... | collective-permute-start | bytes 6291464 | tf_op jit(solution)/shard_map/ppermute | solution.py:35
  143.4 107.3 %collective-permute-start.15 = (bf16[256,4096]{1,0:T(8,128)(2,1)}, bf16[256,4096]{1,0:T(8,128)(2,1)}, u32[]{:S(2)}, u32[]{:S(2)}) collective-permute-start(bf16[256,4096]{1,0:T(8,128)(2,1)} %refs_0_), channel_id=1, source_target_pairs={{0,2},{1,3},{2,0},{3,1},{4,6},{5,7},{6,4},{7,5},{8,10},{9,11},{10,... | collective-permute-start | bytes 6291464 | tf_op jit(solution)/shard_map/ppermute | solution.py:35
  152.7 32.3 %collective-permute-start.7 = (bf16[8,64,256]{2,1,0:T(8,128)(2,1)}, bf16[8,64,256]{2,1,0:T(8,128)(2,1)}, u32[]{:S(2)}, u32[]{:S(2)}) collective-permute-start(bf16[8,64,256]{2,1,0:T(8,128)(2,1)} %slice.483), channel_id=1, source_target_pairs={{0,28},{4,24},{8,20},{12,16},{16,12},{20,8},{24,4},{28,0},{1,29},{... | collective-permute-start | bytes 786440 | tf_op jit(solution)/shard_map/ppermute | solution.py:46
  235.4 26.8 %collective-permute-start.12 = (bf16[1024,1024]{1,0:T(8,128)(2,1)}, bf16[1024,1024]{1,0:T(8,128)(2,1)}, u32[]{:S(2)}, u32[]{:S(2)}) collective-permute-start(bf16[1024,1024]{1,0:T(8,128)(2,1)} %collective-permute-done.11.refs_2_), channel_id=1, source_target_pairs={{0,1},{1,0},{2,3},{3,2},{4,5},{5,4},{6,7},{7,6},{8,9},{9,8},{10,11... | collective-permute-start | bytes 6291464 | tf_op jit(solution)/shard_map/ppermute | solution.py:35
  248.7 11.8 %collective-permute-start.10 = (bf16[8,64,256]{2,1,0:T(8,128)(2,1)}, bf16[8,64,256]{2,1,0:T(8,128)(2,1)}, u32[]{:S(2)}, u32[]{:S(2)}) collective-permute-start(bf16[8,64,256]{2,1,0:T(8,128)(2,1)} %convert_element_type.628), channel_id=1, source_target_pairs={{0,28},{4,24},{8,20},{12,16},{16,12},{20,8},{24,4},{28,0},{1,29},{... | collective-permute-start | bytes 786440 | tf_op jit(solution)/shard_map/ppermute | solution.py:46
  250.6 22.1 %collective-permute-start.16 = (bf16[256,4096]{1,0:T(8,128)(2,1)}, bf16[256,4096]{1,0:T(8,128)(2,1)}, u32[]{:S(2)}, u32[]{:S(2)}) collective-permute-start(bf16[256,4096]{1,0:T(8,128)(2,1)} %collective-permute-done.15.refs_2_), channel_id=1, source_target_pairs={{0,1},{1,0},{2,3},{3,2},{4,5},{5,4},{6,7},{7,6},{8,9},{9,8},{10,11... | collective-permute-start | bytes 6291464 | tf_op jit(solution)/shard_map/ppermute | solution.py:35
  320.4 110.4 %collective-permute-start.29 = (bf16[8,64,256]{2,1,0:T(8,128)(2,1)}, bf16[8,64,256]{2,1,0:T(8,128)(2,1)}, u32[]{:S(2)}, u32[]{:S(2)}) collective-permute-start(bf16[8,64,256]{2,1,0:T(8,128)(2,1)} %slice.525), channel_id=1, source_target_pairs={{0,28},{4,24},{8,20},{12,16},{16,12},{20,8},{24,4},{28,0},{1,29},{... | collective-permute-start | bytes 786440 | tf_op jit(solution)/shard_map/ppermute | solution.py:46
  326.8 89.3 %collective-permute-start.19 = (bf16[512,4096]{1,0:T(8,128)(2,1)}, bf16[512,4096]{1,0:T(8,128)(2,1)}, u32[]{:S(2)}, u32[]{:S(2)}) collective-permute-start(bf16[512,4096]{1,0:T(8,128)(2,1)} %convolution_convert_fusion), channel_id=1, source_target_pairs={{0,1},{1,0},{2,3},{3,2},{4,5},{5,4},{6,7},{7,6},{8,9},{9,8},{10,11... | collective-permute-start | bytes 12582920 | tf_op jit(solution)/shard_map/ppermute | solution.py:35
  328.2 11.7 %collective-permute-start.17 = (bf16[1024,1024]{1,0:T(8,128)(2,1)S(1)}, bf16[1024,1024]{1,0:T(8,128)(2,1)S(1)}, u32[]{:S(2)}, u32[]{:S(2)}) collective-permute-start(bf16[1024,1024]{1,0:T(8,128)(2,1)S(1)} %convolution_convert_fusion.3), channel_id=1, source_target_pairs={{0,1},{1,0},{2,3},{3,2},{4,5},{5,4},{6,7},{7,6},{8,9},{9,8},{10,11... | collective-permute-start | bytes 6291464 | tf_op jit(solution)/shard_map/ppermute | solution.py:35
  335.6 10.6 %collective-permute-start.21 = (bf16[512,1536]{1,0:T(8,128)(2,1)S(1)}, bf16[512,1536]{1,0:T(8,128)(2,1)S(1)}, u32[]{:S(2)}, u32[]{:S(2)}) collective-permute-start(bf16[512,1536]{1,0:T(8,128)(2,1)S(1)} %convolution_convert_fusion.1), channel_id=1, source_target_pairs={{0,1},{1,0},{2,3},{3,2},{4,5},{5,4},{6,7},{7,6},{8,9},{9,8},{10,11... | collective-permute-start | bytes 4718600 | tf_op jit(solution)/shard_map/ppermute | solution.py:35
  339.4 41.6 %collective-permute-start.24 = (bf16[1024,1024]{1,0:T(8,128)(2,1)}, bf16[1024,1024]{1,0:T(8,128)(2,1)}, u32[]{:S(2)}, u32[]{:S(2)}) collective-permute-start(bf16[1024,1024]{1,0:T(8,128)(2,1)} %pad_maximum_fusion.2), channel_id=1, source_target_pairs={{0,1},{1,0},{2,3},{3,2},{4,5},{5,4},{6,7},{7,6},{8,9},{9,8},{10,11... | collective-permute-start | bytes 6291464 | tf_op jit(solution)/shard_map/ppermute | solution.py:35
  340.7 26.1 %collective-permute-start.22 = (bf16[512,1024]{1,0:T(8,128)(2,1)S(1)}, bf16[512,1024]{1,0:T(8,128)(2,1)S(1)}, u32[]{:S(2)}, u32[]{:S(2)}) collective-permute-start(bf16[512,1024]{1,0:T(8,128)(2,1)S(1)} %add_convert_fusion.7), channel_id=1, source_target_pairs={{0,2},{1,3},{2,0},{3,1},{4,6},{5,7},{6,4},{7,5},{8,10},{9,11},{10,... | collective-permute-start | bytes 3145736 | tf_op jit(solution)/shard_map/ppermute | solution.py:35
  348.8 38.6 %collective-permute-start.27 = (bf16[256,1536]{1,0:T(8,128)(2,1)}, bf16[256,1536]{1,0:T(8,128)(2,1)}, u32[]{:S(2)}, u32[]{:S(2)}) collective-permute-start(bf16[256,1536]{1,0:T(8,128)(2,1)} %add_convert_fusion.11), channel_id=1, source_target_pairs={{0,2},{1,3},{2,0},{3,1},{4,6},{5,7},{6,4},{7,5},{8,10},{9,11},{10,... | collective-permute-start | bytes 2359304 | tf_op jit(solution)/shard_map/ppermute | solution.py:35
  368.8 15.1 %collective-permute-start.23 = (bf16[128,2048]{1,0:T(8,128)(2,1)}, bf16[128,2048]{1,0:T(8,128)(2,1)}, u32[]{:S(2)}, u32[]{:S(2)}) collective-permute-start(bf16[128,2048]{1,0:T(8,128)(2,1)} %fusion.93), channel_id=1, source_target_pairs={{0,4},{1,5},{2,6},{3,7},{4,0},{5,1},{6,2},{7,3},{8,12},{9,13},{10,... | collective-permute-start | bytes 1572872 | tf_op jit(solution)/shard_map/ppermute | solution.py:35
  381.0 9.8 %collective-permute-start.18 = (bf16[1536,128]{1,0:T(8,128)(2,1)S(1)}, bf16[1536,128]{1,0:T(8,128)(2,1)}, u32[]{:S(2)}, u32[]{:S(2)}) collective-permute-start(bf16[1536,128]{1,0:T(8,128)(2,1)S(1)} %state_outer.3), channel_id=1, source_target_pairs={{0,4},{1,5},{2,6},{3,7},{4,0},{5,1},{6,2},{7,3},{8,12},{9,13},{10,... | collective-permute-start | bytes 1179656 | tf_op jit(solution)/shard_map/ppermute | solution.py:35
  383.8 23.4 %collective-permute-start.28 = (bf16[512,1024]{1,0:T(8,128)(2,1)}, bf16[512,1024]{1,0:T(8,128)(2,1)}, u32[]{:S(2)}, u32[]{:S(2)}) collective-permute-start(bf16[512,1024]{1,0:T(8,128)(2,1)} %add_convert_fusion.5), channel_id=1, source_target_pairs={{0,2},{1,3},{2,0},{3,1},{4,6},{5,7},{6,4},{7,5},{8,10},{9,11},{10,... | collective-permute-start | bytes 3145736 | tf_op jit(solution)/shard_map/ppermute | solution.py:35
  387.3 96.3 %all-gather.11.cloned.1.call-start = ((), (), s32[]{:S(2)}) async-start(), calls=%async_computation.8 | async-start | bytes 1966080 | tf_op jit(solution)/shard_map/all_gather | solution.py:777
  392.9 155.6 %reduce-scatter.2.cloned.1.call-start = ((), (), s32[]{:S(2)}) async-start(), calls=%async_computation.1 | async-start | bytes 2359296 | tf_op jit(solution)/shard_map/reduce_scatter | solution.py:1045
  410.2 19.4 %collective-permute-start.38 = (bf16[128,3584]{1,0:T(8,128)(2,1)S(1)}, bf16[128,3584]{1,0:T(8,128)(2,1)S(1)}, u32[]{:S(2)}, u32[]{:S(2)}) collective-permute-start(bf16[128,3584]{1,0:T(8,128)(2,1)S(1)} %constant_dynamic-slice_fusion), channel_id=1, source_target_pairs={{0,4},{1,5},{2,6},{3,7},{4,0},{5,1},{6,2},{7,3},{8,12},{9,13},{10,... | collective-permute-start | bytes 2752520 | tf_op jit(solution)/shard_map/ppermute | solution.py:35
  420.5 67.2 %collective-permute-start.20 = (bf16[256,4096]{1,0:T(8,128)(2,1)}, bf16[256,4096]{1,0:T(8,128)(2,1)}, u32[]{:S(2)}, u32[]{:S(2)}) collective-permute-start(bf16[256,4096]{1,0:T(8,128)(2,1)} %add_convert_fusion.2), channel_id=1, source_target_pairs={{0,2},{1,3},{2,0},{3,1},{4,6},{5,7},{6,4},{7,5},{8,10},{9,11},{10,... | collective-permute-start | bytes 6291464 | tf_op jit(solution)/shard_map/ppermute | solution.py:35
  464.0 16.8 %collective-permute-start.42 = (bf16[128,2048]{1,0:T(8,128)(2,1)}, bf16[128,2048]{1,0:T(8,128)(2,1)}, u32[]{:S(2)}, u32[]{:S(2)}) collective-permute-start(bf16[128,2048]{1,0:T(8,128)(2,1)} %all-reduce.22.cloned.1.call-done.refs_1_), channel_id=1, source_target_pairs={{0,4},{1,5},{2,6},{3,7},{4,0},{5,1},{6,2},{7,3},{8,12},{9,13},{10,... | collective-permute-start | bytes 1572872 | tf_op jit(solution)/shard_map/ppermute | solution.py:35
  468.0 9.5 %collective-permute-start.30 = (bf16[8,64,256]{2,1,0:T(8,128)(2,1)}, bf16[8,64,256]{2,1,0:T(8,128)(2,1)}, u32[]{:S(2)}, u32[]{:S(2)}) collective-permute-start(bf16[8,64,256]{2,1,0:T(8,128)(2,1)} %fusion.100), channel_id=1, source_target_pairs={{0,28},{4,24},{8,20},{12,16},{16,12},{20,8},{24,4},{28,0},{1,29},{... | collective-permute-start | bytes 786440 | tf_op jit(solution)/shard_map/ppermute | solution.py:46
  470.0 137.1 %all-reduce.24.cloned.1.call-start = ((), (), s32[]{:S(2)}) async-start(), calls=%async_computation.3 | async-start | bytes 2097152 | tf_op jit(solution)/shard_map/psum | solution.py:208
  513.0 13.3 %collective-permute-start.25 = (f32[3,1792]{1,0:T(4,128)S(1)}, f32[3,1792]{1,0:T(4,128)S(1)}, u32[]{:S(2)}, u32[]{:S(2)}) collective-permute-start(f32[3,1792]{1,0:T(4,128)S(1)} %pad_add_fusion.1), channel_id=1, source_target_pairs={{4,0},{8,4},{12,8},{16,12},{20,16},{24,20},{28,24},{5,1},{9,5},{13... | collective-permute-start | bytes 64520 | tf_op jit(solution)/shard_map/ppermute | solution.py:41
  520.1 21.7 %collective-permute-start.26 = (bf16[128,4096]{1,0:T(8,128)(2,1)}, bf16[128,4096]{1,0:T(8,128)(2,1)}, u32[]{:S(2)}, u32[]{:S(2)}) collective-permute-start(bf16[128,4096]{1,0:T(8,128)(2,1)} %constant_dynamic-slice_fusion.2), channel_id=1, source_target_pairs={{0,4},{1,5},{2,6},{3,7},{4,0},{5,1},{6,2},{7,3},{8,12},{9,13},{10,... | collective-permute-start | bytes 3145736 | tf_op jit(solution)/shard_map/ppermute | solution.py:35
  545.7 19.7 %collective-permute-start.31 = (bf16[512,1792]{1,0:T(8,128)(2,1)}, bf16[512,1792]{1,0:T(8,128)(2,1)}, u32[]{:S(2)}, u32[]{:S(2)}) collective-permute-start(bf16[512,1792]{1,0:T(8,128)(2,1)} %convolution_convert_fusion.2), channel_id=1, source_target_pairs={{0,1},{1,0},{2,3},{3,2},{4,5},{5,4},{6,7},{7,6},{8,9},{9,8},{10,11... | collective-permute-start | bytes 5505032 | tf_op jit(solution)/shard_map/ppermute | solution.py:35
  548.2 108.6 %all-reduce.26.cloned.1.call-start = ((), (), s32[]{:S(2)}) async-start(), calls=%async_computation.4 | async-start | bytes 1835008 | tf_op jit(solution)/shard_map/psum | solution.py:208
  552.9 17.0 %collective-permute-start.33 = (bf16[512,768]{1,0:T(8,128)(2,1)}, bf16[512,768]{1,0:T(8,128)(2,1)}, u32[]{:S(2)}, u32[]{:S(2)}) collective-permute-start(bf16[512,768]{1,0:T(8,128)(2,1)} %convolution_convert_fusion.6), channel_id=1, source_target_pairs={{0,1},{1,0},{2,3},{3,2},{4,5},{5,4},{6,7},{7,6},{8,9},{9,8},{10,11... | collective-permute-start | bytes 2359304 | tf_op jit(solution)/shard_map/ppermute | solution.py:35
  565.4 7.4 %collective-permute-start.35 = (bf16[64,128]{1,0:T(8,128)(2,1)S(1)}, bf16[64,128]{1,0:T(8,128)(2,1)S(1)}, u32[]{:S(2)}, u32[]{:S(2)}) collective-permute-start(bf16[64,128]{1,0:T(8,128)(2,1)S(1)} %pad_maximum_fusion.18), channel_id=1, source_target_pairs={{0,1},{1,0},{2,3},{3,2},{4,5},{5,4},{6,7},{7,6},{8,9},{9,8},{10,11... | collective-permute-start | bytes 49160 | tf_op jit(solution)/shard_map/ppermute | solution.py:35
  568.4 40.2 %collective-permute-start.32 = (bf16[256,1792]{1,0:T(8,128)(2,1)}, bf16[256,1792]{1,0:T(8,128)(2,1)}, u32[]{:S(2)}, u32[]{:S(2)}) collective-permute-start(bf16[256,1792]{1,0:T(8,128)(2,1)} %fusion.26), channel_id=1, source_target_pairs={{0,2},{1,3},{2,0},{3,1},{4,6},{5,7},{6,4},{7,5},{8,10},{9,11},{10,... | collective-permute-start | bytes 2752520 | tf_op jit(solution)/shard_map/ppermute | solution.py:35
  572.2 35.0 %collective-permute-start.34 = (bf16[256,768]{1,0:T(8,128)(2,1)}, bf16[256,768]{1,0:T(8,128)(2,1)S(1)}, u32[]{:S(2)}, u32[]{:S(2)}) collective-permute-start(bf16[256,768]{1,0:T(8,128)(2,1)} %add_convert_fusion.15), channel_id=1, source_target_pairs={{0,2},{1,3},{2,0},{3,1},{4,6},{5,7},{6,4},{7,5},{8,10},{9,11},{10,... | collective-permute-start | bytes 1179656 | tf_op jit(solution)/shard_map/ppermute | solution.py:35
  572.8 34.4 %collective-permute-start.36 = (bf16[32,128]{1,0:T(8,128)(2,1)S(1)}, bf16[32,128]{1,0:T(8,128)(2,1)S(1)}, u32[]{:S(2)}, u32[]{:S(2)}) collective-permute-start(bf16[32,128]{1,0:T(8,128)(2,1)S(1)} %add_convert_fusion.20), channel_id=1, source_target_pairs={{0,2},{1,3},{2,0},{3,1},{4,6},{5,7},{6,4},{7,5},{8,10},{9,11},{10,... | collective-permute-start | bytes 24584 | tf_op jit(solution)/shard_map/ppermute | solution.py:35
  607.1 93.3 %all-reduce.28.cloned.1.call-start = ((), (), s32[]{:S(2)}) async-start(), calls=%async_computation.5 | async-start | bytes 1376256 | tf_op jit(solution)/shard_map/psum | solution.py:208
  611.9 46.4 %collective-permute-start.37 = (bf16[128,2688]{1,0:T(8,128)(2,1)}, bf16[128,2688]{1,0:T(8,128)(2,1)}, u32[]{:S(2)}, u32[]{:S(2)}) collective-permute-start(bf16[128,2688]{1,0:T(8,128)(2,1)} %constant_dynamic-slice_fusion.1), channel_id=1, source_target_pairs={{0,4},{1,5},{2,6},{3,7},{4,0},{5,1},{6,2},{7,3},{8,12},{9,13},{10,... | collective-permute-start | bytes 2064392 | tf_op jit(solution)/shard_map/ppermute | solution.py:35
  615.1 50.4 %collective-permute-start.41 = (bf16[128,4096]{1,0:T(8,128)(2,1)}, bf16[128,4096]{1,0:T(8,128)(2,1)}, u32[]{:S(2)}, u32[]{:S(2)}) collective-permute-start(bf16[128,4096]{1,0:T(8,128)(2,1)} %all-reduce.24.cloned.1.call-done.refs_1_), channel_id=1, source_target_pairs={{0,4},{1,5},{2,6},{3,7},{4,0},{5,1},{6,2},{7,3},{8,12},{9,13},{10,... | collective-permute-start | bytes 3145736 | tf_op jit(solution)/shard_map/ppermute | solution.py:35
  616.4 44.2 %copy-start.45 = (f32[512,1024]{1,0:T(8,128)S(1)}, f32[512,1024]{1,0:T(8,128)}, u32[]{:S(2)}) copy-start(f32[512,1024]{1,0:T(8,128)} %copy-done.42) | copy-start | bytes 6291460
  616.4 44.2 %copy-start.135 = (f32[512]{0:T(512)S(1)}, f32[512]{0:T(512)}, u32[]{:S(2)}) copy-start(f32[512]{0:T(512)} %copy-done.134) | copy-start | bytes 6148
  616.4 44.2 %copy-start.139 = (f32[512]{0:T(512)S(1)}, f32[512]{0:T(512)}, u32[]{:S(2)}) copy-start(f32[512]{0:T(512)} %copy-done.136) | copy-start | bytes 6148
  656.8 45.1 %collective-permute-start.40 = (bf16[128,3584]{1,0:T(8,128)(2,1)}, bf16[128,3584]{1,0:T(8,128)(2,1)}, u32[]{:S(2)}, u32[]{:S(2)}) collective-permute-start(bf16[128,3584]{1,0:T(8,128)(2,1)} %all-reduce.26.cloned.1.call-done.refs_1_), channel_id=1, source_target_pairs={{0,4},{1,5},{2,6},{3,7},{4,0},{5,1},{6,2},{7,3},{8,12},{9,13},{10,... | collective-permute-start | bytes 2752520 | tf_op jit(solution)/shard_map/ppermute | solution.py:35
  665.4 36.5 %copy-start.67 = (bf16[128,3584]{1,0:T(8,128)(2,1)S(1)}, bf16[128,3584]{1,0:T(8,128)(2,1)}, u32[]{:S(2)}) copy-start(bf16[128,3584]{1,0:T(8,128)(2,1)} %all-reduce.26.cloned.1.call-done.refs_1_) | copy-start | bytes 2752516
  700.4 17.4 %collective-permute-start.39 = (bf16[128,2688]{1,0:T(8,128)(2,1)}, bf16[128,2688]{1,0:T(8,128)(2,1)S(1)}, u32[]{:S(2)}, u32[]{:S(2)}) collective-permute-start(bf16[128,2688]{1,0:T(8,128)(2,1)} %all-reduce.28.cloned.1.call-done), channel_id=1, source_target_pairs={{0,4},{1,5},{2,6},{3,7},{4,0},{5,1},{6,2},{7,3},{8,12},{9,13},{10,... | collective-permute-start | bytes 2064392 | tf_op jit(solution)/shard_map/ppermute | solution.py:35
  (152 other events, 984.0 us)
Sparse Core Ops, SparseCore 0:
  120.5 37.9 all-gather.8
  161.1 49.2 all-gather.6
  387.4 39.9 all-reduce.21
  428.9 37.0 all-gather.10
  470.1 70.3 reduce-scatter.1
  548.3 58.7 all-reduce.23
  609.6 47.1 all-reduce.25
  660.7 39.6 all-reduce.27

commit v5 on v4

--- a/solution.py
+++ b/solution.py
@@ -64,7 +64,7 @@
 
 
 def assemble_body(spans, target_ref, *refs):
-    out_ref = refs[len(spans)]
+    out_ref = refs[-1]
     step = pl.program_id(0)
     for piece, (first, size) in zip(refs, spans):
 
@@ -74,7 +74,7 @@
         pl.when((step >= first) & (step < first + size))(put)
 
 
-def assemble(pieces, rows):
+def assemble(pieces, rows, anchors=()):
     spans, offsets, targets = [], [], []
     for _, source, start, size in pieces:
         spans.append((len(targets), size // rows))
@@ -93,7 +93,8 @@
             in_specs=[
                 pl.BlockSpec((rows, columns), source_map(offset, first, size))
                 for offset, (first, size) in zip(offsets, spans)
-            ],
+            ]
+            + [pl.BlockSpec(memory_space=pl.ANY)] * len(anchors),
             out_specs=pl.BlockSpec((rows, columns), lambda i, target: (target[i], 0)),
         ),
         out_shape=jax.ShapeDtypeStruct((rows * len(targets), columns), kind),
@@ -102,10 +103,10 @@
         ),
         cost_estimate=small_cost,
         name="assemble",
-    )(jnp.stack([jnp.asarray(target, jnp.int32) for target in targets]), *[p[0] for p in pieces])
-
-
-def gather_first(shard, rows):
+    )(jnp.stack([jnp.asarray(target, jnp.int32) for target in targets]), *[p[0] for p in pieces], *anchors)
+
+
+def gather_first(shard, rows, anchors):
     part = rows // 4
     w = lax.axis_index("wshard")
     side = lax.axis_index("ctx") % 2
@@ -131,7 +132,7 @@
     small = jnp.concatenate(
         [lax.dynamic_slice_in_dim(tails, w ^ at, 1, 0) for at in range(4)], axis=0
     )
-    return assemble(pieces, part), small, across_direct
+    return assemble(pieces, part, anchors), small, across_direct
 
 
 def start_shards(stacked, after):
@@ -224,10 +225,11 @@
     return jnp.concatenate([piece(1), piece(3)], axis=axis), piece(2), piece(0)
 
 
-def shard_sum(beside, across, own):
+def shard_sum(beside, across, own, after=None):
     rows = own.shape[0]
     got = exchange(beside.astype(jnp.bfloat16), 0, 1)
-    got_across = exchange(add_low(across, got[rows:]), 0, 2)
+    across = add_low(across, got[rows:])
+    got_across = exchange(across if after is None else tie(across, after), 0, 2)
     return add_low(own, got[:rows], got_across), got, got_across
 
 
@@ -240,8 +242,32 @@
     ]
 
 
-def weight_grad(left, right):
-    return shard_sum(*split_products(left, right))
+def weight_grad(left, right, after=None):
+    return shard_sum(*split_products(left, right), after)
+
+
+def sum_small(value):
+    rows = value.shape[0] // 4
+    for flip in (1, 2):
+        value = value + exchange(value, 0, flip)
+    value = lax.dynamic_slice_in_dim(value, lax.axis_index("wshard") * rows, rows, 0)
+    bit = 1
+    while bit < lax.axis_size("ctx"):
+        value = value + exchange(value, bit, 0)
+        bit *= 2
+    return value
+
+
+def scatter_blocks(blocks):
+    position, bit = lax.axis_index("ctx"), 1
+    while blocks.shape[0] > 1:
+        up = (position // bit) % 2
+        halves = blocks.reshape((blocks.shape[0] // 2, 2) + blocks.shape[1:])
+        keep = lax.dynamic_index_in_dim(halves, up, 1, keepdims=False)
+        give = lax.dynamic_index_in_dim(halves, 1 - up, 1, keepdims=False)
+        blocks = add_low(keep, exchange(give, bit, 0))
+        bit *= 2
+    return blocks[0]
 
 
 def mixed_dot(left, right):
@@ -258,12 +284,15 @@
     return jnp.where(position_index >= 0, tally_count, -1)
 
 
-def turn(value, position_index):
-    half = value.shape[-2] // 2
+def turn_tables(position_index):
+    half = HEAD_SIZE // 2
     freq = rope_base ** (-jnp.arange(half, dtype=jnp.float32) / half)
     angle = freq[:, None] * position_index.astype(jnp.float32)[None, :]
-    cosine = jnp.cos(angle)
-    sine = jnp.sin(angle)
+    return jnp.cos(angle), jnp.sin(angle)
+
+
+def turn(value, cosine, sine):
+    half = value.shape[-2] // 2
     first = value[..., :half, :]
     second = value[..., half:, :]
     return jnp.concatenate(
@@ -753,7 +782,7 @@
     return jnp.sum(rows[..., :3, :HM].astype(jnp.float32), axis=-2)
 
 
-def pass_state(part, gain, gains, reverse):
+def pass_state(part, gain, gains, reverse, after=None):
     count, position = lax.axis_size("ctx"), lax.axis_index("ctx")
     side, line_at = position % 2, position // 2
     is_first = (side == 1) if reverse else (side == 0)
@@ -774,6 +803,8 @@
     total = (second_gain * first + second).astype(jnp.bfloat16).reshape(DSSM, NS)
     if not gains:
         total = jnp.concatenate([total, gain_rows(gain * other)], axis=0)
+    if after is not None:
+        total = tie(total, after)
     totals = lax.all_gather(total, "ctx", axis_index_groups=ctx_lines())
     if not gains:
         line_gains = read_gain(totals[:, DSSM:])
@@ -853,52 +884,12 @@
     attend_forward, attend_backward = attention_calls(rows, count, (2, 2))
     state_outer, mixer_join, mixer_forward, mixer_backward = mixer_calls(rows, 4)
 
-    packed = pack_small(norm_gain, conv_weight, conv_bias, skip_gain, mixer_gain, ffn_gain, 1)
-    first_shard = jnp.concatenate([in_proj, query_proj, key_value_projection], axis=1)
-    packed = jnp.pad(packed.reshape(1, -1), ((0, 15), (0, first_shard.shape[1] - 4096)))
-    first_w, small, arrived = gather_first(
-        jnp.concatenate([first_shard, packed], axis=0), in_proj.shape[0]
-    )
-    norm_w, conv_w, conv_b, skip_w, mixer_g, ffn_g = (
-        part.astype(jnp.float32)
-        for part in unpack_small(small[:, :4096], model, channels, HM, shards)
-    )
-    projected_width = in_proj.shape[1]
-    in_w, attn_pair_w = first_w[:, :projected_width], first_w[:, projected_width:]
-    out_pieces = start_shards(
-        jnp.concatenate([mixer_out, attn_out, down_proj], axis=0), arrived
-    )
-    gate_up_pieces = start_shards(gate_up, arrived)
-    query_w = attn_pair_w[:, : QUERY_HEADS * HEAD_SIZE]
-    keyval_w = attn_pair_w[:, QUERY_HEADS * HEAD_SIZE :]
-
     lengths = doc_lengths[0]
     doc_count = lengths.shape[0]
     position_index = block_at * rows + jnp.arange(rows, dtype=jnp.int32)
     docs = doc_numbers(lengths, position_index)
     doc_prev = doc_numbers(lengths, position_index[:1] - 1)[0]
     log_decay = jnp.log(decay[0])
-    source = tokens[0].astype(jnp.float32)
-    normed, norm_pull = jax.vjp(rms_scale, source, norm_w)
-    normed_b = normed.astype(jnp.bfloat16)
-
-    turned_q = turn(
-        lax.dot_general(
-            query_w, normed_b, (((0,), (1,)), ((), ())), preferred_element_type=jnp.float32
-        ).reshape(QUERY_HEADS, HEAD_SIZE, rows),
-        position_index,
-    ).astype(jnp.bfloat16)
-    key_value_pair = lax.dot_general(
-        keyval_w, normed_b, (((0,), (1,)), ((), ())), preferred_element_type=jnp.float32
-    ).reshape(2, KEY_VALUE_HEADS, HEAD_SIZE, rows)
-    keys_b = turn(key_value_pair[0], position_index).astype(jnp.bfloat16)
-    values_b = key_value_pair[1].astype(jnp.bfloat16)
-    pairs = lax.all_gather(
-        jnp.concatenate([keys_b, values_b], axis=1).transpose(0, 2, 1), "ctx"
-    )
-
-    turned_q = turned_q * jnp.asarray(scale, jnp.bfloat16)
-    mirrored_q = swap_mirrored(turned_q[:, :, width:])
     mirrored = count - 1 - block_at
     group_blocks = jnp.stack([block_at, mirrored]).astype(jnp.int32)
     group_positions = jnp.stack(
@@ -916,37 +907,101 @@
         (side_row == group_docs[:, None, :]) | (side_row >= doc_count), 0.0, mask_fill_value
     ).astype(jnp.bfloat16)
 
-    projected = mixed_dot(normed_b, in_w)
-    gate_z = projected[:, :DSSM]
-    pre_b = projected[:, DSSM:].astype(jnp.bfloat16)
-    rim = from_behind(pre_b[rows - (KW - 1) :], "ctx", 1)
-    extended = jnp.concatenate([rim, pre_b], axis=0).astype(jnp.float32)
+    order = jnp.arange(rows)
+    running = jnp.dot(
+        log_decay, (order[:, None] <= order[None, :]).astype(jnp.float32), precision=highest
+    )
+    entry = jnp.where((docs == doc_prev)[None, :], jnp.exp(running), 0.0)
+    tail = jnp.where((docs == docs[-1])[None, :], jnp.exp(running[:, -1:] - running), 0.0)
+    carry_gain = jnp.where(docs[-1] == doc_prev, jnp.exp(running[:, -1]), 0.0)
+
+    mixer_rows = (
+        jnp.stack([running, entry, tail, jnp.zeros_like(tail)])
+        .reshape(4, HM // 2, 2, rows)
+        .transpose(1, 0, 2, 3)
+        .reshape(HM // 2, 8, rows)
+    )
     taps = jnp.stack(
         [
             (doc_numbers(lengths, position_index - (KW - 1) + tap) == docs).astype(jnp.float32)
             for tap in range(KW)
         ]
     )
+    docs_column, docs_row = docs[:, None], docs[None, :]
+    cosine, sine = turn_tables(position_index)
+    mirrored_cosine, mirrored_sine = turn_tables(group_positions[1])
+    prepared = lax.optimization_barrier(
+        (
+            key_side,
+            query_side,
+            mixer_rows,
+            taps,
+            docs_column,
+            docs_row,
+            cosine,
+            sine,
+            mirrored_cosine,
+            mirrored_sine,
+            group_blocks,
+        )
+    )
+    (
+        key_side,
+        query_side,
+        mixer_rows,
+        taps,
+        docs_column,
+        docs_row,
+        cosine,
+        sine,
+        mirrored_cosine,
+        mirrored_sine,
+        group_blocks,
+    ) = prepared
+    packed = pack_small(norm_gain, conv_weight, conv_bias, skip_gain, mixer_gain, ffn_gain, 1)
+    first_shard = jnp.concatenate([in_proj, query_proj, key_value_projection], axis=1)
+    packed = jnp.pad(packed.reshape(1, -1), ((0, 15), (0, first_shard.shape[1] - 4096)))
+    first_w, small, arrived = gather_first(
+        jnp.concatenate([first_shard, packed], axis=0), in_proj.shape[0], prepared
+    )
+    norm_w, conv_w, conv_b, skip_w, mixer_g, ffn_g = (
+        part.astype(jnp.float32)
+        for part in unpack_small(small[:, :4096], model, channels, HM, shards)
+    )
+    projected_width = in_proj.shape[1]
+    in_w, attn_pair_w = first_w[:, :projected_width], first_w[:, projected_width:]
+    out_pieces = start_shards(
+        jnp.concatenate([mixer_out, attn_out, down_proj], axis=0), arrived
+    )
+    gate_up_pieces = start_shards(gate_up, arrived)
+    source = tokens[0].astype(jnp.float32)
+    normed, norm_pull = jax.vjp(rms_scale, source, norm_w)
+    normed_b = normed.astype(jnp.bfloat16)
+    projected = mixed_dot(normed_b, first_w)
+
+    query_width = QUERY_HEADS * HEAD_SIZE
+    attn_inputs = projected[:, projected_width:].T
+    turned_q = turn(
+        attn_inputs[:query_width].reshape(QUERY_HEADS, HEAD_SIZE, rows), cosine, sine
+    ).astype(jnp.bfloat16)
+    key_value_pair = attn_inputs[query_width:].reshape(2, KEY_VALUE_HEADS, HEAD_SIZE, rows)
+    keys_b = turn(key_value_pair[0], cosine, sine).astype(jnp.bfloat16)
+    values_b = key_value_pair[1].astype(jnp.bfloat16)
+    pairs = lax.all_gather(
+        jnp.concatenate([keys_b, values_b], axis=1).transpose(0, 2, 1), "ctx"
+    )
+    turned_q = turned_q * jnp.asarray(scale, jnp.bfloat16)
+    mirrored_q = swap_mirrored(turned_q[:, :, width:])
+
+    gate_z = projected[:, :DSSM]
+    pre_b = projected[:, DSSM:projected_width].astype(jnp.bfloat16)
+    rim = from_behind(pre_b[rows - (KW - 1) :], "ctx", 1)
+    extended = jnp.concatenate([rim, pre_b], axis=0).astype(jnp.float32)
     conv_f, conv_pull = jax.vjp(partial(conv_local, taps), extended, conv_w, conv_b)
     conv_b16 = conv_f.astype(jnp.bfloat16)
-    order = jnp.arange(rows)
-    running = jnp.dot(
-        log_decay, (order[:, None] <= order[None, :]).astype(jnp.float32), precision=highest
-    )
-    entry = jnp.where((docs == doc_prev)[None, :], jnp.exp(running), 0.0)
-    tail = jnp.where((docs == docs[-1])[None, :], jnp.exp(running[:, -1:] - running), 0.0)
-    carry_gain = jnp.where(docs[-1] == doc_prev, jnp.exp(running[:, -1]), 0.0)
-
-    mixer_rows = (
-        jnp.stack([running, entry, tail, jnp.zeros_like(tail)])
-        .reshape(4, HM // 2, 2, rows)
-        .transpose(1, 0, 2, 3)
-        .reshape(HM // 2, 8, rows)
-    )
     skip_wide = jnp.repeat(skip_w, PM).reshape(HM // 2, 1, 2 * PM)
-    docs_column, docs_row = docs[:, None], docs[None, :]
     fresh = state_outer(DSSM // NS, 4, 0)(mixer_rows, conv_b16, conv_b16)
-    state_in, gains = pass_state(fresh, carry_gain, None, False)
+    state_in, gains = pass_state(fresh, carry_gain, None, False, pairs)
     local = mixer_forward(
         skip_wide, conv_b16, conv_b16, conv_b16, mixer_rows, docs_column, docs_row
     )
@@ -988,7 +1043,6 @@
 
     out_low = cotangent[0]
     down_sum, down_beside, down_across = weight_grad(activated_b, out_low)
-    down_half, down_got = ctx_half([down_sum], model // shards)
     (gate_up_grad_v,) = act_pull(nt_dot(out_low, down_w))
     gate_up_low = gate_up_grad_v.astype(jnp.bfloat16)
     gate_up_sum, gate_up_beside, gate_up_across = weight_grad(normed2_b, gate_up_low)
@@ -1005,27 +1059,8 @@
         mixer_rows, mixed_grad.astype(jnp.bfloat16), conv_b16, down_beside
     )
     state_out_grad, _ = pass_state(upward, None, gains, True)
+    down_half, down_got = ctx_half([tie(down_sum, upward)], model // shards)
     gate_z_low = gate_z_grad.astype(jnp.bfloat16)
-    mixer_products = split_products(gated_b, middle_low)
-    attn_products = split_products(heads_t, middle_low, 0)
-    shard_sizes = [mixer_out.shape[0], attn_out.shape[0]]
-
-    def interleaved(parts):
-        return jnp.concatenate(
-            [
-                part[start * size : (start + 1) * size]
-                for start in range(parts[0].shape[0] // shard_sizes[0])
-                for part, size in zip(parts, shard_sizes)
-            ],
-            axis=0,
-        ).astype(jnp.bfloat16)
-
-    mixer_attn_sum, mixer_beside, mixer_across = shard_sum(
-        *[interleaved(parts) for parts in zip(mixer_products, attn_products)]
-    )
-    in_sum_z, in_z_beside, in_z_across = weight_grad(normed_b, gate_z_low)
-    mixer_half, mixer_got = ctx_half([mixer_attn_sum, in_sum_z], model // shards)
-
     query_grad_own, query_grad_mirrored, pairs_grad = attend_backward(
         group_blocks,
         pairs,
@@ -1041,14 +1076,33 @@
         gate_up_beside,
         down_across,
     )
+    mixer_products = split_products(gated_b, middle_low)
+    attn_products = split_products(heads_t, middle_low, 0)
+    shard_sizes = [mixer_out.shape[0], attn_out.shape[0]]
+
+    def interleaved(parts):
+        return jnp.concatenate(
+            [
+                part[start * size : (start + 1) * size]
+                for start in range(parts[0].shape[0] // shard_sizes[0])
+                for part, size in zip(parts, shard_sizes)
+            ],
+            axis=0,
+        ).astype(jnp.bfloat16)
+
+    mixer_attn_sum, mixer_beside, mixer_across = shard_sum(
+        *[interleaved(parts) for parts in zip(mixer_products, attn_products)], pairs_grad
+    )
+    in_sum_z, in_z_beside, in_z_across = weight_grad(normed_b, gate_z_low, pairs_grad)
     pair_grad = (
-        lax.psum_scatter(pairs_grad, "ctx", scatter_dimension=0)
-        .astype(jnp.float32)
-        .transpose(0, 2, 1)
+        scatter_blocks(pairs_grad).astype(jnp.float32).transpose(0, 2, 1)
     )
     query_low_own, query_low_mirrored = (
-        (turn(grad, -group_positions[at]) * scale).astype(jnp.bfloat16)
-        for at, grad in enumerate((query_grad_own, query_grad_mirrored))
+        (turn(grad, *tables) * scale).astype(jnp.bfloat16)
+        for grad, tables in (
+            (query_grad_own, (cosine[:, :width], -sine[:, :width])),
+            (query_grad_mirrored, (mirrored_cosine, -mirrored_sine)),
+        )
     )
     query_low = jnp.concatenate(
         [query_low_own, swap_mirrored(query_low_mirrored)], axis=2
@@ -1070,6 +1124,9 @@
         down_got,
         mixer_beside,
     )
+    mixer_half, mixer_got = ctx_half(
+        [tie(mixer_attn_sum, conv_grad), tie(in_sum_z, conv_grad)], model // shards
+    )
     skip_grad = jnp.sum(skip_parts.reshape(HM, PM), axis=1)
     extended_grad, conv_weight_grad, conv_bias_grad = conv_pull(conv_grad)
     from_above = from_behind(extended_grad[: KW - 1], "ctx", -1)
@@ -1079,7 +1136,7 @@
     projected_low = jnp.concatenate([gate_z_low, pre_low], axis=1)
     normed_grad = nt_dot(projected_low, in_w)
 
-    keys_low = turn(pair_grad[:, :HEAD_SIZE], -position_index)
+    keys_low = turn(pair_grad[:, :HEAD_SIZE], cosine, -sine)
     keyval_low = jnp.concatenate(
         [
             keys_low.reshape(KEY_VALUE_HEADS * HEAD_SIZE, rows),
@@ -1096,8 +1153,8 @@
     small_grad = pack_small(
         norm_grad, conv_weight_grad, conv_bias_grad, skip_grad, mixer_gain_grad, ffn_gain_grad, shards
     )
-    small_sum, _, _ = shard_sum(*shard_pieces(small_grad, 0))
-    last_half, _ = ctx_half([in_sum_pre, attn_pair_sum, small_sum], model // shards)
+    small_share = sum_small(small_grad)
+    last_half, _ = ctx_half([in_sum_pre, attn_pair_sum], model // shards)
     (down_share,), summed = ctx_finish(down_half, [down_sum.shape], 0)
     (gate_up_share,), summed = ctx_finish(tie(gate_up_half, summed), [gate_up_sum.shape], 1)
     (mixer_attn_share, in_share_z), summed = ctx_finish(
@@ -1105,9 +1162,9 @@
     )
     mixer_share = mixer_attn_share[: mixer_out.shape[0]]
     attn_share = mixer_attn_share[mixer_out.shape[0] :]
-    (in_share_pre, attn_pair_share, small_share), _ = ctx_finish(
+    (in_share_pre, attn_pair_share), _ = ctx_finish(
         tie(last_half, summed),
-        [in_sum_pre.shape, attn_pair_sum.shape, small_sum.shape],
+        [in_sum_pre.shape, attn_pair_sum.shape],
         3,
     )
     norm_share, conv_w_share, conv_b_share, skip_share, mixer_g_share, ffn_share = unpack_small(

time: 743 us -> 802 us (1.079)
  waiting for transfers between devices: 243 us -> 265 us
  local copies, waits for them, and re-layouts: 77.3 us -> 96.8 us
  other arithmetic: 124 us -> 138 us
    ppermute x2, waiting for transfers between devices: 0.01 us -> 35.7 us  [from_behind(): return lax.ppermute(block, axis, route)]
    ppermute x37 -> x43, waiting for transfers between devices: 108 us -> 82.5 us  [exchange(): return lax.ppermute(block, MESH_AXES, route)]
    all_gather x1, waiting for transfers between devices: 25.4 us -> 11.6 us  [per_device(): lax.all_gather(jnp.concatenate([keys_b, values_b], axis=1).transpose(0, 2...]
    all_gather x2, waiting for transfers between devices: 0.02 us -> 12.9 us  [pass_state(): totals = lax.all_gather(total, 'ctx', axis_index_groups=ctx_lines())]
    unnamed x332 -> x375, local copies, waits for them, and re-layouts: 24.8 us -> 34.4 us
    dot_general x21, matrix products: 44.3 us -> 53.5 us  [split_products(): lax.dot_general(piece, right, (((1 - axis,), (0,)), ((), ())), preferred_...]
    ppermute x37 -> x43, starting transfers between devices: 34.1 us -> 33.4 us  [exchange(): return lax.ppermute(block, MESH_AXES, route)]
  transfers between devices with their start and end apart: 51 -> 56, of which waited for: 16 -> 22; matrix products, arithmetic and copies ran while one was open for 30% -> 35% of each run, Pallas kernels for 13% -> 14%
where the time goes in v5:
time: 802 us; the launch traced here: 792 us
  waiting for transfers between devices  265 us (33%)
  other arithmetic  138 us (17%)
  Pallas kernels  118 us (15%)
  matrix products  106 us (13%)
  local copies, waits for them, and re-layouts  96.8 us (12%)
  starting transfers between devices  49.4 us (6%)
  between operations  19.1 us (2%)
    psum x4, waiting for transfers between devices, ctx_finish(): mine = lax.psum(mine, 'ctx', axis_index_groups=lines)  105 us
    ppermute x43, waiting for transfers between devices, exchange(): return lax.ppermute(block, MESH_AXES, route)  82.5 us
    dot_general x21, matrix products, split_products(): lax.dot_general(piece, right, (((1 - axis,), (0,)), ((), ())), preferred_...  53.5 us
    ppermute x2, waiting for transfers between devices, from_behind(): return lax.ppermute(block, axis, route)  35.7 us
    unnamed x375, local copies, waits for them, and re-layouts  34.4 us
    ppermute x43, starting transfers between devices, exchange(): return lax.ppermute(block, MESH_AXES, route)  33.4 us
    dot_general x6, matrix products, nt_dot(): lax.dot_general(left, right, (((1,), (1,)), ((), ())), preferred_element_...  32.5 us
    pallas_call x1, Pallas kernels, per_device(): attend_backward(group_blocks, pairs, key_side, turned_q, mirrored_q, quer...  31.7 us
  transfers between devices with their start and end apart: 56, of which 22 were waited for; matrix products, arithmetic and copies ran while one was open for 35% of the time, Pallas kernels for 14%

profile of v5, /device:TPU:0, one launch (start us, length us, event | category | flops | bytes accessed | tf_op | source)
XLA Modules:
  0.0 791.7 jit_solution(9166174771469957892)
XLA Ops:
  42.9 12.5 %collective-permute-done.1.refs_4_ = bf16[144,4096]{1,0:T(8,128)(2,1)} collective-permute-done((bf16[144,4096]{1,0:T(8,128)(2,1)}, bf16[144,4096]{1,0:T(8,128)(2,1)}, u32[]{:S(2)}, u32[]{:S(2)}) %collective-permute-start.1) | collective-permute-done | bytes 1179680 | tf_op jit(solution)/shard_map/ppermute | solution.py:35
  65.3 9.9 %collective-permute-done.4.refs_3_ = bf16[64,4096]{1,0:T(8,128)(2,1)S(1)} collective-permute-done((bf16[64,4096]{1,0:T(8,128)(2,1)}, bf16[64,4096]{1,0:T(8,128)(2,1)S(1)}, u32[]{:S(2)}, u32[]{:S(2)}) %collective-permute-start.4) | collective-permute-done | bytes 524320 | tf_op jit(solution)/shard_map/ppermute | solution.py:35
  83.5 7.7 assemble.5
  91.3 4.6 fusion.208
  95.9 3.3 copy-done.75
  101.3 4.0 collective-permute-start.13
  114.4 5.4 multiply_convert_fusion.1
  119.8 5.6 state_outer.2
  135.4 2.8 collective-permute-done.14
  147.7 7.6 collective-permute-done.7.query_b
  155.4 11.6 %all-gather.7.cloned.1.call-done = bf16[16,512,128]{2,1,0:T(8,128)(2,1)} async-done(((bf16[2,512,128]{2,1,0:T(8,128)(2,1)}), bf16[16,512,128]{2,1,0:T(8,128)(2,1)}) %all-gather.7.cloned.1.call-update) | async-done | bytes 2097168 | tf_op jit(solution)/shard_map/all_gather | solution.py:990
  170.3 22.1 %attend_forward.1 = (f32[8,64,256]{2,1,0:T(8,128)S(1)}, f32[8,64,256]{2,1,0:T(8,128)S(1)}, f32[2,2,1,1024]{3,2,1,0:T(1,128)S(1)}) custom-call(s32[2]{0:T(128)S(1)} %copy-done.48, bf16[8,2,512,128]{3,2,1,0:T(8,128)(2,1)S(1)} %bitcast.257, bf16[4096,128]{1,0:T(8,128)(2,1)S(1)} %fusion.33.refs_8_.side_ref, bf16[8,64,512]{2,1,0:T(8,128)(2,1)S(1)} %copy-done.5, ...), custom_call_target="tpu_custom_call" | custom-call | flops 1024 | bytes 1024 | tf_op jit(solution)/shard_map/attend_forward/pallas_call | solution.py:1009
  211.7 10.0 %mixer_forward.1.local_ref = f32[512,1536]{1,0:T(8,128)S(1)} custom-call(f32[12,1,128]{2,1,0:T(1,128)S(1)} %broadcast_in_dim.96.skip_ref, bf16[512,1792]{1,0:T(8,128)(2,1)S(1)} %get-tuple-element.99.left_ref.right_ref.x_ref.b_ref.c_ref, bf16[512,1792]{1,0:T(8,128)(2,1)S(1)} %get-tuple-element.99.left_ref.right_ref.x_ref.b_ref.c_ref, ...), custom_call_target="tpu_custom_call" | custom-call | flops 1024 | bytes 1024 | tf_op jit(solution)/shard_map/mixer_forward/pallas_call | solution.py:1005
  228.2 2.8 assemble.7
  233.5 3.2 assemble.9
  252.2 4.1 assemble.8
  256.3 3.4 copy-done.2
  259.6 4.5 mixer_join.1
  264.2 3.0 multiply_reduce_fusion.6
  273.1 4.6 fusion.210
  277.7 6.5 bitcast_multiply_fusion.1
  284.3 2.6 convolution_convert_fusion.3
  286.9 4.1 add_convert_fusion
  291.1 10.3 %multiply_reduce_fusion.7 = (f32[1024]{0:T(1024)S(1)}, f32[512]{0:T(512)S(1)}, f32[512,1024]{1,0:T(8,128)S(1)}) fusion(f32[512,1024]{1,0:T(8,128)} %copy-done.61, f32[512]{0:T(512)S(1)} %fusion.165, f32[1024]{0:T(1024)S(1)} %bitcast.292, bf16[512,4096]{1,0:T(8,128)(2,1)S(1)} %add_convert_fusion, bf16[1024,4096]{1,0:T(8,128)(2,1)} %copy-done.2), kind=kOutput, calls=%fused_computation.82 | convolution fusion | flops 4298111488 | bytes 16789504 | tf_op jit(solution)/shard_map/dot_general | solution.py:330
  306.4 4.5 convolution_convert_fusion
  319.4 5.4 fusion.192
  339.7 5.6 state_outer.3.refs_1_
  345.3 13.4 %collective-permute-done.22.refs_1_ = bf16[512,1024]{1,0:T(8,128)(2,1)S(1)} collective-permute-done((bf16[512,1024]{1,0:T(8,128)(2,1)S(1)}, bf16[512,1024]{1,0:T(8,128)(2,1)S(1)}, u32[]{:S(2)}, u32[]{:S(2)}) %collective-permute-start.22) | collective-permute-done | bytes 1048608 | tf_op jit(solution)/shard_map/ppermute | solution.py:35
  358.7 3.2 add_convert_fusion.6.refs_0_
  364.8 6.1 fusion.43
  370.9 6.9 collective-permute-done.23.refs_2_
  379.9 3.2 add_convert_fusion.11.refs_0_
  383.1 4.4 collective-permute-done.18
  389.6 2.9 add_convert_fusion.5.refs_0_
  392.6 5.8 add_convert_fusion.2
  399.9 31.7 %attend_backward.1 = (f32[8,64,256]{2,1,0:T(8,128)S(1)}, f32[8,64,256]{2,1,0:T(8,128)S(1)}, bf16[8,2,512,128]{3,2,1,0:T(8,128)(2,1)}) custom-call(s32[2]{0:T(128)S(1)} %copy-done.49, bf16[8,2,512,128]{3,2,1,0:T(8,128)(2,1)} %bitcast.256, bf16[4096,128]{1,0:T(8,128)(2,1)S(1)} %fusion.33.refs_8_.side_ref, bf16[8,64,512]{2,1,0:T(8,128)(2,1)S(1)} %copy-done.6, ...), custom_call_target="tpu_custom_call" | custom-call | flops 1024 | bytes 1024 | tf_op jit(solution)/shard_map/attend_backward/pallas_call | solution.py:1064
  435.8 2.8 collective-permute-start.30
  443.8 8.6 %collective-permute-done.30 = bf16[8,64,256]{2,1,0:T(8,128)(2,1)} collective-permute-done((bf16[8,64,256]{2,1,0:T(8,128)(2,1)}, bf16[8,64,256]{2,1,0:T(8,128)(2,1)}, u32[]{:S(2)}, u32[]{:S(2)}) %collective-permute-start.30) | collective-permute-done | bytes 262176 | tf_op jit(solution)/shard_map/ppermute | solution.py:46
  455.1 3.1 collective-permute-done.48
  461.4 10.3 %all-gather.11.cloned.1.call-done = bf16[6144,128]{1,0:T(8,128)(2,1)} async-done(((bf16[1536,128]{1,0:T(8,128)(2,1)}), bf16[6144,128]{1,0:T(8,128)(2,1)}) %all-gather.11.cloned.1.call-update) | async-done | bytes 1572880 | tf_op jit(solution)/shard_map/all_gather | solution.py:808
  471.7 3.4 convert_element_type.765
  475.1 2.9 collective-permute-done.31
  482.7 5.2 collective-permute-start.32
  487.9 3.0 select_convert_fusion.state_grad_ref
  491.0 3.1 add_convert_fusion.10.refs_0_
  499.7 3.2 add_convert_fusion.4.refs_0_
  502.9 7.1 collective-permute-done.33
  514.0 3.8 fusion.35
  518.0 18.2 %mixer_backward.1 = (f32[512,1792]{1,0:T(8,128)}, f32[12,1,128]{2,1,0:T(1,128)S(1)}) custom-call(f32[12,1,128]{2,1,0:T(1,128)S(1)} %broadcast_in_dim.96.skip_ref, bf16[512,1792]{1,0:T(8,128)(2,1)S(1)} %get-tuple-element.99.left_ref.right_ref.x_ref.b_ref.c_ref, bf16[512,1792]{1,0:T(8,128)(2,1)S(1)} %get-tuple-element.99.left_ref.right_ref.x_ref.b_ref.c_ref, ...), custom_call_target="tpu_custom_call" | custom-call | flops 1024 | bytes 1024 | tf_op jit(solution)/shard_map/mixer_backward/pallas_call | solution.py:1111
  536.3 5.6 multiply_reduce_fusion.3
  543.4 2.9 pad_add_fusion
  546.4 4.0 add_convert_fusion.1
  561.7 35.7 %collective-permute-done.25 = f32[3,1792]{1,0:T(4,128)S(1)} collective-permute-done((f32[3,1792]{1,0:T(4,128)S(1)}, f32[3,1792]{1,0:T(4,128)S(1)}, u32[]{:S(2)}, u32[]{:S(2)}) %collective-permute-start.25) | collective-permute-done | bytes 21536 | tf_op jit(solution)/shard_map/ppermute | solution.py:41
  597.5 3.6 fusion.8.refs_0_
  604.6 4.1 convolution_convert_fusion.2
  608.7 8.8 %fusion.23 = (f32[1024]{0:T(1024)S(1)}, f32[512]{0:T(512)S(1)}, f32[512,1024]{1,0:T(8,128)}) fusion(bf16[1,512,1024]{2,1,0:T(8,128)(2,1)S(1)} %copy-done.72, f32[512]{0:T(512)S(1)} %copy-done.168, f32[1024]{0:T(1024)S(1)} %bitcast.304, f32[512,1024]{1,0:T(8,128)} %fusion.35, bf16[1024,4096]{1,0:T(8,128)(2,1)} %copy-done.3, ...), kind=kOutput, calls=%fused_computation.66 | convolution fusion | flops 3500669440 | bytes 15478784 | tf_op jit(solution)/shard_map/dot_general | solution.py:330
  622.8 3.5 fusion.18
  632.7 4.9 collective-permute-done.37
  637.6 34.0 %all-reduce.23.cloned.1.call-done.refs_1_ = bf16[128,4096]{1,0:T(8,128)(2,1)} async-done(((bf16[128,4096]{1,0:T(8,128)(2,1)}), bf16[128,4096]{1,0:T(8,128)(2,1)}) %all-reduce.23.cloned.1.call-update) | async-done | bytes 1048592 | tf_op jit(solution)/shard_map/psum | solution.py:209
  676.7 4.1 fusion.26
  684.2 37.0 %all-reduce.25.cloned.1.call-done.refs_1_ = bf16[128,3584]{1,0:T(8,128)(2,1)} async-done(((bf16[128,3584]{1,0:T(8,128)(2,1)}), bf16[128,3584]{1,0:T(8,128)(2,1)}) %all-reduce.25.cloned.1.call-update) | async-done | bytes 917520 | tf_op jit(solution)/shard_map/psum | solution.py:209
  725.5 4.2 fusion.30
  729.6 34.4 %all-reduce.27.cloned.1.call-done = bf16[128,2560]{1,0:T(8,128)(2,1)} async-done(((bf16[128,2560]{1,0:T(8,128)(2,1)}), bf16[128,2560]{1,0:T(8,128)(2,1)}) %all-reduce.27.cloned.1.call-update) | async-done | bytes 655376 | tf_op jit(solution)/shard_map/psum | solution.py:209
  770.9 9.8 %collective-permute-done.46 = bf16[128,2560]{1,0:T(8,128)(2,1)S(1)} collective-permute-done((bf16[128,2560]{1,0:T(8,128)(2,1)}, bf16[128,2560]{1,0:T(8,128)(2,1)S(1)}, u32[]{:S(2)}, u32[]{:S(2)}) %collective-permute-start.46) | collective-permute-done | bytes 655392 | tf_op jit(solution)/shard_map/ppermute | solution.py:35
  (729 shorter events, 252.0 us)
Async XLA Ops:
  7.2 159.8 %all-gather.7.cloned.1.call-start = ((), (), s32[]{:S(2)}) async-start(), calls=%async_computation.4 | async-start | bytes 2359296 | tf_op jit(solution)/shard_map/all_gather | solution.py:990
  13.4 63.1 %collective-permute-start = (bf16[272,4096]{1,0:T(8,128)(2,1)S(1)}, bf16[272,4096]{1,0:T(8,128)(2,1)}, u32[]{:S(2)}, u32[]{:S(2)}) collective-permute-start(bf16[272,4096]{1,0:T(8,128)(2,1)S(1)} %fusion.21.refs_0_), channel_id=1, source_target_pairs={{0,1},{1,0},{2,3},{3,2},{4,5},{5,4},{6,7},{7,6},{8,9},{9,8},{10,11... | collective-permute-start | bytes 6684680 | tf_op jit(solution)/shard_map/ppermute | solution.py:35
  14.7 24.6 %copy-start.70 = (bf16[1,512,1024]{2,1,0:T(8,128)(2,1)S(1)}, bf16[1,512,1024]{2,1,0:T(8,128)(2,1)}, u32[]{:S(2)}) copy-start(bf16[1,512,1024]{2,1,0:T(8,128)(2,1)} %param.17) | copy-start | bytes 3145732
  14.7 45.9 %collective-permute-start.3 = (bf16[64,4096]{1,0:T(8,128)(2,1)}, bf16[64,4096]{1,0:T(8,128)(2,1)}, u32[]{:S(2)}, u32[]{:S(2)}) collective-permute-start(bf16[64,4096]{1,0:T(8,128)(2,1)} %constant_dynamic-slice_fusion.15), channel_id=1, source_target_pairs={{0,2},{1,3},{2,0},{3,1},{4,6},{5,7},{6,4},{7,5},{8,10},{9,11},{10,... | collective-permute-start | bytes 1572872 | tf_op jit(solution)/shard_map/ppermute | solution.py:35
  18.4 37.1 %collective-permute-start.1 = (bf16[144,4096]{1,0:T(8,128)(2,1)}, bf16[144,4096]{1,0:T(8,128)(2,1)}, u32[]{:S(2)}, u32[]{:S(2)}) collective-permute-start(bf16[144,4096]{1,0:T(8,128)(2,1)} %slice.486), channel_id=1, source_target_pairs={{0,2},{1,3},{2,0},{3,1},{4,6},{5,7},{6,4},{7,5},{8,10},{9,11},{10,... | collective-permute-start | bytes 3538952 | tf_op jit(solution)/shard_map/ppermute | solution.py:35
  55.4 23.7 %collective-permute-start.2 = (bf16[144,4096]{1,0:T(8,128)(2,1)}, bf16[144,4096]{1,0:T(8,128)(2,1)}, u32[]{:S(2)}, u32[]{:S(2)}) collective-permute-start(bf16[144,4096]{1,0:T(8,128)(2,1)} %collective-permute-done.1.refs_4_), channel_id=1, source_target_pairs={{0,1},{1,0},{2,3},{3,2},{4,5},{5,4},{6,7},{7,6},{8,9},{9,8},{10,11... | collective-permute-start | bytes 3538952 | tf_op jit(solution)/shard_map/ppermute | solution.py:35
  60.6 14.5 %collective-permute-start.4 = (bf16[64,4096]{1,0:T(8,128)(2,1)}, bf16[64,4096]{1,0:T(8,128)(2,1)S(1)}, u32[]{:S(2)}, u32[]{:S(2)}) collective-permute-start(bf16[64,4096]{1,0:T(8,128)(2,1)} %collective-permute-done.3.refs_2_), channel_id=1, source_target_pairs={{0,4},{1,5},{2,6},{3,7},{4,0},{5,1},{6,2},{7,3},{8,12},{9,13},{10,... | collective-permute-start | bytes 1572872 | tf_op jit(solution)/shard_map/ppermute | solution.py:35
  65.0 18.3 %collective-permute-start.5 = (bf16[64,4096]{1,0:T(8,128)(2,1)}, bf16[64,4096]{1,0:T(8,128)(2,1)S(1)}, u32[]{:S(2)}, u32[]{:S(2)}) collective-permute-start(bf16[64,4096]{1,0:T(8,128)(2,1)} %collective-permute-done.3.refs_2_), channel_id=1, source_target_pairs={{0,1},{1,0},{2,3},{3,2},{4,5},{5,4},{6,7},{7,6},{8,9},{9,8},{10,11... | collective-permute-start | bytes 1572872 | tf_op jit(solution)/shard_map/ppermute | solution.py:35
  75.1 8.3 %collective-permute-start.6 = (bf16[64,4096]{1,0:T(8,128)(2,1)S(1)}, bf16[64,4096]{1,0:T(8,128)(2,1)S(1)}, u32[]{:S(2)}, u32[]{:S(2)}) collective-permute-start(bf16[64,4096]{1,0:T(8,128)(2,1)S(1)} %collective-permute-done.4.refs_3_), channel_id=1, source_target_pairs={{0,1},{1,0},{2,3},{3,2},{4,5},{5,4},{6,7},{7,6},{8,9},{9,8},{10,11... | collective-permute-start | bytes 1572872 | tf_op jit(solution)/shard_map/ppermute | solution.py:35
  75.1 80.2 %collective-permute-start.8 = (bf16[1024,1024]{1,0:T(8,128)(2,1)}, bf16[1024,1024]{1,0:T(8,128)(2,1)}, u32[]{:S(2)}, u32[]{:S(2)}) collective-permute-start(bf16[1024,1024]{1,0:T(8,128)(2,1)} %pad_maximum_fusion.1.refs_0_), channel_id=1, source_target_pairs={{0,1},{1,0},{2,3},{3,2},{4,5},{5,4},{6,7},{7,6},{8,9},{9,8},{10,11... | collective-permute-start | bytes 6291464 | tf_op jit(solution)/shard_map/ppermute | solution.py:35
  76.5 118.0 %collective-permute-start.11 = (bf16[1024,1024]{1,0:T(8,128)(2,1)}, bf16[1024,1024]{1,0:T(8,128)(2,1)}, u32[]{:S(2)}, u32[]{:S(2)}) collective-permute-start(bf16[1024,1024]{1,0:T(8,128)(2,1)} %pad_maximum_fusion.1.refs_0_), channel_id=1, source_target_pairs={{0,2},{1,3},{2,0},{3,1},{4,6},{5,7},{6,4},{7,5},{8,10},{9,11},{10,... | collective-permute-start | bytes 6291464 | tf_op jit(solution)/shard_map/ppermute | solution.py:35
  79.2 76.2 %collective-permute-start.9 = (bf16[256,4096]{1,0:T(8,128)(2,1)}, bf16[256,4096]{1,0:T(8,128)(2,1)}, u32[]{:S(2)}, u32[]{:S(2)}) collective-permute-start(bf16[256,4096]{1,0:T(8,128)(2,1)} %refs_0_), channel_id=1, source_target_pairs={{0,1},{1,0},{2,3},{3,2},{4,5},{5,4},{6,7},{7,6},{8,9},{9,8},{10,11... | collective-permute-start | bytes 6291464 | tf_op jit(solution)/shard_map/ppermute | solution.py:35
  101.3 12.0 %collective-permute-start.13 = (bf16[3,1792]{1,0:T(4,128)(2,1)}, bf16[3,1792]{1,0:T(4,128)(2,1)}, u32[]{:S(2)}, u32[]{:S(2)}) collective-permute-start(bf16[3,1792]{1,0:T(4,128)(2,1)} %slice.500), channel_id=1, source_target_pairs={{0,4},{4,8},{8,12},{12,16},{16,20},{20,24},{24,28},{1,5},{5,9},{9,... | collective-permute-start | bytes 32264 | tf_op jit(solution)/shard_map/ppermute | solution.py:41
  109.6 133.8 %all-gather.9.cloned.1.call-start = ((), (), s32[]{:S(2)}) async-start(), calls=%async_computation.5 | async-start | bytes 1986560 | tf_op jit(solution)/shard_map/all_gather | solution.py:808
  126.2 12.1 %collective-permute-start.14 = (bf16[1552,128]{1,0:T(8,128)(2,1)}, bf16[1552,128]{1,0:T(8,128)(2,1)}, u32[]{:S(2)}, u32[]{:S(2)}) collective-permute-start(bf16[1552,128]{1,0:T(8,128)(2,1)} %pad_maximum_fusion.10), channel_id=1, source_target_pairs={{0,4},{1,5},{2,6},{3,7},{4,0},{5,1},{6,2},{7,3},{8,12},{9,13},{10,... | collective-permute-start | bytes 1191944 | tf_op jit(solution)/shard_map/ppermute | solution.py:35
  127.1 98.9 %collective-permute-start.15 = (bf16[256,4096]{1,0:T(8,128)(2,1)}, bf16[256,4096]{1,0:T(8,128)(2,1)}, u32[]{:S(2)}, u32[]{:S(2)}) collective-permute-start(bf16[256,4096]{1,0:T(8,128)(2,1)} %refs_0_), channel_id=1, source_target_pairs={{0,2},{1,3},{2,0},{3,1},{4,6},{5,7},{6,4},{7,5},{8,10},{9,11},{10,... | collective-permute-start | bytes 6291464 | tf_op jit(solution)/shard_map/ppermute | solution.py:35
  138.3 17.1 %collective-permute-start.7 = (bf16[8,64,256]{2,1,0:T(8,128)(2,1)}, bf16[8,64,256]{2,1,0:T(8,128)(2,1)}, u32[]{:S(2)}, u32[]{:S(2)}) collective-permute-start(bf16[8,64,256]{2,1,0:T(8,128)(2,1)} %slice.497), channel_id=1, source_target_pairs={{0,28},{4,24},{8,20},{12,16},{16,12},{20,8},{24,4},{28,0},{1,29},{... | collective-permute-start | bytes 786440 | tf_op jit(solution)/shard_map/ppermute | solution.py:46
  194.6 33.6 %collective-permute-start.12 = (bf16[1024,1024]{1,0:T(8,128)(2,1)}, bf16[1024,1024]{1,0:T(8,128)(2,1)}, u32[]{:S(2)}, u32[]{:S(2)}) collective-permute-start(bf16[1024,1024]{1,0:T(8,128)(2,1)} %collective-permute-done.11.refs_2_), channel_id=1, source_target_pairs={{0,1},{1,0},{2,3},{3,2},{4,5},{5,4},{6,7},{7,6},{8,9},{9,8},{10,11... | collective-permute-start | bytes 6291464 | tf_op jit(solution)/shard_map/ppermute | solution.py:35
  195.4 243.3 %all-reduce.21.cloned.1.call-start = ((), (), s32[]{:S(2)}) async-start(), calls=%async_computation | async-start | bytes 1048576 | tf_op jit(solution)/shard_map/psum | solution.py:209
  203.3 23.1 %collective-permute-start.10 = (bf16[8,64,256]{2,1,0:T(8,128)(2,1)}, bf16[8,64,256]{2,1,0:T(8,128)(2,1)}, u32[]{:S(2)}, u32[]{:S(2)}) collective-permute-start(bf16[8,64,256]{2,1,0:T(8,128)(2,1)} %convert_element_type.640), channel_id=1, source_target_pairs={{0,28},{4,24},{8,20},{12,16},{16,12},{20,8},{24,4},{28,0},{1,29},{... | collective-permute-start | bytes 786440 | tf_op jit(solution)/shard_map/ppermute | solution.py:46
  211.7 89.8 %copy-start.143 = (f32[1,2,4,128]{3,1,2,0:T(2,128)}, f32[1,2,4,128]{3,1,2,0:T(2,128)S(1)}, u32[]{:S(2)}) copy-start(f32[1,2,4,128]{3,1,2,0:T(2,128)S(1)} %copy.108) | copy-start | bytes 12292
  226.1 26.1 %collective-permute-start.16 = (bf16[256,4096]{1,0:T(8,128)(2,1)}, bf16[256,4096]{1,0:T(8,128)(2,1)}, u32[]{:S(2)}, u32[]{:S(2)}) collective-permute-start(bf16[256,4096]{1,0:T(8,128)(2,1)} %collective-permute-done.15.refs_2_), channel_id=1, source_target_pairs={{0,1},{1,0},{2,3},{3,2},{4,5},{5,4},{6,7},{7,6},{8,9},{9,8},{10,11... | collective-permute-start | bytes 6291464 | tf_op jit(solution)/shard_map/ppermute | solution.py:35
  270.9 30.5 %copy-start.162 = (f32[512]{0:T(512)}, f32[512]{0:T(512)S(1)}, u32[]{:S(2)}) copy-start(f32[512]{0:T(512)S(1)} %fusion.165) | copy-start | bytes 6148
  286.9 43.7 %collective-permute-start.17 = (bf16[1024,1024]{1,0:T(8,128)(2,1)}, bf16[1024,1024]{1,0:T(8,128)(2,1)}, u32[]{:S(2)}, u32[]{:S(2)}) collective-permute-start(bf16[1024,1024]{1,0:T(8,128)(2,1)} %convolution_convert_fusion.3), channel_id=1, source_target_pairs={{0,1},{1,0},{2,3},{3,2},{4,5},{5,4},{6,7},{7,6},{8,9},{9,8},{10,11... | collective-permute-start | bytes 6291464 | tf_op jit(solution)/shard_map/ppermute | solution.py:35
  310.8 81.8 %collective-permute-start.19 = (bf16[512,4096]{1,0:T(8,128)(2,1)}, bf16[512,4096]{1,0:T(8,128)(2,1)}, u32[]{:S(2)}, u32[]{:S(2)}) collective-permute-start(bf16[512,4096]{1,0:T(8,128)(2,1)} %convolution_convert_fusion), channel_id=1, source_target_pairs={{0,1},{1,0},{2,3},{3,2},{4,5},{5,4},{6,7},{7,6},{8,9},{9,8},{10,11... | collective-permute-start | bytes 12582920 | tf_op jit(solution)/shard_map/ppermute | solution.py:35
  315.6 74.0 %collective-permute-start.24 = (bf16[1024,1024]{1,0:T(8,128)(2,1)}, bf16[1024,1024]{1,0:T(8,128)(2,1)}, u32[]{:S(2)}, u32[]{:S(2)}) collective-permute-start(bf16[1024,1024]{1,0:T(8,128)(2,1)} %pad_maximum_fusion.2), channel_id=1, source_target_pairs={{0,1},{1,0},{2,3},{3,2},{4,5},{5,4},{6,7},{7,6},{8,9},{9,8},{10,11... | collective-permute-start | bytes 6291464 | tf_op jit(solution)/shard_map/ppermute | solution.py:35
  317.1 82.7 %collective-permute-start.27 = (bf16[8,64,256]{2,1,0:T(8,128)(2,1)}, bf16[8,64,256]{2,1,0:T(8,128)(2,1)}, u32[]{:S(2)}, u32[]{:S(2)}) collective-permute-start(bf16[8,64,256]{2,1,0:T(8,128)(2,1)} %slice.536), channel_id=1, source_target_pairs={{0,28},{4,24},{8,20},{12,16},{16,12},{20,8},{24,4},{28,0},{1,29},{... | collective-permute-start | bytes 786440 | tf_op jit(solution)/shard_map/ppermute | solution.py:46
  327.1 52.8 %collective-permute-start.21 = (bf16[512,1536]{1,0:T(8,128)(2,1)}, bf16[512,1536]{1,0:T(8,128)(2,1)}, u32[]{:S(2)}, u32[]{:S(2)}) collective-permute-start(bf16[512,1536]{1,0:T(8,128)(2,1)} %convolution_convert_fusion.1), channel_id=1, source_target_pairs={{0,1},{1,0},{2,3},{3,2},{4,5},{5,4},{6,7},{7,6},{8,9},{9,8},{10,11... | collective-permute-start | bytes 4718600 | tf_op jit(solution)/shard_map/ppermute | solution.py:35
  333.2 25.5 %collective-permute-start.22 = (bf16[512,1024]{1,0:T(8,128)(2,1)S(1)}, bf16[512,1024]{1,0:T(8,128)(2,1)S(1)}, u32[]{:S(2)}, u32[]{:S(2)}) collective-permute-start(bf16[512,1024]{1,0:T(8,128)(2,1)S(1)} %add_convert_fusion.7), channel_id=1, source_target_pairs={{0,2},{1,3},{2,0},{3,1},{4,6},{5,7},{6,4},{7,5},{8,10},{9,11},{10,... | collective-permute-start | bytes 3145736 | tf_op jit(solution)/shard_map/ppermute | solution.py:35
  364.3 13.4 %collective-permute-start.23 = (bf16[128,2048]{1,0:T(8,128)(2,1)S(1)}, bf16[128,2048]{1,0:T(8,128)(2,1)S(1)}, u32[]{:S(2)}, u32[]{:S(2)}) collective-permute-start(bf16[128,2048]{1,0:T(8,128)(2,1)S(1)} %fusion.81), channel_id=1, source_target_pairs={{0,4},{1,5},{2,6},{3,7},{4,0},{5,1},{6,2},{7,3},{8,12},{9,13},{10,... | collective-permute-start | bytes 1572872 | tf_op jit(solution)/shard_map/ppermute | solution.py:35
  377.8 9.7 %collective-permute-start.18 = (bf16[1536,128]{1,0:T(8,128)(2,1)S(1)}, bf16[1536,128]{1,0:T(8,128)(2,1)}, u32[]{:S(2)}, u32[]{:S(2)}) collective-permute-start(bf16[1536,128]{1,0:T(8,128)(2,1)S(1)} %copy-done.9), channel_id=1, source_target_pairs={{0,4},{1,5},{2,6},{3,7},{4,0},{5,1},{6,2},{7,3},{8,12},{9,13},{10,... | collective-permute-start | bytes 1179656 | tf_op jit(solution)/shard_map/ppermute | solution.py:35
  379.8 91.9 %all-gather.11.cloned.1.call-start = ((), (), s32[]{:S(2)}) async-start(), calls=%async_computation.6 | async-start | bytes 1966080 | tf_op jit(solution)/shard_map/all_gather | solution.py:808
  389.6 282.1 %all-reduce.23.cloned.1.call-start = ((), (), s32[]{:S(2)}) async-start(), calls=%async_computation.1 | async-start | bytes 2097152 | tf_op jit(solution)/shard_map/psum | solution.py:209
  398.4 119.5 %collective-permute-start.20 = (bf16[256,4096]{1,0:T(8,128)(2,1)}, bf16[256,4096]{1,0:T(8,128)(2,1)}, u32[]{:S(2)}, u32[]{:S(2)}) collective-permute-start(bf16[256,4096]{1,0:T(8,128)(2,1)} %add_convert_fusion.2), channel_id=1, source_target_pairs={{0,2},{1,3},{2,0},{3,1},{4,6},{5,7},{6,4},{7,5},{8,10},{9,11},{10,... | collective-permute-start | bytes 6291464 | tf_op jit(solution)/shard_map/ppermute | solution.py:35
  433.2 66.5 %collective-permute-start.29 = (bf16[512,1024]{1,0:T(8,128)(2,1)}, bf16[512,1024]{1,0:T(8,128)(2,1)}, u32[]{:S(2)}, u32[]{:S(2)}) collective-permute-start(bf16[512,1024]{1,0:T(8,128)(2,1)} %tie.13), channel_id=1, source_target_pairs={{0,2},{1,3},{2,0},{3,1},{4,6},{5,7},{6,4},{7,5},{8,10},{9,11},{10,... | collective-permute-start | bytes 3145736 | tf_op jit(solution)/shard_map/ppermute | solution.py:35
  435.8 16.6 %collective-permute-start.30 = (bf16[8,64,256]{2,1,0:T(8,128)(2,1)}, bf16[8,64,256]{2,1,0:T(8,128)(2,1)}, u32[]{:S(2)}, u32[]{:S(2)}) collective-permute-start(bf16[8,64,256]{2,1,0:T(8,128)(2,1)} %fusion.86), channel_id=1, source_target_pairs={{0,28},{4,24},{8,20},{12,16},{16,12},{20,8},{24,4},{28,0},{1,29},{... | collective-permute-start | bytes 786440 | tf_op jit(solution)/shard_map/ppermute | solution.py:46
  438.6 19.5 %collective-permute-start.48 = (bf16[128,2048]{1,0:T(8,128)(2,1)}, bf16[128,2048]{1,0:T(8,128)(2,1)}, u32[]{:S(2)}, u32[]{:S(2)}) collective-permute-start(bf16[128,2048]{1,0:T(8,128)(2,1)} %all-reduce.21.cloned.1.call-done.refs_1_), channel_id=1, source_target_pairs={{0,4},{1,5},{2,6},{3,7},{4,0},{5,1},{6,2},{7,3},{8,12},{9,13},{10,... | collective-permute-start | bytes 1572872 | tf_op jit(solution)/shard_map/ppermute | solution.py:35
  442.7 35.3 %collective-permute-start.31 = (bf16[4,2,512,128]{3,2,1,0:T(8,128)(2,1)}, bf16[4,2,512,128]{3,2,1,0:T(8,128)(2,1)}, u32[]{:S(2)}, u32[]{:S(2)}) collective-permute-start(bf16[4,2,512,128]{3,2,1,0:T(8,128)(2,1)} %dynamic-slice_bitcast_fusion), channel_id=1, source_target_pairs={{0,4},{1,5},{2,6},{3,7},{4,0},{5,1},{6,2},{7,3},{8,12},{9,13},{10,... | collective-permute-start | bytes 3145736 | tf_op jit(solution)/shard_map/ppermute | solution.py:35
  452.4 38.6 %collective-permute-start.28 = (bf16[256,1536]{1,0:T(8,128)(2,1)}, bf16[256,1536]{1,0:T(8,128)(2,1)}, u32[]{:S(2)}, u32[]{:S(2)}) collective-permute-start(bf16[256,1536]{1,0:T(8,128)(2,1)} %tie.12), channel_id=1, source_target_pairs={{0,2},{1,3},{2,0},{3,1},{4,6},{5,7},{6,4},{7,5},{8,10},{9,11},{10,... | collective-permute-start | bytes 2359304 | tf_op jit(solution)/shard_map/ppermute | solution.py:35
  482.7 14.7 %collective-permute-start.32 = (bf16[2,2,512,128]{2,3,1,0:T(8,128)(2,1)}, bf16[2,2,512,128]{2,3,1,0:T(8,128)(2,1)}, u32[]{:S(2)}, u32[]{:S(2)}) collective-permute-start(bf16[2,2,512,128]{2,3,1,0:T(8,128)(2,1)} %bitcast.90), channel_id=1, source_target_pairs={{0,8},{1,9},{2,10},{3,11},{4,12},{5,13},{6,14},{7,15},{8,0},{9,1},... | collective-permute-start | bytes 1572872 | tf_op jit(solution)/shard_map/ppermute | solution.py:35
  498.8 11.2 %collective-permute-start.33 = (bf16[1,2,512,128]{2,3,1,0:T(8,128)(2,1)S(1)}, bf16[1,2,512,128]{2,3,1,0:T(8,128)(2,1)S(1)}, u32[]{:S(2)}, u32[]{:S(2)}) collective-permute-start(bf16[1,2,512,128]{2,3,1,0:T(8,128)(2,1)S(1)} %constant_dynamic-slice_fusion.1), channel_id=1, source_target_pairs={{0,16},{1,17},{2,18},{3,19},{4,20},{5,21},{6,22},{7,23},{8,24},{9,... | collective-permute-start | bytes 786440 | tf_op jit(solution)/shard_map/ppermute | solution.py:35
  511.8 89.4 %collective-permute-start.43 = (bf16[512,768]{1,0:T(8,128)(2,1)}, bf16[512,768]{1,0:T(8,128)(2,1)}, u32[]{:S(2)}, u32[]{:S(2)}) collective-permute-start(bf16[512,768]{1,0:T(8,128)(2,1)} %convolution_convert_fusion.5), channel_id=1, source_target_pairs={{0,1},{1,0},{2,3},{3,2},{4,5},{5,4},{6,7},{7,6},{8,9},{9,8},{10,11... | collective-permute-start | bytes 2359304 | tf_op jit(solution)/shard_map/ppermute | solution.py:35
  551.4 52.1 %collective-permute-start.26 = (bf16[128,4096]{1,0:T(8,128)(2,1)}, bf16[128,4096]{1,0:T(8,128)(2,1)S(1)}, u32[]{:S(2)}, u32[]{:S(2)}) collective-permute-start(bf16[128,4096]{1,0:T(8,128)(2,1)} %constant_dynamic-slice_fusion.4), channel_id=1, source_target_pairs={{0,4},{1,5},{2,6},{3,7},{4,0},{5,1},{6,2},{7,3},{8,12},{9,13},{10,... | collective-permute-start | bytes 3145736 | tf_op jit(solution)/shard_map/ppermute | solution.py:35
  557.5 69.0 %collective-permute-start.39 = (bf16[128,3584]{1,0:T(8,128)(2,1)}, bf16[128,3584]{1,0:T(8,128)(2,1)}, u32[]{:S(2)}, u32[]{:S(2)}) collective-permute-start(bf16[128,3584]{1,0:T(8,128)(2,1)} %constant_dynamic-slice_fusion), channel_id=1, source_target_pairs={{0,4},{1,5},{2,6},{3,7},{4,0},{5,1},{6,2},{7,3},{8,12},{9,13},{10,... | collective-permute-start | bytes 2752520 | tf_op jit(solution)/shard_map/ppermute | solution.py:35
  559.6 37.9 %collective-permute-start.25 = (f32[3,1792]{1,0:T(4,128)S(1)}, f32[3,1792]{1,0:T(4,128)S(1)}, u32[]{:S(2)}, u32[]{:S(2)}) collective-permute-start(f32[3,1792]{1,0:T(4,128)S(1)} %pad_add_fusion.1), channel_id=1, source_target_pairs={{4,0},{8,4},{12,8},{16,12},{20,16},{24,20},{28,24},{5,1},{9,5},{13... | collective-permute-start | bytes 64520 | tf_op jit(solution)/shard_map/ppermute | solution.py:41
  561.7 39.4 %copy-start.122 = (bf16[8,64,512]{2,1,0:T(8,128)(2,1)S(1)}, bf16[8,64,512]{2,1,0:T(8,128)(2,1)}, u32[]{:S(2)}) copy-start(bf16[8,64,512]{2,1,0:T(8,128)(2,1)} %pad_maximum_fusion.9) | copy-start | bytes 1572868
  561.7 39.4 %copy-start.134 = (bf16[2,64,512]{2,1,0:T(8,128)(2,1)S(1)}, bf16[2,64,512]{2,1,0:T(8,128)(2,1)}, u32[]{:S(2)}) copy-start(bf16[2,64,512]{2,1,0:T(8,128)(2,1)} %copy-done.133) | copy-start | bytes 393220
  603.4 25.6 %collective-permute-start.44 = (bf16[256,768]{1,0:T(8,128)(2,1)}, bf16[256,768]{1,0:T(8,128)(2,1)}, u32[]{:S(2)}, u32[]{:S(2)}) collective-permute-start(bf16[256,768]{1,0:T(8,128)(2,1)} %add_convert_fusion.15), channel_id=1, source_target_pairs={{0,2},{1,3},{2,0},{3,1},{4,6},{5,7},{6,4},{7,5},{8,10},{9,11},{10,... | collective-permute-start | bytes 1179656 | tf_op jit(solution)/shard_map/ppermute | solution.py:35
  608.7 14.1 %collective-permute-start.41 = (bf16[512,1792]{1,0:T(8,128)(2,1)}, bf16[512,1792]{1,0:T(8,128)(2,1)}, u32[]{:S(2)}, u32[]{:S(2)}) collective-permute-start(bf16[512,1792]{1,0:T(8,128)(2,1)} %convolution_convert_fusion.2), channel_id=1, source_target_pairs={{0,1},{1,0},{2,3},{3,2},{4,5},{5,4},{6,7},{7,6},{8,9},{9,8},{10,11... | collective-permute-start | bytes 5505032 | tf_op jit(solution)/shard_map/ppermute | solution.py:35
  617.8 3.1 collective-permute-start.34
  620.8 100.4 %all-reduce.25.cloned.1.call-start = ((), (), s32[]{:S(2)}) async-start(), calls=%async_computation.2 | async-start | bytes 1835008 | tf_op jit(solution)/shard_map/psum | solution.py:209
  620.9 8.0 %collective-permute-start.35 = (f32[128,128]{1,0:T(8,128)S(1)}, f32[128,128]{1,0:T(8,128)S(1)}, u32[]{:S(2)}, u32[]{:S(2)}) collective-permute-start(f32[128,128]{1,0:T(8,128)S(1)} %add.770), channel_id=1, source_target_pairs={{0,2},{1,3},{2,0},{3,1},{4,6},{5,7},{6,4},{7,5},{8,10},{9,11},{10,... | collective-permute-start | bytes 196616 | tf_op jit(solution)/shard_map/ppermute | solution.py:35
  626.2 45.5 %collective-permute-start.42 = (bf16[256,1792]{1,0:T(8,128)(2,1)}, bf16[256,1792]{1,0:T(8,128)(2,1)}, u32[]{:S(2)}, u32[]{:S(2)}) collective-permute-start(bf16[256,1792]{1,0:T(8,128)(2,1)} %fusion.18), channel_id=1, source_target_pairs={{0,2},{1,3},{2,0},{3,1},{4,6},{5,7},{6,4},{7,5},{8,10},{9,11},{10,... | collective-permute-start | bytes 2752520 | tf_op jit(solution)/shard_map/ppermute | solution.py:35
  628.9 3.8 collective-permute-start.36
  630.2 41.6 %copy-start.79 = (bf16[512,1792]{1,0:T(8,128)(2,1)S(1)}, bf16[512,1792]{1,0:T(8,128)(2,1)}, u32[]{:S(2)}) copy-start(bf16[512,1792]{1,0:T(8,128)(2,1)} %tie.14) | copy-start | bytes 5505028
  632.7 5.0 collective-permute-start.37
  637.6 43.1 %collective-permute-start.38 = (f32[32,128]{1,0:T(8,128)S(1)}, f32[32,128]{1,0:T(8,128)S(1)}, u32[]{:S(2)}, u32[]{:S(2)}) collective-permute-start(f32[32,128]{1,0:T(8,128)S(1)} %add.774), channel_id=1, source_target_pairs={{0,16},{1,17},{2,18},{3,19},{4,20},{5,21},{6,22},{7,23},{8,24},{9,... | collective-permute-start | bytes 49160 | tf_op jit(solution)/shard_map/ppermute | solution.py:35
  671.7 92.3 %all-reduce.27.cloned.1.call-start = ((), (), s32[]{:S(2)}) async-start(), calls=%async_computation.3 | async-start | bytes 1310720 | tf_op jit(solution)/shard_map/psum | solution.py:209
  675.2 47.5 %collective-permute-start.45 = (bf16[128,2560]{1,0:T(8,128)(2,1)}, bf16[128,2560]{1,0:T(8,128)(2,1)}, u32[]{:S(2)}, u32[]{:S(2)}) collective-permute-start(bf16[128,2560]{1,0:T(8,128)(2,1)} %fusion.78), channel_id=1, source_target_pairs={{0,4},{1,5},{2,6},{3,7},{4,0},{5,1},{6,2},{7,3},{8,12},{9,13},{10,... | collective-permute-start | bytes 1966088 | tf_op jit(solution)/shard_map/ppermute | solution.py:35
  676.7 46.0 %copy-start.91 = (bf16[256,1792]{1,0:T(8,128)(2,1)S(1)}, bf16[256,1792]{1,0:T(8,128)(2,1)}, u32[]{:S(2)}) copy-start(bf16[256,1792]{1,0:T(8,128)(2,1)} %copy-done.90) | copy-start | bytes 2752516
  682.0 43.5 %collective-permute-start.47 = (bf16[128,4096]{1,0:T(8,128)(2,1)S(1)}, bf16[128,4096]{1,0:T(8,128)(2,1)}, u32[]{:S(2)}, u32[]{:S(2)}) collective-permute-start(bf16[128,4096]{1,0:T(8,128)(2,1)S(1)} %copy-done.89), channel_id=1, source_target_pairs={{0,4},{1,5},{2,6},{3,7},{4,0},{5,1},{6,2},{7,3},{8,12},{9,13},{10,... | collective-permute-start | bytes 3145736 | tf_op jit(solution)/shard_map/ppermute | solution.py:35
  721.2 44.3 %collective-permute-start.40 = (bf16[128,3584]{1,0:T(8,128)(2,1)}, bf16[128,3584]{1,0:T(8,128)(2,1)}, u32[]{:S(2)}, u32[]{:S(2)}) collective-permute-start(bf16[128,3584]{1,0:T(8,128)(2,1)} %all-reduce.25.cloned.1.call-done.refs_1_), channel_id=1, source_target_pairs={{0,4},{1,5},{2,6},{3,7},{4,0},{5,1},{6,2},{7,3},{8,12},{9,13},{10,... | collective-permute-start | bytes 2752520 | tf_op jit(solution)/shard_map/ppermute | solution.py:35
  725.4 40.1 %copy-start.92 = (bf16[128,3584]{1,0:T(8,128)(2,1)S(1)}, bf16[128,3584]{1,0:T(8,128)(2,1)}, u32[]{:S(2)}) copy-start(bf16[128,3584]{1,0:T(8,128)(2,1)} %all-reduce.25.cloned.1.call-done.refs_1_) | copy-start | bytes 2752516
  764.0 16.7 %collective-permute-start.46 = (bf16[128,2560]{1,0:T(8,128)(2,1)}, bf16[128,2560]{1,0:T(8,128)(2,1)S(1)}, u32[]{:S(2)}, u32[]{:S(2)}) collective-permute-start(bf16[128,2560]{1,0:T(8,128)(2,1)} %all-reduce.27.cloned.1.call-done), channel_id=1, source_target_pairs={{0,4},{1,5},{2,6},{3,7},{4,0},{5,1},{6,2},{7,3},{8,12},{9,13},{10,... | collective-permute-start | bytes 1966088 | tf_op jit(solution)/shard_map/ppermute | solution.py:35
  (179 other events, 1248.5 us)
Sparse Core Ops, SparseCore 0:
  109.7 57.1 all-gather.6
  195.5 47.8 all-gather.8
  379.9 41.3 all-reduce.20
  423.4 48.2 all-gather.10
  620.9 50.7 all-reduce.22
  674.0 47.1 all-reduce.24
  724.9 39.0 all-reduce.26

commit v6 on v5

--- a/solution.py
+++ b/solution.py
@@ -190,8 +190,9 @@
     side = lax.axis_index("ctx") % 2
     whole = lay_side_by_side(blocks, rows)
     half = rows // 2
-    got = exchange(lax.dynamic_slice_in_dim(whole, (1 - side) * half, half, 0), 1, 0)
-    return add_low(lax.dynamic_slice_in_dim(whole, side * half, half, 0), got), got
+    give = lax.dynamic_slice_in_dim(whole, (1 - side) * half, half, 0)
+    got = exchange(give, 1, 0)
+    return add_low(lax.dynamic_slice_in_dim(whole, side * half, half, 0), got), got, give
 
 
 def ctx_lines():
@@ -225,12 +226,12 @@
     return jnp.concatenate([piece(1), piece(3)], axis=axis), piece(2), piece(0)
 
 
-def shard_sum(beside, across, own, after=None):
+def shard_sum(beside, across, own):
     rows = own.shape[0]
     got = exchange(beside.astype(jnp.bfloat16), 0, 1)
-    across = add_low(across, got[rows:])
-    got_across = exchange(across if after is None else tie(across, after), 0, 2)
-    return add_low(own, got[:rows], got_across), got, got_across
+    sent = add_low(across, got[rows:])
+    got_across = exchange(sent, 0, 2)
+    return add_low(own, got[:rows], got_across), got, got_across, sent
 
 
 def split_products(left, right, axis=1):
@@ -242,8 +243,20 @@
     ]
 
 
-def weight_grad(left, right, after=None):
-    return shard_sum(*split_products(left, right), after)
+def weight_grad(left, right):
+    return shard_sum(*split_products(left, right))
+
+
+def start_sum(beside, across, own, after):
+    rows = own.shape[0]
+    got = exchange(beside.astype(jnp.bfloat16), 0, 1)
+    got_across = exchange(tie(add_low(across, got[rows:]), after), 0, 2)
+    return own, got, got_across
+
+
+def finish_sum(started, after):
+    own, got, got_across = started
+    return add_low(own, got[: own.shape[0]], tie(got_across, after))
 
 
 def sum_small(value):
@@ -258,14 +271,17 @@
     return value
 
 
-def scatter_blocks(blocks):
+def scatter_blocks(blocks, after):
     position, bit = lax.axis_index("ctx"), 1
     while blocks.shape[0] > 1:
         up = (position // bit) % 2
         halves = blocks.reshape((blocks.shape[0] // 2, 2) + blocks.shape[1:])
         keep = lax.dynamic_index_in_dim(halves, up, 1, keepdims=False)
         give = lax.dynamic_index_in_dim(halves, 1 - up, 1, keepdims=False)
-        blocks = add_low(keep, exchange(give, bit, 0))
+        got = exchange(give, bit, 0)
+        if bit == 1:
+            got = tie(got, after)
+        blocks = add_low(keep, got)
         bit *= 2
     return blocks[0]
 
@@ -817,7 +833,7 @@
         entering = entering + jnp.where(reached, factor, 0.0)[:, None, None] * totals[at]
         factor = factor * jnp.where(reached, line_gains[at], 1.0)
     state = jnp.where(is_first, entering, first_gain * entering + first)
-    return state.astype(jnp.bfloat16).reshape(DSSM, NS), (gain, other, line_gains)
+    return state.astype(jnp.bfloat16).reshape(DSSM, NS), (gain, other, line_gains), total
 
 
 def pack_small(norm, conv_weight, conv_bias, skip, mixer, ffn, shards):
@@ -881,7 +897,7 @@
     sequence_total = rows * count
     heads_per_group = QUERY_HEADS // KEY_VALUE_HEADS
     scale = HEAD_SIZE ** (-0.5)
-    attend_forward, attend_backward = attention_calls(rows, count, (2, 2))
+    attend_forward, attend_backward = attention_calls(rows, count, (3, 3))
     state_outer, mixer_join, mixer_forward, mixer_backward = mixer_calls(rows, 4)
 
     lengths = doc_lengths[0]
@@ -1001,7 +1017,7 @@
     conv_b16 = conv_f.astype(jnp.bfloat16)
     skip_wide = jnp.repeat(skip_w, PM).reshape(HM // 2, 1, 2 * PM)
     fresh = state_outer(DSSM // NS, 4, 0)(mixer_rows, conv_b16, conv_b16)
-    state_in, gains = pass_state(fresh, carry_gain, None, False, pairs)
+    state_in, gains, _ = pass_state(fresh, carry_gain, None, False, pairs)
     local = mixer_forward(
         skip_wide, conv_b16, conv_b16, conv_b16, mixer_rows, docs_column, docs_row
     )
@@ -1015,6 +1031,7 @@
         query_side,
         out_pieces[1],
         gate_up_pieces[1],
+        local,
     )
     mixer_w, attn_w, down_w = finish_shards(
         out_pieces,
@@ -1042,11 +1059,11 @@
     layer_out = (middle + mixed_dot(activated_b, down_w)).astype(jnp.bfloat16)
 
     out_low = cotangent[0]
-    down_sum, down_beside, down_across = weight_grad(activated_b, out_low)
+    down_sum, down_beside, down_across, _ = weight_grad(activated_b, out_low)
     (gate_up_grad_v,) = act_pull(nt_dot(out_low, down_w))
     gate_up_low = gate_up_grad_v.astype(jnp.bfloat16)
-    gate_up_sum, gate_up_beside, gate_up_across = weight_grad(normed2_b, gate_up_low)
-    gate_up_half, gate_up_got = ctx_half([gate_up_sum], model // shards)
+    gate_up_sum, gate_up_beside, _, gate_up_sent = weight_grad(normed2_b, gate_up_low)
+    gate_up_half, gate_up_got, gate_up_give = ctx_half([gate_up_sum], model // shards)
     middle_norm_grad, ffn_gain_grad = ffn_pull(nt_dot(gate_up_low, gate_up_w))
     middle_grad = out_low.astype(jnp.float32) + middle_norm_grad
     middle_low = middle_grad.astype(jnp.bfloat16)
@@ -1055,11 +1072,11 @@
     mirrored_low = swap_mirrored(heads_low[:, :, width:])
     gated_grad = nt_dot(middle_low, mixer_w)
     mixed_grad, gate_z_grad, mixer_gain_grad = gate_pull(gated_grad)
-    upward = state_outer(DSSM // NS + 1, 2, 1)(
-        mixer_rows, mixed_grad.astype(jnp.bfloat16), conv_b16, down_beside
-    )
-    state_out_grad, _ = pass_state(upward, None, gains, True)
-    down_half, down_got = ctx_half([tie(down_sum, upward)], model // shards)
+    upward = state_outer(DSSM // NS + 1, 2, 2)(
+        mixer_rows, mixed_grad.astype(jnp.bfloat16), conv_b16, down_beside, gate_up_sent
+    )
+    state_out_grad, _, pair_total = pass_state(upward, None, gains, True)
+    down_half, down_got, _ = ctx_half([tie(down_sum, upward)], model // shards)
     gate_z_low = gate_z_grad.astype(jnp.bfloat16)
     query_grad_own, query_grad_mirrored, pairs_grad = attend_backward(
         group_blocks,
@@ -1075,6 +1092,7 @@
         mirrored_low,
         gate_up_beside,
         down_across,
+        pair_total,
     )
     mixer_products = split_products(gated_b, middle_low)
     attn_products = split_products(heads_t, middle_low, 0)
@@ -1090,13 +1108,10 @@
             axis=0,
         ).astype(jnp.bfloat16)
 
-    mixer_attn_sum, mixer_beside, mixer_across = shard_sum(
+    mixer_attn_started = start_sum(
         *[interleaved(parts) for parts in zip(mixer_products, attn_products)], pairs_grad
     )
-    in_sum_z, in_z_beside, in_z_across = weight_grad(normed_b, gate_z_low, pairs_grad)
-    pair_grad = (
-        scatter_blocks(pairs_grad).astype(jnp.float32).transpose(0, 2, 1)
-    )
+    in_z_started = start_sum(*split_products(normed_b, gate_z_low), pairs_grad)
     query_low_own, query_low_mirrored = (
         (turn(grad, *tables) * scale).astype(jnp.bfloat16)
         for grad, tables in (
@@ -1119,20 +1134,21 @@
         state_in,
         state_out_grad,
         mixed_grad,
-        gate_up_across,
-        in_z_beside,
+        gate_up_give,
+        in_z_started[1],
         down_got,
-        mixer_beside,
-    )
-    mixer_half, mixer_got = ctx_half(
-        [tie(mixer_attn_sum, conv_grad), tie(in_sum_z, conv_grad)], model // shards
-    )
+        mixer_attn_started[1],
+    )
+    pair_grad = scatter_blocks(pairs_grad, conv_grad).astype(jnp.float32).transpose(0, 2, 1)
     skip_grad = jnp.sum(skip_parts.reshape(HM, PM), axis=1)
     extended_grad, conv_weight_grad, conv_bias_grad = conv_pull(conv_grad)
     from_above = from_behind(extended_grad[: KW - 1], "ctx", -1)
     pre_grad = extended_grad[KW - 1 :] + jnp.pad(from_above, ((rows - (KW - 1), 0), (0, 0)))
-    pre_low = tie(pre_grad.astype(jnp.bfloat16), gate_up_got, in_z_across, mixer_across)
-    in_sum_pre, _, _ = weight_grad(normed_b, pre_low)
+    pre_low = tie(pre_grad.astype(jnp.bfloat16), gate_up_got)
+    mixer_attn_sum = finish_sum(mixer_attn_started, pre_low)
+    in_sum_z = finish_sum(in_z_started, pre_low)
+    mixer_half, _, _ = ctx_half([mixer_attn_sum, in_sum_z], model // shards)
+    in_sum_pre = weight_grad(normed_b, pre_low)[0]
     projected_low = jnp.concatenate([gate_z_low, pre_low], axis=1)
     normed_grad = nt_dot(projected_low, in_w)
 
@@ -1145,7 +1161,7 @@
         axis=0,
     ).astype(jnp.bfloat16)
     attn_pair_low = jnp.concatenate([query_low, keyval_low], axis=0).T
-    attn_pair_sum, _, _ = weight_grad(normed_b, attn_pair_low)
+    attn_pair_sum = weight_grad(normed_b, attn_pair_low)[0]
     normed_grad = normed_grad + nt_dot(attn_pair_low, attn_pair_w)
     source_grad, norm_grad = norm_pull(normed_grad)
     tokens_grad = (middle_grad + source_grad)[None]
@@ -1154,9 +1170,11 @@
         norm_grad, conv_weight_grad, conv_bias_grad, skip_grad, mixer_gain_grad, ffn_gain_grad, shards
     )
     small_share = sum_small(small_grad)
-    last_half, _ = ctx_half([in_sum_pre, attn_pair_sum], model // shards)
-    (down_share,), summed = ctx_finish(down_half, [down_sum.shape], 0)
-    (gate_up_share,), summed = ctx_finish(tie(gate_up_half, summed), [gate_up_sum.shape], 1)
+    last_half, _, _ = ctx_half([in_sum_pre, attn_pair_sum], model // shards)
+    (gate_up_share,), summed = ctx_finish(
+        tie(gate_up_half, state_out_grad), [gate_up_sum.shape], 1
+    )
+    (down_share,), summed = ctx_finish(tie(down_half, summed), [down_sum.shape], 0)
     (mixer_attn_share, in_share_z), summed = ctx_finish(
         tie(mixer_half, summed), [mixer_attn_sum.shape, in_sum_z.shape], 2
     )

time: 802 us -> 756 us (0.943)
  waiting for transfers between devices: 265 us -> 214 us
  matrix products: 106 us -> 93.6 us
  starting transfers between devices: 49.4 us -> 59.6 us
    ppermute x2, waiting for transfers between devices: 35.7 us -> 0.61 us  [from_behind(): return lax.ppermute(block, axis, route)]
    psum x4, waiting for transfers between devices: 105 us -> 128 us  [ctx_finish(): mine = lax.psum(mine, 'ctx', axis_index_groups=lines)]
    ppermute x43, waiting for transfers between devices: 82.5 us -> 63.7 us  [exchange(): return lax.ppermute(block, MESH_AXES, route)]
    ppermute x4, waiting for transfers between devices: 16.2 us -> 5.24 us  [swap_mirrored(): lax.ppermute(block, 'ctx', [(i, count - 1 - i) for i in range(count)])]
    ppermute x43, starting transfers between devices: 33.4 us -> 43.4 us  [exchange(): return lax.ppermute(block, MESH_AXES, route)]
    all_gather x1, waiting for transfers between devices: 11.6 us -> 1.81 us  [per_device(): lax.all_gather(jnp.concatenate([keys_b, values_b], axis=1).transpose(0, 2...]
    unnamed x375 -> x395, local copies, waits for them, and re-layouts: 34.4 us -> 41.2 us
    convert_element_type x9 -> x11, other arithmetic: 18 us -> 23.9 us  [add_low(): return total.astype(jnp.bfloat16)]
  transfers between devices with their start and end apart: 56 -> 56, of which waited for: 22 -> 20; matrix products, arithmetic and copies ran while one was open for 35% -> 33% of each run, Pallas kernels for 14% -> 14%
where the time goes in v6:
time: 756 us; the launch traced here: 747 us
  waiting for transfers between devices  214 us (28%)
  other arithmetic  143 us (19%)
  Pallas kernels  117 us (15%)
  local copies, waits for them, and re-layouts  99.4 us (13%)
  matrix products  93.6 us (12%)
  starting transfers between devices  59.6 us (8%)
  between operations  19.7 us (3%)
    psum x4, waiting for transfers between devices, ctx_finish(): mine = lax.psum(mine, 'ctx', axis_index_groups=lines)  128 us
    ppermute x43, waiting for transfers between devices, exchange(): return lax.ppermute(block, MESH_AXES, route)  63.7 us
    dot_general x21, matrix products, split_products(): lax.dot_general(piece, right, (((1 - axis,), (0,)), ((), ())), preferred_...  50.8 us
    ppermute x43, starting transfers between devices, exchange(): return lax.ppermute(block, MESH_AXES, route)  43.4 us
    unnamed x395, local copies, waits for them, and re-layouts  41.2 us
    pallas_call x1, Pallas kernels, per_device(): attend_backward(group_blocks, pairs, key_side, turned_q, mirrored_q, quer...  31.5 us
    dot_general x6, matrix products, nt_dot(): lax.dot_general(left, right, (((1,), (1,)), ((), ())), preferred_element_...  24.5 us
    convert_element_type x11, other arithmetic, add_low(): return total.astype(jnp.bfloat16)  23.9 us
  transfers between devices with their start and end apart: 56, of which 20 were waited for; matrix products, arithmetic and copies ran while one was open for 33% of the time, Pallas kernels for 14%

profile of v6, /device:TPU:0, one launch (start us, length us, event | category | flops | bytes accessed | tf_op | source)
XLA Modules:
  0.0 747.2 jit_solution(9646890139940499068)
XLA Ops:
  15.0 2.5 collective-permute-start.1
  49.8 5.9 collective-permute-done.3.refs_2_
  60.2 9.5 %collective-permute-done.4.refs_3_ = bf16[64,4096]{1,0:T(8,128)(2,1)S(1)} collective-permute-done((bf16[64,4096]{1,0:T(8,128)(2,1)}, bf16[64,4096]{1,0:T(8,128)(2,1)S(1)}, u32[]{:S(2)}, u32[]{:S(2)}) %collective-permute-start.4) | collective-permute-done | bytes 524320 | tf_op jit(solution)/shard_map/ppermute | solution.py:35
  78.3 7.7 %assemble.5 = bf16[1024,4096]{1,0:T(8,128)(2,1)S(1)} custom-call(s32[16]{0:T(128)S(1)} %copy-done.56, bf16[272,4096]{1,0:T(8,128)(2,1)S(1)} %fusion.21.refs_0_, bf16[272,4096]{1,0:T(8,128)(2,1)} %collective-permute-done.refs_1_, bf16[64,4096]{1,0:T(8,128)(2,1)} %collective-permute-done.3.refs_2_, bf16[64,4096]{1,0:T(8,128)(2,1)S(1)} %collective-permute-done.4.refs_3_, ...), custom_call_target="tpu_custom_call" | custom-call | flops 1024 | bytes 1024 | tf_op jit(solution)/shard_map/assemble/pallas_call | solution.py:88
  86.0 6.1 fusion.204
  92.1 3.3 copy-done.75
  100.1 3.9 collective-permute-start.10
  107.7 5.3 multiply_convert_fusion.1
  113.1 5.6 state_outer.2
  122.8 2.5 copy.100
  132.5 9.8 %mixer_forward.1.refs_2_.local_ref = f32[512,1536]{1,0:T(8,128)S(1)} custom-call(f32[12,1,128]{2,1,0:T(1,128)S(1)} %copy-done.42, bf16[512,1792]{1,0:T(8,128)(2,1)S(1)} %get-tuple-element.99.x_ref.b_ref.c_ref.left_ref.right_ref, bf16[512,1792]{1,0:T(8,128)(2,1)S(1)} %get-tuple-element.99.x_ref.b_ref.c_ref.left_ref.right_ref, ...), custom_call_target="tpu_custom_call" | custom-call | flops 1024 | bytes 1024 | tf_op jit(solution)/shard_map/mixer_forward/pallas_call | solution.py:1021
  144.0 3.5 collective-permute-start.7
  154.6 3.4 collective-permute-done.7.query_b
  163.1 22.0 %attend_forward.1 = (f32[8,64,256]{2,1,0:T(8,128)S(1)}, f32[8,64,256]{2,1,0:T(8,128)S(1)}, f32[2,2,1,1024]{3,2,1,0:T(1,128)S(1)}) custom-call(s32[2]{0:T(128)S(1)} %copy-done.50, bf16[8,2,512,128]{3,2,1,0:T(8,128)(2,1)S(1)} %bitcast.257, bf16[4096,128]{1,0:T(8,128)(2,1)S(1)} %fusion.33.refs_8_.side_ref, bf16[8,64,512]{2,1,0:T(8,128)(2,1)S(1)} %copy-done.6, ...), custom_call_target="tpu_custom_call" | custom-call | flops 1024 | bytes 1024 | tf_op jit(solution)/shard_map/attend_forward/pallas_call | solution.py:1025
  209.4 2.7 assemble.7
  213.9 3.1 assemble.9
  221.2 14.6 %all-gather.9.cloned.1.call-done = bf16[6208,128]{1,0:T(8,128)(2,1)} async-done(((bf16[1552,128]{1,0:T(8,128)(2,1)}), bf16[6208,128]{1,0:T(8,128)(2,1)}) %all-gather.9.cloned.1.call-update) | async-done | bytes 1589264 | tf_op jit(solution)/shard_map/all_gather | solution.py:824
  242.6 4.7 assemble.8
  247.3 3.3 copy-done.3
  250.6 4.5 mixer_join.1
  255.2 3.0 multiply_reduce_fusion.6
  264.8 4.6 fusion.206
  269.4 6.5 bitcast_multiply_fusion.1
  276.0 6.3 add_convert_fusion
  282.2 8.5 %multiply_reduce_fusion.7 = (f32[1024]{0:T(1024)S(1)}, f32[512]{0:T(512)S(1)}, f32[512,1024]{1,0:T(8,128)S(1)}) fusion(f32[512,1024]{1,0:T(8,128)S(1)} %copy-done.64, f32[512]{0:T(512)S(1)} %fusion.161, f32[1024]{0:T(1024)S(1)} %bitcast.294, bf16[512,4096]{1,0:T(8,128)(2,1)} %add_convert_fusion, bf16[1024,4096]{1,0:T(8,128)(2,1)} %copy-done.3), kind=kOutput, calls=%fused_computation.83 | convolution fusion | flops 4298111488 | bytes 16789504 | tf_op jit(solution)/shard_map/dot_general | solution.py:346
  298.7 4.4 convolution_convert_fusion
  305.8 5.8 fusion.190
  321.4 2.9 fusion.115
  324.6 3.3 fusion.43
  335.7 5.7 fusion.96
  341.4 2.8 add_convert_fusion.11.refs_0_
  344.3 2.8 add_convert_fusion.5.refs_0_
  347.1 8.6 %collective-permute-done.22.refs_1_ = bf16[512,1024]{1,0:T(8,128)(2,1)} collective-permute-done((bf16[512,1024]{1,0:T(8,128)(2,1)}, bf16[512,1024]{1,0:T(8,128)(2,1)}, u32[]{:S(2)}, u32[]{:S(2)}) %collective-permute-start.22) | collective-permute-done | bytes 1048608 | tf_op jit(solution)/shard_map/ppermute | solution.py:35
  355.6 3.2 add_convert_fusion.6.refs_0_
  358.8 4.4 add_convert_fusion.2.refs_1_
  364.8 5.6 state_outer.3.refs_1_
  375.4 7.1 collective-permute-done.19
  387.9 31.5 %attend_backward.1 = (f32[8,64,256]{2,1,0:T(8,128)S(1)}, f32[8,64,256]{2,1,0:T(8,128)S(1)}, bf16[8,2,512,128]{3,2,1,0:T(8,128)(2,1)}) custom-call(s32[2]{0:T(128)S(1)} %copy-done.51, bf16[8,2,512,128]{3,2,1,0:T(8,128)(2,1)} %bitcast.256, bf16[4096,128]{1,0:T(8,128)(2,1)S(1)} %fusion.33.refs_8_.side_ref, bf16[8,64,512]{2,1,0:T(8,128)(2,1)S(1)} %copy-done.7, ...), custom_call_target="tpu_custom_call" | custom-call | flops 1024 | bytes 1024 | tf_op jit(solution)/shard_map/attend_backward/pallas_call | solution.py:1081
  422.5 4.3 collective-permute-start.28
  433.7 4.4 add_convert_fusion.1
  444.1 17.9 %mixer_backward.1 = (f32[512,1792]{1,0:T(8,128)}, f32[12,1,128]{2,1,0:T(1,128)S(1)}) custom-call(f32[12,1,128]{2,1,0:T(1,128)S(1)} %copy-done.43, bf16[512,1792]{1,0:T(8,128)(2,1)} %copy-done, bf16[512,1792]{1,0:T(8,128)(2,1)} %copy-done, bf16[512,1792]{1,0:T(8,128)(2,1)} %copy-done, f32[12,8,512]{2,1,0:T(8,128)S(1)} %reshape.836.refs_10_.row_ref.rows_ref, ...), custom_call_target="tpu_custom_call" | custom-call | flops 1024 | bytes 1024 | tf_op jit(solution)/shard_map/mixer_backward/pallas_call | solution.py:1126
  466.2 6.1 collective-permute-start.30
  472.4 10.4 %multiply_reduce_fusion.3 = (f32[1792]{0:T(1024)S(1)}, f32[1792]{0:T(1024)S(1)}, f32[1792]{0:T(1024)S(1)}, f32[1792]{0:T(1024)S(1)}, f32[1792]{0:T(1024)S(1)}, /*index=5*/f32[512,1792]{1,0:T(8,128)S(1)}) fusion(f32[515,1792]{1,0:T(8,128)} %copy-done.57, f32[512]{0:T(512)S(1)} %bitcast.312, f32[512]{0:T(512)S(1)} %bitcast.315, f32[512]{0:T(512)S(1)} %bitcast.318, ...), kind=kLoop, calls=%fused_computation.32 | loop fusion | flops 20176128 | bytes 25734144 | tf_op jit(solution)/shard_map/transpose(jvp())/reduce_sum | solution.py:324
  485.7 2.9 pad_add_fusion
  490.1 3.6 fusion.8.refs_0_
  494.7 3.9 convolution_convert_fusion.2
  501.8 2.3 add_convert_fusion.4
  511.4 10.1 %collective-permute-done.31 = bf16[1,2,512,128]{2,3,1,0:T(8,128)(2,1)S(1)} collective-permute-done((bf16[1,2,512,128]{2,3,1,0:T(8,128)(2,1)S(1)}, bf16[1,2,512,128]{2,3,1,0:T(8,128)(2,1)S(1)}, u32[]{:S(2)}, u32[]{:S(2)}) %collective-permute-start.31) | collective-permute-done | bytes 262176 | tf_op jit(solution)/shard_map/ppermute | solution.py:35
  524.2 5.4 fusion.23
  529.9 2.8 add_convert_fusion.3.refs_0_
  533.7 4.0 collective-permute-done.33
  539.7 2.7 convolution_convert_fusion.5
  542.7 4.3 fusion.26
  547.4 3.0 collective-permute-start.36
  555.5 30.3 %all-reduce.21.cloned.1.call-done.refs_1_ = bf16[128,4096]{1,0:T(8,128)(2,1)} async-done(((bf16[128,4096]{1,0:T(8,128)(2,1)}), bf16[128,4096]{1,0:T(8,128)(2,1)}) %all-reduce.21.cloned.1.call-update) | async-done | bytes 1048592 | tf_op jit(solution)/shard_map/psum | solution.py:210
  585.8 2.3 add_convert_fusion.15
  589.6 2.8 fusion.18
  595.3 30.4 %all-reduce.23.cloned.1.call-done.refs_1_ = bf16[128,2048]{1,0:T(8,128)(2,1)} async-done(((bf16[128,2048]{1,0:T(8,128)(2,1)}), bf16[128,2048]{1,0:T(8,128)(2,1)}) %all-reduce.23.cloned.1.call-update) | async-done | bytes 524304 | tf_op jit(solution)/shard_map/psum | solution.py:210
  628.5 2.4 fusion.17
  634.6 6.3 collective-permute-done.48
  642.6 33.8 %all-reduce.25.cloned.1.call-done.refs_1_ = bf16[128,3584]{1,0:T(8,128)(2,1)} async-done(((bf16[128,3584]{1,0:T(8,128)(2,1)}), bf16[128,3584]{1,0:T(8,128)(2,1)}) %all-reduce.25.cloned.1.call-update) | async-done | bytes 917520 | tf_op jit(solution)/shard_map/psum | solution.py:210
  681.6 4.2 fusion.30
  685.8 33.4 %all-reduce.27.cloned.1.call-done = bf16[128,2560]{1,0:T(8,128)(2,1)} async-done(((bf16[128,2560]{1,0:T(8,128)(2,1)}), bf16[128,2560]{1,0:T(8,128)(2,1)}) %all-reduce.27.cloned.1.call-update) | async-done | bytes 655376 | tf_op jit(solution)/shard_map/psum | solution.py:210
  726.2 9.7 %collective-permute-done.46 = bf16[128,2560]{1,0:T(8,128)(2,1)S(1)} collective-permute-done((bf16[128,2560]{1,0:T(8,128)(2,1)}, bf16[128,2560]{1,0:T(8,128)(2,1)S(1)}, u32[]{:S(2)}, u32[]{:S(2)}) %collective-permute-start.46) | collective-permute-done | bytes 655392 | tf_op jit(solution)/shard_map/ppermute | solution.py:35
  (754 shorter events, 242.5 us)
Async XLA Ops:
  7.2 152.6 %all-gather.7.cloned.1.call-start = ((), (), s32[]{:S(2)}) async-start(), calls=%async_computation.4 | async-start | bytes 2359296 | tf_op jit(solution)/shard_map/all_gather | solution.py:1006
  13.4 57.6 %collective-permute-start = (bf16[272,4096]{1,0:T(8,128)(2,1)S(1)}, bf16[272,4096]{1,0:T(8,128)(2,1)}, u32[]{:S(2)}, u32[]{:S(2)}) collective-permute-start(bf16[272,4096]{1,0:T(8,128)(2,1)S(1)} %fusion.21.refs_0_), channel_id=1, source_target_pairs={{0,1},{1,0},{2,3},{3,2},{4,5},{5,4},{6,7},{7,6},{8,9},{9,8},{10,11... | collective-permute-start | bytes 6684680 | tf_op jit(solution)/shard_map/ppermute | solution.py:35
  15.0 29.7 %collective-permute-start.1 = (bf16[144,4096]{1,0:T(8,128)(2,1)}, bf16[144,4096]{1,0:T(8,128)(2,1)}, u32[]{:S(2)}, u32[]{:S(2)}) collective-permute-start(bf16[144,4096]{1,0:T(8,128)(2,1)} %slice.486), channel_id=1, source_target_pairs={{0,2},{1,3},{2,0},{3,1},{4,6},{5,7},{6,4},{7,5},{8,10},{9,11},{10,... | collective-permute-start | bytes 3538952 | tf_op jit(solution)/shard_map/ppermute | solution.py:35
  18.4 37.3 %collective-permute-start.3 = (bf16[64,4096]{1,0:T(8,128)(2,1)}, bf16[64,4096]{1,0:T(8,128)(2,1)}, u32[]{:S(2)}, u32[]{:S(2)}) collective-permute-start(bf16[64,4096]{1,0:T(8,128)(2,1)} %constant_dynamic-slice_fusion.15), channel_id=1, source_target_pairs={{0,2},{1,3},{2,0},{3,1},{4,6},{5,7},{6,4},{7,5},{8,10},{9,11},{10,... | collective-permute-start | bytes 1572872 | tf_op jit(solution)/shard_map/ppermute | solution.py:35
  44.7 28.8 %collective-permute-start.2 = (bf16[144,4096]{1,0:T(8,128)(2,1)}, bf16[144,4096]{1,0:T(8,128)(2,1)}, u32[]{:S(2)}, u32[]{:S(2)}) collective-permute-start(bf16[144,4096]{1,0:T(8,128)(2,1)} %collective-permute-done.1.refs_4_), channel_id=1, source_target_pairs={{0,1},{1,0},{2,3},{3,2},{4,5},{5,4},{6,7},{7,6},{8,9},{9,8},{10,11... | collective-permute-start | bytes 3538952 | tf_op jit(solution)/shard_map/ppermute | solution.py:35
  48.5 29.7 %copy-start.41 = (f32[4,512]{1,0:T(4,128)S(1)}, f32[4,512]{1,0:T(4,128)}, u32[]{:S(2)}) copy-start(f32[4,512]{1,0:T(4,128)} %maximum_maximum_fusion.refs_11_) | copy-start | bytes 24580
  48.5 29.7 %copy-start.44 = (s32[1,512]{1,0:T(1,128)S(1)}, s32[1,512]{1,0:T(1,128)}, u32[]{:S(2)}) copy-start(s32[1,512]{1,0:T(1,128)} %compare_select_fusion.2.refs_13_.docs_row) | copy-start | bytes 6148
  48.5 29.7 %copy-start.49 = (s32[2]{0:T(128)S(1)}, s32[2]{0:T(128)}, u32[]{:S(2)}) copy-start(s32[2]{0:T(128)} %pad_add_fusion.4.refs_18_.blocks) | copy-start | bytes 28
  55.7 14.0 %collective-permute-start.4 = (bf16[64,4096]{1,0:T(8,128)(2,1)}, bf16[64,4096]{1,0:T(8,128)(2,1)S(1)}, u32[]{:S(2)}, u32[]{:S(2)}) collective-permute-start(bf16[64,4096]{1,0:T(8,128)(2,1)} %collective-permute-done.3.refs_2_), channel_id=1, source_target_pairs={{0,4},{1,5},{2,6},{3,7},{4,0},{5,1},{6,2},{7,3},{8,12},{9,13},{10,... | collective-permute-start | bytes 1572872 | tf_op jit(solution)/shard_map/ppermute | solution.py:35
  60.2 17.4 %collective-permute-start.5 = (bf16[64,4096]{1,0:T(8,128)(2,1)}, bf16[64,4096]{1,0:T(8,128)(2,1)S(1)}, u32[]{:S(2)}, u32[]{:S(2)}) collective-permute-start(bf16[64,4096]{1,0:T(8,128)(2,1)} %collective-permute-done.3.refs_2_), channel_id=1, source_target_pairs={{0,1},{1,0},{2,3},{3,2},{4,5},{5,4},{6,7},{7,6},{8,9},{9,8},{10,11... | collective-permute-start | bytes 1572872 | tf_op jit(solution)/shard_map/ppermute | solution.py:35
  69.7 8.5 %collective-permute-start.6 = (bf16[64,4096]{1,0:T(8,128)(2,1)S(1)}, bf16[64,4096]{1,0:T(8,128)(2,1)S(1)}, u32[]{:S(2)}, u32[]{:S(2)}) collective-permute-start(bf16[64,4096]{1,0:T(8,128)(2,1)S(1)} %collective-permute-done.4.refs_3_), channel_id=1, source_target_pairs={{0,1},{1,0},{2,3},{3,2},{4,5},{5,4},{6,7},{7,6},{8,9},{9,8},{10,11... | collective-permute-start | bytes 1572872 | tf_op jit(solution)/shard_map/ppermute | solution.py:35
  69.7 88.3 %collective-permute-start.8 = (bf16[1024,1024]{1,0:T(8,128)(2,1)}, bf16[1024,1024]{1,0:T(8,128)(2,1)}, u32[]{:S(2)}, u32[]{:S(2)}) collective-permute-start(bf16[1024,1024]{1,0:T(8,128)(2,1)} %pad_maximum_fusion.1.refs_0_), channel_id=1, source_target_pairs={{0,1},{1,0},{2,3},{3,2},{4,5},{5,4},{6,7},{7,6},{8,9},{9,8},{10,11... | collective-permute-start | bytes 6291464 | tf_op jit(solution)/shard_map/ppermute | solution.py:35
  71.0 116.2 %collective-permute-start.12 = (bf16[1024,1024]{1,0:T(8,128)(2,1)}, bf16[1024,1024]{1,0:T(8,128)(2,1)}, u32[]{:S(2)}, u32[]{:S(2)}) collective-permute-start(bf16[1024,1024]{1,0:T(8,128)(2,1)} %pad_maximum_fusion.1.refs_0_), channel_id=1, source_target_pairs={{0,2},{1,3},{2,0},{3,1},{4,6},{5,7},{6,4},{7,5},{8,10},{9,11},{10,... | collective-permute-start | bytes 6291464 | tf_op jit(solution)/shard_map/ppermute | solution.py:35
  73.5 84.5 %collective-permute-start.9 = (bf16[256,4096]{1,0:T(8,128)(2,1)}, bf16[256,4096]{1,0:T(8,128)(2,1)}, u32[]{:S(2)}, u32[]{:S(2)}) collective-permute-start(bf16[256,4096]{1,0:T(8,128)(2,1)} %refs_0_), channel_id=1, source_target_pairs={{0,1},{1,0},{2,3},{3,2},{4,5},{5,4},{6,7},{7,6},{8,9},{9,8},{10,11... | collective-permute-start | bytes 6291464 | tf_op jit(solution)/shard_map/ppermute | solution.py:35
  77.6 127.5 %collective-permute-start.15 = (bf16[256,4096]{1,0:T(8,128)(2,1)}, bf16[256,4096]{1,0:T(8,128)(2,1)}, u32[]{:S(2)}, u32[]{:S(2)}) collective-permute-start(bf16[256,4096]{1,0:T(8,128)(2,1)} %refs_0_), channel_id=1, source_target_pairs={{0,2},{1,3},{2,0},{3,1},{4,6},{5,7},{6,4},{7,5},{8,10},{9,11},{10,... | collective-permute-start | bytes 6291464 | tf_op jit(solution)/shard_map/ppermute | solution.py:35
  99.3 136.5 %all-gather.9.cloned.1.call-start = ((), (), s32[]{:S(2)}) async-start(), calls=%async_computation.5 | async-start | bytes 1986560 | tf_op jit(solution)/shard_map/all_gather | solution.py:824
  100.1 6.9 collective-permute-start.10
  113.1 251.7 %copy-start = (bf16[512,1792]{1,0:T(8,128)(2,1)}, bf16[512,1792]{1,0:T(8,128)(2,1)S(1)}, u32[]{:S(2)}) copy-start(bf16[512,1792]{1,0:T(8,128)(2,1)S(1)} %get-tuple-element.99.x_ref.b_ref.c_ref.left_ref.right_ref) | copy-start | bytes 5505028
  119.5 24.5 %collective-permute-start.14 = (bf16[1552,128]{1,0:T(8,128)(2,1)}, bf16[1552,128]{1,0:T(8,128)(2,1)}, u32[]{:S(2)}, u32[]{:S(2)}) collective-permute-start(bf16[1552,128]{1,0:T(8,128)(2,1)} %pad_maximum_fusion.10), channel_id=1, source_target_pairs={{0,4},{1,5},{2,6},{3,7},{4,0},{5,1},{6,2},{7,3},{8,12},{9,13},{10,... | collective-permute-start | bytes 1191944 | tf_op jit(solution)/shard_map/ppermute | solution.py:35
  144.0 14.0 %collective-permute-start.7 = (bf16[8,64,256]{2,1,0:T(8,128)(2,1)}, bf16[8,64,256]{2,1,0:T(8,128)(2,1)}, u32[]{:S(2)}, u32[]{:S(2)}) collective-permute-start(bf16[8,64,256]{2,1,0:T(8,128)(2,1)} %slice.497), channel_id=1, source_target_pairs={{0,28},{4,24},{8,20},{12,16},{16,12},{20,8},{24,4},{28,0},{1,29},{... | collective-permute-start | bytes 786440 | tf_op jit(solution)/shard_map/ppermute | solution.py:46
  187.3 20.0 %collective-permute-start.13 = (bf16[1024,1024]{1,0:T(8,128)(2,1)}, bf16[1024,1024]{1,0:T(8,128)(2,1)}, u32[]{:S(2)}, u32[]{:S(2)}) collective-permute-start(bf16[1024,1024]{1,0:T(8,128)(2,1)} %collective-permute-done.12.refs_2_), channel_id=1, source_target_pairs={{0,1},{1,0},{2,3},{3,2},{4,5},{5,4},{6,7},{7,6},{8,9},{9,8},{10,11... | collective-permute-start | bytes 6291464 | tf_op jit(solution)/shard_map/ppermute | solution.py:35
  188.1 252.9 %all-gather.11.cloned.1.call-start = ((), (), s32[]{:S(2)}) async-start(), calls=%async_computation.6 | async-start | bytes 1966080 | tf_op jit(solution)/shard_map/all_gather | solution.py:824
  192.2 13.2 %collective-permute-start.11 = (bf16[8,64,256]{2,1,0:T(8,128)(2,1)}, bf16[8,64,256]{2,1,0:T(8,128)(2,1)}, u32[]{:S(2)}, u32[]{:S(2)}) collective-permute-start(bf16[8,64,256]{2,1,0:T(8,128)(2,1)} %convert_element_type.652), channel_id=1, source_target_pairs={{0,28},{4,24},{8,20},{12,16},{16,12},{20,8},{24,4},{28,0},{1,29},{... | collective-permute-start | bytes 786440 | tf_op jit(solution)/shard_map/ppermute | solution.py:46
  199.3 91.5 %copy-start.155 = (f32[1,2,4,128]{3,1,2,0:T(2,128)}, f32[1,2,4,128]{3,1,2,0:T(2,128)S(1)}, u32[]{:S(2)}) copy-start(f32[1,2,4,128]{3,1,2,0:T(2,128)S(1)} %copy.110) | copy-start | bytes 12292
  205.2 37.4 %collective-permute-start.16 = (bf16[256,4096]{1,0:T(8,128)(2,1)}, bf16[256,4096]{1,0:T(8,128)(2,1)}, u32[]{:S(2)}, u32[]{:S(2)}) collective-permute-start(bf16[256,4096]{1,0:T(8,128)(2,1)} %collective-permute-done.15.refs_2_), channel_id=1, source_target_pairs={{0,1},{1,0},{2,3},{3,2},{4,5},{5,4},{6,7},{7,6},{8,9},{9,8},{10,11... | collective-permute-start | bytes 6291464 | tf_op jit(solution)/shard_map/ppermute | solution.py:35
  297.9 85.8 %collective-permute-start.27 = (bf16[8,64,256]{2,1,0:T(8,128)(2,1)}, bf16[8,64,256]{2,1,0:T(8,128)(2,1)}, u32[]{:S(2)}, u32[]{:S(2)}) collective-permute-start(bf16[8,64,256]{2,1,0:T(8,128)(2,1)} %slice.536), channel_id=1, source_target_pairs={{0,28},{4,24},{8,20},{12,16},{16,12},{20,8},{24,4},{28,0},{1,29},{... | collective-permute-start | bytes 786440 | tf_op jit(solution)/shard_map/ppermute | solution.py:46
  303.2 55.6 %collective-permute-start.18 = (bf16[512,4096]{1,0:T(8,128)(2,1)}, bf16[512,4096]{1,0:T(8,128)(2,1)}, u32[]{:S(2)}, u32[]{:S(2)}) collective-permute-start(bf16[512,4096]{1,0:T(8,128)(2,1)} %convolution_convert_fusion), channel_id=1, source_target_pairs={{0,1},{1,0},{2,3},{3,2},{4,5},{5,4},{6,7},{7,6},{8,9},{9,8},{10,11... | collective-permute-start | bytes 12582920 | tf_op jit(solution)/shard_map/ppermute | solution.py:35
  305.7 22.3 %collective-permute-start.17 = (bf16[1024,1024]{1,0:T(8,128)(2,1)S(1)}, bf16[1024,1024]{1,0:T(8,128)(2,1)S(1)}, u32[]{:S(2)}, u32[]{:S(2)}) collective-permute-start(bf16[1024,1024]{1,0:T(8,128)(2,1)S(1)} %convolution_convert_fusion.3), channel_id=1, source_target_pairs={{0,1},{1,0},{2,3},{3,2},{4,5},{5,4},{6,7},{7,6},{8,9},{9,8},{10,11... | collective-permute-start | bytes 6291464 | tf_op jit(solution)/shard_map/ppermute | solution.py:35
  313.8 27.6 %collective-permute-start.21 = (bf16[512,1536]{1,0:T(8,128)(2,1)}, bf16[512,1536]{1,0:T(8,128)(2,1)}, u32[]{:S(2)}, u32[]{:S(2)}) collective-permute-start(bf16[512,1536]{1,0:T(8,128)(2,1)} %convolution_convert_fusion.1), channel_id=1, source_target_pairs={{0,1},{1,0},{2,3},{3,2},{4,5},{5,4},{6,7},{7,6},{8,9},{9,8},{10,11... | collective-permute-start | bytes 4718600 | tf_op jit(solution)/shard_map/ppermute | solution.py:35
  318.4 25.9 %collective-permute-start.24 = (bf16[1024,1024]{1,0:T(8,128)(2,1)}, bf16[1024,1024]{1,0:T(8,128)(2,1)}, u32[]{:S(2)}, u32[]{:S(2)}) collective-permute-start(bf16[1024,1024]{1,0:T(8,128)(2,1)} %pad_maximum_fusion.2), channel_id=1, source_target_pairs={{0,1},{1,0},{2,3},{3,2},{4,5},{5,4},{6,7},{7,6},{8,9},{9,8},{10,11... | collective-permute-start | bytes 6291464 | tf_op jit(solution)/shard_map/ppermute | solution.py:35
  329.7 25.9 %collective-permute-start.22 = (bf16[512,1024]{1,0:T(8,128)(2,1)}, bf16[512,1024]{1,0:T(8,128)(2,1)}, u32[]{:S(2)}, u32[]{:S(2)}) collective-permute-start(bf16[512,1024]{1,0:T(8,128)(2,1)} %add_convert_fusion.7), channel_id=1, source_target_pairs={{0,2},{1,3},{2,0},{3,1},{4,6},{5,7},{6,4},{7,5},{8,10},{9,11},{10,... | collective-permute-start | bytes 3145736 | tf_op jit(solution)/shard_map/ppermute | solution.py:35
  363.2 70.5 %collective-permute-start.20 = (bf16[256,4096]{1,0:T(8,128)(2,1)}, bf16[256,4096]{1,0:T(8,128)(2,1)}, u32[]{:S(2)}, u32[]{:S(2)}) collective-permute-start(bf16[256,4096]{1,0:T(8,128)(2,1)} %add_convert_fusion.2.refs_1_), channel_id=1, source_target_pairs={{0,2},{1,3},{2,0},{3,1},{4,6},{5,7},{6,4},{7,5},{8,10},{9,11},{10,... | collective-permute-start | bytes 6291464 | tf_op jit(solution)/shard_map/ppermute | solution.py:35
  370.3 12.1 %collective-permute-start.19 = (bf16[1536,128]{1,0:T(8,128)(2,1)S(1)}, bf16[1536,128]{1,0:T(8,128)(2,1)S(1)}, u32[]{:S(2)}, u32[]{:S(2)}) collective-permute-start(bf16[1536,128]{1,0:T(8,128)(2,1)S(1)} %state_outer.3.refs_1_), channel_id=1, source_target_pairs={{0,4},{1,5},{2,6},{3,7},{4,0},{5,1},{6,2},{7,3},{8,12},{9,13},{10,... | collective-permute-start | bytes 1179656 | tf_op jit(solution)/shard_map/ppermute | solution.py:35
  374.0 53.4 %collective-permute-start.23 = (bf16[128,2048]{1,0:T(8,128)(2,1)}, bf16[128,2048]{1,0:T(8,128)(2,1)S(1)}, u32[]{:S(2)}, u32[]{:S(2)}) collective-permute-start(bf16[128,2048]{1,0:T(8,128)(2,1)} %fusion.81), channel_id=1, source_target_pairs={{0,4},{1,5},{2,6},{3,7},{4,0},{5,1},{6,2},{7,3},{8,12},{9,13},{10,... | collective-permute-start | bytes 1572872 | tf_op jit(solution)/shard_map/ppermute | solution.py:35
  383.5 202.2 %all-reduce.21.cloned.1.call-start = ((), (), s32[]{:S(2)}) async-start(), calls=%async_computation | async-start | bytes 2097152 | tf_op jit(solution)/shard_map/psum | solution.py:210
  421.7 40.3 %collective-permute-start.29 = (bf16[4,2,512,128]{3,2,1,0:T(8,128)(2,1)}, bf16[4,2,512,128]{3,2,1,0:T(8,128)(2,1)}, u32[]{:S(2)}, u32[]{:S(2)}) collective-permute-start(bf16[4,2,512,128]{3,2,1,0:T(8,128)(2,1)} %dynamic-slice_bitcast_fusion), channel_id=1, source_target_pairs={{0,4},{1,5},{2,6},{3,7},{4,0},{5,1},{6,2},{7,3},{8,12},{9,13},{10,... | collective-permute-start | bytes 3145736 | tf_op jit(solution)/shard_map/ppermute | solution.py:35
  422.5 9.4 %collective-permute-start.28 = (bf16[8,64,256]{2,1,0:T(8,128)(2,1)S(1)}, bf16[8,64,256]{2,1,0:T(8,128)(2,1)}, u32[]{:S(2)}, u32[]{:S(2)}) collective-permute-start(bf16[8,64,256]{2,1,0:T(8,128)(2,1)S(1)} %fusion.86), channel_id=1, source_target_pairs={{0,28},{4,24},{8,20},{12,16},{16,12},{20,8},{24,4},{28,0},{1,29},{... | collective-permute-start | bytes 786440 | tf_op jit(solution)/shard_map/ppermute | solution.py:46
  426.9 71.8 %collective-permute-start.38 = (bf16[256,1536]{1,0:T(8,128)(2,1)}, bf16[256,1536]{1,0:T(8,128)(2,1)}, u32[]{:S(2)}, u32[]{:S(2)}) collective-permute-start(bf16[256,1536]{1,0:T(8,128)(2,1)} %tie.18), channel_id=1, source_target_pairs={{0,2},{1,3},{2,0},{3,1},{4,6},{5,7},{6,4},{7,5},{8,10},{9,11},{10,... | collective-permute-start | bytes 2359304 | tf_op jit(solution)/shard_map/ppermute | solution.py:35
  427.5 71.1 %collective-permute-start.37 = (bf16[512,1024]{1,0:T(8,128)(2,1)}, bf16[512,1024]{1,0:T(8,128)(2,1)}, u32[]{:S(2)}, u32[]{:S(2)}) collective-permute-start(bf16[512,1024]{1,0:T(8,128)(2,1)} %tie.16), channel_id=1, source_target_pairs={{0,2},{1,3},{2,0},{3,1},{4,6},{5,7},{6,4},{7,5},{8,10},{9,11},{10,... | collective-permute-start | bytes 3145736 | tf_op jit(solution)/shard_map/ppermute | solution.py:35
  439.7 54.0 %collective-permute-start.26 = (bf16[128,4096]{1,0:T(8,128)(2,1)S(1)}, bf16[128,4096]{1,0:T(8,128)(2,1)}, u32[]{:S(2)}, u32[]{:S(2)}) collective-permute-start(bf16[128,4096]{1,0:T(8,128)(2,1)S(1)} %constant_dynamic-slice_fusion.10.refs_0_), channel_id=1, source_target_pairs={{0,4},{1,5},{2,6},{3,7},{4,0},{5,1},{6,2},{7,3},{8,12},{9,13},{10,... | collective-permute-start | bytes 3145736 | tf_op jit(solution)/shard_map/ppermute | solution.py:35
  466.2 38.2 %collective-permute-start.30 = (bf16[2,2,512,128]{2,3,1,0:T(8,128)(2,1)}, bf16[2,2,512,128]{2,3,1,0:T(8,128)(2,1)}, u32[]{:S(2)}, u32[]{:S(2)}) collective-permute-start(bf16[2,2,512,128]{2,3,1,0:T(8,128)(2,1)} %bitcast.90), channel_id=1, source_target_pairs={{0,8},{1,9},{2,10},{3,11},{4,12},{5,13},{6,14},{7,15},{8,0},{9,1},... | collective-permute-start | bytes 1572872 | tf_op jit(solution)/shard_map/ppermute | solution.py:35
  484.3 5.8 collective-permute-start.25
  498.6 91.0 %collective-permute-start.41 = (bf16[512,1792]{1,0:T(8,128)(2,1)}, bf16[512,1792]{1,0:T(8,128)(2,1)}, u32[]{:S(2)}, u32[]{:S(2)}) collective-permute-start(bf16[512,1792]{1,0:T(8,128)(2,1)} %convolution_convert_fusion.2), channel_id=1, source_target_pairs={{0,1},{1,0},{2,3},{3,2},{4,5},{5,4},{6,7},{7,6},{8,9},{9,8},{10,11... | collective-permute-start | bytes 5505032 | tf_op jit(solution)/shard_map/ppermute | solution.py:35
  506.3 15.3 %collective-permute-start.31 = (bf16[1,2,512,128]{2,3,1,0:T(8,128)(2,1)S(1)}, bf16[1,2,512,128]{2,3,1,0:T(8,128)(2,1)S(1)}, u32[]{:S(2)}, u32[]{:S(2)}) collective-permute-start(bf16[1,2,512,128]{2,3,1,0:T(8,128)(2,1)S(1)} %constant_dynamic-slice_fusion.1), channel_id=1, source_target_pairs={{0,16},{1,17},{2,18},{3,19},{4,20},{5,21},{6,22},{7,23},{8,24},{9,... | collective-permute-start | bytes 786440 | tf_op jit(solution)/shard_map/ppermute | solution.py:35
  509.4 83.5 %collective-permute-start.39 = (bf16[128,3584]{1,0:T(8,128)(2,1)}, bf16[128,3584]{1,0:T(8,128)(2,1)}, u32[]{:S(2)}, u32[]{:S(2)}) collective-permute-start(bf16[128,3584]{1,0:T(8,128)(2,1)} %constant_dynamic-slice_fusion), channel_id=1, source_target_pairs={{0,4},{1,5},{2,6},{3,7},{4,0},{5,1},{6,2},{7,3},{8,12},{9,13},{10,... | collective-permute-start | bytes 2752520 | tf_op jit(solution)/shard_map/ppermute | solution.py:35
  529.8 3.2 collective-permute-start.32
  532.7 93.0 %all-reduce.23.cloned.1.call-start = ((), (), s32[]{:S(2)}) async-start(), calls=%async_computation.1 | async-start | bytes 1048576 | tf_op jit(solution)/shard_map/psum | solution.py:210
  533.1 4.6 collective-permute-start.33
  537.6 4.8 collective-permute-start.34
  542.4 43.4 %collective-permute-start.43 = (bf16[512,768]{1,0:T(8,128)(2,1)}, bf16[512,768]{1,0:T(8,128)(2,1)}, u32[]{:S(2)}, u32[]{:S(2)}) collective-permute-start(bf16[512,768]{1,0:T(8,128)(2,1)} %convolution_convert_fusion.5), channel_id=1, source_target_pairs={{0,1},{1,0},{2,3},{3,2},{4,5},{5,4},{6,7},{7,6},{8,9},{9,8},{10,11... | collective-permute-start | bytes 2359304 | tf_op jit(solution)/shard_map/ppermute | solution.py:35
  542.4 5.0 collective-permute-start.35
  547.4 38.4 %copy-start.101 = (bf16[512,1024]{1,0:T(8,128)(2,1)S(1)}, bf16[512,1024]{1,0:T(8,128)(2,1)}, u32[]{:S(2)}) copy-start(bf16[512,1024]{1,0:T(8,128)(2,1)} %copy-done.100) | copy-start | bytes 3145732
  547.4 5.5 collective-permute-start.36
  585.7 90.7 %all-reduce.25.cloned.1.call-start = ((), (), s32[]{:S(2)}) async-start(), calls=%async_computation.2 | async-start | bytes 1835008 | tf_op jit(solution)/shard_map/psum | solution.py:210
  588.1 39.2 %collective-permute-start.44 = (bf16[256,768]{1,0:T(8,128)(2,1)}, bf16[256,768]{1,0:T(8,128)(2,1)S(1)}, u32[]{:S(2)}, u32[]{:S(2)}) collective-permute-start(bf16[256,768]{1,0:T(8,128)(2,1)} %add_convert_fusion.15), channel_id=1, source_target_pairs={{0,2},{1,3},{2,0},{3,1},{4,6},{5,7},{6,4},{7,5},{8,10},{9,11},{10,... | collective-permute-start | bytes 1179656 | tf_op jit(solution)/shard_map/ppermute | solution.py:35
  592.4 36.1 %collective-permute-start.42 = (bf16[256,1792]{1,0:T(8,128)(2,1)}, bf16[256,1792]{1,0:T(8,128)(2,1)}, u32[]{:S(2)}, u32[]{:S(2)}) collective-permute-start(bf16[256,1792]{1,0:T(8,128)(2,1)} %fusion.18), channel_id=1, source_target_pairs={{0,2},{1,3},{2,0},{3,1},{4,6},{5,7},{6,4},{7,5},{8,10},{9,11},{10,... | collective-permute-start | bytes 2752520 | tf_op jit(solution)/shard_map/ppermute | solution.py:35
  595.3 32.1 %copy-start.111 = (f32[256,768]{1,0:T(8,128)S(1)}, f32[256,768]{1,0:T(8,128)}, u32[]{:S(2)}) copy-start(f32[256,768]{1,0:T(8,128)} %fusion.112) | copy-start | bytes 2359300
  625.7 93.5 %all-reduce.27.cloned.1.call-start = ((), (), s32[]{:S(2)}) async-start(), calls=%async_computation.3 | async-start | bytes 1310720 | tf_op jit(solution)/shard_map/psum | solution.py:210
  625.8 15.1 %collective-permute-start.48 = (bf16[128,2048]{1,0:T(8,128)(2,1)}, bf16[128,2048]{1,0:T(8,128)(2,1)S(1)}, u32[]{:S(2)}, u32[]{:S(2)}) collective-permute-start(bf16[128,2048]{1,0:T(8,128)(2,1)} %all-reduce.23.cloned.1.call-done.refs_1_), channel_id=1, source_target_pairs={{0,4},{1,5},{2,6},{3,7},{4,0},{5,1},{6,2},{7,3},{8,12},{9,13},{10,... | collective-permute-start | bytes 1572872 | tf_op jit(solution)/shard_map/ppermute | solution.py:35
  631.9 46.0 %collective-permute-start.45 = (bf16[128,2560]{1,0:T(8,128)(2,1)}, bf16[128,2560]{1,0:T(8,128)(2,1)}, u32[]{:S(2)}, u32[]{:S(2)}) collective-permute-start(bf16[128,2560]{1,0:T(8,128)(2,1)} %fusion.78), channel_id=1, source_target_pairs={{0,4},{1,5},{2,6},{3,7},{4,0},{5,1},{6,2},{7,3},{8,12},{9,13},{10,... | collective-permute-start | bytes 1966088 | tf_op jit(solution)/shard_map/ppermute | solution.py:35
  633.1 48.5 %collective-permute-start.47 = (bf16[128,4096]{1,0:T(8,128)(2,1)S(1)}, bf16[128,4096]{1,0:T(8,128)(2,1)}, u32[]{:S(2)}, u32[]{:S(2)}) collective-permute-start(bf16[128,4096]{1,0:T(8,128)(2,1)S(1)} %copy-done.90), channel_id=1, source_target_pairs={{0,4},{1,5},{2,6},{3,7},{4,0},{5,1},{6,2},{7,3},{8,12},{9,13},{10,... | collective-permute-start | bytes 3145736 | tf_op jit(solution)/shard_map/ppermute | solution.py:35
  676.4 44.3 %collective-permute-start.40 = (bf16[128,3584]{1,0:T(8,128)(2,1)}, bf16[128,3584]{1,0:T(8,128)(2,1)}, u32[]{:S(2)}, u32[]{:S(2)}) collective-permute-start(bf16[128,3584]{1,0:T(8,128)(2,1)} %all-reduce.25.cloned.1.call-done.refs_1_), channel_id=1, source_target_pairs={{0,4},{1,5},{2,6},{3,7},{4,0},{5,1},{6,2},{7,3},{8,12},{9,13},{10,... | collective-permute-start | bytes 2752520 | tf_op jit(solution)/shard_map/ppermute | solution.py:35
  681.6 39.1 %copy-start.96 = (bf16[128,3584]{1,0:T(8,128)(2,1)S(1)}, bf16[128,3584]{1,0:T(8,128)(2,1)}, u32[]{:S(2)}) copy-start(bf16[128,3584]{1,0:T(8,128)(2,1)} %all-reduce.25.cloned.1.call-done.refs_1_) | copy-start | bytes 2752516
  719.2 16.7 %collective-permute-start.46 = (bf16[128,2560]{1,0:T(8,128)(2,1)}, bf16[128,2560]{1,0:T(8,128)(2,1)S(1)}, u32[]{:S(2)}, u32[]{:S(2)}) collective-permute-start(bf16[128,2560]{1,0:T(8,128)(2,1)} %all-reduce.27.cloned.1.call-done), channel_id=1, source_target_pairs={{0,4},{1,5},{2,6},{3,7},{4,0},{5,1},{6,2},{7,3},{8,12},{9,13},{10,... | collective-permute-start | bytes 1966088 | tf_op jit(solution)/shard_map/ppermute | solution.py:35
  (189 other events, 1269.0 us)
Sparse Core Ops, SparseCore 0:
  99.4 60.3 all-gather.6
  188.2 47.5 all-gather.8
  383.6 40.2 all-gather.10
  532.8 52.8 all-reduce.20
  588.0 37.6 all-reduce.22
  628.7 47.7 all-reduce.24
  680.3 38.9 all-reduce.26

commit v7 on v6

--- a/solution.py
+++ b/solution.py
@@ -200,20 +200,22 @@
     return [list(range(start, count, 2)) for start in range(2)]
 
 
-def ctx_finish(mine, shapes, turn_at):
-    side = lax.axis_index("ctx") % 2
+def line_sum(mine, turn_at):
     lines = ctx_lines()
     if turn_at % 2:
         lines = lines[::-1]
     if turn_at // 2:
         lines = [line[::-1] for line in lines]
-    mine = lax.psum(mine, "ctx", axis_index_groups=lines)
-    summed = mine
+    return lax.psum(mine, "ctx", axis_index_groups=lines)
+
+
+def ctx_finish(mine, shapes):
+    side = lax.axis_index("ctx") % 2
     got = exchange(mine, 1, 0)
     whole = jnp.where(
         side == 0, jnp.concatenate([mine, got], axis=0), jnp.concatenate([got, mine], axis=0)
     ).astype(jnp.float32)
-    return take_apart(whole, shapes), summed
+    return take_apart(whole, shapes)
 
 
 def shard_pieces(array, axis):
@@ -256,7 +258,9 @@
 
 def finish_sum(started, after):
     own, got, got_across = started
-    return add_low(own, got[: own.shape[0]], tie(got_across, after))
+    if after is not None:
+        got_across = tie(got_across, after)
+    return add_low(own, got[: own.shape[0]], got_across)
 
 
 def sum_small(value):
@@ -1063,7 +1067,7 @@
     (gate_up_grad_v,) = act_pull(nt_dot(out_low, down_w))
     gate_up_low = gate_up_grad_v.astype(jnp.bfloat16)
     gate_up_sum, gate_up_beside, _, gate_up_sent = weight_grad(normed2_b, gate_up_low)
-    gate_up_half, gate_up_got, gate_up_give = ctx_half([gate_up_sum], model // shards)
+    gate_up_half, _, gate_up_give = ctx_half([gate_up_sum], model // shards)
     middle_norm_grad, ffn_gain_grad = ffn_pull(nt_dot(gate_up_low, gate_up_w))
     middle_grad = out_low.astype(jnp.float32) + middle_norm_grad
     middle_low = middle_grad.astype(jnp.bfloat16)
@@ -1076,7 +1080,7 @@
         mixer_rows, mixed_grad.astype(jnp.bfloat16), conv_b16, down_beside, gate_up_sent
     )
     state_out_grad, _, pair_total = pass_state(upward, None, gains, True)
-    down_half, down_got, _ = ctx_half([tie(down_sum, upward)], model // shards)
+    down_half, _, _ = ctx_half([tie(down_sum, upward)], model // shards)
     gate_z_low = gate_z_grad.astype(jnp.bfloat16)
     query_grad_own, query_grad_mirrored, pairs_grad = attend_backward(
         group_blocks,
@@ -1136,19 +1140,22 @@
         mixed_grad,
         gate_up_give,
         in_z_started[1],
-        down_got,
+        down_half,
         mixer_attn_started[1],
     )
+    ffn_half = jnp.concatenate([gate_up_half, down_half], axis=1)
+    conv_grad = tie(conv_grad, ffn_half)
+    ffn_summed = line_sum(ffn_half, 0)
     pair_grad = scatter_blocks(pairs_grad, conv_grad).astype(jnp.float32).transpose(0, 2, 1)
     skip_grad = jnp.sum(skip_parts.reshape(HM, PM), axis=1)
     extended_grad, conv_weight_grad, conv_bias_grad = conv_pull(conv_grad)
     from_above = from_behind(extended_grad[: KW - 1], "ctx", -1)
     pre_grad = extended_grad[KW - 1 :] + jnp.pad(from_above, ((rows - (KW - 1), 0), (0, 0)))
-    pre_low = tie(pre_grad.astype(jnp.bfloat16), gate_up_got)
+    pre_low = pre_grad.astype(jnp.bfloat16)
     mixer_attn_sum = finish_sum(mixer_attn_started, pre_low)
     in_sum_z = finish_sum(in_z_started, pre_low)
     mixer_half, _, _ = ctx_half([mixer_attn_sum, in_sum_z], model // shards)
-    in_sum_pre = weight_grad(normed_b, pre_low)[0]
+    in_sum_pre, _, _, in_pre_sent = weight_grad(normed_b, pre_low)
     projected_low = jnp.concatenate([gate_z_low, pre_low], axis=1)
     normed_grad = nt_dot(projected_low, in_w)
 
@@ -1160,8 +1167,10 @@
         ],
         axis=0,
     ).astype(jnp.bfloat16)
-    attn_pair_low = jnp.concatenate([query_low, keyval_low], axis=0).T
-    attn_pair_sum = weight_grad(normed_b, attn_pair_low)[0]
+    attn_pair_low = tie(jnp.concatenate([query_low, keyval_low], axis=0).T, in_pre_sent, ffn_summed)
+    attn_pair_sum = finish_sum(
+        start_sum(*split_products(normed_b, attn_pair_low), mixer_half), None
+    )
     normed_grad = normed_grad + nt_dot(attn_pair_low, attn_pair_w)
     source_grad, norm_grad = norm_pull(normed_grad)
     tokens_grad = (middle_grad + source_grad)[None]
@@ -1171,19 +1180,17 @@
     )
     small_share = sum_small(small_grad)
     last_half, _, _ = ctx_half([in_sum_pre, attn_pair_sum], model // shards)
-    (gate_up_share,), summed = ctx_finish(
-        tie(gate_up_half, state_out_grad), [gate_up_sum.shape], 1
-    )
-    (down_share,), summed = ctx_finish(tie(down_half, summed), [down_sum.shape], 0)
-    (mixer_attn_share, in_share_z), summed = ctx_finish(
-        tie(mixer_half, summed), [mixer_attn_sum.shape, in_sum_z.shape], 2
+    mixer_summed = line_sum(tie(mixer_half, ffn_summed), 2)
+    gate_up_share, down_share = ctx_finish(
+        tie(ffn_summed, last_half), [gate_up_sum.shape, down_sum.shape]
+    )
+    mixer_attn_share, in_share_z = ctx_finish(
+        mixer_summed, [mixer_attn_sum.shape, in_sum_z.shape]
     )
     mixer_share = mixer_attn_share[: mixer_out.shape[0]]
     attn_share = mixer_attn_share[mixer_out.shape[0] :]
-    (in_share_pre, attn_pair_share), _ = ctx_finish(
-        tie(last_half, summed),
-        [in_sum_pre.shape, attn_pair_sum.shape],
-        3,
+    in_share_pre, attn_pair_share = ctx_finish(
+        line_sum(tie(last_half, mixer_summed), 3), [in_sum_pre.shape, attn_pair_sum.shape]
     )
     norm_share, conv_w_share, conv_b_share, skip_share, mixer_g_share, ffn_share = unpack_small(
         small_share, model, channels, HM, 1

time: 756 us -> 782 us (1.034)
  waiting for transfers between devices: 214 us -> 250 us
  other arithmetic: 143 us -> 132 us
    ppermute x43 -> x42, waiting for transfers between devices: 63.7 us -> 148 us  [exchange(): return lax.ppermute(block, MESH_AXES, route)]
    psum x4 -> x3, waiting for transfers between devices: 128 us -> 78 us  [line_sum(): return lax.psum(mine, 'ctx', axis_index_groups=lines)]
    ppermute x43 -> x42, starting transfers between devices: 43.4 us -> 36.6 us  [exchange(): return lax.ppermute(block, MESH_AXES, route)]
    unnamed x395 -> x403, local copies, waits for them, and re-layouts: 41.2 us -> 40 us
  transfers between devices with their start and end apart: 56 -> 54, of which waited for: 20 -> 18; matrix products, arithmetic and copies ran while one was open for 33% -> 31% of each run, Pallas kernels for 14% -> 14%
where the time goes in v7:
time: 782 us; the launch traced here: 771 us
  waiting for transfers between devices  250 us (32%)
  other arithmetic  132 us (17%)
  Pallas kernels  117 us (15%)
  matrix products  100 us (13%)
  local copies, waits for them, and re-layouts  99.9 us (13%)
  starting transfers between devices  52.2 us (7%)
  between operations  19.5 us (2%)
    ppermute x42, waiting for transfers between devices, exchange(): return lax.ppermute(block, MESH_AXES, route)  148 us
    psum x3, waiting for transfers between devices, line_sum(): return lax.psum(mine, 'ctx', axis_index_groups=lines)  78 us
    dot_general x21, matrix products, split_products(): lax.dot_general(piece, right, (((1 - axis,), (0,)), ((), ())), preferred_...  51.3 us
    unnamed x403, local copies, waits for them, and re-layouts  40 us
    ppermute x42, starting transfers between devices, exchange(): return lax.ppermute(block, MESH_AXES, route)  36.6 us
    dot_general x6, matrix products, nt_dot(): lax.dot_general(left, right, (((1,), (1,)), ((), ())), preferred_element_...  32.2 us
    pallas_call x1, Pallas kernels, per_device(): attend_backward(group_blocks, pairs, key_side, turned_q, mirrored_q, quer...  31.5 us
    convert_element_type x11, other arithmetic, add_low(): return total.astype(jnp.bfloat16)  22.1 us
  transfers between devices with their start and end apart: 54, of which 18 were waited for; matrix products, arithmetic and copies ran while one was open for 31% of the time, Pallas kernels for 14%

profile of v7, /device:TPU:0, one launch (start us, length us, event | category | flops | bytes accessed | tf_op | source)
XLA Modules:
  0.0 771.3 jit_solution(4949505077200567189)
XLA Ops:
  14.7 2.6 collective-permute-start.3
  39.0 16.4 %collective-permute-done.1.refs_4_ = bf16[144,4096]{1,0:T(8,128)(2,1)} collective-permute-done((bf16[144,4096]{1,0:T(8,128)(2,1)}, bf16[144,4096]{1,0:T(8,128)(2,1)}, u32[]{:S(2)}, u32[]{:S(2)}) %collective-permute-start.1) | collective-permute-done | bytes 1179680 | tf_op jit(solution)/shard_map/ppermute | solution.py:35
  66.2 9.9 %collective-permute-done.4.refs_3_ = bf16[64,4096]{1,0:T(8,128)(2,1)S(1)} collective-permute-done((bf16[64,4096]{1,0:T(8,128)(2,1)}, bf16[64,4096]{1,0:T(8,128)(2,1)S(1)}, u32[]{:S(2)}, u32[]{:S(2)}) %collective-permute-start.4) | collective-permute-done | bytes 524320 | tf_op jit(solution)/shard_map/ppermute | solution.py:35
  84.8 7.7 %assemble.5 = bf16[1024,4096]{1,0:T(8,128)(2,1)S(1)} custom-call(s32[16]{0:T(128)S(1)} %copy-done.56, bf16[272,4096]{1,0:T(8,128)(2,1)S(1)} %fusion.22.refs_0_, bf16[272,4096]{1,0:T(8,128)(2,1)} %collective-permute-done.refs_1_, bf16[64,4096]{1,0:T(8,128)(2,1)} %collective-permute-done.3.refs_2_, bf16[64,4096]{1,0:T(8,128)(2,1)S(1)} %collective-permute-done.4.refs_3_, ...), custom_call_target="tpu_custom_call" | custom-call | flops 1024 | bytes 1024 | tf_op jit(solution)/shard_map/assemble/pallas_call | solution.py:88
  92.5 4.6 fusion.203
  97.1 3.2 copy-done.79
  102.5 4.2 collective-permute-start.10
  114.8 5.4 multiply_convert_fusion.1
  120.2 5.6 state_outer.2
  133.5 2.5 copy.113
  139.0 9.8 %mixer_forward.1.refs_2_.local_ref = f32[512,1536]{1,0:T(8,128)S(1)} custom-call(f32[12,1,128]{2,1,0:T(1,128)S(1)} %copy-done.42, bf16[512,1792]{1,0:T(8,128)(2,1)S(1)} %get-tuple-element.99.x_ref.b_ref.c_ref.left_ref.right_ref, bf16[512,1792]{1,0:T(8,128)(2,1)S(1)} %get-tuple-element.99.x_ref.b_ref.c_ref.left_ref.right_ref, ...), custom_call_target="tpu_custom_call" | custom-call | flops 1024 | bytes 1024 | tf_op jit(solution)/shard_map/mixer_forward/pallas_call | solution.py:1025
  150.5 3.5 collective-permute-start.7
  161.2 5.8 collective-permute-done.7.query_b
  167.0 2.5 all-gather.7.cloned.1.call-done
  172.8 22.0 %attend_forward.1 = (f32[8,64,256]{2,1,0:T(8,128)S(1)}, f32[8,64,256]{2,1,0:T(8,128)S(1)}, f32[2,2,1,1024]{3,2,1,0:T(1,128)S(1)}) custom-call(s32[2]{0:T(128)S(1)} %copy-done.50, bf16[8,2,512,128]{3,2,1,0:T(8,128)(2,1)S(1)} %bitcast.263, bf16[4096,128]{1,0:T(8,128)(2,1)S(1)} %fusion.33.refs_8_.side_ref, bf16[8,64,512]{2,1,0:T(8,128)(2,1)S(1)} %copy-done.6, ...), custom_call_target="tpu_custom_call" | custom-call | flops 1024 | bytes 1024 | tf_op jit(solution)/shard_map/attend_forward/pallas_call | solution.py:1029
  217.6 3.0 assemble.7
  224.4 3.1 assemble.9
  231.6 13.4 %all-gather.9.cloned.1.call-done = bf16[6208,128]{1,0:T(8,128)(2,1)} async-done(((bf16[1552,128]{1,0:T(8,128)(2,1)}), bf16[6208,128]{1,0:T(8,128)(2,1)}) %all-gather.9.cloned.1.call-update) | async-done | bytes 1589264 | tf_op jit(solution)/shard_map/all_gather | solution.py:828
  253.7 4.1 assemble.8
  257.8 3.3 copy-done.3
  261.1 4.5 mixer_join.1
  265.6 3.0 multiply_reduce_fusion.6
  269.1 2.6 copy-done.23
  276.2 4.6 fusion.205
  280.8 6.7 bitcast_multiply_fusion.1
  287.5 4.1 add_convert_fusion
  291.6 10.9 %multiply_reduce_fusion.7 = (f32[1024]{0:T(1024)}, f32[512]{0:T(512)S(1)}, f32[512,1024]{1,0:T(8,128)S(1)}) fusion(f32[512,1024]{1,0:T(8,128)} %copy-done.64, f32[512]{0:T(512)S(1)} %fusion.160, f32[1024]{0:T(1024)S(1)} %bitcast.289, bf16[512,4096]{1,0:T(8,128)(2,1)S(1)} %add_convert_fusion, bf16[1024,4096]{1,0:T(8,128)(2,1)} %copy-done.3), kind=kOutput, calls=%fused_computation.82 | convolution fusion | flops 4298111488 | bytes 16789504 | tf_op jit(solution)/shard_map/dot_general | solution.py:350
  305.2 2.7 multiply_reduce_fusion.4
  315.1 4.4 convolution_convert_fusion
  319.7 2.8 convolution_convert_fusion.3
  327.4 5.3 fusion.189
  332.7 3.0 fusion.105
  343.2 5.7 fusion.95
  349.0 3.3 fusion.43
  356.0 2.7 add_convert_fusion.11.refs_0_
  358.7 2.6 add_convert_fusion.4.refs_0_
  361.4 4.3 add_convert_fusion.2.refs_1_
  366.5 14.0 %collective-permute-done.22.refs_1_ = bf16[512,1024]{1,0:T(8,128)(2,1)S(1)} collective-permute-done((bf16[512,1024]{1,0:T(8,128)(2,1)S(1)}, bf16[512,1024]{1,0:T(8,128)(2,1)S(1)}, u32[]{:S(2)}, u32[]{:S(2)}) %collective-permute-start.22) | collective-permute-done | bytes 1048608 | tf_op jit(solution)/shard_map/ppermute | solution.py:35
  380.5 3.4 add_convert_fusion.6.refs_0_
  383.9 6.0 state_outer.3.refs_1_
  394.4 7.7 collective-permute-done.19
  407.5 31.5 %attend_backward.1 = (f32[8,64,256]{2,1,0:T(8,128)S(1)}, f32[8,64,256]{2,1,0:T(8,128)S(1)}, bf16[8,2,512,128]{3,2,1,0:T(8,128)(2,1)}) custom-call(s32[2]{0:T(128)S(1)} %copy-done.51, bf16[8,2,512,128]{3,2,1,0:T(8,128)(2,1)} %bitcast.262, bf16[4096,128]{1,0:T(8,128)(2,1)S(1)} %fusion.33.refs_8_.side_ref, bf16[8,64,512]{2,1,0:T(8,128)(2,1)S(1)} %copy-done.7, ...), custom_call_target="tpu_custom_call" | custom-call | flops 1024 | bytes 1024 | tf_op jit(solution)/shard_map/attend_backward/pallas_call | solution.py:1085
  442.0 2.8 collective-permute-start.28
  447.6 4.4 add_convert_fusion.1
  457.9 17.9 %mixer_backward.1 = (f32[512,1792]{1,0:T(8,128)}, f32[12,1,128]{2,1,0:T(1,128)S(1)}) custom-call(f32[12,1,128]{2,1,0:T(1,128)S(1)} %copy-done.43, bf16[512,1792]{1,0:T(8,128)(2,1)} %copy-done, bf16[512,1792]{1,0:T(8,128)(2,1)} %copy-done, bf16[512,1792]{1,0:T(8,128)(2,1)} %copy-done, f32[12,8,512]{2,1,0:T(8,128)S(1)} %reshape.836.refs_10_.row_ref.rows_ref, ...), custom_call_target="tpu_custom_call" | custom-call | flops 1024 | bytes 1024 | tf_op jit(solution)/shard_map/mixer_backward/pallas_call | solution.py:1130
  476.2 18.7 %collective-permute-done.25 = bf16[128,4096]{1,0:T(8,128)(2,1)} collective-permute-done((bf16[128,4096]{1,0:T(8,128)(2,1)S(1)}, bf16[128,4096]{1,0:T(8,128)(2,1)}, u32[]{:S(2)}, u32[]{:S(2)}) %collective-permute-start.25) | collective-permute-done | bytes 1048608 | tf_op jit(solution)/shard_map/ppermute | solution.py:35
  498.7 10.3 %multiply_reduce_fusion.3 = (f32[1792]{0:T(1024)S(1)}, f32[1792]{0:T(1024)S(1)}, f32[1792]{0:T(1024)S(1)}, f32[1792]{0:T(1024)S(1)}, f32[1792]{0:T(1024)S(1)}, /*index=5*/f32[512,1792]{1,0:T(8,128)S(1)}) fusion(f32[515,1792]{1,0:T(8,128)} %copy-done.57, f32[512]{0:T(512)S(1)} %bitcast.307, f32[512]{0:T(512)S(1)} %bitcast.310, f32[512]{0:T(512)S(1)} %bitcast.313, ...), kind=kLoop, calls=%fused_computation.32 | loop fusion | flops 20176128 | bytes 25734144 | tf_op jit(solution)/shard_map/transpose(jvp())/reduce_sum | solution.py:328
  511.8 2.9 pad_add_fusion
  519.0 5.5 collective-permute-start.30
  525.9 2.5 fusion.8.refs_1_
  536.4 12.1 %collective-permute-done.30 = bf16[2,2,512,128]{2,3,1,0:T(8,128)(2,1)} collective-permute-done((bf16[2,2,512,128]{2,3,1,0:T(8,128)(2,1)}, bf16[2,2,512,128]{2,3,1,0:T(8,128)(2,1)}, u32[]{:S(2)}, u32[]{:S(2)}) %collective-permute-start.30) | collective-permute-done | bytes 524320 | tf_op jit(solution)/shard_map/ppermute | solution.py:35
  549.7 2.5 collective-permute-start.31
  554.1 21.9 %collective-permute-done.31 = bf16[1,2,512,128]{2,3,1,0:T(8,128)(2,1)S(1)} collective-permute-done((bf16[1,2,512,128]{2,3,1,0:T(8,128)(2,1)S(1)}, bf16[1,2,512,128]{2,3,1,0:T(8,128)(2,1)S(1)}, u32[]{:S(2)}, u32[]{:S(2)}) %collective-permute-start.31) | collective-permute-done | bytes 262176 | tf_op jit(solution)/shard_map/ppermute | solution.py:35
  577.4 2.9 fusion.19.refs_1_
  580.3 9.0 %all-reduce.20.cloned.1.call-done.refs_2_.refs_1_.refs_0_ = bf16[128,6144]{1,0:T(8,128)(2,1)} async-done(((bf16[128,6144]{1,0:T(8,128)(2,1)}), bf16[128,6144]{1,0:T(8,128)(2,1)}) %all-reduce.20.cloned.1.call-update) | async-done | bytes 1572880 | tf_op jit(solution)/shard_map/psum | solution.py:209
  589.3 2.8 fusion.35
  592.2 8.3 %fusion.24 = (f32[1024]{0:T(1024)S(1)}, f32[512]{0:T(512)S(1)}, f32[512,1024]{1,0:T(8,128)}) fusion(bf16[1,512,1024]{2,1,0:T(8,128)(2,1)S(1)} %copy-done.75, f32[512]{0:T(512)S(1)} %copy-done.182, f32[1024]{0:T(1024)S(1)} %bitcast.301, f32[512,1024]{1,0:T(8,128)S(1)} %fusion.35, bf16[1024,4096]{1,0:T(8,128)(2,1)} %copy-done.4, ...), kind=kOutput, calls=%fused_computation.68 | convolution fusion | flops 3500669440 | bytes 15478784 | tf_op jit(solution)/shard_map/dot_general | solution.py:350
  607.5 19.7 %collective-permute-done.34 = f32[128,128]{1,0:T(8,128)S(1)} collective-permute-done((f32[128,128]{1,0:T(8,128)S(1)}, f32[128,128]{1,0:T(8,128)S(1)}, u32[]{:S(2)}, u32[]{:S(2)}) %collective-permute-start.34) | collective-permute-done | bytes 65568 | tf_op jit(solution)/shard_map/ppermute | solution.py:35
  633.0 2.5 fusion.102
  638.4 3.9 collective-permute-done.44
  647.3 2.5 collective-permute-done.37
  650.4 33.2 %all-reduce.22.cloned.1.call-done.refs_1_ = bf16[128,3584]{1,0:T(8,128)(2,1)} async-done(((bf16[128,3584]{1,0:T(8,128)(2,1)}), bf16[128,3584]{1,0:T(8,128)(2,1)}) %all-reduce.22.cloned.1.call-update) | async-done | bytes 917520 | tf_op jit(solution)/shard_map/psum | solution.py:209
  690.2 35.8 %all-reduce.24.cloned.1.call-done = bf16[128,2560]{1,0:T(8,128)(2,1)} async-done(((bf16[128,2560]{1,0:T(8,128)(2,1)}), bf16[128,2560]{1,0:T(8,128)(2,1)}) %all-reduce.24.cloned.1.call-update) | async-done | bytes 655376 | tf_op jit(solution)/shard_map/psum | solution.py:209
  732.8 20.9 %collective-permute-done.46 = bf16[128,2560]{1,0:T(8,128)(2,1)S(1)} collective-permute-done((bf16[128,2560]{1,0:T(8,128)(2,1)}, bf16[128,2560]{1,0:T(8,128)(2,1)S(1)}, u32[]{:S(2)}, u32[]{:S(2)}) %collective-permute-start.46) | collective-permute-done | bytes 655392 | tf_op jit(solution)/shard_map/ppermute | solution.py:35
  (762 shorter events, 240.5 us)
Async XLA Ops:
  7.2 162.3 %all-gather.7.cloned.1.call-start = ((), (), s32[]{:S(2)}) async-start(), calls=%async_computation.3 | async-start | bytes 2359296 | tf_op jit(solution)/shard_map/all_gather | solution.py:1010
  13.4 64.0 %collective-permute-start = (bf16[272,4096]{1,0:T(8,128)(2,1)S(1)}, bf16[272,4096]{1,0:T(8,128)(2,1)}, u32[]{:S(2)}, u32[]{:S(2)}) collective-permute-start(bf16[272,4096]{1,0:T(8,128)(2,1)S(1)} %fusion.22.refs_0_), channel_id=1, source_target_pairs={{0,1},{1,0},{2,3},{3,2},{4,5},{5,4},{6,7},{7,6},{8,9},{9,8},{10,11... | collective-permute-start | bytes 6684680 | tf_op jit(solution)/shard_map/ppermute | solution.py:35
  14.7 46.8 %collective-permute-start.3 = (bf16[64,4096]{1,0:T(8,128)(2,1)}, bf16[64,4096]{1,0:T(8,128)(2,1)}, u32[]{:S(2)}, u32[]{:S(2)}) collective-permute-start(bf16[64,4096]{1,0:T(8,128)(2,1)} %constant_dynamic-slice_fusion.15), channel_id=1, source_target_pairs={{0,2},{1,3},{2,0},{3,1},{4,6},{5,7},{6,4},{7,5},{8,10},{9,11},{10,... | collective-permute-start | bytes 1572872 | tf_op jit(solution)/shard_map/ppermute | solution.py:35
  18.4 37.0 %collective-permute-start.1 = (bf16[144,4096]{1,0:T(8,128)(2,1)}, bf16[144,4096]{1,0:T(8,128)(2,1)}, u32[]{:S(2)}, u32[]{:S(2)}) collective-permute-start(bf16[144,4096]{1,0:T(8,128)(2,1)} %slice.490), channel_id=1, source_target_pairs={{0,2},{1,3},{2,0},{3,1},{4,6},{5,7},{6,4},{7,5},{8,10},{9,11},{10,... | collective-permute-start | bytes 3538952 | tf_op jit(solution)/shard_map/ppermute | solution.py:35
  28.1 27.3 %copy-start.117 = (bf16[512,1024]{1,0:T(8,128)(2,1)S(1)}, bf16[512,1024]{1,0:T(8,128)(2,1)}, u32[]{:S(2)}) copy-start(bf16[512,1024]{1,0:T(8,128)(2,1)} %param.33) | copy-start | bytes 3145732
  28.1 27.3 %copy-start.119 = (bf16[384,1024]{1,0:T(8,128)(2,1)S(1)}, bf16[384,1024]{1,0:T(8,128)(2,1)}, u32[]{:S(2)}) copy-start(bf16[384,1024]{1,0:T(8,128)(2,1)} %param.27) | copy-start | bytes 2359300
  55.4 24.6 %collective-permute-start.2 = (bf16[144,4096]{1,0:T(8,128)(2,1)}, bf16[144,4096]{1,0:T(8,128)(2,1)}, u32[]{:S(2)}, u32[]{:S(2)}) collective-permute-start(bf16[144,4096]{1,0:T(8,128)(2,1)} %collective-permute-done.1.refs_4_), channel_id=1, source_target_pairs={{0,1},{1,0},{2,3},{3,2},{4,5},{5,4},{6,7},{7,6},{8,9},{9,8},{10,11... | collective-permute-start | bytes 3538952 | tf_op jit(solution)/shard_map/ppermute | solution.py:35
  61.5 14.5 %collective-permute-start.4 = (bf16[64,4096]{1,0:T(8,128)(2,1)}, bf16[64,4096]{1,0:T(8,128)(2,1)S(1)}, u32[]{:S(2)}, u32[]{:S(2)}) collective-permute-start(bf16[64,4096]{1,0:T(8,128)(2,1)} %collective-permute-done.3.refs_2_), channel_id=1, source_target_pairs={{0,4},{1,5},{2,6},{3,7},{4,0},{5,1},{6,2},{7,3},{8,12},{9,13},{10,... | collective-permute-start | bytes 1572872 | tf_op jit(solution)/shard_map/ppermute | solution.py:35
  66.0 18.3 %collective-permute-start.5 = (bf16[64,4096]{1,0:T(8,128)(2,1)}, bf16[64,4096]{1,0:T(8,128)(2,1)S(1)}, u32[]{:S(2)}, u32[]{:S(2)}) collective-permute-start(bf16[64,4096]{1,0:T(8,128)(2,1)} %collective-permute-done.3.refs_2_), channel_id=1, source_target_pairs={{0,1},{1,0},{2,3},{3,2},{4,5},{5,4},{6,7},{7,6},{8,9},{9,8},{10,11... | collective-permute-start | bytes 1572872 | tf_op jit(solution)/shard_map/ppermute | solution.py:35
  76.1 8.6 %collective-permute-start.6 = (bf16[64,4096]{1,0:T(8,128)(2,1)S(1)}, bf16[64,4096]{1,0:T(8,128)(2,1)S(1)}, u32[]{:S(2)}, u32[]{:S(2)}) collective-permute-start(bf16[64,4096]{1,0:T(8,128)(2,1)S(1)} %collective-permute-done.4.refs_3_), channel_id=1, source_target_pairs={{0,1},{1,0},{2,3},{3,2},{4,5},{5,4},{6,7},{7,6},{8,9},{9,8},{10,11... | collective-permute-start | bytes 1572872 | tf_op jit(solution)/shard_map/ppermute | solution.py:35
  76.1 91.0 %collective-permute-start.9 = (bf16[256,4096]{1,0:T(8,128)(2,1)}, bf16[256,4096]{1,0:T(8,128)(2,1)}, u32[]{:S(2)}, u32[]{:S(2)}) collective-permute-start(bf16[256,4096]{1,0:T(8,128)(2,1)} %refs_0_), channel_id=1, source_target_pairs={{0,1},{1,0},{2,3},{3,2},{4,5},{5,4},{6,7},{7,6},{8,9},{9,8},{10,11... | collective-permute-start | bytes 6291464 | tf_op jit(solution)/shard_map/ppermute | solution.py:35
  77.4 135.2 %collective-permute-start.15 = (bf16[256,4096]{1,0:T(8,128)(2,1)}, bf16[256,4096]{1,0:T(8,128)(2,1)}, u32[]{:S(2)}, u32[]{:S(2)}) collective-permute-start(bf16[256,4096]{1,0:T(8,128)(2,1)} %refs_0_), channel_id=1, source_target_pairs={{0,2},{1,3},{2,0},{3,1},{4,6},{5,7},{6,4},{7,5},{8,10},{9,11},{10,... | collective-permute-start | bytes 6291464 | tf_op jit(solution)/shard_map/ppermute | solution.py:35
  80.1 86.9 %collective-permute-start.8 = (bf16[1024,1024]{1,0:T(8,128)(2,1)}, bf16[1024,1024]{1,0:T(8,128)(2,1)}, u32[]{:S(2)}, u32[]{:S(2)}) collective-permute-start(bf16[1024,1024]{1,0:T(8,128)(2,1)} %pad_maximum_fusion.1.refs_0_), channel_id=1, source_target_pairs={{0,1},{1,0},{2,3},{3,2},{4,5},{5,4},{6,7},{7,6},{8,9},{9,8},{10,11... | collective-permute-start | bytes 6291464 | tf_op jit(solution)/shard_map/ppermute | solution.py:35
  84.3 112.7 %collective-permute-start.12 = (bf16[1024,1024]{1,0:T(8,128)(2,1)}, bf16[1024,1024]{1,0:T(8,128)(2,1)}, u32[]{:S(2)}, u32[]{:S(2)}) collective-permute-start(bf16[1024,1024]{1,0:T(8,128)(2,1)} %pad_maximum_fusion.1.refs_0_), channel_id=1, source_target_pairs={{0,2},{1,3},{2,0},{3,1},{4,6},{5,7},{6,4},{7,5},{8,10},{9,11},{10,... | collective-permute-start | bytes 6291464 | tf_op jit(solution)/shard_map/ppermute | solution.py:35
  102.5 11.0 %collective-permute-start.10 = (bf16[3,1792]{1,0:T(4,128)(2,1)}, bf16[3,1792]{1,0:T(4,128)(2,1)}, u32[]{:S(2)}, u32[]{:S(2)}) collective-permute-start(bf16[3,1792]{1,0:T(4,128)(2,1)} %slice.504), channel_id=1, source_target_pairs={{0,4},{4,8},{8,12},{12,16},{16,20},{20,24},{24,28},{1,5},{5,9},{9,... | collective-permute-start | bytes 32264 | tf_op jit(solution)/shard_map/ppermute | solution.py:41
  111.2 133.8 %all-gather.9.cloned.1.call-start = ((), (), s32[]{:S(2)}) async-start(), calls=%async_computation.4 | async-start | bytes 1986560 | tf_op jit(solution)/shard_map/all_gather | solution.py:828
  120.1 263.8 %copy-start = (bf16[512,1792]{1,0:T(8,128)(2,1)}, bf16[512,1792]{1,0:T(8,128)(2,1)S(1)}, u32[]{:S(2)}) copy-start(bf16[512,1792]{1,0:T(8,128)(2,1)S(1)} %get-tuple-element.99.x_ref.b_ref.c_ref.left_ref.right_ref) | copy-start | bytes 5505028
  126.6 23.9 %collective-permute-start.14 = (bf16[1552,128]{1,0:T(8,128)(2,1)}, bf16[1552,128]{1,0:T(8,128)(2,1)}, u32[]{:S(2)}, u32[]{:S(2)}) collective-permute-start(bf16[1552,128]{1,0:T(8,128)(2,1)} %pad_maximum_fusion.10), channel_id=1, source_target_pairs={{0,4},{1,5},{2,6},{3,7},{4,0},{5,1},{6,2},{7,3},{8,12},{9,13},{10,... | collective-permute-start | bytes 1191944 | tf_op jit(solution)/shard_map/ppermute | solution.py:35
  150.5 16.5 %collective-permute-start.7 = (bf16[8,64,256]{2,1,0:T(8,128)(2,1)}, bf16[8,64,256]{2,1,0:T(8,128)(2,1)}, u32[]{:S(2)}, u32[]{:S(2)}) collective-permute-start(bf16[8,64,256]{2,1,0:T(8,128)(2,1)} %slice.501), channel_id=1, source_target_pairs={{0,28},{4,24},{8,20},{12,16},{16,12},{20,8},{24,4},{28,0},{1,29},{... | collective-permute-start | bytes 786440 | tf_op jit(solution)/shard_map/ppermute | solution.py:46
  197.0 20.7 %collective-permute-start.13 = (bf16[1024,1024]{1,0:T(8,128)(2,1)}, bf16[1024,1024]{1,0:T(8,128)(2,1)}, u32[]{:S(2)}, u32[]{:S(2)}) collective-permute-start(bf16[1024,1024]{1,0:T(8,128)(2,1)} %collective-permute-done.12.refs_2_), channel_id=1, source_target_pairs={{0,1},{1,0},{2,3},{3,2},{4,5},{5,4},{6,7},{7,6},{8,9},{9,8},{10,11... | collective-permute-start | bytes 6291464 | tf_op jit(solution)/shard_map/ppermute | solution.py:35
  197.8 257.2 %all-gather.11.cloned.1.call-start = ((), (), s32[]{:S(2)}) async-start(), calls=%async_computation.5 | async-start | bytes 1966080 | tf_op jit(solution)/shard_map/all_gather | solution.py:828
  202.0 13.8 %collective-permute-start.11 = (bf16[8,64,256]{2,1,0:T(8,128)(2,1)}, bf16[8,64,256]{2,1,0:T(8,128)(2,1)}, u32[]{:S(2)}, u32[]{:S(2)}) collective-permute-start(bf16[8,64,256]{2,1,0:T(8,128)(2,1)} %convert_element_type.649), channel_id=1, source_target_pairs={{0,28},{4,24},{8,20},{12,16},{16,12},{20,8},{24,4},{28,0},{1,29},{... | collective-permute-start | bytes 786440 | tf_op jit(solution)/shard_map/ppermute | solution.py:46
  212.7 41.0 %collective-permute-start.16 = (bf16[256,4096]{1,0:T(8,128)(2,1)}, bf16[256,4096]{1,0:T(8,128)(2,1)}, u32[]{:S(2)}, u32[]{:S(2)}) collective-permute-start(bf16[256,4096]{1,0:T(8,128)(2,1)} %collective-permute-done.15.refs_2_), channel_id=1, source_target_pairs={{0,1},{1,0},{2,3},{3,2},{4,5},{5,4},{6,7},{7,6},{8,9},{9,8},{10,11... | collective-permute-start | bytes 6291464 | tf_op jit(solution)/shard_map/ppermute | solution.py:35
  313.5 45.3 %collective-permute-start.24 = (bf16[1024,1024]{1,0:T(8,128)(2,1)}, bf16[1024,1024]{1,0:T(8,128)(2,1)}, u32[]{:S(2)}, u32[]{:S(2)}) collective-permute-start(bf16[1024,1024]{1,0:T(8,128)(2,1)} %pad_maximum_fusion.2), channel_id=1, source_target_pairs={{0,1},{1,0},{2,3},{3,2},{4,5},{5,4},{6,7},{7,6},{8,9},{9,8},{10,11... | collective-permute-start | bytes 6291464 | tf_op jit(solution)/shard_map/ppermute | solution.py:35
  319.5 41.8 %collective-permute-start.18 = (bf16[512,4096]{1,0:T(8,128)(2,1)}, bf16[512,4096]{1,0:T(8,128)(2,1)}, u32[]{:S(2)}, u32[]{:S(2)}) collective-permute-start(bf16[512,4096]{1,0:T(8,128)(2,1)} %convolution_convert_fusion), channel_id=1, source_target_pairs={{0,1},{1,0},{2,3},{3,2},{4,5},{5,4},{6,7},{7,6},{8,9},{9,8},{10,11... | collective-permute-start | bytes 12582920 | tf_op jit(solution)/shard_map/ppermute | solution.py:35
  322.5 29.9 %collective-permute-start.17 = (bf16[1024,1024]{1,0:T(8,128)(2,1)}, bf16[1024,1024]{1,0:T(8,128)(2,1)}, u32[]{:S(2)}, u32[]{:S(2)}) collective-permute-start(bf16[1024,1024]{1,0:T(8,128)(2,1)} %convolution_convert_fusion.3), channel_id=1, source_target_pairs={{0,1},{1,0},{2,3},{3,2},{4,5},{5,4},{6,7},{7,6},{8,9},{9,8},{10,11... | collective-permute-start | bytes 6291464 | tf_op jit(solution)/shard_map/ppermute | solution.py:35
  323.7 79.5 %collective-permute-start.27 = (bf16[8,64,256]{2,1,0:T(8,128)(2,1)}, bf16[8,64,256]{2,1,0:T(8,128)(2,1)}, u32[]{:S(2)}, u32[]{:S(2)}) collective-permute-start(bf16[8,64,256]{2,1,0:T(8,128)(2,1)} %slice.540), channel_id=1, source_target_pairs={{0,28},{4,24},{8,20},{12,16},{16,12},{20,8},{24,4},{28,0},{1,29},{... | collective-permute-start | bytes 786440 | tf_op jit(solution)/shard_map/ppermute | solution.py:46
  339.4 16.7 %collective-permute-start.21 = (bf16[512,1536]{1,0:T(8,128)(2,1)}, bf16[512,1536]{1,0:T(8,128)(2,1)}, u32[]{:S(2)}, u32[]{:S(2)}) collective-permute-start(bf16[512,1536]{1,0:T(8,128)(2,1)} %convolution_convert_fusion.1), channel_id=1, source_target_pairs={{0,1},{1,0},{2,3},{3,2},{4,5},{5,4},{6,7},{7,6},{8,9},{9,8},{10,11... | collective-permute-start | bytes 4718600 | tf_op jit(solution)/shard_map/ppermute | solution.py:35
  354.5 26.0 %collective-permute-start.22 = (bf16[512,1024]{1,0:T(8,128)(2,1)S(1)}, bf16[512,1024]{1,0:T(8,128)(2,1)S(1)}, u32[]{:S(2)}, u32[]{:S(2)}) collective-permute-start(bf16[512,1024]{1,0:T(8,128)(2,1)S(1)} %add_convert_fusion.7), channel_id=1, source_target_pairs={{0,2},{1,3},{2,0},{3,1},{4,6},{5,7},{6,4},{7,5},{8,10},{9,11},{10,... | collective-permute-start | bytes 3145736 | tf_op jit(solution)/shard_map/ppermute | solution.py:35
  365.7 80.4 %collective-permute-start.20 = (bf16[256,4096]{1,0:T(8,128)(2,1)}, bf16[256,4096]{1,0:T(8,128)(2,1)}, u32[]{:S(2)}, u32[]{:S(2)}) collective-permute-start(bf16[256,4096]{1,0:T(8,128)(2,1)} %add_convert_fusion.2.refs_1_), channel_id=1, source_target_pairs={{0,2},{1,3},{2,0},{3,1},{4,6},{5,7},{6,4},{7,5},{8,10},{9,11},{10,... | collective-permute-start | bytes 6291464 | tf_op jit(solution)/shard_map/ppermute | solution.py:35
  389.9 12.1 %collective-permute-start.19 = (bf16[1536,128]{1,0:T(8,128)(2,1)S(1)}, bf16[1536,128]{1,0:T(8,128)(2,1)S(1)}, u32[]{:S(2)}, u32[]{:S(2)}) collective-permute-start(bf16[1536,128]{1,0:T(8,128)(2,1)S(1)} %state_outer.3.refs_1_), channel_id=1, source_target_pairs={{0,4},{1,5},{2,6},{3,7},{4,0},{5,1},{6,2},{7,3},{8,12},{9,13},{10,... | collective-permute-start | bytes 1179656 | tf_op jit(solution)/shard_map/ppermute | solution.py:35
  393.0 59.0 %collective-permute-start.23 = (bf16[128,2048]{1,0:T(8,128)(2,1)}, bf16[128,2048]{1,0:T(8,128)(2,1)}, u32[]{:S(2)}, u32[]{:S(2)}) collective-permute-start(bf16[128,2048]{1,0:T(8,128)(2,1)} %fusion.79), channel_id=1, source_target_pairs={{0,4},{1,5},{2,6},{3,7},{4,0},{5,1},{6,2},{7,3},{8,12},{9,13},{10,... | collective-permute-start | bytes 1572872 | tf_op jit(solution)/shard_map/ppermute | solution.py:35
  439.8 91.0 %collective-permute-start.38 = (bf16[512,1024]{1,0:T(8,128)(2,1)}, bf16[512,1024]{1,0:T(8,128)(2,1)}, u32[]{:S(2)}, u32[]{:S(2)}) collective-permute-start(bf16[512,1024]{1,0:T(8,128)(2,1)} %tie.18), channel_id=1, source_target_pairs={{0,2},{1,3},{2,0},{3,1},{4,6},{5,7},{6,4},{7,5},{8,10},{9,11},{10,... | collective-permute-start | bytes 3145736 | tf_op jit(solution)/shard_map/ppermute | solution.py:35
  441.3 89.5 %collective-permute-start.39 = (bf16[256,1536]{1,0:T(8,128)(2,1)}, bf16[256,1536]{1,0:T(8,128)(2,1)}, u32[]{:S(2)}, u32[]{:S(2)}) collective-permute-start(bf16[256,1536]{1,0:T(8,128)(2,1)} %tie.20), channel_id=1, source_target_pairs={{0,2},{1,3},{2,0},{3,1},{4,6},{5,7},{6,4},{7,5},{8,10},{9,11},{10,... | collective-permute-start | bytes 2359304 | tf_op jit(solution)/shard_map/ppermute | solution.py:35
  442.0 11.8 %collective-permute-start.28 = (bf16[8,64,256]{2,1,0:T(8,128)(2,1)S(1)}, bf16[8,64,256]{2,1,0:T(8,128)(2,1)S(1)}, u32[]{:S(2)}, u32[]{:S(2)}) collective-permute-start(bf16[8,64,256]{2,1,0:T(8,128)(2,1)S(1)} %fusion.85), channel_id=1, source_target_pairs={{0,28},{4,24},{8,20},{12,16},{16,12},{20,8},{24,4},{28,0},{1,29},{... | collective-permute-start | bytes 786440 | tf_op jit(solution)/shard_map/ppermute | solution.py:46
  446.0 68.8 %collective-permute-start.29 = (bf16[4,2,512,128]{3,2,1,0:T(8,128)(2,1)}, bf16[4,2,512,128]{3,2,1,0:T(8,128)(2,1)}, u32[]{:S(2)}, u32[]{:S(2)}) collective-permute-start(bf16[4,2,512,128]{3,2,1,0:T(8,128)(2,1)} %dynamic-slice_bitcast_fusion), channel_id=1, source_target_pairs={{0,4},{1,5},{2,6},{3,7},{4,0},{5,1},{6,2},{7,3},{8,12},{9,13},{10,... | collective-permute-start | bytes 3145736 | tf_op jit(solution)/shard_map/ppermute | solution.py:35
  452.1 42.8 %collective-permute-start.25 = (bf16[128,4096]{1,0:T(8,128)(2,1)S(1)}, bf16[128,4096]{1,0:T(8,128)(2,1)}, u32[]{:S(2)}, u32[]{:S(2)}) collective-permute-start(bf16[128,4096]{1,0:T(8,128)(2,1)S(1)} %constant_dynamic-slice_fusion.10.refs_0_), channel_id=1, source_target_pairs={{0,4},{1,5},{2,6},{3,7},{4,0},{5,1},{6,2},{7,3},{8,12},{9,13},{10,... | collective-permute-start | bytes 3145736 | tf_op jit(solution)/shard_map/ppermute | solution.py:35
  498.0 91.3 %all-reduce.20.cloned.1.call-start = ((), (), s32[]{:S(2)}) async-start(), calls=%async_computation | async-start | bytes 3145728 | tf_op jit(solution)/shard_map/psum | solution.py:209
  498.6 185.0 %all-reduce.22.cloned.1.call-start = ((), (), s32[]{:S(2)}) async-start(), calls=%async_computation.1 | async-start | bytes 1835008 | tf_op jit(solution)/shard_map/psum | solution.py:209
  510.5 15.3 %collective-permute-start.26 = (f32[3,1792]{1,0:T(4,128)S(1)}, f32[3,1792]{1,0:T(4,128)S(1)}, u32[]{:S(2)}, u32[]{:S(2)}) collective-permute-start(f32[3,1792]{1,0:T(4,128)S(1)} %pad_add_fusion.1), channel_id=1, source_target_pairs={{4,0},{8,4},{12,8},{16,12},{20,16},{24,20},{28,24},{5,1},{9,5},{13... | collective-permute-start | bytes 64520 | tf_op jit(solution)/shard_map/ppermute | solution.py:41
  519.0 29.5 %collective-permute-start.30 = (bf16[2,2,512,128]{2,3,1,0:T(8,128)(2,1)}, bf16[2,2,512,128]{2,3,1,0:T(8,128)(2,1)}, u32[]{:S(2)}, u32[]{:S(2)}) collective-permute-start(bf16[2,2,512,128]{2,3,1,0:T(8,128)(2,1)} %bitcast.90), channel_id=1, source_target_pairs={{0,8},{1,9},{2,10},{3,11},{4,12},{5,13},{6,14},{7,15},{8,0},{9,1},... | collective-permute-start | bytes 1572872 | tf_op jit(solution)/shard_map/ppermute | solution.py:35
  530.8 46.7 %collective-permute-start.32 = (bf16[512,1792]{1,0:T(8,128)(2,1)}, bf16[512,1792]{1,0:T(8,128)(2,1)}, u32[]{:S(2)}, u32[]{:S(2)}) collective-permute-start(bf16[512,1792]{1,0:T(8,128)(2,1)} %convolution_convert_fusion.2), channel_id=1, source_target_pairs={{0,1},{1,0},{2,3},{3,2},{4,5},{5,4},{6,7},{7,6},{8,9},{9,8},{10,11... | collective-permute-start | bytes 5505032 | tf_op jit(solution)/shard_map/ppermute | solution.py:35
  536.4 39.7 %copy-start.80 = (bf16[256,3584]{1,0:T(8,128)(2,1)}, bf16[256,3584]{1,0:T(8,128)(2,1)S(1)}, u32[]{:S(2)}) copy-start(bf16[256,3584]{1,0:T(8,128)(2,1)S(1)} %pad_maximum_fusion.4) | copy-start | bytes 5505028
  536.4 39.7 %copy-start.31 = (f32[32,512]{1,0:T(8,128)S(1)}, f32[32,512]{1,0:T(8,128)}, u32[]{:S(2)}) copy-start(f32[32,512]{1,0:T(8,128)} %get-tuple-element.45.refs_14_) | copy-start | bytes 196612
  536.4 39.7 %copy-start.144 = (f32[32,512]{1,0:T(8,128)S(1)}, f32[32,512]{1,0:T(8,128)}, u32[]{:S(2)}) copy-start(f32[32,512]{1,0:T(8,128)} %neg.37) | copy-start | bytes 196612
  549.7 26.8 %copy-start.109 = (bf16[512,512]{0,1:T(8,128)(2,1)S(1)}, bf16[512,512]{0,1:T(8,128)(2,1)}, u32[]{:S(2)}) copy-start(bf16[512,512]{0,1:T(8,128)(2,1)} %copy.118) | copy-start | bytes 1572868
  549.7 26.2 %collective-permute-start.31 = (bf16[1,2,512,128]{2,3,1,0:T(8,128)(2,1)S(1)}, bf16[1,2,512,128]{2,3,1,0:T(8,128)(2,1)S(1)}, u32[]{:S(2)}, u32[]{:S(2)}) collective-permute-start(bf16[1,2,512,128]{2,3,1,0:T(8,128)(2,1)S(1)} %constant_dynamic-slice_fusion.1), channel_id=1, source_target_pairs={{0,16},{1,17},{2,18},{3,19},{4,20},{5,21},{6,22},{7,23},{8,24},{9,... | collective-permute-start | bytes 786440 | tf_op jit(solution)/shard_map/ppermute | solution.py:35
  553.2 52.0 %collective-permute-start.40 = (bf16[128,3584]{1,0:T(8,128)(2,1)}, bf16[128,3584]{1,0:T(8,128)(2,1)}, u32[]{:S(2)}, u32[]{:S(2)}) collective-permute-start(bf16[128,3584]{1,0:T(8,128)(2,1)} %constant_dynamic-slice_fusion), channel_id=1, source_target_pairs={{0,4},{1,5},{2,6},{3,7},{4,0},{5,1},{6,2},{7,3},{8,12},{9,13},{10,... | collective-permute-start | bytes 2752520 | tf_op jit(solution)/shard_map/ppermute | solution.py:35
  600.7 28.8 %copy-start.82 = (bf16[512,768]{1,0:T(8,128)(2,1)S(1)}, bf16[512,768]{1,0:T(8,128)(2,1)}, u32[]{:S(2)}) copy-start(bf16[512,768]{1,0:T(8,128)(2,1)} %tie.17) | copy-start | bytes 2359300
  600.7 3.9 collective-permute-start.33
  602.8 33.1 %collective-permute-start.42 = (bf16[256,1792]{1,0:T(8,128)(2,1)}, bf16[256,1792]{1,0:T(8,128)(2,1)}, u32[]{:S(2)}, u32[]{:S(2)}) collective-permute-start(bf16[256,1792]{1,0:T(8,128)(2,1)} %fusion.19.refs_1_), channel_id=1, source_target_pairs={{0,2},{1,3},{2,0},{3,1},{4,6},{5,7},{6,4},{7,5},{8,10},{9,11},{10,... | collective-permute-start | bytes 2752520 | tf_op jit(solution)/shard_map/ppermute | solution.py:35
  604.4 24.2 %collective-permute-start.43 = (bf16[512,768]{1,0:T(8,128)(2,1)S(1)}, bf16[512,768]{1,0:T(8,128)(2,1)S(1)}, u32[]{:S(2)}, u32[]{:S(2)}) collective-permute-start(bf16[512,768]{1,0:T(8,128)(2,1)S(1)} %convolution_convert_fusion.5), channel_id=1, source_target_pairs={{0,1},{1,0},{2,3},{3,2},{4,5},{5,4},{6,7},{7,6},{8,9},{9,8},{10,11... | collective-permute-start | bytes 2359304 | tf_op jit(solution)/shard_map/ppermute | solution.py:35
  604.7 22.6 %collective-permute-start.34 = (f32[128,128]{1,0:T(8,128)S(1)}, f32[128,128]{1,0:T(8,128)S(1)}, u32[]{:S(2)}, u32[]{:S(2)}) collective-permute-start(f32[128,128]{1,0:T(8,128)S(1)} %add.768), channel_id=1, source_target_pairs={{0,2},{1,3},{2,0},{3,1},{4,6},{5,7},{6,4},{7,5},{8,10},{9,11},{10,... | collective-permute-start | bytes 196616 | tf_op jit(solution)/shard_map/ppermute | solution.py:35
  627.2 8.2 %collective-permute-start.35 = (f32[32,128]{1,0:T(8,128)S(1)}, f32[32,128]{1,0:T(8,128)S(1)}, u32[]{:S(2)}, u32[]{:S(2)}) collective-permute-start(f32[32,128]{1,0:T(8,128)S(1)} %dynamic-slice_add_fusion), channel_id=1, source_target_pairs={{0,4},{1,5},{2,6},{3,7},{4,0},{5,1},{6,2},{7,3},{8,12},{9,13},{10,... | collective-permute-start | bytes 49160 | tf_op jit(solution)/shard_map/ppermute | solution.py:35
  631.6 10.7 %collective-permute-start.44 = (bf16[256,768]{1,0:T(8,128)(2,1)}, bf16[256,768]{1,0:T(8,128)(2,1)S(1)}, u32[]{:S(2)}, u32[]{:S(2)}) collective-permute-start(bf16[256,768]{1,0:T(8,128)(2,1)} %tie.23), channel_id=1, source_target_pairs={{0,2},{1,3},{2,0},{3,1},{4,6},{5,7},{6,4},{7,5},{8,10},{9,11},{10,... | collective-permute-start | bytes 1179656 | tf_op jit(solution)/shard_map/ppermute | solution.py:35
  635.5 8.8 %collective-permute-start.36 = (f32[32,128]{1,0:T(8,128)S(1)}, f32[32,128]{1,0:T(8,128)S(1)}, u32[]{:S(2)}, u32[]{:S(2)}) collective-permute-start(f32[32,128]{1,0:T(8,128)S(1)} %add.771), channel_id=1, source_target_pairs={{0,8},{1,9},{2,10},{3,11},{4,12},{5,13},{6,14},{7,15},{8,0},{9,1},... | collective-permute-start | bytes 49160 | tf_op jit(solution)/shard_map/ppermute | solution.py:35
  635.6 90.5 %all-reduce.24.cloned.1.call-start = ((), (), s32[]{:S(2)}) async-start(), calls=%async_computation.2 | async-start | bytes 1310720 | tf_op jit(solution)/shard_map/psum | solution.py:209
  643.5 41.5 %collective-permute-start.45 = (bf16[128,2560]{1,0:T(8,128)(2,1)S(1)}, bf16[128,2560]{1,0:T(8,128)(2,1)}, u32[]{:S(2)}, u32[]{:S(2)}) collective-permute-start(bf16[128,2560]{1,0:T(8,128)(2,1)S(1)} %fusion.77), channel_id=1, source_target_pairs={{0,4},{1,5},{2,6},{3,7},{4,0},{5,1},{6,2},{7,3},{8,12},{9,13},{10,... | collective-permute-start | bytes 1966088 | tf_op jit(solution)/shard_map/ppermute | solution.py:35
  644.3 5.5 collective-permute-start.37
  644.9 40.1 %copy-start.102 = (bf16[256,1792]{1,0:T(8,128)(2,1)S(1)}, bf16[256,1792]{1,0:T(8,128)(2,1)}, u32[]{:S(2)}) copy-start(bf16[256,1792]{1,0:T(8,128)(2,1)} %copy-done.101) | copy-start | bytes 2752516
  683.5 44.0 %collective-permute-start.41 = (bf16[128,3584]{1,0:T(8,128)(2,1)}, bf16[128,3584]{1,0:T(8,128)(2,1)}, u32[]{:S(2)}, u32[]{:S(2)}) collective-permute-start(bf16[128,3584]{1,0:T(8,128)(2,1)} %all-reduce.22.cloned.1.call-done.refs_1_), channel_id=1, source_target_pairs={{0,4},{1,5},{2,6},{3,7},{4,0},{5,1},{6,2},{7,3},{8,12},{9,13},{10,... | collective-permute-start | bytes 2752520 | tf_op jit(solution)/shard_map/ppermute | solution.py:35
  687.1 40.5 %copy-start.103 = (bf16[128,3584]{1,0:T(8,128)(2,1)S(1)}, bf16[128,3584]{1,0:T(8,128)(2,1)}, u32[]{:S(2)}) copy-start(bf16[128,3584]{1,0:T(8,128)(2,1)} %all-reduce.22.cloned.1.call-done.refs_1_) | copy-start | bytes 2752516
  689.7 68.1 %collective-permute-start.47 = (bf16[128,6144]{1,0:T(8,128)(2,1)S(1)}, bf16[128,6144]{1,0:T(8,128)(2,1)}, u32[]{:S(2)}, u32[]{:S(2)}) collective-permute-start(bf16[128,6144]{1,0:T(8,128)(2,1)S(1)} %copy-done.63), channel_id=1, source_target_pairs={{0,4},{1,5},{2,6},{3,7},{4,0},{5,1},{6,2},{7,3},{8,12},{9,13},{10,... | collective-permute-start | bytes 4718600 | tf_op jit(solution)/shard_map/ppermute | solution.py:35
  726.1 27.7 %collective-permute-start.46 = (bf16[128,2560]{1,0:T(8,128)(2,1)}, bf16[128,2560]{1,0:T(8,128)(2,1)S(1)}, u32[]{:S(2)}, u32[]{:S(2)}) collective-permute-start(bf16[128,2560]{1,0:T(8,128)(2,1)} %all-reduce.24.cloned.1.call-done), channel_id=1, source_target_pairs={{0,4},{1,5},{2,6},{3,7},{4,0},{5,1},{6,2},{7,3},{8,12},{9,13},{10,... | collective-permute-start | bytes 1966088 | tf_op jit(solution)/shard_map/ppermute | solution.py:35
  (191 other events, 1159.2 us)
Sparse Core Ops, SparseCore 0:
  111.3 58.1 all-gather.6
  197.9 47.0 all-gather.8
  403.3 39.6 all-gather.10
  501.4 87.7 all-reduce.19
  635.7 47.7 all-reduce.21
  687.2 38.8 all-reduce.23

commit v8 on v6

--- a/solution.py
+++ b/solution.py
@@ -1171,12 +1171,10 @@
     )
     small_share = sum_small(small_grad)
     last_half, _, _ = ctx_half([in_sum_pre, attn_pair_sum], model // shards)
-    (gate_up_share,), summed = ctx_finish(
-        tie(gate_up_half, state_out_grad), [gate_up_sum.shape], 1
-    )
-    (down_share,), summed = ctx_finish(tie(down_half, summed), [down_sum.shape], 0)
-    (mixer_attn_share, in_share_z), summed = ctx_finish(
-        tie(mixer_half, summed), [mixer_attn_sum.shape, in_sum_z.shape], 2
+    (gate_up_share, down_share, mixer_attn_share, in_share_z), summed = ctx_finish(
+        jnp.concatenate([gate_up_half, down_half, mixer_half], axis=1),
+        [gate_up_sum.shape, down_sum.shape, mixer_attn_sum.shape, in_sum_z.shape],
+        0,
     )
     mixer_share = mixer_attn_share[: mixer_out.shape[0]]
     attn_share = mixer_attn_share[mixer_out.shape[0] :]

time: 756 us -> 735 us (0.972)
  waiting for transfers between devices: 214 us -> 188 us
  local copies, waits for them, and re-layouts: 99.4 us -> 110 us
    psum x4 -> x2, waiting for transfers between devices: 128 us -> 83.3 us  [ctx_finish(): mine = lax.psum(mine, 'ctx', axis_index_groups=lines)]
    ppermute x43 -> x41, waiting for transfers between devices: 63.7 us -> 86 us  [exchange(): return lax.ppermute(block, MESH_AXES, route)]
    ppermute x43 -> x41, starting transfers between devices: 43.4 us -> 38 us  [exchange(): return lax.ppermute(block, MESH_AXES, route)]
    unnamed x395 -> x375, local copies, waits for them, and re-layouts: 41.2 us -> 43 us
  transfers between devices with their start and end apart: 56 -> 52, of which waited for: 20 -> 16; matrix products, arithmetic and copies ran while one was open for 33% -> 34% of each run, Pallas kernels for 14% -> 15%
where the time goes in v8:
time: 735 us; the launch traced here: 725 us
  waiting for transfers between devices  188 us (26%)
  other arithmetic  137 us (19%)
  Pallas kernels  117 us (16%)
  local copies, waits for them, and re-layouts  110 us (15%)
  matrix products  99.8 us (14%)
  starting transfers between devices  54 us (7%)
  between operations  18.9 us (3%)
    ppermute x41, waiting for transfers between devices, exchange(): return lax.ppermute(block, MESH_AXES, route)  86 us
    psum x2, waiting for transfers between devices, ctx_finish(): mine = lax.psum(mine, 'ctx', axis_index_groups=lines)  83.3 us
    dot_general x21, matrix products, split_products(): lax.dot_general(piece, right, (((1 - axis,), (0,)), ((), ())), preferred_...  49.4 us
    unnamed x375, local copies, waits for them, and re-layouts  43 us
    ppermute x41, starting transfers between devices, exchange(): return lax.ppermute(block, MESH_AXES, route)  38 us
    dot_general x6, matrix products, nt_dot(): lax.dot_general(left, right, (((1,), (1,)), ((), ())), preferred_element_...  32.1 us
    pallas_call x1, Pallas kernels, per_device(): attend_backward(group_blocks, pairs, key_side, turned_q, mirrored_q, quer...  31.7 us
    pallas_call x1, Pallas kernels, per_device(): attend_forward(group_blocks, pairs, key_side, turned_q, mirrored_q, query...  22 us
  transfers between devices with their start and end apart: 52, of which 16 were waited for; matrix products, arithmetic and copies ran while one was open for 34% of the time, Pallas kernels for 15%

profile of v8, /device:TPU:0, one launch (start us, length us, event | category | flops | bytes accessed | tf_op | source)
XLA Modules:
  0.0 725.1 jit_solution(7022719567574935962)
XLA Ops:
  15.6 2.5 collective-permute-start.1
  39.6 5.7 collective-permute-done.1.refs_4_
  45.3 2.4 pad_maximum_fusion.2.refs_0_
  51.3 5.0 collective-permute-done.3.refs_2_
  60.8 9.5 %collective-permute-done.4.refs_3_ = bf16[64,4096]{1,0:T(8,128)(2,1)S(1)} collective-permute-done((bf16[64,4096]{1,0:T(8,128)(2,1)}, bf16[64,4096]{1,0:T(8,128)(2,1)S(1)}, u32[]{:S(2)}, u32[]{:S(2)}) %collective-permute-start.4) | collective-permute-done | bytes 524320 | tf_op jit(solution)/shard_map/ppermute | solution.py:35
  78.9 7.7 %assemble.5 = bf16[1024,4096]{1,0:T(8,128)(2,1)S(1)} custom-call(s32[16]{0:T(128)S(1)} %copy-done.55, bf16[272,4096]{1,0:T(8,128)(2,1)S(1)} %fusion.22.refs_0_, bf16[272,4096]{1,0:T(8,128)(2,1)} %collective-permute-done.refs_1_, bf16[64,4096]{1,0:T(8,128)(2,1)} %collective-permute-done.3.refs_2_, bf16[64,4096]{1,0:T(8,128)(2,1)S(1)} %collective-permute-done.4.refs_3_, ...), custom_call_target="tpu_custom_call" | custom-call | flops 1024 | bytes 1024 | tf_op jit(solution)/shard_map/assemble/pallas_call | solution.py:88
  86.6 6.1 fusion.201
  92.7 3.3 copy-done.76
  100.7 3.9 collective-permute-start.10
  108.3 5.3 multiply_convert_fusion.1
  113.7 5.6 state_outer.2
  123.4 2.5 copy.97
  133.1 9.8 %mixer_forward.1.refs_2_.local_ref = f32[512,1536]{1,0:T(8,128)S(1)} custom-call(f32[12,1,128]{2,1,0:T(1,128)S(1)} %copy-done.41, bf16[512,1792]{1,0:T(8,128)(2,1)S(1)} %get-tuple-element.99.x_ref.b_ref.c_ref.left_ref.right_ref, bf16[512,1792]{1,0:T(8,128)(2,1)S(1)} %get-tuple-element.99.x_ref.b_ref.c_ref.left_ref.right_ref, ...), custom_call_target="tpu_custom_call" | custom-call | flops 1024 | bytes 1024 | tf_op jit(solution)/shard_map/mixer_forward/pallas_call | solution.py:1021
  144.6 3.5 collective-permute-start.7
  155.3 3.3 collective-permute-done.7.query_b
  163.7 22.0 %attend_forward.1 = (f32[8,64,256]{2,1,0:T(8,128)S(1)}, f32[8,64,256]{2,1,0:T(8,128)S(1)}, f32[2,2,1,1024]{3,2,1,0:T(1,128)S(1)}) custom-call(s32[2]{0:T(128)S(1)} %copy-done.49, bf16[8,2,512,128]{3,2,1,0:T(8,128)(2,1)S(1)} %bitcast.257, bf16[4096,128]{1,0:T(8,128)(2,1)S(1)} %fusion.33.refs_8_.side_ref, bf16[8,64,512]{2,1,0:T(8,128)(2,1)S(1)} %copy-done.6, ...), custom_call_target="tpu_custom_call" | custom-call | flops 1024 | bytes 1024 | tf_op jit(solution)/shard_map/attend_forward/pallas_call | solution.py:1025
  213.9 2.7 assemble.7
  218.4 3.1 assemble.9
  225.7 10.9 %all-gather.9.cloned.1.call-done = bf16[6208,128]{1,0:T(8,128)(2,1)} async-done(((bf16[1552,128]{1,0:T(8,128)(2,1)}), bf16[6208,128]{1,0:T(8,128)(2,1)}) %all-gather.9.cloned.1.call-update) | async-done | bytes 1589264 | tf_op jit(solution)/shard_map/all_gather | solution.py:824
  246.3 2.5 select_convert_fusion.1.state_ref
  248.9 4.7 assemble.8
  253.6 3.4 copy-done.3
  256.9 4.5 mixer_join.1
  261.5 3.0 multiply_reduce_fusion.6
  264.9 2.6 copy-done.23
  272.0 4.6 fusion.203
  276.6 6.7 bitcast_multiply_fusion.1
  283.3 4.1 add_convert_fusion
  287.5 10.3 %multiply_reduce_fusion.7 = (f32[1024]{0:T(1024)S(1)}, f32[512]{0:T(512)S(1)}, f32[512,1024]{1,0:T(8,128)S(1)}) fusion(f32[512,1024]{1,0:T(8,128)} %copy-done.63, f32[512]{0:T(512)S(1)} %fusion.159, f32[1024]{0:T(1024)S(1)} %bitcast.292, bf16[512,4096]{1,0:T(8,128)(2,1)S(1)} %add_convert_fusion, bf16[1024,4096]{1,0:T(8,128)(2,1)} %copy-done.3), kind=kOutput, calls=%fused_computation.84 | convolution fusion | flops 4298111488 | bytes 16789504 | tf_op jit(solution)/shard_map/dot_general | solution.py:346
  305.4 4.5 convolution_convert_fusion
  311.9 5.5 fusion.188
  326.7 2.7 fusion.113
  337.2 5.7 fusion.94
  342.9 2.9 add_convert_fusion.11.refs_0_
  345.8 2.6 add_convert_fusion.4.refs_0_
  348.4 8.2 %collective-permute-done.22.refs_1_ = bf16[512,1024]{1,0:T(8,128)(2,1)} collective-permute-done((bf16[512,1024]{1,0:T(8,128)(2,1)}, bf16[512,1024]{1,0:T(8,128)(2,1)}, u32[]{:S(2)}, u32[]{:S(2)}) %collective-permute-start.22) | collective-permute-done | bytes 1048608 | tf_op jit(solution)/shard_map/ppermute | solution.py:35
  356.6 3.2 add_convert_fusion.6.refs_0_
  359.8 4.4 add_convert_fusion.2.refs_1_
  365.7 5.6 state_outer.3.refs_1_
  376.4 7.0 collective-permute-done.19
  389.4 31.7 %attend_backward.1 = (f32[8,64,256]{2,1,0:T(8,128)S(1)}, f32[8,64,256]{2,1,0:T(8,128)S(1)}, bf16[8,2,512,128]{3,2,1,0:T(8,128)(2,1)}) custom-call(s32[2]{0:T(128)S(1)} %copy-done.50, bf16[8,2,512,128]{3,2,1,0:T(8,128)(2,1)} %bitcast.256, bf16[4096,128]{1,0:T(8,128)(2,1)S(1)} %fusion.33.refs_8_.side_ref, bf16[8,64,512]{2,1,0:T(8,128)(2,1)S(1)} %copy-done.7, ...), custom_call_target="tpu_custom_call" | custom-call | flops 1024 | bytes 1024 | tf_op jit(solution)/shard_map/attend_backward/pallas_call | solution.py:1081
  421.1 2.3 dynamic-slice_bitcast_fusion
  424.3 4.3 collective-permute-start.28
  435.5 4.4 add_convert_fusion.1
  445.6 18.0 %mixer_backward.1 = (f32[512,1792]{1,0:T(8,128)}, f32[12,1,128]{2,1,0:T(1,128)S(1)}) custom-call(f32[12,1,128]{2,1,0:T(1,128)S(1)} %copy-done.42, bf16[512,1792]{1,0:T(8,128)(2,1)} %copy-done, bf16[512,1792]{1,0:T(8,128)(2,1)} %copy-done, bf16[512,1792]{1,0:T(8,128)(2,1)} %copy-done, f32[12,8,512]{2,1,0:T(8,128)S(1)} %reshape.836.refs_10_.row_ref.rows_ref, ...), custom_call_target="tpu_custom_call" | custom-call | flops 1024 | bytes 1024 | tf_op jit(solution)/shard_map/mixer_backward/pallas_call | solution.py:1126
  467.8 5.2 collective-permute-start.30
  473.0 10.6 %multiply_reduce_fusion.3 = (f32[1792]{0:T(1024)S(1)}, f32[1792]{0:T(1024)S(1)}, f32[1792]{0:T(1024)S(1)}, f32[1792]{0:T(1024)S(1)}, f32[1792]{0:T(1024)S(1)}, /*index=5*/f32[512,1792]{1,0:T(8,128)S(1)}) fusion(f32[515,1792]{1,0:T(8,128)} %copy-done.56, f32[512]{0:T(512)S(1)} %bitcast.310, f32[512]{0:T(512)S(1)} %bitcast.313, f32[512]{0:T(512)S(1)} %bitcast.316, ...), kind=kLoop, calls=%fused_computation.34 | loop fusion | flops 20176128 | bytes 25734144 | tf_op jit(solution)/shard_map/transpose(jvp())/reduce_sum | solution.py:324
  486.5 3.0 pad_add_fusion
  490.9 3.6 fusion.9.refs_0_
  495.6 3.9 convolution_convert_fusion.2
  513.5 10.4 %collective-permute-done.31 = bf16[1,2,512,128]{2,3,1,0:T(8,128)(2,1)S(1)} collective-permute-done((bf16[1,2,512,128]{2,3,1,0:T(8,128)(2,1)S(1)}, bf16[1,2,512,128]{2,3,1,0:T(8,128)(2,1)S(1)}, u32[]{:S(2)}, u32[]{:S(2)}) %collective-permute-start.31) | collective-permute-done | bytes 262176 | tf_op jit(solution)/shard_map/ppermute | solution.py:35
  525.7 3.8 fusion.34
  533.2 2.4 add_convert_fusion.15
  536.4 3.2 fusion.19
  540.8 8.3 %fusion.24 = (f32[1024]{0:T(1024)S(1)}, f32[512]{0:T(512)S(1)}, f32[512,1024]{1,0:T(8,128)}) fusion(bf16[1,512,1024]{2,1,0:T(8,128)(2,1)S(1)} %copy-done.72, f32[512]{0:T(512)S(1)} %copy-done.170, f32[1024]{0:T(1024)S(1)} %bitcast.304, f32[512,1024]{1,0:T(8,128)S(1)} %copy-done.183, bf16[1024,4096]{1,0:T(8,128)(2,1)} %copy-done.4, ...), kind=kOutput, calls=%fused_computation.69 | convolution fusion | flops 3500669440 | bytes 15478784 | tf_op jit(solution)/shard_map/dot_general | solution.py:346
  553.1 15.3 %collective-permute-done.33 = f32[128,128]{1,0:T(8,128)S(1)} collective-permute-done((f32[128,128]{1,0:T(8,128)S(1)}, f32[128,128]{1,0:T(8,128)S(1)}, u32[]{:S(2)}, u32[]{:S(2)}) %collective-permute-start.33) | collective-permute-done | bytes 65568 | tf_op jit(solution)/shard_map/ppermute | solution.py:35
  570.3 2.5 fusion.18
  575.4 3.3 fusion.42
  578.8 52.3 %all-reduce.19.cloned.1.call-done.refs_1_ = bf16[128,9728]{1,0:T(8,128)(2,1)} async-done(((bf16[128,9728]{1,0:T(8,128)(2,1)}), bf16[128,9728]{1,0:T(8,128)(2,1)}) %all-reduce.19.cloned.1.call-update) | async-done | bytes 2490384 | tf_op jit(solution)/shard_map/psum | solution.py:210
  636.9 5.0 fusion.27
  642.4 31.0 %all-reduce.21.cloned.1.call-done = bf16[128,2560]{1,0:T(8,128)(2,1)} async-done(((bf16[128,2560]{1,0:T(8,128)(2,1)}), bf16[128,2560]{1,0:T(8,128)(2,1)}) %all-reduce.21.cloned.1.call-update) | async-done | bytes 655376 | tf_op jit(solution)/shard_map/psum | solution.py:210
  677.5 23.6 %collective-permute-done.46 = bf16[128,2560]{1,0:T(8,128)(2,1)S(1)} collective-permute-done((bf16[128,2560]{1,0:T(8,128)(2,1)}, bf16[128,2560]{1,0:T(8,128)(2,1)S(1)}, u32[]{:S(2)}, u32[]{:S(2)}) %collective-permute-start.46) | collective-permute-done | bytes 655392 | tf_op jit(solution)/shard_map/ppermute | solution.py:35
  705.7 4.1 fusion.2
  711.3 2.4 slice.568
  (719 shorter events, 238.2 us)
Async XLA Ops:
  7.2 153.2 %all-gather.7.cloned.1.call-start = ((), (), s32[]{:S(2)}) async-start(), calls=%async_computation.2 | async-start | bytes 2359296 | tf_op jit(solution)/shard_map/all_gather | solution.py:1006
  14.0 57.6 %collective-permute-start = (bf16[272,4096]{1,0:T(8,128)(2,1)S(1)}, bf16[272,4096]{1,0:T(8,128)(2,1)}, u32[]{:S(2)}, u32[]{:S(2)}) collective-permute-start(bf16[272,4096]{1,0:T(8,128)(2,1)S(1)} %fusion.22.refs_0_), channel_id=1, source_target_pairs={{0,1},{1,0},{2,3},{3,2},{4,5},{5,4},{6,7},{7,6},{8,9},{9,8},{10,11... | collective-permute-start | bytes 6684680 | tf_op jit(solution)/shard_map/ppermute | solution.py:35
  15.6 29.7 %collective-permute-start.1 = (bf16[144,4096]{1,0:T(8,128)(2,1)}, bf16[144,4096]{1,0:T(8,128)(2,1)}, u32[]{:S(2)}, u32[]{:S(2)}) collective-permute-start(bf16[144,4096]{1,0:T(8,128)(2,1)} %slice.490), channel_id=1, source_target_pairs={{0,2},{1,3},{2,0},{3,1},{4,6},{5,7},{6,4},{7,5},{8,10},{9,11},{10,... | collective-permute-start | bytes 3538952 | tf_op jit(solution)/shard_map/ppermute | solution.py:35
  19.0 37.3 %collective-permute-start.3 = (bf16[64,4096]{1,0:T(8,128)(2,1)}, bf16[64,4096]{1,0:T(8,128)(2,1)}, u32[]{:S(2)}, u32[]{:S(2)}) collective-permute-start(bf16[64,4096]{1,0:T(8,128)(2,1)} %constant_dynamic-slice_fusion.15), channel_id=1, source_target_pairs={{0,2},{1,3},{2,0},{3,1},{4,6},{5,7},{6,4},{7,5},{8,10},{9,11},{10,... | collective-permute-start | bytes 1572872 | tf_op jit(solution)/shard_map/ppermute | solution.py:35
  45.3 28.8 %collective-permute-start.2 = (bf16[144,4096]{1,0:T(8,128)(2,1)}, bf16[144,4096]{1,0:T(8,128)(2,1)}, u32[]{:S(2)}, u32[]{:S(2)}) collective-permute-start(bf16[144,4096]{1,0:T(8,128)(2,1)} %collective-permute-done.1.refs_4_), channel_id=1, source_target_pairs={{0,1},{1,0},{2,3},{3,2},{4,5},{5,4},{6,7},{7,6},{8,9},{9,8},{10,11... | collective-permute-start | bytes 3538952 | tf_op jit(solution)/shard_map/ppermute | solution.py:35
  50.0 28.8 %copy-start.11 = (s32[512,1]{1,0:T(8,128)S(1)}, s32[512,1]{1,0:T(8,128)}, u32[]{:S(2)}) copy-start(s32[512,1]{1,0:T(8,128)} %fusion.100.refs_12_.docs_column) | copy-start | bytes 6148
  50.0 28.8 %copy-start.32 = (f32[32,512]{1,0:T(8,128)S(1)}, f32[32,512]{1,0:T(8,128)}, u32[]{:S(2)}) copy-start(f32[32,512]{1,0:T(8,128)} %get-tuple-element.45.refs_14_) | copy-start | bytes 196612
  50.0 28.8 %copy-start.37 = (f32[32,256]{1,0:T(8,128)S(1)}, f32[32,256]{1,0:T(8,128)}, u32[]{:S(2)}) copy-start(f32[32,256]{1,0:T(8,128)} %get-tuple-element.47.refs_16_) | copy-start | bytes 98308
  50.0 28.8 %copy-start.39 = (f32[32,256]{1,0:T(8,128)S(1)}, f32[32,256]{1,0:T(8,128)}, u32[]{:S(2)}) copy-start(f32[32,256]{1,0:T(8,128)} %get-tuple-element.48.refs_17_) | copy-start | bytes 98308
  50.0 28.8 %copy-start.40 = (f32[4,512]{1,0:T(4,128)S(1)}, f32[4,512]{1,0:T(4,128)}, u32[]{:S(2)}) copy-start(f32[4,512]{1,0:T(4,128)} %maximum_maximum_fusion.refs_11_) | copy-start | bytes 24580
  50.0 28.8 %copy-start.43 = (s32[1,512]{1,0:T(1,128)S(1)}, s32[1,512]{1,0:T(1,128)}, u32[]{:S(2)}) copy-start(s32[1,512]{1,0:T(1,128)} %compare_select_fusion.2.refs_13_.docs_row) | copy-start | bytes 6148
  50.0 28.8 %copy-start.48 = (s32[2]{0:T(128)S(1)}, s32[2]{0:T(128)}, u32[]{:S(2)}) copy-start(s32[2]{0:T(128)} %pad_add_fusion.4.refs_18_.blocks) | copy-start | bytes 28
  50.0 28.8 %copy-start.55 = (s32[16]{0:T(128)S(1)}, s32[16]{0:T(128)}, u32[]{:S(2)}) copy-start(s32[16]{0:T(128)} %stack.181.target_ref) | copy-start | bytes 196
  56.3 14.0 %collective-permute-start.4 = (bf16[64,4096]{1,0:T(8,128)(2,1)}, bf16[64,4096]{1,0:T(8,128)(2,1)S(1)}, u32[]{:S(2)}, u32[]{:S(2)}) collective-permute-start(bf16[64,4096]{1,0:T(8,128)(2,1)} %collective-permute-done.3.refs_2_), channel_id=1, source_target_pairs={{0,4},{1,5},{2,6},{3,7},{4,0},{5,1},{6,2},{7,3},{8,12},{9,13},{10,... | collective-permute-start | bytes 1572872 | tf_op jit(solution)/shard_map/ppermute | solution.py:35
  60.8 17.4 %collective-permute-start.5 = (bf16[64,4096]{1,0:T(8,128)(2,1)}, bf16[64,4096]{1,0:T(8,128)(2,1)S(1)}, u32[]{:S(2)}, u32[]{:S(2)}) collective-permute-start(bf16[64,4096]{1,0:T(8,128)(2,1)} %collective-permute-done.3.refs_2_), channel_id=1, source_target_pairs={{0,1},{1,0},{2,3},{3,2},{4,5},{5,4},{6,7},{7,6},{8,9},{9,8},{10,11... | collective-permute-start | bytes 1572872 | tf_op jit(solution)/shard_map/ppermute | solution.py:35
  70.3 8.5 %collective-permute-start.6 = (bf16[64,4096]{1,0:T(8,128)(2,1)S(1)}, bf16[64,4096]{1,0:T(8,128)(2,1)S(1)}, u32[]{:S(2)}, u32[]{:S(2)}) collective-permute-start(bf16[64,4096]{1,0:T(8,128)(2,1)S(1)} %collective-permute-done.4.refs_3_), channel_id=1, source_target_pairs={{0,1},{1,0},{2,3},{3,2},{4,5},{5,4},{6,7},{7,6},{8,9},{9,8},{10,11... | collective-permute-start | bytes 1572872 | tf_op jit(solution)/shard_map/ppermute | solution.py:35
  70.3 88.3 %collective-permute-start.8 = (bf16[1024,1024]{1,0:T(8,128)(2,1)}, bf16[1024,1024]{1,0:T(8,128)(2,1)}, u32[]{:S(2)}, u32[]{:S(2)}) collective-permute-start(bf16[1024,1024]{1,0:T(8,128)(2,1)} %pad_maximum_fusion.2.refs_0_), channel_id=1, source_target_pairs={{0,1},{1,0},{2,3},{3,2},{4,5},{5,4},{6,7},{7,6},{8,9},{9,8},{10,11... | collective-permute-start | bytes 6291464 | tf_op jit(solution)/shard_map/ppermute | solution.py:35
  71.6 116.3 %collective-permute-start.12 = (bf16[1024,1024]{1,0:T(8,128)(2,1)}, bf16[1024,1024]{1,0:T(8,128)(2,1)}, u32[]{:S(2)}, u32[]{:S(2)}) collective-permute-start(bf16[1024,1024]{1,0:T(8,128)(2,1)} %pad_maximum_fusion.2.refs_0_), channel_id=1, source_target_pairs={{0,2},{1,3},{2,0},{3,1},{4,6},{5,7},{6,4},{7,5},{8,10},{9,11},{10,... | collective-permute-start | bytes 6291464 | tf_op jit(solution)/shard_map/ppermute | solution.py:35
  74.1 84.5 %collective-permute-start.9 = (bf16[256,4096]{1,0:T(8,128)(2,1)}, bf16[256,4096]{1,0:T(8,128)(2,1)}, u32[]{:S(2)}, u32[]{:S(2)}) collective-permute-start(bf16[256,4096]{1,0:T(8,128)(2,1)} %refs_0_), channel_id=1, source_target_pairs={{0,1},{1,0},{2,3},{3,2},{4,5},{5,4},{6,7},{7,6},{8,9},{9,8},{10,11... | collective-permute-start | bytes 6291464 | tf_op jit(solution)/shard_map/ppermute | solution.py:35
  78.2 131.6 %collective-permute-start.15 = (bf16[256,4096]{1,0:T(8,128)(2,1)}, bf16[256,4096]{1,0:T(8,128)(2,1)}, u32[]{:S(2)}, u32[]{:S(2)}) collective-permute-start(bf16[256,4096]{1,0:T(8,128)(2,1)} %refs_0_), channel_id=1, source_target_pairs={{0,2},{1,3},{2,0},{3,1},{4,6},{5,7},{6,4},{7,5},{8,10},{9,11},{10,... | collective-permute-start | bytes 6291464 | tf_op jit(solution)/shard_map/ppermute | solution.py:35
  99.9 136.7 %all-gather.9.cloned.1.call-start = ((), (), s32[]{:S(2)}) async-start(), calls=%async_computation.3 | async-start | bytes 1986560 | tf_op jit(solution)/shard_map/all_gather | solution.py:824
  100.7 6.9 collective-permute-start.10
  113.6 252.1 %copy-start = (bf16[512,1792]{1,0:T(8,128)(2,1)}, bf16[512,1792]{1,0:T(8,128)(2,1)S(1)}, u32[]{:S(2)}) copy-start(bf16[512,1792]{1,0:T(8,128)(2,1)S(1)} %get-tuple-element.99.x_ref.b_ref.c_ref.left_ref.right_ref) | copy-start | bytes 5505028
  120.1 24.5 %collective-permute-start.14 = (bf16[1552,128]{1,0:T(8,128)(2,1)}, bf16[1552,128]{1,0:T(8,128)(2,1)}, u32[]{:S(2)}, u32[]{:S(2)}) collective-permute-start(bf16[1552,128]{1,0:T(8,128)(2,1)} %pad_maximum_fusion.11), channel_id=1, source_target_pairs={{0,4},{1,5},{2,6},{3,7},{4,0},{5,1},{6,2},{7,3},{8,12},{9,13},{10,... | collective-permute-start | bytes 1191944 | tf_op jit(solution)/shard_map/ppermute | solution.py:35
  144.6 14.0 %collective-permute-start.7 = (bf16[8,64,256]{2,1,0:T(8,128)(2,1)}, bf16[8,64,256]{2,1,0:T(8,128)(2,1)}, u32[]{:S(2)}, u32[]{:S(2)}) collective-permute-start(bf16[8,64,256]{2,1,0:T(8,128)(2,1)} %slice.501), channel_id=1, source_target_pairs={{0,28},{4,24},{8,20},{12,16},{16,12},{20,8},{24,4},{28,0},{1,29},{... | collective-permute-start | bytes 786440 | tf_op jit(solution)/shard_map/ppermute | solution.py:46
  187.9 24.0 %collective-permute-start.13 = (bf16[1024,1024]{1,0:T(8,128)(2,1)}, bf16[1024,1024]{1,0:T(8,128)(2,1)}, u32[]{:S(2)}, u32[]{:S(2)}) collective-permute-start(bf16[1024,1024]{1,0:T(8,128)(2,1)} %collective-permute-done.12.refs_2_), channel_id=1, source_target_pairs={{0,1},{1,0},{2,3},{3,2},{4,5},{5,4},{6,7},{7,6},{8,9},{9,8},{10,11... | collective-permute-start | bytes 6291464 | tf_op jit(solution)/shard_map/ppermute | solution.py:35
  188.7 253.9 %all-gather.11.cloned.1.call-start = ((), (), s32[]{:S(2)}) async-start(), calls=%async_computation.4 | async-start | bytes 1966080 | tf_op jit(solution)/shard_map/all_gather | solution.py:824
  193.0 17.1 %collective-permute-start.11 = (bf16[8,64,256]{2,1,0:T(8,128)(2,1)}, bf16[8,64,256]{2,1,0:T(8,128)(2,1)}, u32[]{:S(2)}, u32[]{:S(2)}) collective-permute-start(bf16[8,64,256]{2,1,0:T(8,128)(2,1)} %convert_element_type.646), channel_id=1, source_target_pairs={{0,28},{4,24},{8,20},{12,16},{16,12},{20,8},{24,4},{28,0},{1,29},{... | collective-permute-start | bytes 786440 | tf_op jit(solution)/shard_map/ppermute | solution.py:46
  209.9 39.0 %collective-permute-start.16 = (bf16[256,4096]{1,0:T(8,128)(2,1)}, bf16[256,4096]{1,0:T(8,128)(2,1)}, u32[]{:S(2)}, u32[]{:S(2)}) collective-permute-start(bf16[256,4096]{1,0:T(8,128)(2,1)} %collective-permute-done.15.refs_2_), channel_id=1, source_target_pairs={{0,1},{1,0},{2,3},{3,2},{4,5},{5,4},{6,7},{7,6},{8,9},{9,8},{10,11... | collective-permute-start | bytes 6291464 | tf_op jit(solution)/shard_map/ppermute | solution.py:35
  304.6 80.7 %collective-permute-start.27 = (bf16[8,64,256]{2,1,0:T(8,128)(2,1)}, bf16[8,64,256]{2,1,0:T(8,128)(2,1)}, u32[]{:S(2)}, u32[]{:S(2)}) collective-permute-start(bf16[8,64,256]{2,1,0:T(8,128)(2,1)} %slice.540), channel_id=1, source_target_pairs={{0,28},{4,24},{8,20},{12,16},{16,12},{20,8},{24,4},{28,0},{1,29},{... | collective-permute-start | bytes 786440 | tf_op jit(solution)/shard_map/ppermute | solution.py:46
  309.9 49.9 %collective-permute-start.18 = (bf16[512,4096]{1,0:T(8,128)(2,1)}, bf16[512,4096]{1,0:T(8,128)(2,1)}, u32[]{:S(2)}, u32[]{:S(2)}) collective-permute-start(bf16[512,4096]{1,0:T(8,128)(2,1)} %convolution_convert_fusion), channel_id=1, source_target_pairs={{0,1},{1,0},{2,3},{3,2},{4,5},{5,4},{6,7},{7,6},{8,9},{9,8},{10,11... | collective-permute-start | bytes 12582920 | tf_op jit(solution)/shard_map/ppermute | solution.py:35
  311.3 18.1 %collective-permute-start.17 = (bf16[1024,1024]{1,0:T(8,128)(2,1)S(1)}, bf16[1024,1024]{1,0:T(8,128)(2,1)S(1)}, u32[]{:S(2)}, u32[]{:S(2)}) collective-permute-start(bf16[1024,1024]{1,0:T(8,128)(2,1)S(1)} %convolution_convert_fusion.3), channel_id=1, source_target_pairs={{0,1},{1,0},{2,3},{3,2},{4,5},{5,4},{6,7},{7,6},{8,9},{9,8},{10,11... | collective-permute-start | bytes 6291464 | tf_op jit(solution)/shard_map/ppermute | solution.py:35
  319.6 23.3 %collective-permute-start.21 = (bf16[512,1536]{1,0:T(8,128)(2,1)}, bf16[512,1536]{1,0:T(8,128)(2,1)}, u32[]{:S(2)}, u32[]{:S(2)}) collective-permute-start(bf16[512,1536]{1,0:T(8,128)(2,1)} %convolution_convert_fusion.1), channel_id=1, source_target_pairs={{0,1},{1,0},{2,3},{3,2},{4,5},{5,4},{6,7},{7,6},{8,9},{9,8},{10,11... | collective-permute-start | bytes 4718600 | tf_op jit(solution)/shard_map/ppermute | solution.py:35
  322.9 22.9 %collective-permute-start.24 = (bf16[1024,1024]{1,0:T(8,128)(2,1)}, bf16[1024,1024]{1,0:T(8,128)(2,1)}, u32[]{:S(2)}, u32[]{:S(2)}) collective-permute-start(bf16[1024,1024]{1,0:T(8,128)(2,1)} %pad_maximum_fusion.3), channel_id=1, source_target_pairs={{0,1},{1,0},{2,3},{3,2},{4,5},{5,4},{6,7},{7,6},{8,9},{9,8},{10,11... | collective-permute-start | bytes 6291464 | tf_op jit(solution)/shard_map/ppermute | solution.py:35
  331.2 25.4 %collective-permute-start.22 = (bf16[512,1024]{1,0:T(8,128)(2,1)}, bf16[512,1024]{1,0:T(8,128)(2,1)}, u32[]{:S(2)}, u32[]{:S(2)}) collective-permute-start(bf16[512,1024]{1,0:T(8,128)(2,1)} %add_convert_fusion.7), channel_id=1, source_target_pairs={{0,2},{1,3},{2,0},{3,1},{4,6},{5,7},{6,4},{7,5},{8,10},{9,11},{10,... | collective-permute-start | bytes 3145736 | tf_op jit(solution)/shard_map/ppermute | solution.py:35
  364.2 71.3 %collective-permute-start.20 = (bf16[256,4096]{1,0:T(8,128)(2,1)}, bf16[256,4096]{1,0:T(8,128)(2,1)}, u32[]{:S(2)}, u32[]{:S(2)}) collective-permute-start(bf16[256,4096]{1,0:T(8,128)(2,1)} %add_convert_fusion.2.refs_1_), channel_id=1, source_target_pairs={{0,2},{1,3},{2,0},{3,1},{4,6},{5,7},{6,4},{7,5},{8,10},{9,11},{10,... | collective-permute-start | bytes 6291464 | tf_op jit(solution)/shard_map/ppermute | solution.py:35
  371.3 12.1 %collective-permute-start.19 = (bf16[1536,128]{1,0:T(8,128)(2,1)S(1)}, bf16[1536,128]{1,0:T(8,128)(2,1)S(1)}, u32[]{:S(2)}, u32[]{:S(2)}) collective-permute-start(bf16[1536,128]{1,0:T(8,128)(2,1)S(1)} %state_outer.3.refs_1_), channel_id=1, source_target_pairs={{0,4},{1,5},{2,6},{3,7},{4,0},{5,1},{6,2},{7,3},{8,12},{9,13},{10,... | collective-permute-start | bytes 1179656 | tf_op jit(solution)/shard_map/ppermute | solution.py:35
  375.1 54.2 %collective-permute-start.23 = (bf16[128,2048]{1,0:T(8,128)(2,1)}, bf16[128,2048]{1,0:T(8,128)(2,1)S(1)}, u32[]{:S(2)}, u32[]{:S(2)}) collective-permute-start(bf16[128,2048]{1,0:T(8,128)(2,1)} %fusion.79), channel_id=1, source_target_pairs={{0,4},{1,5},{2,6},{3,7},{4,0},{5,1},{6,2},{7,3},{8,12},{9,13},{10,... | collective-permute-start | bytes 1572872 | tf_op jit(solution)/shard_map/ppermute | solution.py:35
  385.2 39.0 %copy-start.38 = (f32[32,256]{1,0:T(8,128)S(1)}, f32[32,256]{1,0:T(8,128)}, u32[]{:S(2)}) copy-start(f32[32,256]{1,0:T(8,128)} %get-tuple-element.47.refs_16_) | copy-start | bytes 98308
  385.2 39.0 %copy-start.138 = (f32[32,256]{1,0:T(8,128)S(1)}, f32[32,256]{1,0:T(8,128)}, u32[]{:S(2)}) copy-start(f32[32,256]{1,0:T(8,128)} %neg.36) | copy-start | bytes 98308
  385.2 245.9 %all-reduce.19.cloned.1.call-start = ((), (), s32[]{:S(2)}) async-start(), calls=%async_computation | async-start | bytes 4980736 | tf_op jit(solution)/shard_map/psum | solution.py:210
  423.4 40.2 %collective-permute-start.29 = (bf16[4,2,512,128]{3,2,1,0:T(8,128)(2,1)}, bf16[4,2,512,128]{3,2,1,0:T(8,128)(2,1)}, u32[]{:S(2)}, u32[]{:S(2)}) collective-permute-start(bf16[4,2,512,128]{3,2,1,0:T(8,128)(2,1)} %dynamic-slice_bitcast_fusion), channel_id=1, source_target_pairs={{0,4},{1,5},{2,6},{3,7},{4,0},{5,1},{6,2},{7,3},{8,12},{9,13},{10,... | collective-permute-start | bytes 3145736 | tf_op jit(solution)/shard_map/ppermute | solution.py:35
  424.3 9.4 %collective-permute-start.28 = (bf16[8,64,256]{2,1,0:T(8,128)(2,1)S(1)}, bf16[8,64,256]{2,1,0:T(8,128)(2,1)}, u32[]{:S(2)}, u32[]{:S(2)}) collective-permute-start(bf16[8,64,256]{2,1,0:T(8,128)(2,1)S(1)} %fusion.84), channel_id=1, source_target_pairs={{0,28},{4,24},{8,20},{12,16},{16,12},{20,8},{24,4},{28,0},{1,29},{... | collective-permute-start | bytes 786440 | tf_op jit(solution)/shard_map/ppermute | solution.py:46
  428.6 75.3 %collective-permute-start.38 = (bf16[256,1536]{1,0:T(8,128)(2,1)}, bf16[256,1536]{1,0:T(8,128)(2,1)}, u32[]{:S(2)}, u32[]{:S(2)}) collective-permute-start(bf16[256,1536]{1,0:T(8,128)(2,1)} %tie.15), channel_id=1, source_target_pairs={{0,2},{1,3},{2,0},{3,1},{4,6},{5,7},{6,4},{7,5},{8,10},{9,11},{10,... | collective-permute-start | bytes 2359304 | tf_op jit(solution)/shard_map/ppermute | solution.py:35
  429.3 70.2 %collective-permute-start.37 = (bf16[512,1024]{1,0:T(8,128)(2,1)}, bf16[512,1024]{1,0:T(8,128)(2,1)}, u32[]{:S(2)}, u32[]{:S(2)}) collective-permute-start(bf16[512,1024]{1,0:T(8,128)(2,1)} %tie.13), channel_id=1, source_target_pairs={{0,2},{1,3},{2,0},{3,1},{4,6},{5,7},{6,4},{7,5},{8,10},{9,11},{10,... | collective-permute-start | bytes 3145736 | tf_op jit(solution)/shard_map/ppermute | solution.py:35
  441.3 53.3 %collective-permute-start.26 = (bf16[128,4096]{1,0:T(8,128)(2,1)S(1)}, bf16[128,4096]{1,0:T(8,128)(2,1)}, u32[]{:S(2)}, u32[]{:S(2)}) collective-permute-start(bf16[128,4096]{1,0:T(8,128)(2,1)S(1)} %constant_dynamic-slice_fusion.10.refs_0_), channel_id=1, source_target_pairs={{0,4},{1,5},{2,6},{3,7},{4,0},{5,1},{6,2},{7,3},{8,12},{9,13},{10,... | collective-permute-start | bytes 3145736 | tf_op jit(solution)/shard_map/ppermute | solution.py:35
  467.8 41.0 %collective-permute-start.30 = (bf16[2,2,512,128]{2,3,1,0:T(8,128)(2,1)}, bf16[2,2,512,128]{2,3,1,0:T(8,128)(2,1)}, u32[]{:S(2)}, u32[]{:S(2)}) collective-permute-start(bf16[2,2,512,128]{2,3,1,0:T(8,128)(2,1)} %bitcast.90), channel_id=1, source_target_pairs={{0,8},{1,9},{2,10},{3,11},{4,12},{5,13},{6,14},{7,15},{8,0},{9,1},... | collective-permute-start | bytes 1572872 | tf_op jit(solution)/shard_map/ppermute | solution.py:35
  485.2 5.8 collective-permute-start.25
  499.4 36.9 %collective-permute-start.41 = (bf16[512,1792]{1,0:T(8,128)(2,1)}, bf16[512,1792]{1,0:T(8,128)(2,1)}, u32[]{:S(2)}, u32[]{:S(2)}) collective-permute-start(bf16[512,1792]{1,0:T(8,128)(2,1)} %convolution_convert_fusion.2), channel_id=1, source_target_pairs={{0,1},{1,0},{2,3},{3,2},{4,5},{5,4},{6,7},{7,6},{8,9},{9,8},{10,11... | collective-permute-start | bytes 5505032 | tf_op jit(solution)/shard_map/ppermute | solution.py:35
  506.6 22.8 %collective-permute-start.39 = (bf16[128,3584]{1,0:T(8,128)(2,1)S(1)}, bf16[128,3584]{1,0:T(8,128)(2,1)S(1)}, u32[]{:S(2)}, u32[]{:S(2)}) collective-permute-start(bf16[128,3584]{1,0:T(8,128)(2,1)S(1)} %constant_dynamic-slice_fusion), channel_id=1, source_target_pairs={{0,4},{1,5},{2,6},{3,7},{4,0},{5,1},{6,2},{7,3},{8,12},{9,13},{10,... | collective-permute-start | bytes 2752520 | tf_op jit(solution)/shard_map/ppermute | solution.py:35
  510.1 13.8 %collective-permute-start.31 = (bf16[1,2,512,128]{2,3,1,0:T(8,128)(2,1)S(1)}, bf16[1,2,512,128]{2,3,1,0:T(8,128)(2,1)S(1)}, u32[]{:S(2)}, u32[]{:S(2)}) collective-permute-start(bf16[1,2,512,128]{2,3,1,0:T(8,128)(2,1)S(1)} %constant_dynamic-slice_fusion.1), channel_id=1, source_target_pairs={{0,16},{1,17},{2,18},{3,19},{4,20},{5,21},{6,22},{7,23},{8,24},{9,... | collective-permute-start | bytes 786440 | tf_op jit(solution)/shard_map/ppermute | solution.py:35
  525.7 6.7 collective-permute-start.43
  532.1 141.3 %all-reduce.21.cloned.1.call-start = ((), (), s32[]{:S(2)}) async-start(), calls=%async_computation.1 | async-start | bytes 1310720 | tf_op jit(solution)/shard_map/psum | solution.py:210
  535.6 33.3 %collective-permute-start.44 = (bf16[256,768]{1,0:T(8,128)(2,1)}, bf16[256,768]{1,0:T(8,128)(2,1)}, u32[]{:S(2)}, u32[]{:S(2)}) collective-permute-start(bf16[256,768]{1,0:T(8,128)(2,1)} %add_convert_fusion.15), channel_id=1, source_target_pairs={{0,2},{1,3},{2,0},{3,1},{4,6},{5,7},{6,4},{7,5},{8,10},{9,11},{10,... | collective-permute-start | bytes 1179656 | tf_op jit(solution)/shard_map/ppermute | solution.py:35
  539.6 30.6 %collective-permute-start.42 = (bf16[256,1792]{1,0:T(8,128)(2,1)}, bf16[256,1792]{1,0:T(8,128)(2,1)}, u32[]{:S(2)}, u32[]{:S(2)}) collective-permute-start(bf16[256,1792]{1,0:T(8,128)(2,1)} %fusion.19), channel_id=1, source_target_pairs={{0,2},{1,3},{2,0},{3,1},{4,6},{5,7},{6,4},{7,5},{8,10},{9,11},{10,... | collective-permute-start | bytes 2752520 | tf_op jit(solution)/shard_map/ppermute | solution.py:35
  549.3 1.3 collective-permute-start.32
  550.6 17.8 %collective-permute-start.33 = (f32[128,128]{1,0:T(8,128)S(1)}, f32[128,128]{1,0:T(8,128)S(1)}, u32[]{:S(2)}, u32[]{:S(2)}) collective-permute-start(f32[128,128]{1,0:T(8,128)S(1)} %add.761), channel_id=1, source_target_pairs={{0,2},{1,3},{2,0},{3,1},{4,6},{5,7},{6,4},{7,5},{8,10},{9,11},{10,... | collective-permute-start | bytes 196616 | tf_op jit(solution)/shard_map/ppermute | solution.py:35
  568.4 10.3 %collective-permute-start.34 = (f32[32,128]{1,0:T(8,128)S(1)}, f32[32,128]{1,0:T(8,128)S(1)}, u32[]{:S(2)}, u32[]{:S(2)}) collective-permute-start(f32[32,128]{1,0:T(8,128)S(1)} %dynamic-slice_add_fusion), channel_id=1, source_target_pairs={{0,4},{1,5},{2,6},{3,7},{4,0},{5,1},{6,2},{7,3},{8,12},{9,13},{10,... | collective-permute-start | bytes 49160 | tf_op jit(solution)/shard_map/ppermute | solution.py:35
  573.7 58.9 %copy-start.94 = (bf16[256,1792]{1,0:T(8,128)(2,1)S(1)}, bf16[256,1792]{1,0:T(8,128)(2,1)}, u32[]{:S(2)}) copy-start(bf16[256,1792]{1,0:T(8,128)(2,1)} %copy-done.93) | copy-start | bytes 2752516
  573.7 58.8 %collective-permute-start.45 = (bf16[128,2560]{1,0:T(8,128)(2,1)S(1)}, bf16[128,2560]{1,0:T(8,128)(2,1)}, u32[]{:S(2)}, u32[]{:S(2)}) collective-permute-start(bf16[128,2560]{1,0:T(8,128)(2,1)S(1)} %fusion.76), channel_id=1, source_target_pairs={{0,4},{1,5},{2,6},{3,7},{4,0},{5,1},{6,2},{7,3},{8,12},{9,13},{10,... | collective-permute-start | bytes 1966088 | tf_op jit(solution)/shard_map/ppermute | solution.py:35
  578.7 56.6 %collective-permute-start.35 = (f32[32,128]{1,0:T(8,128)S(1)}, f32[32,128]{1,0:T(8,128)S(1)}, u32[]{:S(2)}, u32[]{:S(2)}) collective-permute-start(f32[32,128]{1,0:T(8,128)S(1)} %add.764), channel_id=1, source_target_pairs={{0,8},{1,9},{2,10},{3,11},{4,12},{5,13},{6,14},{7,15},{8,0},{9,1},... | collective-permute-start | bytes 49160 | tf_op jit(solution)/shard_map/ppermute | solution.py:35
  631.1 73.4 %collective-permute-start.40 = (bf16[128,9728]{1,0:T(8,128)(2,1)}, bf16[128,9728]{1,0:T(8,128)(2,1)}, u32[]{:S(2)}, u32[]{:S(2)}) collective-permute-start(bf16[128,9728]{1,0:T(8,128)(2,1)} %all-reduce.19.cloned.1.call-done.refs_1_), channel_id=1, source_target_pairs={{0,4},{1,5},{2,6},{3,7},{4,0},{5,1},{6,2},{7,3},{8,12},{9,13},{10,... | collective-permute-start | bytes 7471112 | tf_op jit(solution)/shard_map/ppermute | solution.py:35
  635.4 6.5 collective-permute-start.36
  673.4 27.7 %collective-permute-start.46 = (bf16[128,2560]{1,0:T(8,128)(2,1)}, bf16[128,2560]{1,0:T(8,128)(2,1)S(1)}, u32[]{:S(2)}, u32[]{:S(2)}) collective-permute-start(bf16[128,2560]{1,0:T(8,128)(2,1)} %all-reduce.21.cloned.1.call-done), channel_id=1, source_target_pairs={{0,4},{1,5},{2,6},{3,7},{4,0},{5,1},{6,2},{7,3},{8,12},{9,13},{10,... | collective-permute-start | bytes 1966088 | tf_op jit(solution)/shard_map/ppermute | solution.py:35
  (175 other events, 1042.6 us)
Sparse Core Ops, SparseCore 0:
  100.0 60.3 all-gather.6
  188.8 47.6 all-gather.8
  385.3 40.0 all-gather.10
  532.3 98.8 all-reduce.18
  634.8 38.5 all-reduce.20
